TPU v7x, 32 devices: a whole 2x2x4 slice. The times are simulated.
32 devices in a mesh: dp: 8 (over y, x, core), tensor: 4 (over z).
Axes of the slice: x: 2, y: 2, z: 4, core: 2. Of those that a mesh axis runs over, the one named last changes fastest.
Arguments:
- tokens: bfloat16 [8, 2048, 2048], P('dp', 'tensor'), may hold values from -6 to 6
- cotangent: bfloat16 [8, 2048, 2048], P('dp', 'tensor'), may hold values from -6 to 6
- lengths: int32 [8], P('dp'), may hold values from 512 to 2048, as said below
- adapter_ids: int32 [8], P('dp'), may hold values from 0 to 7, as said below
- pre_gain: float32 [2048], replicated, may hold values from 0.1 to 1.9
- in_inner: bfloat16 [2048, 2, 4096], P('dp', None, 'tensor'), may hold values from -0.125 to 0.125
- in_maps: bfloat16 [2048, 256], P('dp'), may hold values from -0.125 to 0.125
- in_steps: bfloat16 [2048, 64], P('dp', 'tensor'), may hold values from -0.125 to 0.125
- conv_inner: float32 [4, 4096], P(None, 'tensor'), may hold values from -3 to 3
- conv_maps: float32 [4, 256], replicated, may hold values from -3 to 3
- step_bias: float32 [64], P('tensor'), may hold values from -8 to -3
- decay_log: float32 [64], P('tensor'), may hold values from 0 to 2.77
- skip_gain: float32 [64], P('tensor'), may hold values from 0.5 to 1.5
- norm_gain: float32 [4096], P('tensor'), may hold values from 0.1 to 1.9
- out_weight: bfloat16 [4096, 2048], P('tensor', 'dp'), may hold values from -0.09375 to 0.09375
- adapter_in_down: bfloat16 [8, 2048, 16], replicated, may hold values from -0.125 to 0.125
- adapter_in_up: bfloat16 [8, 16, 2, 4096], P(None, None, None, 'tensor'), may hold values from -0.75 to 0.75
- adapter_out_down: bfloat16 [8, 4096, 16], P(None, 'tensor'), may hold values from -0.09375 to 0.09375
- adapter_out_up: bfloat16 [8, 16, 2048], replicated, may hold values from -0.75 to 0.75
Outputs:
- mixed: bfloat16 [8, 2048, 2048], P('dp', 'tensor')
- tokens_grad: bfloat16 [8, 2048, 2048], P('dp', 'tensor')
- adapter_in_down_grad: float32 [8, 2048, 16], replicated
- adapter_in_up_grad: float32 [8, 16, 2, 4096], P(None, None, None, 'tensor')
- adapter_out_down_grad: float32 [8, 4096, 16], P(None, 'tensor')
- adapter_out_up_grad: float32 [8, 16, 2048], replicated
Inputs may be any that keep to these rules, and one draw needn't show every extreme that they name: `lengths`: the valid positions of a sequence come first; the rest of its slot is padding. `adapter_ids`: every adapter is used by at least one sequence.
All inputs are finite; a program needn't handle non-finite values.
Results may differ from a plain program's by a relative error of at most 0.0072.
Values may be sent and summed in bfloat16 or wider, within the bound.
No kernel may reach another device: no remote copies, remote signals or barrier semaphores. Data moves between devices by JAX's collectives and lax.ppermute only.
A program may use at most 320 MiB of HBM per device.

v0:
```python
import jax
import jax.numpy as jnp
from jax import lax
from jax.sharding import PartitionSpec as P

BLOCK = 256


epsilon = 1e-05
highest = lax.Precision.HIGHEST


def causal_conv(values, kernel):
    tap_count = kernel.shape[0]
    row_count = values.shape[0]
    padded = jnp.pad(values, ((tap_count - 1, 0), (0, 0)))
    running = padded[0:row_count] * kernel[0]
    for tap_index in range(1, tap_count):
        running = running + padded[tap_index : tap_index + row_count] * kernel[tap_index]
    return running


def block_terms(pieces):
    values, b_block, c_block, log_decay = pieces
    cumulative = jnp.cumsum(log_decay, axis=0)
    cum_heads = cumulative.T
    gap_log = cum_heads[:, :, None] - cum_heads[:, None, :]
    block_size = log_decay.shape[0]
    causal_mask = jnp.arange(block_size)[:, None] >= jnp.arange(block_size)[None, :]
    decay_mask = jnp.where(causal_mask, jnp.exp(jnp.where(causal_mask, gap_log, 0.0)), 0.0)
    inner_terms = jnp.dot(c_block, b_block.T, precision=highest)
    weighting = decay_mask * inner_terms
    within = jnp.einsum("hij,jhp->ihp", weighting, values, precision=highest)
    to_end = jnp.exp(cumulative[-1][None, :] - cumulative)
    block_state = jnp.einsum("jh,jhp,js->hps", to_end, values, b_block, precision=highest)
    return (within, block_state, cumulative)


def mix_heads(
    inner_raw,
    maps_raw,
    steps_raw,
    conv_inner,
    conv_maps,
    step_bias,
    decay_log,
    skip_gain,
    block_len,
):
    row_count = inner_raw.shape[0]
    head_count = steps_raw.shape[1]
    head_width = inner_raw.shape[1] // head_count
    state_width = maps_raw.shape[1] // 2
    inner_conv = jax.nn.silu(causal_conv(inner_raw, conv_inner))
    maps_conv = jax.nn.silu(causal_conv(maps_raw, conv_maps))
    delta = jax.nn.softplus(steps_raw + step_bias)
    rates = -delta * jnp.exp(decay_log)
    blocks = row_count // block_len
    scaled = inner_conv.reshape(row_count, head_count, head_width) * delta[:, :, None]
    pieces = (
        scaled.reshape(blocks, block_len, head_count, head_width),
        maps_conv[:, :state_width].reshape(blocks, block_len, state_width),
        maps_conv[:, state_width:].reshape(blocks, block_len, state_width),
        rates.reshape(blocks, block_len, head_count),
    )
    within, states, cumulative = lax.map(jax.checkpoint(block_terms), pieces)

    def carry_step(carried, inputs):
        state_here, totals = inputs
        return (carried * jnp.exp(totals)[:, None, None] + state_here, carried)

    initial = jnp.zeros((head_count, head_width, state_width), jnp.float32)
    _, entering = lax.scan(carry_step, initial, (states, cumulative[:, -1, :]))
    carried_out = jnp.einsum(
        "cis,chps,cih->cihp", pieces[2], entering, jnp.exp(cumulative), precision=highest
    )
    mixed_inner = (within + carried_out).reshape(row_count, head_count * head_width)
    return mixed_inner + inner_conv * jnp.repeat(skip_gain, head_width)


def body(
    tokens,
    cotangent,
    lengths,
    adapter_ids,
    pre_gain,
    in_inner,
    in_maps,
    in_steps,
    conv_inner,
    conv_maps,
    step_bias,
    decay_log,
    skip_gain,
    norm_gain,
    out_weight,
    adapter_in_down,
    adapter_in_up,
    adapter_out_down,
    adapter_out_up,
):
    groups = lax.axis_size("tensor")
    place = lax.axis_index("tensor")
    share = tokens.shape[1]
    seq_total = share * groups
    width = tokens.shape[2]
    inner_here = in_inner.shape[2]
    inner_all = inner_here * groups
    rank_size = adapter_in_down.shape[2]
    adapter_count = adapter_in_down.shape[0]
    residual = tokens[0].astype(jnp.float32)
    stat = jnp.mean(residual * residual, axis=-1, keepdims=True)
    root_inv = lax.rsqrt(stat + epsilon)
    normed_low = (residual * root_inv * pre_gain).astype(jnp.bfloat16)
    gathered = lax.all_gather(normed_low, "tensor", axis=0, tiled=True)
    inner_w, maps_w, steps_w = (
        lax.all_gather(in_inner, "dp", axis=0, tiled=True),
        lax.all_gather(in_maps, "dp", axis=0, tiled=True),
        lax.all_gather(in_steps, "dp", axis=0, tiled=True),
    )
    out_w = lax.all_gather(out_weight, "dp", axis=1, tiled=True)
    pick = adapter_ids[0]
    down_in = lax.dynamic_index_in_dim(adapter_in_down, pick, 0, keepdims=False)
    up_in = (
        lax.dynamic_index_in_dim(adapter_in_up, pick, 0, keepdims=False)
        .reshape(rank_size, 2 * inner_here)
        .astype(jnp.float32)
    )
    down_out = lax.dynamic_index_in_dim(adapter_out_down, pick, 0, keepdims=False)
    up_out_raw = lax.dynamic_index_in_dim(adapter_out_up, pick, 0, keepdims=False)
    up_out = up_out_raw.astype(jnp.float32)
    low_hidden = jnp.dot(gathered, down_in, preferred_element_type=jnp.float32)
    gate_inner = jnp.dot(
        gathered, inner_w.reshape(width, 2 * inner_here), preferred_element_type=jnp.float32
    )
    gate_inner = gate_inner + jnp.dot(low_hidden, up_in, precision=highest)
    paired = gate_inner.reshape(seq_total, 2, inner_here)
    gate_part = paired[:, 0]
    inner_raw = paired[:, 1]
    maps_raw = jnp.dot(gathered, maps_w, preferred_element_type=jnp.float32)
    steps_raw = jnp.dot(gathered, steps_w, preferred_element_type=jnp.float32)

    def local_mix(inner_in, maps_in, steps_in):
        return mix_heads(
            inner_in,
            maps_in,
            steps_in,
            conv_inner,
            conv_maps,
            step_bias,
            decay_log,
            skip_gain,
            BLOCK,
        )

    mixed_inner, mix_back = jax.vjp(local_mix, inner_raw, maps_raw, steps_raw)
    sigmoid_gate = jax.nn.sigmoid(gate_part)
    silu_gate = gate_part * sigmoid_gate
    gated = mixed_inner * silu_gate
    squares = lax.psum(jnp.sum(gated * gated, axis=-1), "tensor")
    scale_row = lax.rsqrt(squares / inner_all + epsilon)[:, None]
    out_low = (gated * scale_row * norm_gain).astype(jnp.bfloat16)
    positions = place * share + jnp.arange(share)
    valid = (positions < lengths[0]).astype(jnp.float32)[:, None]
    masked_cot = (cotangent[0].astype(jnp.float32) * valid).astype(jnp.bfloat16)
    out_hidden = jnp.dot(out_low, down_out, preferred_element_type=jnp.float32)
    partial_out = jnp.dot(out_low, out_w, preferred_element_type=jnp.float32) + jnp.dot(
        out_hidden, up_out, precision=highest
    )
    summed = lax.psum_scatter(partial_out, "tensor", scatter_dimension=0, tiled=True)
    mixed = (valid * (residual + summed)).astype(jnp.bfloat16)[None]
    cot_all = lax.all_gather(masked_cot, "tensor", axis=0, tiled=True)
    inner_back, maps_back, steps_back = (
        lax.all_gather(in_inner, "dp", axis=0, tiled=True),
        lax.all_gather(in_maps, "dp", axis=0, tiled=True),
        lax.all_gather(in_steps, "dp", axis=0, tiled=True),
    )
    out_back = lax.all_gather(out_weight, "dp", axis=1, tiled=True)
    back_hidden = jnp.einsum("ld,rd->lr", cot_all, up_out_raw, preferred_element_type=jnp.float32)
    d_out = jnp.einsum("ld,kd->lk", cot_all, out_back, preferred_element_type=jnp.float32)
    d_out = d_out + jnp.einsum(
        "lr,kr->lk", back_hidden, down_out.astype(jnp.float32), precision=highest
    )
    grad_out_up = jnp.einsum(
        "lr,ld->rd", out_hidden, cot_all.astype(jnp.float32), precision=highest
    )
    grad_out_down = jnp.einsum(
        "lk,lr->kr", out_low.astype(jnp.float32), back_hidden, precision=highest
    )
    weighted = d_out * norm_gain
    dots = lax.psum(jnp.sum(weighted * gated, axis=-1), "tensor")
    cubed = scale_row * scale_row * scale_row
    d_gated = scale_row * weighted - gated * cubed * (dots / inner_all)[:, None]
    d_mixed = d_gated * silu_gate
    d_gate = d_gated * mixed_inner * sigmoid_gate * (1.0 + gate_part * (1.0 - sigmoid_gate))
    d_inner, d_maps, d_steps = mix_back(d_mixed)
    d_pair = (
        jnp.stack([d_gate, d_inner], axis=1).reshape(seq_total, 2 * inner_here).astype(jnp.bfloat16)
    )
    d_steps_low = d_steps.astype(jnp.bfloat16)
    d_pair_wide = d_pair.astype(jnp.float32)
    d_low_in = jnp.dot(d_pair_wide, up_in.T, precision=highest)
    maps_high = d_maps.astype(jnp.bfloat16)
    maps_rest = (d_maps - maps_high.astype(jnp.float32)).astype(jnp.bfloat16)
    d_normed = jnp.einsum(
        "lk,dk->ld",
        d_pair,
        inner_back.reshape(width, 2 * inner_here),
        preferred_element_type=jnp.float32,
    )
    d_normed = d_normed + jnp.einsum(
        "ls,ds->ld", maps_high, maps_back, preferred_element_type=jnp.float32
    )
    d_normed = d_normed + jnp.einsum(
        "ls,ds->ld", maps_rest, maps_back, preferred_element_type=jnp.float32
    )
    d_normed = d_normed + jnp.einsum(
        "lh,dh->ld", d_steps_low, steps_back, preferred_element_type=jnp.float32
    )
    d_normed = d_normed + jnp.einsum(
        "lr,dr->ld", d_low_in, down_in.astype(jnp.float32), precision=highest
    )
    grad_in_up = jnp.einsum("lr,lk->rk", low_hidden, d_pair_wide, precision=highest)
    grad_in_down = jnp.einsum(
        "ld,lr->dr", gathered.astype(jnp.float32), d_low_in, precision=highest
    )
    d_rows = lax.psum_scatter(d_normed, "tensor", scatter_dimension=0, tiled=True)
    d_scaled = d_rows * pre_gain
    d_resid = root_inv * d_scaled - residual * root_inv * root_inv * root_inv * jnp.mean(
        d_scaled * residual, axis=-1, keepdims=True
    )
    tokens_grad = (masked_cot.astype(jnp.float32) + d_resid).astype(jnp.bfloat16)[None]
    chosen = (jnp.arange(adapter_count) == pick).astype(jnp.float32)
    shared = lax.psum(
        (chosen[:, None, None] * grad_in_down[None], chosen[:, None, None] * grad_out_up[None]),
        ("dp", "tensor"),
    )
    headwise = lax.psum(
        (
            chosen[:, None, None, None] * grad_in_up.reshape(rank_size, 2, inner_here)[None],
            chosen[:, None, None] * grad_out_down[None],
        ),
        "dp",
    )
    return (mixed, tokens_grad, shared[0], headwise[0], headwise[1], shared[1])


def solution(mesh):
    placed = (
        P("dp", "tensor", None),
        P("dp", "tensor", None),
        P("dp"),
        P("dp"),
        P(),
        P("dp", None, "tensor"),
        P("dp", None),
        P("dp", "tensor"),
        P(None, "tensor"),
        P(),
        P("tensor"),
        P("tensor"),
        P("tensor"),
        P("tensor"),
        P("tensor", "dp"),
        P(),
        P(None, None, None, "tensor"),
        P(None, "tensor", None),
        P(),
    )
    return jax.shard_map(
        body,
        mesh=mesh,
        in_specs=placed,
        out_specs=(
            P("dp", "tensor", None),
            P("dp", "tensor", None),
            P(),
            P(None, None, None, "tensor"),
            P(None, "tensor", None),
            P(),
        ),
        check_vma=False,
    )
```

profile of v0, /device:TPU:0, one launch (start us, length us, event | category | flops | bytes accessed | tf_op | source)
XLA Modules:
  0.0 2131.2 jit_solution(9511696662606335599)
XLA Ops:
  23.0 10.5 all_gather.24
  34.3 131.9 %all-gather.6.cloned.1.call-done = bf16[2048,2048]{1,0:T(8,128)(2,1)} async-done(((bf16[512,2048]{1,0:T(8,128)(2,1)}), bf16[2048,2048]{1,0:T(8,128)(2,1)}) %all-gather.6.cloned.1.call-update) | async-done | bytes 8388624 | tf_op jit(solution)/shard_map/all_gather | solution.py:115
  178.0 9.8 copy.108
  193.4 122.7 %all-gather.14.cloned.1.call-done = bf16[2048,2048]{1,0:T(8,128)(2,1)} async-done(((bf16[512,2048]{1,0:T(8,128)(2,1)}), bf16[2048,2048]{1,0:T(8,128)(2,1)}) %all-gather.14.cloned.1.call-update) | async-done | bytes 8388624 | tf_op jit(solution)/shard_map/all_gather | solution.py:172
  322.4 17.4 all-gather.10.cloned.1.call-done
  348.6 30.4 %all-gather.12.cloned.1.call-done = bf16[1024,2048]{1,0:T(8,128)(2,1)} async-done(((bf16[1024,256]{1,0:T(8,128)(2,1)}), bf16[1024,2048]{1,0:T(8,128)(2,1)}) %all-gather.12.cloned.1.call-update) | async-done | bytes 4194320 | tf_op jit(solution)/shard_map/all_gather | solution.py:121
  379.0 14.5 fusion.180
  393.5 42.3 %all-gather.8.cloned.1.call-done = bf16[2048,2,1024]{2,0,1:T(8,128)(2,1)} async-done(((bf16[256,2,1024]{2,0,1:T(8,128)(2,1)}), bf16[2048,2,1024]{2,0,1:T(8,128)(2,1)}) %all-gather.8.cloned.1.call-update) | async-done | bytes 8388624 | tf_op jit(solution)/shard_map/all_gather | solution.py:117
  435.8 11.6 copy.89
  447.4 24.6 %fusion.177 = f32[2048,2048]{0,1:T(8,128)} fusion(bf16[2048,2048]{1,0:T(8,128)(2,1)} %all-gather.6.cloned.1.call-done, bf16[2048,2048]{0,1:T(8,128)(2,1)} %bitcast.501), kind=kOutput, calls=%fused_computation.266 | convolution fusion | flops 17179869184 | bytes 33554432 | tf_op jit(solution)/shard_map/dot_general | solution.py:133
  472.1 10.8 convolution_add_fusion.2
  489.4 9.3 copy.134
  498.7 18.0 fusion.96
  516.7 9.3 copy.91
  546.9 99.0 %while.75 = (s32[]{:T(128)}, f32[8,256,16,64]{1,3,2,0:T(8,128)}, f32[8,16,64,128]{3,2,1,0:T(8,128)}, f32[8,256,16]{1,2,0:T(8,128)S(1)}, f32[8,256,16,64]{1,3,2,0...) while((s32[]{:T(128)}, f32[8,256,16,64]{1,3,2,0:T(8,128)}, ...), condition=%wide.region_4.5_spmd.clone.clone, body=%wide.region_1.4_spmd.clone.clone.sunk | while | flops 1313615872 | bytes 4888953 | solution.py:66
  651.0 20.9 while.76
  673.4 13.6 fusion.94
  687.0 14.5 copy.126
  701.5 14.5 reshape.357
  716.0 9.8 copy.135
  725.8 19.1 multiply_reduce_fusion.4
  744.9 18.7 all-reduce.16
  763.7 18.2 fusion.93
  783.0 10.5 fusion.113
  793.4 13.3 reshape.359
  806.8 13.9 copy.104
  820.7 12.0 fusion.86
  842.5 23.8 %while.77 = (s32[]{:T(128)}, f32[16,64,128]{2,1,0:T(8,128)S(1)}, f32[8,16,64,128]{3,2,1,0:T(8,128)}, f32[8,16]{1,0:T(8,128)S(1)}, f32[8,16,64,128]{3,2,1,0:T(8,1...) while((s32[]{:T(128)}, f32[16,64,128]{2,1,0:T(8,128)S(1)}, ...), condition=%wide.region_14.15_spmd.clone, body=%wide.region_12.14_spmd.clone.sunk | while | flops 786436 | bytes 3146456 | solution.py:73
  878.0 264.8 %while.74 = (s32[]{:T(128)}, f32[8,256,16,64]{1,3,2,0:T(8,128)}, f32[8,256,128]{2,1,0:T(8,128)}, f32[8,256,128]{2,1,0:T(8,128)}, f32[8,256,16]{1,0,2:T(8,128)}, ...) while((s32[]{:T(128)}, f32[8,256,16,64]{1,3,2,0:T(8,128)}, ...), condition=%wide.region_24.25_spmd, body=%wide.region_15.24_spmd.sunk | while | flops 2736062464 | bytes 28248832 | solution.py:66
  1142.8 14.5 copy.127
  1157.3 14.7 reshape.358
  1172.0 19.1 broadcast_multiply_fusion.1
  1191.2 9.9 broadcast_multiply_fusion.2
  1201.1 12.0 fusion.81
  1219.4 12.1 copy.112
  1238.9 13.4 fusion.126
  1269.2 10.4 fusion.142
  1279.7 8.3 fusion.137
  1291.4 22.3 %fusion.175 = f32[2048,2048,1]{1,0,2:T(8,128)} fusion(bf16[2048,2,1024]{2,0,1:T(8,128)(2,1)} %all-gather.8.cloned.1.call-done, bf16[2048,1,1024]{2,0,1:T(8,128)(2,1)S(1)} %copy-done.13, bf16[2048,1,1024]{2,0,1:T(8,128)(2,1)S(1)} %copy-done.12), kind=kOutput, calls=%fused_computation.264 | convolution fusion | flops 17184063488 | bytes 33554432 | tf_op jit(solution)/shard_map/lk,dk->ld/dot_general | solution.py:205
  1313.7 8.1 fusion.130
  1321.8 28.6 %fusion.78 = f32[2048,2048]{1,0:T(8,128)} fusion(f32[2048,2048]{1,0:T(8,128)} %fusion.142, f32[2048,2048]{1,0:T(8,128)} %fusion.137, f32[2048,2048]{1,0:T(8,128)} %fusion.130, f32[2048,2048,1]{1,0,2:T(8,128)} %fusion.175, bf16[2048,256]{1,0:T(8,128)(2,1)} %all-gather.10.cloned.1.call-done, f32[2048,256]{1,0:T(8,128)S(1)} %pad_add_fusion.3), kind=kOutput, calls=%fused_computation.112 | convolution fusion | flops 2166358016 | bytes 87031808 | tf_op jit(solution)/shard_map/ls,ds->ld/dot_general | solution.py:214
  1353.9 12.6 fusion.179
  1366.5 12.0 convolution_add_fusion.1
  1379.4 9.3 fusion.82
  1407.1 221.0 %reduce-scatter.5.cloned.1.call-done = f32[512,2048]{1,0:T(8,128)} async-done(((f32[2048,2048]{1,0:T(8,128)}), f32[512,2048]{1,0:T(8,128)}) %reduce-scatter.5.cloned.1.call-update) | async-done | bytes 4194320 | tf_op jit(solution)/shard_map/reduce_scatter | solution.py:227
  1630.9 280.7 %reduce-scatter.3.cloned.1.call-done = f32[512,2048]{1,0:T(8,128)} async-done(((f32[2048,2048]{1,0:T(8,128)}), f32[512,2048]{1,0:T(8,128)}) %reduce-scatter.3.cloned.1.call-update) | async-done | bytes 4194320 | tf_op jit(solution)/shard_map/reduce_scatter | solution.py:170
  1918.1 57.2 %all-reduce.22.cloned.1.call-done = (f32[8,16,2,1024]{3,2,1,0:T(2,128)}, f32[8,1024,16]{1,2,0:T(8,128)}) async-done(((f32[8,16,2,1024]{3,2,1,0:T(2,128)}, f32[8,1024,16]{1,2,0:T(8,128)}), (f32[8,16,2,1024]{3,2,1,0:T(2,128)}, f32[8,1024,16]{1,2,0:T(8,128)})) %all-reduce.22.cloned.1.call-update) | async-done | bytes 1572880 | tf_op jit(solution)/shard_map/psum | solution.py:238
  1975.3 140.4 %all-reduce.20.cloned.1.call-done = (f32[8,2048,16]{1,2,0:T(8,128)}, f32[8,16,2048]{2,1,0:T(8,128)}) async-done(((f32[8,2048,16]{1,2,0:T(8,128)}, f32[8,16,2048]{2,1,0:T(8,128)}), (f32[8,2048,16]{1,2,0:T(8,128)}, f32[8,16,2048]{2,1,0:T(8,128)})) %all-reduce.20.cloned.1.call-update) | async-done | bytes 2097168 | tf_op jit(solution)/shard_map/psum | solution.py:234
  (708 shorter events, 585.7 us)
Async XLA Ops:
  7.2 180.6 %copy-start = (bf16[8,2048,16]{1,2,0:T(8,128)(2,1)S(1)}, bf16[8,2048,16]{1,2,0:T(8,128)(2,1)}, u32[]{:S(2)}) copy-start(bf16[8,2048,16]{1,2,0:T(8,128)(2,1)} %param.42) | copy-start | bytes 1572868
  7.2 158.9 %all-gather.6.cloned.1.call-start = ((), (), s32[]{:S(2)}) async-start(), calls=%async_computation.2 | async-start | bytes 10485760 | tf_op jit(solution)/shard_map/all_gather | solution.py:115
  9.5 12.7 copy-start.71
  9.5 12.7 copy-start.70
  9.5 13.5 copy-start.66
  10.1 24.0 %copy-start.69 = (f32[4,256]{1,0:T(4,128)S(1)}, f32[4,256]{1,0:T(4,128)}, u32[]{:S(2)}) copy-start(f32[4,256]{1,0:T(4,128)} %param.36) | copy-start | bytes 12292
  10.1 24.1 %copy-start.55 = (f32[4,1024]{1,0:T(4,128)S(1)}, f32[4,1024]{1,0:T(4,128)}, u32[]{:S(2)}) copy-start(f32[4,1024]{1,0:T(4,128)} %param.35) | copy-start | bytes 49156
  10.1 156.0 %copy-start.67 = (f32[16]{0:T(128)S(1)}, f32[16]{0:T(128)}, u32[]{:S(2)}) copy-start(f32[16]{0:T(128)} %param.37) | copy-start | bytes 196
  13.6 302.5 %all-gather.14.cloned.1.call-start = ((), (), s32[]{:S(2)}) async-start(), calls=%async_computation.7 | async-start | bytes 10485760 | tf_op jit(solution)/shard_map/all_gather | solution.py:172
  16.7 323.2 %all-gather.10.cloned.1.call-start = ((), (), s32[]{:S(2)}) async-start(), calls=%async_computation.4 | async-start | bytes 1179648 | tf_op jit(solution)/shard_map/all_gather | solution.py:118
  17.4 361.6 %all-gather.12.cloned.1.call-start = ((), (), s32[]{:S(2)}) async-start(), calls=%async_computation.5 | async-start | bytes 4718592 | tf_op jit(solution)/shard_map/all_gather | solution.py:121
  18.0 417.8 %all-gather.8.cloned.1.call-start = ((), (), s32[]{:S(2)}) async-start(), calls=%async_computation.3 | async-start | bytes 9437184 | tf_op jit(solution)/shard_map/all_gather | solution.py:117
  20.5 1607.5 %reduce-scatter.5.cloned.1.call-start = ((), (), s32[]{:S(2)}) async-start(), calls=%async_computation.8 | async-start | bytes 20971520 | tf_op jit(solution)/shard_map/reduce_scatter | solution.py:227
  22.2 449.9 %copy-start.29 = (bf16[2,8,2,1024]{3,1,2,0:T(8,128)(2,1)}, bf16[2,8,2,1024]{3,1,2,0:T(8,128)(2,1)S(1)}, u32[]{:S(2)}) copy-start(bf16[2,8,2,1024]{3,1,2,0:T(8,128)(2,1)S(1)} %copy.162) | copy-start | bytes 196612
  22.2 155.8 %copy-start.56 = (f32[16]{0:T(128)}, f32[16]{0:T(128)S(1)}, u32[]{:S(2)}) copy-start(f32[16]{0:T(128)S(1)} %exp.78) | copy-start | bytes 196
  33.5 144.5 %copy-start.34 = (bf16[2048,16]{0,1:T(8,128)(2,1)}, bf16[2048,16]{0,1:T(8,128)(2,1)S(1)}, u32[]{:S(2)}) copy-start(bf16[2048,16]{0,1:T(8,128)(2,1)S(1)} %all_gather.24) | copy-start | bytes 196612
  34.2 311.8 %copy-start.58 = (f32[1,256]{1,0:T(1,128)}, f32[1,256]{1,0:T(1,128)S(1)}, u32[]{:S(2)}) copy-start(f32[1,256]{1,0:T(1,128)S(1)} %get-tuple-element.868) | copy-start | bytes 3076
  34.2 311.8 %copy-start.60 = (f32[1,256]{1,0:T(1,128)}, f32[1,256]{1,0:T(1,128)S(1)}, u32[]{:S(2)}) copy-start(f32[1,256]{1,0:T(1,128)S(1)} %get-tuple-element.869) | copy-start | bytes 3076
  34.2 311.8 %copy-start.62 = (f32[1,256]{1,0:T(1,128)}, f32[1,256]{1,0:T(1,128)S(1)}, u32[]{:S(2)}) copy-start(f32[1,256]{1,0:T(1,128)S(1)} %get-tuple-element.871) | copy-start | bytes 3076
  34.2 311.8 %copy-start.64 = (f32[1,256]{1,0:T(1,128)}, f32[1,256]{1,0:T(1,128)S(1)}, u32[]{:S(2)}) copy-start(f32[1,256]{1,0:T(1,128)S(1)} %get-tuple-element.870) | copy-start | bytes 3076
  34.2 464.4 %copy-start.41 = (f32[1,1024]{1,0:T(1,128)}, f32[1,1024]{1,0:T(1,128)S(1)}, u32[]{:S(2)}) copy-start(f32[1,1024]{1,0:T(1,128)S(1)} %get-tuple-element.862) | copy-start | bytes 12292
  34.2 464.4 %copy-start.43 = (f32[1,1024]{1,0:T(1,128)}, f32[1,1024]{1,0:T(1,128)S(1)}, u32[]{:S(2)}) copy-start(f32[1,1024]{1,0:T(1,128)S(1)} %get-tuple-element.863) | copy-start | bytes 12292
  34.2 464.4 %copy-start.45 = (f32[1,1024]{1,0:T(1,128)}, f32[1,1024]{1,0:T(1,128)S(1)}, u32[]{:S(2)}) copy-start(f32[1,1024]{1,0:T(1,128)S(1)} %get-tuple-element.865) | copy-start | bytes 12292
  34.2 464.4 %copy-start.49 = (f32[1,1024]{1,0:T(1,128)}, f32[1,1024]{1,0:T(1,128)S(1)}, u32[]{:S(2)}) copy-start(f32[1,1024]{1,0:T(1,128)S(1)} %get-tuple-element.864) | copy-start | bytes 12292
  193.4 278.6 %copy-start.25 = (f32[2048,16]{0,1:T(8,128)}, f32[2048,16]{0,1:T(8,128)S(1)}, u32[]{:S(2)}) copy-start(f32[2048,16]{0,1:T(8,128)S(1)} %fusion.144) | copy-start | bytes 393220
  546.9 104.0 %copy-start.6 = (f32[16,64,128]{2,1,0:T(8,128)S(1)}, f32[16,64,128]{2,1,0:T(8,128)}, u32[]{:S(2)}) copy-start(f32[16,64,128]{2,1,0:T(8,128)} %custom-call) | copy-start | bytes 1572868
  673.4 147.4 %copy-start.27 = (f32[8,256,16]{1,2,0:T(8,128)}, f32[8,256,16]{1,2,0:T(8,128)S(1)}, u32[]{:S(2)}) copy-start(f32[8,256,16]{1,2,0:T(8,128)S(1)} %copy.95) | copy-start | bytes 393220
  763.7 18.2 copy-start.2
  763.7 19.3 copy-start.8
  1157.3 14.7 copy-start.48
  1157.3 14.7 copy-start.50
  1172.0 19.2 copy-start.42
  1172.0 19.2 copy-start.44
  1172.0 19.1 copy-start.46
  1236.3 16.0 copy-start.20
  1236.3 16.0 copy-start.24
  1236.3 16.0 copy-start.65
  1238.9 15.6 copy-start.59
  1238.9 15.6 copy-start.61
  1238.9 15.6 copy-start.63
  1291.4 22.3 %copy-start.22 = (bf16[2048,256]{1,0:T(8,128)(2,1)S(1)}, bf16[2048,256]{1,0:T(8,128)(2,1)}, u32[]{:S(2)}) copy-start(bf16[2048,256]{1,0:T(8,128)(2,1)} %all-gather.10.cloned.1.call-done) | copy-start | bytes 3145732
  1350.4 561.2 %reduce-scatter.3.cloned.1.call-start = ((), (), s32[]{:S(2)}) async-start(), calls=%async_computation.6 | async-start | bytes 20971520 | tf_op jit(solution)/shard_map/reduce_scatter | solution.py:170
  1378.5 596.8 %all-reduce.22.cloned.1.call-start = ((), (), s32[]{:S(2)}) async-start(), calls=%async_computation.10 | async-start | bytes 3145728 | tf_op jit(solution)/shard_map/psum | solution.py:238
  1392.9 722.8 %all-reduce.20.cloned.1.call-start = ((), (), s32[]{:S(2)}) async-start(), calls=%async_computation.9 | async-start | bytes 4194304 | tf_op jit(solution)/shard_map/psum | solution.py:234
  1398.9 229.2 %copy-start.7 = (bf16[1,512,2048]{2,1,0:T(8,128)(2,1)S(1)}, bf16[1,512,2048]{2,1,0:T(8,128)(2,1)}, u32[]{:S(2)}) copy-start(bf16[1,512,2048]{2,1,0:T(8,128)(2,1)} %param.27) | copy-start | bytes 6291460
  1398.9 229.2 %copy-start.39 = (f32[2048]{0:T(1024)S(1)}, f32[2048]{0:T(1024)}, u32[]{:S(2)}) copy-start(f32[2048]{0:T(1024)} %param.31) | copy-start | bytes 24580
  1404.8 506.8 %copy-start.52 = (f32[512]{0:T(512)S(1)}, f32[512]{0:T(512)}, u32[]{:S(2)}) copy-start(f32[512]{0:T(512)} %copy-done.51) | copy-start | bytes 6148
  1404.8 506.8 %copy-start.54 = (f32[512]{0:T(512)S(1)}, f32[512]{0:T(512)}, u32[]{:S(2)}) copy-start(f32[512]{0:T(512)} %copy-done.53) | copy-start | bytes 6148
  (67 other events, 450.6 us)
Sparse Core Ops, SparseCore 0:
  13.7 152.3 all-gather.5
  168.2 147.8 all-gather.13
  318.0 21.7 all-gather.9
  341.5 37.4 all-gather.11
  381.3 54.3 all-gather.7
  1350.5 277.4 reduce-scatter.4
  1630.5 281.0 reduce-scatter.2
  1915.5 59.7 all-reduce.21
  1982.3 133.3 all-reduce.19
where the time goes:
time: 2140 us; the launch traced here: 2130 us
  waiting for transfers between devices  1050 us (49%)
  matrix products  517 us (24%)
  local copies, waits for them, and re-layouts  307 us (14%)
  other arithmetic  215 us (10%)
  blocking collectives  29.2 us (1%)
    reduce_scatter x1, waiting for transfers between devices, body(): lax.psum_scatter(partial_out, 'tensor', scatter_dimension=0, tiled=True)  281 us
    reduce_scatter x1, waiting for transfers between devices, body(): lax.psum_scatter(d_normed, 'tensor', scatter_dimension=0, tiled=True)  221 us
    dot_general x24, matrix products, block_terms(): within = jnp.einsum('hij,jhp->ihp', weighting, values, precision=highest)  157 us
    psum x1, waiting for transfers between devices, body(): lax.psum((chosen[:, None, None] * grad_in_down[None], chosen[:, None, Non...  140 us
    all_gather x1, waiting for transfers between devices, body(): gathered = lax.all_gather(normed_low, 'tensor', axis=0, tiled=True)  132 us
    all_gather x1, waiting for transfers between devices, body(): cot_all = lax.all_gather(masked_cot, 'tensor', axis=0, tiled=True)  123 us
    psum x1, waiting for transfers between devices, body(): lax.psum((chosen[:, None, None, None] * grad_in_up.reshape(rank_size, 2,...  57.2 us
    unnamed x160, local copies, waits for them, and re-layouts  54.7 us
  transfers between devices with their start and end apart: 9, of which 9 were waited for; matrix products, arithmetic and copies ran while one was open for 6% of the time, Pallas kernels for 0%

commit v1 on v0

v1 whole, which is shorter than its diff:
```python
import functools

import jax
import jax.numpy as jnp
from jax import lax
from jax.experimental import pallas as pl
from jax.experimental.pallas import tpu as pltpu
from jax.sharding import PartitionSpec as P

f32 = jnp.float32
bf16 = jnp.bfloat16
epsilon = 1e-05
highest = lax.Precision.HIGHEST
LOG2E = 1.4426950408889634
HEAD = 64
HALO = 128
SUB = 256
CB = 256

NN = ((1,), (0,))
NT = ((1,), (1,))
TN = ((0,), (0,))


def dot(a, b, dims=NN):
    return lax.dot_general(a, b, (dims, ((), ())), preferred_element_type=f32)


def compiler_params(grid_rank):
    return pltpu.CompilerParams(
        dimension_semantics=("arbitrary",) * grid_rank, vmem_limit_bytes=60 * 2**20
    )


def cost(flops, size):
    return pl.CostEstimate(flops=int(flops), bytes_accessed=int(size), transcendentals=0)


def sigmoid(v):
    return 0.5 + 0.5 * jnp.tanh(0.5 * v)


def conv_values(raw, chan):
    out = raw * chan[:, 3:4]
    for k in range(3):
        out = out + pltpu.roll(raw, 3 - k, 1) * chan[:, k : k + 1]
    return out[:, HALO:]


def per_head(values, rows):
    hb = rows.shape[0]
    parts = [values[h * HEAD : (h + 1) * HEAD] * rows[h : h + 1] for h in range(hb)]
    return jnp.concatenate(parts, axis=0)


def head_sums(values, hb):
    parts = [
        jnp.sum(values[h * HEAD : (h + 1) * HEAD], axis=0, keepdims=True) for h in range(hb)
    ]
    return jnp.concatenate(parts, axis=0)


def weight_dots(refs, orders, right, width):
    acc = None
    for ref, offsets in zip(refs, orders):
        for b, off in enumerate(offsets):
            term = dot(ref[b], right[off : off + width])
            acc = term if acc is None else acc + term
    return acc


def fwd_kernel(zo, xo, kb, hb, sub, *refs):
    nz, nx = len(zo), len(xo)
    zrefs, xrefs = refs[:nz], refs[nz : nz + nx]
    (nt, low, upz, upx, chan_r, hp_r, cumn_r, ct, bn, cbt) = refs[nz + nx : nz + nx + 10]
    z_out, xr_out, mix_out, ent_out, st_out = refs[-5:]
    chan = chan_r[...]
    hp = hp_r[...]
    length = ct.shape[1]
    z = weight_dots(zrefs, zo, nt[:, HALO:], kb) + dot(upz[...], low[:, HALO:])
    z_out[...] = z.astype(bf16)
    xr = weight_dots(xrefs, xo, nt, kb) + dot(upx[...], low[...])
    xr_out[...] = xr.astype(bf16)
    xc = conv_values(xr, chan)
    x = xc * sigmoid(xc)
    xs = per_head(x, hp[2 * hb : 3 * hb])
    xs_low = xs.astype(bf16)
    state = None
    for s in range(length // sub):
        cols = slice(s * sub, (s + 1) * sub)
        cum = hp[:hb, cols]
        rows_n = cumn_r[cols, :]
        within = []
        for h in range(hb):
            gap = jnp.minimum(cum[h : h + 1] - rows_n[:, h : h + 1], 0.0)
            weight = (jnp.exp2(gap) * cbt[s]).astype(bf16)
            within.append(dot(xs_low[h * HEAD : (h + 1) * HEAD, cols], weight))
        y = jnp.concatenate(within, axis=0)
        last = cum[:, sub - 1 : sub]
        ends = jnp.exp2(last - cum)
        add = dot(per_head(xs[:, cols], ends).astype(bf16), bn[cols, :])
        if s > 0:
            ent_out[s - 1] = state
            y = y + per_head(dot(state.astype(bf16), ct[:, cols]), jnp.exp2(cum))
            state = per_head(state, jnp.exp2(last)) + add
        else:
            state = add
        mix_out[:, cols] = y + x[:, cols] * chan[:, 4:5]
    if length // sub == 1:
        ent_out[0] = state
    st_out[...] = state


def forward_slot(j, zw, xw, zo, xo, nt, low, upz, upx, chan, hp, cumn, ct, bn, cbt, bufs):
    slots, ch = upz.shape[0], upz.shape[1]
    length = ct.shape[1]
    ext = nt.shape[1]
    hb = CB // HEAD
    ncb = ch // CB
    kb = zw[0].shape[2]
    nsub = length // SUB
    full = lambda a: pl.BlockSpec(a.shape, lambda i: (0,) * a.ndim)
    wspec = lambda a: pl.BlockSpec((a.shape[0], CB, a.shape[2]), lambda i: (0, i, 0))
    per_chan = lambda a: pl.BlockSpec((None, CB, a.shape[2]), lambda i: (j, i, 0))
    per_blk = lambda a: pl.BlockSpec((None,) + a.shape[1:], lambda i: (j * ncb + i, 0, 0))
    ops = list(zw) + list(xw) + [nt, low, upz, upx, chan, hp, cumn, ct, bn, cbt]
    specs = (
        [wspec(a) for a in list(zw) + list(xw)]
        + [full(nt), full(low), per_chan(upz), per_chan(upx), per_chan(chan)]
        + [per_blk(hp), per_blk(cumn), full(ct), full(bn), full(cbt)]
    )
    shapes = [
        jax.ShapeDtypeStruct((slots, ch, length), bf16),
        jax.ShapeDtypeStruct((slots, ch, ext), bf16),
        jax.ShapeDtypeStruct((slots, ch, length), f32),
        jax.ShapeDtypeStruct((slots, max(nsub - 1, 1), ch, 128), f32),
        jax.ShapeDtypeStruct((slots, ch, 128), f32),
    ]
    outs = [
        pl.BlockSpec((None, CB, length), lambda i: (j, i, 0)),
        pl.BlockSpec((None, CB, ext), lambda i: (j, i, 0)),
        pl.BlockSpec((None, CB, length), lambda i: (j, i, 0)),
        pl.BlockSpec((None, max(nsub - 1, 1), CB, 128), lambda i: (j, 0, i, 0)),
        pl.BlockSpec((None, CB, 128), lambda i: (j, i, 0)),
    ]
    aliases = {}
    if bufs is not None:
        aliases = {len(ops) + k: k for k in range(5)}
        ops += list(bufs)
        specs += [pl.BlockSpec(memory_space=pl.ANY)] * 5
    return pl.pallas_call(
        functools.partial(fwd_kernel, zo, xo, kb, hb, SUB),
        grid=(ncb,),
        in_specs=specs,
        out_specs=outs,
        out_shape=shapes,
        input_output_aliases=aliases,
        compiler_params=compiler_params(1),
        cost_estimate=cost(2 * ch * 2048 * (length + ext), 2 * ch * 2048 * 2 + ch * length * 10),
        name="forward_slot",
    )(*ops)


def gate_kernel(sets, kb, hb, inner, *refs):
    n_w = sum(len(orders) for _, orders in sets)
    wrefs = refs[:n_w]
    (gt, bh, dn, chan_r, hp_r, mix_r, z_r, ent_r, ct, cn) = refs[n_w : n_w + 10]
    nout_o, dmix_o, dz_o, sl_o = refs[n_w + 10 : n_w + 14]
    dsc, wsc, msc, sq_sc, dot_sc = refs[n_w + 14 :]
    phase, slot, c = pl.program_id(0), pl.program_id(1), pl.program_id(2)
    blk = slot * pl.num_programs(2) + c
    length = gt.shape[1]
    z = z_r[...].astype(f32)
    sig = sigmoid(z)
    silu = z * sig
    chan = chan_r[...]
    gain = chan[:, 5:6]
    hp = hp_r[...]
    cum_all = hp[hb : 2 * hb]

    @pl.when((phase == 0) & (blk == 0))
    def _():
        sq_sc[...] = jnp.zeros_like(sq_sc)
        dot_sc[...] = jnp.zeros_like(dot_sc)

    at = 0
    for (lo, hi), orders in sets:
        mine = wrefs[at : at + len(orders)]
        at += len(orders)

        @pl.when((phase == 0) & (slot >= lo) & (slot < hi))
        def _(mine=mine, orders=orders):
            dsc[...] = weight_dots(mine, orders, gt, kb)

    @pl.when(phase == 0)
    def _():
        weighted = (dsc[...] + dot(dn[...], bh[...])) * gain
        mix = mix_r[...] + per_head(dot(ent_r[...], ct[...]), jnp.exp2(cum_all))
        gated = mix * silu
        wsc[blk] = weighted
        msc[blk] = mix
        sq_sc[...] += jnp.sum((gated * gated).reshape(CB // 8, 8, length), axis=0)
        dot_sc[...] += jnp.sum((gated * weighted).reshape(CB // 8, 8, length), axis=0)

    @pl.when(phase == 1)
    def _():
        r = lax.rsqrt(jnp.sum(sq_sc[...], axis=0, keepdims=True) * (1.0 / inner) + epsilon)
        coef = r * r * r * (jnp.sum(dot_sc[...], axis=0, keepdims=True) * (1.0 / inner))
        mix = msc[blk]
        gated = mix * silu
        nout_o[...] = (gated * r * gain).astype(bf16)
        d_gated = r * wsc[blk] - gated * coef
        d_mix = d_gated * silu
        dmix_o[...] = d_mix.astype(bf16)
        dz_o[...] = (d_gated * mix * (sig + silu * (1.0 - sig))).astype(bf16)
        sl_o[...] = dot(per_head(d_mix, jnp.exp2(cum_all)).astype(bf16), cn[...])


def gate_call(ow, oo, gt, bh, dn, chan, hp, mix, z, ent, ct, cn, inner):
    slots, ch, length = mix.shape
    ncb = ch // CB
    hb = CB // HEAD
    kb = ow[0][1][0].shape[3]
    full = lambda a: pl.BlockSpec(a.shape, lambda p, s, c: (0,) * a.ndim)
    per_chan = lambda a: pl.BlockSpec((None, CB, a.shape[2]), lambda p, s, c: (s, c, 0))
    first = lambda a: pl.BlockSpec(
        (None, CB, a.shape[2]),
        lambda p, s, c: (jnp.where(p == 0, s, slots - 1), jnp.where(p == 0, c, ncb - 1), 0),
    )
    per_blk = lambda a: pl.BlockSpec((None,) + a.shape[1:], lambda p, s, c: (s * ncb + c, 0, 0))
    later = lambda w: pl.BlockSpec(
        (None, CB, w), lambda p, s, c: (jnp.where(p == 1, s, 0), jnp.where(p == 1, c, 0), 0)
    )
    ops, specs, sets = [], [], []
    for ((lo, hi), arrays), orders in zip(ow, oo):
        sets.append(((lo, hi), orders))
        for a in arrays:
            ops.append(a)

            def index(p, s, c, lo=lo, hi=hi):
                t = jnp.where(p == 0, s, slots)
                cc = jnp.where(t < lo, 0, jnp.where(t >= hi, ncb - 1, c))
                return (0, jnp.clip(t, lo, hi - 1) - lo, cc, 0)

            specs.append(pl.BlockSpec((a.shape[0], None, CB, a.shape[3]), index))
    ops += [gt, bh, dn, chan, hp, mix, z, ent, ct, cn]
    specs += [full(gt), full(bh), first(dn), per_chan(chan), per_blk(hp), first(mix)]
    specs += [per_chan(z), first(ent), full(ct), full(cn)]
    blocks = slots * ncb
    return pl.pallas_call(
        functools.partial(gate_kernel, sets, kb, hb, inner),
        grid=(2, slots, ncb),
        in_specs=specs,
        out_specs=[later(length), later(length), later(length), later(128)],
        out_shape=[
            jax.ShapeDtypeStruct((slots, ch, length), bf16),
            jax.ShapeDtypeStruct((slots, ch, length), bf16),
            jax.ShapeDtypeStruct((slots, ch, length), bf16),
            jax.ShapeDtypeStruct((slots, ch, 128), f32),
        ],
        scratch_shapes=[
            pltpu.VMEM((CB, length), f32),
            pltpu.VMEM((blocks, CB, length), f32),
            pltpu.VMEM((blocks, CB, length), f32),
            pltpu.VMEM((8, length), f32),
            pltpu.VMEM((8, length), f32),
        ],
        compiler_params=compiler_params(3),
        cost_estimate=cost(2 * slots * ch * 2048 * length, slots * ch * (4096 + length * 18)),
        name="gate",
    )(*ops)


def back_kernel(hb, sub, *refs):
    (dy_r, xr_r, chan_r, hp_r, cumn_r, ent_r, loc_r, ct, cn, bt, cbt) = refs[:11]
    dxs_o, u1_o, u2_o, kl_o, dcb_o, db_o, dc_o = refs[11:]
    blk = pl.program_id(0) * pl.num_programs(1) + pl.program_id(1)
    chan = chan_r[...]
    hp = hp_r[...]
    length = ct.shape[1]
    nsub = length // sub

    @pl.when(blk == 0)
    def _():
        dcb_o[...] = jnp.zeros_like(dcb_o)
        db_o[...] = jnp.zeros_like(db_o)
        dc_o[...] = jnp.zeros_like(dc_o)

    xc = conv_values(xr_r[...].astype(f32), chan)
    x = xc * sigmoid(xc)
    xs = per_head(x, hp[2 * hb : 3 * hb])
    xs_low = xs.astype(bf16)
    adj = None
    kl = []
    for s in reversed(range(nsub)):
        cols = slice(s * sub, (s + 1) * sub)
        cum = hp[:hb, cols]
        rows_n = cumn_r[cols, :]
        ecum = jnp.exp2(cum)
        last = cum[:, sub - 1 : sub]
        state = ent_r[...].astype(f32)
        if s > 0:
            before = hp[hb : 2 * hb, s * sub - 1 : s * sub]
            state = loc_r[s - 1] + per_head(state, jnp.exp2(before))
        state_low = state.astype(bf16)
        dy_low = dy_r[:, cols]
        dy = dy_low.astype(f32)
        y_in = per_head(dot(state_low, ct[:, cols]), ecum)
        ed = per_head(dy, ecum).astype(bf16)
        dc_o[:, cols] += dot(state_low, ed, TN)
        dxw, yw = [], []
        for h in range(hb):
            hs = slice(h * HEAD, (h + 1) * HEAD)
            gap = jnp.minimum(cum[h : h + 1] - rows_n[:, h : h + 1], 0.0)
            decay = jnp.exp2(gap)
            weight = (decay * cbt[s]).astype(bf16)
            yw.append(dot(xs_low[hs, cols], weight))
            dxw.append(dot(dy_low[hs], weight, NT))
            dcb_o[s] += decay * dot(xs_low[hs, cols], dy_low[hs], TN)
        yw = jnp.concatenate(yw, axis=0)
        dxs = jnp.concatenate(dxw, axis=0)
        u1_o[:, cols] = head_sums(dy * (yw + y_in) - xs_low[:, cols].astype(f32) * dxs, hb)
        add = dot(ed, cn[cols, :])
        if adj is None:
            u2_o[:, cols] = jnp.zeros((hb, sub), f32)
            kl.append(jnp.zeros((hb, 128), f32))
            adj = add
        else:
            ends = jnp.exp2(last - cum)
            adj_low = adj.astype(bf16)
            dxi = per_head(dot(adj_low, bt[:, cols]), ends)
            xs_s = xs[:, cols]
            u2_o[:, cols] = head_sums(xs_s * dxi, hb)
            kl.append(head_sums(adj * state, hb) * jnp.exp2(last))
            db_o[:, cols] += dot(adj_low, per_head(xs_s, ends).astype(bf16), TN)
            dxs = dxs + dxi
            adj = per_head(adj, jnp.exp2(last)) + add
        dxs_o[:, cols] = dxs
    for s in range(nsub):
        kl_o[:, s * 128 : (s + 1) * 128] = kl[nsub - 1 - s]


def back_call(dy, xr, chan, hp, cumn, ent, loc, ct, cn, bt, cbt):
    slots, ch, length = dy.shape
    ncb = ch // CB
    hb = CB // HEAD
    nsub = length // SUB
    full = lambda a: pl.BlockSpec(a.shape, lambda s, c: (0,) * a.ndim)
    per_chan = lambda a: pl.BlockSpec((None, CB, a.shape[2]), lambda s, c: (s, c, 0))
    per_blk = lambda a: pl.BlockSpec((None,) + a.shape[1:], lambda s, c: (s * ncb + c, 0, 0))
    blk_out = lambda w: pl.BlockSpec((None, hb, w), lambda s, c: (s * ncb + c, 0, 0))
    loc_spec = pl.BlockSpec((None, loc.shape[1], CB, 128), lambda s, c: (s, 0, c, 0))
    blocks = slots * ncb
    return pl.pallas_call(
        functools.partial(back_kernel, hb, SUB),
        grid=(slots, ncb),
        in_specs=[per_chan(dy), per_chan(xr), per_chan(chan), per_blk(hp), per_blk(cumn)]
        + [per_chan(ent), loc_spec, full(ct), full(cn), full(bt), full(cbt)],
        out_specs=[
            pl.BlockSpec((None, CB, length), lambda s, c: (s, c, 0)),
            blk_out(length),
            blk_out(length),
            blk_out(128 * nsub),
            pl.BlockSpec((nsub, SUB, SUB), lambda s, c: (0, 0, 0)),
            pl.BlockSpec((128, length), lambda s, c: (0, 0)),
            pl.BlockSpec((128, length), lambda s, c: (0, 0)),
        ],
        out_shape=[
            jax.ShapeDtypeStruct((slots, ch, length), f32),
            jax.ShapeDtypeStruct((blocks, hb, length), f32),
            jax.ShapeDtypeStruct((blocks, hb, length), f32),
            jax.ShapeDtypeStruct((blocks, hb, 128 * nsub), f32),
            jax.ShapeDtypeStruct((nsub, SUB, SUB), f32),
            jax.ShapeDtypeStruct((128, length), f32),
            jax.ShapeDtypeStruct((128, length), f32),
        ],
        compiler_params=compiler_params(2),
        cost_estimate=cost(slots * ch * length * SUB * 40, slots * ch * length * 12),
        name="state_back",
    )(dy, xr, chan, hp, cumn, ent, loc, ct, cn, bt, cbt)


def finish_kernel(hb, *refs):
    (dxs_r, dy_r, xr_r, chan_r, hp_r, ent_r, adj_r, bt) = refs[:8]
    dconv_o, dd_o, u2_o, kf_o, db_o = refs[8:]
    blk = pl.program_id(0) * pl.num_programs(1) + pl.program_id(1)
    chan = chan_r[...]
    hp = hp_r[...]
    length = bt.shape[1]

    @pl.when(blk == 0)
    def _():
        db_o[...] = jnp.zeros_like(db_o)

    xc = conv_values(xr_r[...].astype(f32), chan)
    sig = sigmoid(xc)
    x = xc * sig
    delta = hp[2 * hb : 3 * hb]
    xs = per_head(x, delta)
    total = hp[hb : 2 * hb]
    last = total[:, length - 1 : length]
    ends = jnp.exp2(last - total)
    adj_low = adj_r[...]
    extra = per_head(dot(adj_low, bt[...]), ends)
    u2_o[...] = head_sums(xs * extra, hb)
    kf_o[...] = head_sums(adj_low.astype(f32) * ent_r[...].astype(f32), hb) * jnp.exp2(last)
    db_o[...] += dot(adj_low, per_head(xs, ends).astype(bf16), TN)
    dxs = dxs_r[...] + extra
    dd_o[...] = head_sums(x * dxs, hb)
    dx = per_head(dxs, delta) + dy_r[...].astype(f32) * chan[:, 4:5]
    dconv_o[...] = dx * (sig + x * (1.0 - sig))


def finish_call(dxs, dy, xr, chan, hp, ent, adj, bt):
    slots, ch, length = dy.shape
    ncb = ch // CB
    hb = CB // HEAD
    full = lambda a: pl.BlockSpec(a.shape, lambda s, c: (0,) * a.ndim)
    per_chan = lambda a: pl.BlockSpec((None, CB, a.shape[2]), lambda s, c: (s, c, 0))
    per_blk = lambda a: pl.BlockSpec((None,) + a.shape[1:], lambda s, c: (s * ncb + c, 0, 0))
    blk_out = lambda w: pl.BlockSpec((None, hb, w), lambda s, c: (s * ncb + c, 0, 0))
    blocks = slots * ncb
    return pl.pallas_call(
        functools.partial(finish_kernel, hb),
        grid=(slots, ncb),
        in_specs=[per_chan(dxs), per_chan(dy), per_chan(xr), per_chan(chan), per_blk(hp)]
        + [per_chan(ent), per_chan(adj), full(bt)],
        out_specs=[
            pl.BlockSpec((None, CB, length), lambda s, c: (s, c, 0)),
            blk_out(length),
            blk_out(length),
            blk_out(128),
            pl.BlockSpec((128, length), lambda s, c: (0, 0)),
        ],
        out_shape=[
            jax.ShapeDtypeStruct((slots, ch, length), f32),
            jax.ShapeDtypeStruct((blocks, hb, length), f32),
            jax.ShapeDtypeStruct((blocks, hb, length), f32),
            jax.ShapeDtypeStruct((blocks, hb, 128), f32),
            jax.ShapeDtypeStruct((128, length), f32),
        ],
        compiler_params=compiler_params(2),
        cost_estimate=cost(slots * ch * length * 512, slots * ch * length * 14),
        name="finish_back",
    )(dxs, dy, xr, chan, hp, ent, adj, bt)


def pair_kernel(*refs):
    (dconv_r, halo_r, dz_r, chan_r, upz, upx, low) = refs[:7]
    dx_o, gz_o, gx_o, dl_o = refs[7:]
    blk = pl.program_id(0) * pl.num_programs(1) + pl.program_id(1)
    chan = chan_r[...]

    @pl.when(blk == 0)
    def _():
        dl_o[...] = jnp.zeros_like(dl_o)

    ext = jnp.concatenate([dconv_r[...], halo_r[...]], axis=1)
    width = ext.shape[1]
    out = ext * chan[:, 3:4]
    for k in range(3):
        out = out + pltpu.roll(ext, width - (3 - k), 1) * chan[:, k : k + 1]
    dx = out[:, : width - HALO].astype(bf16)
    dx_o[...] = dx
    dz = dz_r[...]
    gz_o[...] = dot(dz, low[...], NT)
    gx_o[...] = dot(dx, low[...], NT)
    dl_o[...] += dot(upz[...], dz, TN) + dot(upx[...], dx, TN)


def pair_call(dconv, halo, dz, chan, upz, upx, low):
    slots, ch, length = dz.shape
    ncb = ch // CB
    rank2 = low.shape[0]
    full = lambda a: pl.BlockSpec(a.shape, lambda s, c: (0,) * a.ndim)
    per_chan = lambda a: pl.BlockSpec((None, CB, a.shape[2]), lambda s, c: (s, c, 0))
    return pl.pallas_call(
        pair_kernel,
        grid=(slots, ncb),
        in_specs=[per_chan(a) for a in (dconv, halo, dz, chan, upz, upx)] + [full(low)],
        out_specs=[
            pl.BlockSpec((None, CB, length), lambda s, c: (s, c, 0)),
            pl.BlockSpec((None, CB, rank2), lambda s, c: (s, c, 0)),
            pl.BlockSpec((None, CB, rank2), lambda s, c: (s, c, 0)),
            pl.BlockSpec((rank2, length), lambda s, c: (0, 0)),
        ],
        out_shape=[
            jax.ShapeDtypeStruct((slots, ch, length), bf16),
            jax.ShapeDtypeStruct((slots, ch, rank2), f32),
            jax.ShapeDtypeStruct((slots, ch, rank2), f32),
            jax.ShapeDtypeStruct((rank2, length), f32),
        ],
        compiler_params=compiler_params(2),
        cost_estimate=cost(slots * ch * length * 256, slots * ch * length * 8),
        name="pair",
    )(dconv, halo, dz, chan, upz, upx, low)


def project_kernel(sets, kb, *refs):
    n_left = len({left for _, left, _ in sets})
    lefts = refs[:n_left]
    n_w = sum(len(orders) for _, _, orders in sets)
    wrefs = refs[n_left : n_left + n_w]
    out = refs[-2]
    acc = refs[-1]
    slot, c = pl.program_id(0), pl.program_id(1)

    @pl.when((slot == 0) & (c == 0))
    def _():
        acc[...] = jnp.zeros_like(acc)

    turned = [jnp.transpose(ref[...]) for ref in lefts]
    at = 0
    for (lo, hi), left, orders in sets:
        mine = wrefs[at : at + len(orders)]
        at += len(orders)

        @pl.when((slot >= lo) & (slot < hi))
        def _(mine=mine, orders=orders, left=left):
            for ref, offsets in zip(mine, orders):
                for b, off in enumerate(offsets):
                    acc[:, off : off + kb] += dot(turned[left], ref[b])

    @pl.when((slot == pl.num_programs(0) - 1) & (c == pl.num_programs(1) - 1))
    def _():
        out[...] = acc[...]


def project_call(lefts, weights, orders, width, name):
    slots, ch, length = lefts[0].shape
    ncb = ch // CB
    ops = list(lefts)
    specs = [pl.BlockSpec((None, CB, length), lambda s, c: (s, c, 0)) for _ in lefts]
    sets = []
    for ((lo, hi), left, arrays), order in zip(weights, orders):
        sets.append(((lo, hi), left, order))
        for a in arrays:
            ops.append(a)

            def index(s, c, lo=lo, hi=hi, nd=a.ndim):
                cc = jnp.where(s < lo, 0, jnp.where(s >= hi, ncb - 1, c))
                if nd == 3:
                    return (0, cc, 0)
                return (0, jnp.clip(s, lo, hi - 1) - lo, cc, 0)

            shape = (a.shape[0], CB, a.shape[2]) if a.ndim == 3 else (
                a.shape[0], None, CB, a.shape[3])
            specs.append(pl.BlockSpec(shape, index))
    kb = weights[0][2][0].shape[-1]
    n_l = len(lefts)
    return pl.pallas_call(
        functools.partial(project_kernel, sets, kb),
        grid=(slots, ncb),
        in_specs=specs,
        out_specs=pl.BlockSpec((length, width), lambda s, c: (0, 0)),
        out_shape=jax.ShapeDtypeStruct((length, width), f32),
        scratch_shapes=[pltpu.VMEM((length, width), f32)],
        compiler_params=compiler_params(2),
        cost_estimate=cost(2 * n_l * slots * ch * length * width, n_l * slots * ch * width * 2),
        name=name,
    )(*ops)


def body(
    tokens,
    cotangent,
    lengths,
    adapter_ids,
    pre_gain,
    in_inner,
    in_maps,
    in_steps,
    conv_inner,
    conv_maps,
    step_bias,
    decay_log,
    skip_gain,
    norm_gain,
    out_weight,
    adapter_in_down,
    adapter_in_up,
    adapter_out_down,
    adapter_out_up,
):
    planes = lax.axis_size("tensor")
    seqs = lax.axis_size("dp")
    place = lax.axis_index("tensor")
    mine = lax.axis_index("dp")
    length = tokens.shape[1]
    width = tokens.shape[2]
    rows_here = in_inner.shape[0]
    ch = in_inner.shape[2]
    inner = ch * planes
    hs = in_steps.shape[1]
    heads = hs * planes
    rank = adapter_in_down.shape[2]
    adapters = adapter_in_down.shape[0]
    state_w = in_maps.shape[1] // 2
    hb = CB // HEAD
    ncb = ch // CB
    nblk = planes * ncb
    nsub = length // SUB
    quick = seqs == 8 and planes == 4

    def from_plane(v, j):
        return lax.ppermute(v, "tensor", [((s + j) % planes, s) for s in range(planes)])

    def flip(v, bit):
        return lax.ppermute(v, "dp", [(i, i ^ bit) for i in range(seqs)])

    def slot_order(v):
        twice = jnp.concatenate([v, v], axis=0)
        return lax.dynamic_slice_in_dim(twice, place, planes, 0)

    def rel(v):
        if not quick:
            return v
        parts = [
            lax.dynamic_slice_in_dim(v, (mine ^ m) * rows_here, rows_here, 1) for m in range(8)
        ]
        return jnp.concatenate(parts, axis=1)

    wt = jnp.transpose(in_inner, (1, 2, 0))
    if quick:

        def plane_gather(a, b):
            ax, by = flip(a, 2), flip(b, 4)
            a1, b1 = jnp.stack([a, ax]), jnp.stack([b, by])
            a2, b2 = flip(a1, 4), flip(b1, 2)
            return (
                [a1, a2, flip(a1, 1), flip(a2, 1)],
                [b1, b2, flip(b1, 1), flip(b2, 1)],
            )

        k = rows_here
        order_a = [[0, 2 * k], [4 * k, 6 * k], [1 * k, 3 * k], [5 * k, 7 * k]]
        order_b = [[0, 4 * k], [2 * k, 6 * k], [1 * k, 5 * k], [3 * k, 7 * k]]
        slot_w = []
        for j in range(planes):
            w = wt if j == 0 else from_plane(wt, j)
            slot_w.append(plane_gather(w[0], w[1]))
        outs = [out_weight] + [from_plane(out_weight, j) for j in range(1, planes)]
        half = planes // 2
        oa, ob = plane_gather(jnp.stack(outs[:half]), jnp.stack(outs[half:]))
        ow = [((0, half), oa), ((half, planes), ob)]
        oo = [order_a, order_b]
    else:
        order_a = order_b = [[0]]
        w = lax.all_gather(in_inner, "dp", axis=0, tiled=True)
        w = slot_order(lax.all_gather(jnp.transpose(w, (1, 2, 0)), "tensor", axis=0))
        slot_w = [([w[j, 0][None]], [w[j, 1][None]]) for j in range(planes)]
        o = lax.all_gather(out_weight, "dp", axis=1, tiled=True)
        ow = [((0, planes), [slot_order(lax.all_gather(o, "tensor", axis=0))[None]])]
        oo = [[[0]]]

    pick = adapter_ids[0]
    down_in = lax.dynamic_index_in_dim(adapter_in_down, pick, 0, keepdims=False)
    up_here = lax.dynamic_index_in_dim(adapter_in_up, pick, 0, keepdims=False)
    down_here = lax.dynamic_index_in_dim(adapter_out_down, pick, 0, keepdims=False)
    up_out = lax.dynamic_index_in_dim(adapter_out_up, pick, 0, keepdims=False)
    packed = jnp.concatenate(
        [
            jnp.transpose(up_here, (1, 0, 2)).reshape(2 * rank, ch).astype(f32),
            down_here.T.astype(f32),
            conv_inner,
            jnp.repeat(skip_gain, HEAD)[None],
            norm_gain[None],
            jnp.pad(jnp.stack([step_bias, decay_log]), ((0, 0), (0, ch - hs))),
        ],
        axis=0,
    )
    packed = slot_order(lax.all_gather(packed, "tensor", axis=0))
    up_z = jnp.swapaxes(packed[:, :rank], 1, 2).astype(bf16)
    up_x = jnp.swapaxes(packed[:, rank : 2 * rank], 1, 2).astype(bf16)
    down_out = jnp.swapaxes(packed[:, 2 * rank : 3 * rank], 1, 2).astype(bf16)
    chan = jnp.swapaxes(packed[:, 3 * rank : 3 * rank + 6], 1, 2)
    chan = jnp.pad(chan, ((0, 0), (0, 0), (0, 2)))
    bias = packed[:, 3 * rank + 6, :hs].reshape(heads)
    speed = jnp.exp(packed[:, 3 * rank + 7, :hs].reshape(heads))
    up_z2 = jnp.concatenate([up_z, up_z], axis=2)
    up_x2 = jnp.concatenate([up_x, up_x], axis=2)
    down_out2 = jnp.concatenate([down_out, down_out], axis=2)
    steps_all = slot_order(lax.all_gather(in_steps, "tensor", axis=0))
    steps_all = jnp.swapaxes(steps_all, 0, 1).reshape(rows_here, heads)
    small_w = lax.all_gather(
        jnp.concatenate([in_maps, steps_all], axis=1), "dp", axis=0, tiled=True
    )
    ids = lax.all_gather(adapter_ids, "dp", axis=0, tiled=True)

    residual = tokens[0].astype(f32)
    stat = jnp.mean(residual * residual, axis=-1, keepdims=True)
    root = lax.rsqrt(stat + epsilon)
    normed = (residual * root * pre_gain).astype(bf16)
    before = lax.ppermute(normed[-16:], "tensor", [(s, s + 1) for s in range(planes - 1)])
    ext = jnp.concatenate([before, normed], axis=0)
    wide = jnp.concatenate([jnp.zeros((HALO - 16, width), bf16), ext], axis=0)
    nt = jnp.transpose(rel(wide))
    low_t = dot(down_in, wide, ((0,), (1,)))
    low_hi = low_t.astype(bf16)
    low2 = jnp.concatenate([low_hi, (low_t - low_hi.astype(f32)).astype(bf16)], axis=0)

    small = dot(ext, small_w)
    maps_ext = small[:, : 2 * state_w]
    steps = small[16:, 2 * state_w :] + bias
    maps_pre = sum(maps_ext[13 + k : 13 + k + length] * conv_maps[k] for k in range(4))
    maps_sig = jax.nn.sigmoid(maps_pre)
    maps = (maps_pre * maps_sig).astype(bf16)
    b_low, c_low = maps[:, :state_w], maps[:, state_w:]
    bt, ct = b_low.T, c_low.T
    delta = jax.nn.softplus(steps)
    rates = -delta * speed
    upto = (jnp.arange(SUB)[:, None] >= jnp.arange(SUB)[None, :]).astype(f32)
    cum = jnp.einsum(
        "ij,sjh->sih", upto, rates.reshape(nsub, SUB, heads), precision=highest
    )
    ends_before = jnp.concatenate(
        [jnp.zeros((1, heads), f32), jnp.cumsum(cum[:-1, -1], axis=0)], axis=0
    ) if nsub > 1 else jnp.zeros((1, heads), f32)
    cum_all = (cum + ends_before[:, None, :]).reshape(length, heads) * LOG2E
    cum = cum.reshape(length, heads) * LOG2E
    cumn = jnp.transpose(cum.reshape(length, nblk, hb), (1, 0, 2))
    lanes = lambda v: v.T.reshape(nblk, hb, length)
    hp = jnp.concatenate([lanes(cum), lanes(cum_all), lanes(delta)], axis=1)
    by_sub = lambda v: v.reshape(nsub, SUB, state_w)
    keep = upto.T[None]
    cbt = keep * jnp.einsum(
        "sjn,sin->sji", by_sub(b_low), by_sub(c_low), preferred_element_type=f32
    )

    positions = place * length + jnp.arange(length)
    valid = (positions < lengths[0]).astype(f32)[:, None]
    masked = (cotangent[0].astype(f32) * valid).astype(bf16)
    gt = jnp.transpose(rel(masked))
    back_t = dot(up_out, masked, NT)
    back_hi = back_t.astype(bf16)
    back2 = jnp.concatenate([back_hi, (back_t - back_hi.astype(f32)).astype(bf16)], axis=0)

    bufs = None
    for j in range(planes):
        zw, xw = slot_w[j]
        bufs = forward_slot(
            j, zw, xw, order_a, order_b, nt, low2, up_z2, up_x2, chan, hp, cumn, ct, b_low, cbt,
            bufs,
        )
    z, xr, mix, loc, s_end = bufs

    total = jnp.exp2(jnp.repeat(cum_all[-1].reshape(planes, hs), HEAD, axis=1))[:, :, None]
    ent = jnp.zeros((planes, ch, state_w), bf16)
    for _ in range(planes - 1):
        send = (ent.astype(f32) * total + s_end).astype(bf16)
        got = lax.ppermute(send, "tensor", [(s, s + 1) for s in range(planes - 1)])
        ent = jnp.roll(got, -1, axis=0)

    nout, dy, dz, sl = gate_call(
        ow, oo, gt, back2, down_out2, chan, hp, mix, z, ent, ct, c_low, inner
    )

    adj = jnp.zeros((planes, ch, state_w), bf16)
    for _ in range(planes - 1):
        send = (adj.astype(f32) * total + sl).astype(bf16)
        got = lax.ppermute(send, "tensor", [(s + 1, s) for s in range(planes - 1)])
        adj = jnp.roll(got, 1, axis=0)

    dxs, u1, u2, kl, dcb, db1, dc1 = back_call(
        dy, xr, chan, hp, cumn, ent, loc, ct, c_low, bt, cbt
    )
    dconv, ddelta, u2f, kf, db2 = finish_call(dxs, dy, xr, chan, hp, ent, adj, bt)

    dcb = (dcb * keep).astype(bf16)
    d_b = (db1 + db2).T + jnp.einsum(
        "sji,sin->sjn", dcb, by_sub(c_low), preferred_element_type=f32
    ).reshape(length, state_w)
    d_c = dc1.T + jnp.einsum(
        "sji,sjn->sin", dcb, by_sub(b_low), preferred_element_type=f32
    ).reshape(length, state_w)
    d_maps_pre = jnp.concatenate([d_b, d_c], axis=1) * (
        maps_sig * (1.0 + maps_pre * (1.0 - maps_sig))
    )
    flat = lambda v: v.reshape(heads, length)
    rate_in = jnp.einsum(
        "hst,tu->hsu", flat(u1).reshape(heads, nsub, SUB), upto, precision=highest
    )
    rate_in += jnp.einsum(
        "hst,tu->hsu", flat(u2).reshape(heads, nsub, SUB), 1.0 - upto, precision=highest
    )
    rate_in += jnp.sum(kl.reshape(heads, nsub, 128), axis=-1, keepdims=True)
    after = (jnp.arange(length)[:, None] < jnp.arange(length)[None, :]).astype(f32)
    d_rate = rate_in.reshape(heads, length) + jnp.dot(flat(u2f), after, precision=highest)
    d_rate += jnp.sum(kf.reshape(heads, 128), axis=-1, keepdims=True)
    d_delta = flat(ddelta) - speed[:, None] * d_rate
    d_steps = (d_delta * jax.nn.sigmoid(steps.T)).astype(bf16)

    near = lax.ppermute(
        jnp.concatenate(
            [jnp.swapaxes(dconv[:, :, :4], 1, 2).reshape(planes * 4 * ch),
             d_maps_pre[:4].reshape(8 * state_w)]
        ),
        "tensor",
        [(s + 1, s) for s in range(planes - 1)],
    )
    near_x = jnp.swapaxes(near[: planes * 4 * ch].reshape(planes, 4, ch), 1, 2)
    near_x = jnp.pad(jnp.roll(near_x, 1, axis=0), ((0, 0), (0, 0), (0, HALO - 4)))
    near_maps = near[planes * 4 * ch :].reshape(4, 2 * state_w)
    maps_more = jnp.concatenate([d_maps_pre, near_maps], axis=0)
    d_maps = sum(maps_more[3 - k : 3 - k + length] * conv_maps[k] for k in range(4))

    dx, grad_z, grad_x, d_low2 = pair_call(
        dconv, near_x, dz, chan, up_z2, up_x2, low2[:, HALO:]
    )
    d_low = d_low2[:rank]

    weights = []
    orders = []
    for j in range(planes):
        for left in range(2):
            weights.append(((j, j + 1), left, slot_w[j][left]))
            orders.append((order_a, order_b)[left])
    d_normed = project_call([dz, dx], weights, orders, width, "input_back")
    left = jnp.concatenate([d_maps.astype(bf16), d_steps.T, d_low.T.astype(bf16)], axis=1)
    right = jnp.concatenate([small_w, down_in], axis=1)
    d_normed = rel(d_normed) + dot(left, right, NT)
    d_scaled = d_normed * pre_gain
    d_resid = root * d_scaled - residual * root * root * root * jnp.mean(
        d_scaled * residual, axis=-1, keepdims=True
    )
    tokens_grad = (masked.astype(f32) + d_resid).astype(bf16)[None]

    branch = rel(
        project_call(
            [nout], [(span, 0, arrays) for span, arrays in ow], oo, width, "output"
        )
    )
    hidden_t = jnp.einsum("jkr,jkt->rt", down_out, nout, preferred_element_type=f32)
    branch = branch + dot(hidden_t.astype(bf16), up_out, TN)
    mixed = (valid * (residual + branch)).astype(bf16)[None]

    grad_up = jnp.stack(
        [grad_z[..., :rank] + grad_z[..., rank:], grad_x[..., :rank] + grad_x[..., rank:]], axis=1
    )
    grad_down_out = jnp.einsum("jkt,rt->jkr", nout, back_hi, preferred_element_type=f32)
    grad_down = dot(normed, d_low.T.astype(bf16), TN)
    grad_up_out = dot(hidden_t.astype(bf16), masked)
    to_planes = jnp.concatenate(
        [
            grad_up.reshape(planes, 2 * ch * rank),
            grad_down_out.reshape(planes, ch * rank),
            slot_order(grad_down.reshape(planes, width * rank // planes)),
            slot_order(grad_up_out.reshape(planes, width * rank // planes)),
        ],
        axis=1,
    )
    summed = to_planes[0]
    for j in range(1, planes):
        part = to_planes[j].astype(bf16)
        summed += lax.ppermute(
            part, "tensor", [(s, (s + j) % planes) for s in range(planes)]
        ).astype(f32)
    chosen = (ids[None, :] == jnp.arange(adapters)[:, None]).astype(bf16)
    head_part = 3 * ch * rank
    by_seq = lax.all_gather(summed.astype(bf16), "dp", axis=0)
    headwise = dot(chosen, by_seq[:, :head_part])
    shared = lax.all_gather(
        dot(chosen, by_seq[:, head_part:]).astype(bf16), "tensor", axis=0
    ).astype(f32)
    shared = jnp.transpose(shared.reshape(planes, adapters, 2, -1), (2, 1, 0, 3))
    g_down = shared[0].reshape(adapters, width, rank)
    g_up_out = shared[1].reshape(adapters, rank, width)
    g_up = jnp.transpose(
        headwise[:, : 2 * ch * rank].reshape(adapters, 2, ch, rank), (0, 3, 1, 2)
    )
    g_down_out = headwise[:, 2 * ch * rank :].reshape(adapters, ch, rank)
    return (mixed, tokens_grad, g_down, g_up, g_down_out, g_up_out)


def solution(mesh):
    placed = (
        P("dp", "tensor", None),
        P("dp", "tensor", None),
        P("dp"),
        P("dp"),
        P(),
        P("dp", None, "tensor"),
        P("dp", None),
        P("dp", "tensor"),
        P(None, "tensor"),
        P(),
        P("tensor"),
        P("tensor"),
        P("tensor"),
        P("tensor"),
        P("tensor", "dp"),
        P(),
        P(None, None, None, "tensor"),
        P(None, "tensor", None),
        P(),
    )
    return jax.shard_map(
        body,
        mesh=mesh,
        in_specs=placed,
        out_specs=(
            P("dp", "tensor", None),
            P("dp", "tensor", None),
            P(),
            P(None, None, None, "tensor"),
            P(None, "tensor", None),
            P(),
        ),
        check_vma=False,
    )
```

time: 2140 us -> 903 us (0.42)
  waiting for transfers between devices: 1050 us -> 176 us
  matrix products: 517 us -> 30.3 us
  Pallas kernels: 0 us -> 231 us
  other arithmetic: 215 us -> 64.2 us
  local copies, waits for them, and re-layouts: 307 us -> 177 us
  starting transfers between devices: 0.36 us -> 93 us
  blocking collectives: 29.2 us -> 101 us
    reduce_scatter x2 -> x0, waiting for transfers between devices: 502 us -> none  [the longest x1 281 us: body(): lax.psum_scatter(partial_out, 'tensor', scatter_dimension=0, tiled=True)]
    dot_general x104 -> x18, matrix products: 517 us -> 30.3 us  [the longest x9 19.7 us: dot(): return lax.dot_general(a, b, (dims, ((), ())), preferred_element_type=f32)]
    all_gather x5 -> x3, waiting for transfers between devices: 345 us -> 0.55 us  [the longest x1 0.53 us: body(): lax.all_gather(dot(chosen, by_seq[:, head_part:]).astype(bf16), 'tensor',...]
    pallas_call x0 -> x10, Pallas kernels: none -> 231 us  [the longest x2 56.5 us: project_call(): pl.pallas_call(functools.partial(project_kernel, sets, kb), grid=(slots,...]
    psum x2 -> x0, waiting for transfers between devices: 198 us -> none  [the longest x1 140 us: body(): lax.psum((chosen[:, None, None] * grad_in_down[None], chosen[:, None, Non...]
    ppermute x0 -> x57, waiting for transfers between devices: none -> 176 us  [the longest x40 76.2 us: flip(): return lax.ppermute(v, 'dp', [(i, i ^ bit) for i in range(seqs)])]
    ppermute x0 -> x57, starting transfers between devices: none -> 92.9 us  [the longest x3 45.3 us: body(): got = lax.ppermute(send, 'tensor', [(s, s + 1) for s in range(planes - 1)])]
    all_gather x1 -> x2, blocking collectives: 10.5 us -> 93.6 us  [the longest x1 75.2 us: body(): steps_all = slot_order(lax.all_gather(in_steps, 'tensor', axis=0))]
  transfers between devices with their start and end apart: 9 -> 60, of which waited for: 9 -> 17; matrix products, arithmetic and copies ran while one was open for 6% -> 22% of each run, Pallas kernels for 0% -> 17%
where the time goes in v1:
time: 903 us; the launch traced here: 890 us
  Pallas kernels  231 us (26%)
  local copies, waits for them, and re-layouts  177 us (20%)
  waiting for transfers between devices  176 us (19%)
  blocking collectives  101 us (11%)
  starting transfers between devices  93 us (10%)
  other arithmetic  64.2 us (7%)
  matrix products  30.3 us (3%)
  between operations  17 us (2%)
    ppermute x40, waiting for transfers between devices, flip(): return lax.ppermute(v, 'dp', [(i, i ^ bit) for i in range(seqs)])  76.2 us
    all_gather x1, blocking collectives, body(): steps_all = slot_order(lax.all_gather(in_steps, 'tensor', axis=0))  75.2 us
    unnamed x228, local copies, waits for them, and re-layouts  64.6 us
    pallas_call x2, Pallas kernels, project_call(): pl.pallas_call(functools.partial(project_kernel, sets, kb), grid=(slots,...  56.5 us
    pallas_call x4, Pallas kernels, forward_slot(): pl.pallas_call(functools.partial(fwd_kernel, zo, xo, kb, hb, SUB), grid=(...  56 us
    ppermute x3, starting transfers between devices, body(): got = lax.ppermute(send, 'tensor', [(s, s + 1) for s in range(planes - 1)])  45.3 us
    ppermute x6, waiting for transfers between devices, from_plane(): lax.ppermute(v, 'tensor', [((s + j) % planes, s) for s in range(planes)])  43.9 us
    pallas_call x1, Pallas kernels, gate_call(): pl.pallas_call(functools.partial(gate_kernel, sets, kb, hb, inner), grid=...  41.8 us
  transfers between devices with their start and end apart: 60, of which 17 were waited for; matrix products, arithmetic and copies ran while one was open for 22% of the time, Pallas kernels for 17%

profile of v1, /device:TPU:0, one launch (start us, length us, event | category | flops | bytes accessed | tf_op | source)
XLA Modules:
  0.0 890.1 jit_solution(11512316794434748875)
XLA Ops:
  7.3 3.8 copy.250
  11.0 5.0 collective-permute-start.30
  16.1 75.2 %all-gather.1 = bf16[1024,16]{0,1:T(8,128)(2,1)S(1)} all-gather(bf16[256,16]{0,1:T(8,128)(2,1)} %param.26), channel_id=3, replica_groups=mesh['dp'=8,'tensor'=4] {'tensor'}, dimensions={0}, use_global_device_ids=true | all-gather | bytes 40960 | tf_op jit(solution)/shard_map/all_gather | solution.py:683
  105.2 18.3 %all-gather = f32[224,1024]{1,0:T(8,128)S(1)} all-gather(f32[56,1024]{1,0:T(8,128)S(1)} %concatenate.102), channel_id=2, replica_groups=mesh['dp'=8,'tensor'=4] {'tensor'}, dimensions={0}, use_global_device_ids=true | all-gather | bytes 1146880 | tf_op jit(solution)/shard_map/all_gather | solution.py:672
  143.6 26.2 %collective-permute-done.5 = bf16[1024,256]{1,0:T(8,128)(2,1)S(1)} collective-permute-done((bf16[1024,256]{1,0:T(8,128)(2,1)S(1)}, bf16[1024,256]{1,0:T(8,128)(2,1)S(1)}, u32[]{:S(2)}, u32[]{:S(2)}) %collective-permute-start.5) | collective-permute-done | bytes 524320 | tf_op jit(solution)/shard_map/ppermute | solution.py:606
  176.9 17.6 %collective-permute-done.12 = bf16[2,1024,256]{2,1,0:T(8,128)(2,1)S(1)} collective-permute-done((bf16[2,1024,256]{2,1,0:T(8,128)(2,1)S(1)}, bf16[2,1024,256]{2,1,0:T(8,128)(2,1)S(1)}, u32[]{:S(2)}, u32[]{:S(2)}) %collective-permute-start.12) | collective-permute-done | bytes 1048608 | tf_op jit(solution)/shard_map/ppermute | solution.py:606
  203.0 6.4 collective-permute-done.31
  213.5 7.1 collective-permute-done.22
  223.0 22.8 %collective-permute-done.26 = bf16[1024,256]{1,0:T(8,128)(2,1)S(1)} collective-permute-done((bf16[1024,256]{1,0:T(8,128)(2,1)S(1)}, bf16[1024,256]{1,0:T(8,128)(2,1)S(1)}, u32[]{:S(2)}, u32[]{:S(2)}) %collective-permute-start.26) | collective-permute-done | bytes 524320 | tf_op jit(solution)/shard_map/ppermute | solution.py:609
  248.1 3.8 collective-permute-done.13
  257.6 4.6 copy.265.refs_8_
  275.2 4.1 collective-permute-done.36.refs_5_.refs_15_
  286.1 13.7 %collective-permute-done.23.refs_1_.refs_19_ = bf16[2,1024,256]{2,1,0:T(8,128)(2,1)} collective-permute-done((bf16[2,1024,256]{2,1,0:T(8,128)(2,1)}, bf16[2,1024,256]{2,1,0:T(8,128)(2,1)}, u32[]{:S(2)}, u32[]{:S(2)}) %collective-permute-start.23) | collective-permute-done | bytes 1048608 | tf_op jit(solution)/shard_map/ppermute | solution.py:609
  300.4 5.2 collective-permute-done.27.refs_5_.refs_23_
  310.4 11.3 %collective-permute-done.14.refs_1_.refs_27_ = bf16[2,1024,256]{2,1,0:T(8,128)(2,1)} collective-permute-done((bf16[2,1024,256]{2,1,0:T(8,128)(2,1)}, bf16[2,1024,256]{2,1,0:T(8,128)(2,1)}, u32[]{:S(2)}, u32[]{:S(2)}) %collective-permute-start.14) | collective-permute-done | bytes 1048608 | tf_op jit(solution)/shard_map/ppermute | solution.py:609
  329.2 13.9 %forward_slot.4 = (bf16[4,1024,512]{2,1,0:T(8,128)(2,1)}, bf16[4,1024,640]{2,1,0:T(8,128)(2,1)}, f32[4,1024,512]{2,1,0:T(8,128)}, f32[4,1,1024,128]{3,2,1,0:T(8,128)}, f32[4,1024,128]{2,1,0:T(8,128)}) custom-call(bf16[2,1024,256]{2,1,0:T(8,128)(2,1)} %copy-done.18, bf16[2,1024,256]{2,1,0:T(8,128)(2,1)} %collective-permute-done.40.refs_1_.refs_3_, ...), custom_call_target="tpu_custom_call" | custom-call | flops 4831838208 | bytes 13631488 | tf_op jit(solution)/shard_map/forward_slot/pallas_call | solution.py:151
  343.1 13.9 %forward_slot.5 = (bf16[4,1024,512]{2,1,0:T(8,128)(2,1)}, bf16[4,1024,640]{2,1,0:T(8,128)(2,1)}, f32[4,1024,512]{2,1,0:T(8,128)}, f32[4,1,1024,128]{3,2,1,0:T(8,128)}, f32[4,1024,128]{2,1,0:T(8,128)}) custom-call(bf16[2,1024,256]{2,1,0:T(8,128)(2,1)} %pad_maximum_fusion.13.refs_0_.refs, ...), custom_call_target="tpu_custom_call", output_to_operand_aliasing={{0}: (18, {}), {1}: (19, {}), {2}: (20, {}), {3}: (21, {}),... | custom-call | flops 4831838208 | bytes 13631488 | tf_op jit(solution)/shard_map/forward_slot/pallas_call | solution.py:151
  357.5 14.2 %forward_slot.6 = (bf16[4,1024,512]{2,1,0:T(8,128)(2,1)}, bf16[4,1024,640]{2,1,0:T(8,128)(2,1)}, f32[4,1024,512]{2,1,0:T(8,128)}, f32[4,1,1024,128]{3,2,1,0:T(8,128)}, f32[4,1024,128]{2,1,0:T(8,128)}) custom-call(bf16[2,1024,256]{2,1,0:T(8,128)(2,1)} %pad_maximum_fusion.11.refs_0_.refs, ...), custom_call_target="tpu_custom_call", output_to_operand_aliasing={{0}: (18, {}), {1}: (19, {}), {2}: (20, {}), {3}: (21, {}),... | custom-call | flops 4831838208 | bytes 13631488 | tf_op jit(solution)/shard_map/forward_slot/pallas_call | solution.py:151
  372.3 14.0 %forward_slot.7 = (bf16[4,1024,512]{2,1,0:T(8,128)(2,1)}, bf16[4,1024,640]{2,1,0:T(8,128)(2,1)}, f32[4,1024,512]{2,1,0:T(8,128)}, f32[4,1,1024,128]{3,2,1,0:T(8,128)}, f32[4,1024,128]{2,1,0:T(8,128)}) custom-call(bf16[2,1024,256]{2,1,0:T(8,128)(2,1)} %pad_maximum_fusion.7.refs_0_.refs_, ...), custom_call_target="tpu_custom_call", output_to_operand_aliasing={{0}: (18, {}), {1}: (19, {}), {2}: (20, {}), {3}: (21, {}),... | custom-call | flops 4831838208 | bytes 13631488 | tf_op jit(solution)/shard_map/forward_slot/pallas_call | solution.py:151
  389.1 34.3 %collective-permute-start.47 = (bf16[4,1024,128]{2,1,0:T(8,128)(2,1)}, bf16[4,1024,128]{2,1,0:T(8,128)(2,1)}, u32[]{:S(2)}, u32[]{:S(2)}) collective-permute-start(bf16[4,1024,128]{2,1,0:T(8,128)(2,1)} %add_convert_fusion.5), channel_id=1, source_target_pairs={{0,1},{1,2},{2,3},{4,5},{5,6},{6,7},{8,9},{9,10},{10,11},{12,13},{... | collective-permute-start | bytes 3145736 | tf_op jit(solution)/shard_map/ppermute | solution.py:751
  424.1 21.0 %collective-permute-done.47 = bf16[4,1024,128]{2,1,0:T(8,128)(2,1)} collective-permute-done((bf16[4,1024,128]{2,1,0:T(8,128)(2,1)}, bf16[4,1024,128]{2,1,0:T(8,128)(2,1)}, u32[]{:S(2)}, u32[]{:S(2)}) %collective-permute-start.47) | collective-permute-done | bytes 1048608 | tf_op jit(solution)/shard_map/ppermute | solution.py:751
  449.0 5.6 collective-permute-start.48
  465.5 9.9 %collective-permute-done.48 = bf16[4,1024,128]{2,1,0:T(8,128)(2,1)} collective-permute-done((bf16[4,1024,128]{2,1,0:T(8,128)(2,1)}, bf16[4,1024,128]{2,1,0:T(8,128)(2,1)}, u32[]{:S(2)}, u32[]{:S(2)}) %collective-permute-start.48) | collective-permute-done | bytes 1048608 | tf_op jit(solution)/shard_map/ppermute | solution.py:751
  479.1 5.4 collective-permute-start.49
  486.2 7.3 all-reduce.4
  499.8 3.9 copy.267.refs_8_
  510.6 41.8 %gate.1 = (bf16[4,1024,512]{2,1,0:T(8,128)(2,1)}, bf16[4,1024,512]{2,1,0:T(8,128)(2,1)}, bf16[4,1024,512]{2,1,0:T(8,128)(2,1)}, f32[4,1024,128]{2,1,0:T(8,128)}) custom-call(bf16[2,2,1024,256]{3,2,1,0:T(8,128)(2,1)} %pad_maximum_fusion.2.refs_0_.refs_1_, bf16[2,2,1024,256]{3,2,1,0:T(8,128)(2,1)} %collective-permute-done.2.refs_1_.refs_2_, ...), custom_call_target="tpu_custom_call" | custom-call | flops 8589934592 | bytes 54525952 | tf_op jit(solution)/shard_map/gate/pallas_call | solution.py:250
  555.6 21.7 %output.1 = f32[512,2048]{1,0:T(8,128)} custom-call(bf16[4,1024,512]{2,1,0:T(8,128)(2,1)} %get-tuple-element.64.refs_0_, bf16[2,2,1024,256]{3,2,1,0:T(8,128)(2,1)} %pad_maximum_fusion.2.refs_0_.refs_1_, bf16[2,2,1024,256]{3,2,1,0:T(8,128)(2,1)} %collective-permute-done.2.refs_1_.refs_2_, bf16[2,2,1024,256]{3,2,1,0:T(8,128)(2,1)} %collective-permute-done.3.refs_2_.refs_3_, ...), custom_call_target="tpu_custom_call" | custom-call | flops 8589934592 | bytes 16777216 | tf_op jit(solution)/shard_map/output/pallas_call | solution.py:551
  579.2 34.5 %state_back.1 = (f32[4,1024,512]{2,1,0:T(8,128)}, f32[16,4,512]{2,1,0:T(4,128)}, f32[16,4,512]{2,1,0:T(4,128)}, f32[16,4,256]{2,1,0:T(4,128)}, f32[2,256,256]{2,...) custom-call(bf16[4,1024,512]{2,1,0:T(8,128)(2,1)} %get-tuple-element.66.refs_0_.refs_1_, ...), custom_call_target="tpu_custom_call" | custom-call | flops 21474836480 | bytes 25165824 | tf_op jit(solution)/shard_map/state_back/pallas_call | solution.py:354
  637.5 18.8 %collective-permute-done.51 = bf16[4,1024,128]{2,1,0:T(8,128)(2,1)S(1)} collective-permute-done((bf16[4,1024,128]{2,1,0:T(8,128)(2,1)S(1)}, bf16[4,1024,128]{2,1,0:T(8,128)(2,1)S(1)}, u32[]{:S(2)}, u32[]{:S(2)}) %collective-permute-start.51) | collective-permute-done | bytes 1048608 | tf_op jit(solution)/shard_map/ppermute | solution.py:761
  676.3 4.3 fusion.15
  685.7 23.0 %finish_back.1 = (f32[4,1024,512]{2,1,0:T(8,128)}, f32[16,4,512]{2,1,0:T(4,128)}, f32[16,4,512]{2,1,0:T(4,128)}, f32[16,4,128]{2,1,0:T(4,128)}, f32[128,512]{1,0:T(8,128)}) custom-call(f32[4,1024,512]{2,1,0:T(8,128)} %get-tuple-element.69.refs_0_, bf16[4,1024,512]{2,1,0:T(8,128)(2,1)} %get-tuple-element.66.refs_0_.refs_1_, ...), custom_call_target="tpu_custom_call" | custom-call | flops 1073741824 | bytes 29360128 | tf_op jit(solution)/shard_map/finish_back/pallas_call | solution.py:423
  713.5 3.1 slice_bitcast_fusion.1
  730.2 3.0 pad.15.refs_1_
  733.3 19.5 %pair.1 = (bf16[4,1024,512]{2,1,0:T(8,128)(2,1)}, f32[4,1024,32]{2,1,0:T(8,128)}, f32[4,1024,32]{2,1,0:T(8,128)}, f32[32,512]{1,0:T(8,128)}) custom-call(f32[4,1024,512]{2,1,0:T(8,128)} %get-tuple-element.71.refs_0_, f32[4,1024,128]{2,1,0:T(8,128)} %pad.15.refs_1_, bf16[4,1024,512]{2,1,0:T(8,128)(2,1)} %get-tuple-element.65.refs_2_.refs_0_, ...), custom_call_target="tpu_custom_call" | custom-call | flops 536870912 | bytes 16777216 | tf_op jit(solution)/shard_map/pair/pallas_call | solution.py:477
  752.7 4.6 add_bitcast_fusion
  759.9 5.1 reshape.208
  765.1 3.3 fusion.88
  783.3 4.0 collective-permute-done.55
  788.1 34.8 %input_back.1 = f32[512,2048]{1,0:T(8,128)} custom-call(bf16[4,1024,512]{2,1,0:T(8,128)(2,1)} %get-tuple-element.65.refs_2_.refs_0_, bf16[4,1024,512]{2,1,0:T(8,128)(2,1)} %get-tuple-element.76.refs_1_, bf16[2,1024,256]{2,1,0:T(8,128)(2,1)} %copy-done.18, bf16[2,1024,256]{2,1,0:T(8,128)(2,1)} %collective-permute-done.40.refs_1_.refs_3_, ...), custom_call_target="tpu_custom_call" | custom-call | flops 17179869184 | bytes 33554432 | tf_op jit(solution)/shard_map/input_back/pallas_call | solution.py:551
  840.7 4.6 fusion.14
  845.4 3.0 fusion.23
  848.9 6.2 reshape.213
  855.1 6.1 copy.290
  861.2 3.4 reshape.214
  864.6 3.5 copy.291
  870.8 4.8 reshape_squeeze.8
  875.6 6.0 copy.289
  (495 shorter events, 245.4 us)
Async XLA Ops:
  7.2 273.8 %all-gather.8.cloned.1.call-start = ((), (), s32[]{:S(2)}) async-start(), calls=%async_computation | async-start | bytes 1769472 | tf_op jit(solution)/shard_map/all_gather | solution.py:685
  11.0 162.6 %collective-permute-start.30 = (bf16[2,1024,256]{2,1,0:T(8,128)(2,1)}, bf16[2,1024,256]{2,1,0:T(8,128)(2,1)}, u32[]{:S(2)}, u32[]{:S(2)}) collective-permute-start(bf16[2,1024,256]{2,1,0:T(8,128)(2,1)} %bitcast.216), channel_id=1, source_target_pairs={{1,0},{2,1},{3,2},{0,3},{5,4},{6,5},{7,6},{4,7},{9,8},{10,9},{11,1... | collective-permute-start | bytes 3145736 | tf_op jit(solution)/shard_map/ppermute | solution.py:606
  16.1 157.6 %collective-permute-start.21 = (bf16[2,1024,256]{2,1,0:T(8,128)(2,1)}, bf16[2,1024,256]{2,1,0:T(8,128)(2,1)}, u32[]{:S(2)}, u32[]{:S(2)}) collective-permute-start(bf16[2,1024,256]{2,1,0:T(8,128)(2,1)} %bitcast.217), channel_id=1, source_target_pairs={{2,0},{3,1},{0,2},{1,3},{6,4},{7,5},{4,6},{5,7},{10,8},{11,9},{8,1... | collective-permute-start | bytes 3145736 | tf_op jit(solution)/shard_map/ppermute | solution.py:606
  93.2 742.9 %all-gather.10.cloned.1.call-start = ((), (), s32[]{:S(2)}) async-start(), calls=%async_computation.1 | async-start | bytes 1179648 | tf_op jit(solution)/shard_map/all_gather | solution.py:860
  96.4 41.1 %collective-permute-start.11 = (bf16[16,2048]{1,0:T(8,128)(2,1)}, bf16[16,2048]{1,0:T(8,128)(2,1)}, u32[]{:S(2)}, u32[]{:S(2)}) collective-permute-start(bf16[16,2048]{1,0:T(8,128)(2,1)} %slice.295), channel_id=1, source_target_pairs={{0,1},{1,2},{2,3},{4,5},{5,6},{6,7},{8,9},{9,10},{10,11},{12,13},{... | collective-permute-start | bytes 196616 | tf_op jit(solution)/shard_map/ppermute | solution.py:694
  99.6 38.7 %collective-permute-start.39 = (bf16[1024,256]{1,0:T(8,128)(2,1)}, bf16[1024,256]{1,0:T(8,128)(2,1)}, u32[]{:S(2)}, u32[]{:S(2)}) collective-permute-start(bf16[1024,256]{1,0:T(8,128)(2,1)} %get-tuple-element.132), channel_id=1, source_target_pairs={{0,8},{4,12},{8,0},{12,4},{16,24},{20,28},{24,16},{28,20},{1,9},{5... | collective-permute-start | bytes 1572872 | tf_op jit(solution)/shard_map/ppermute | solution.py:609
  101.1 38.6 %collective-permute-start.43 = (bf16[1024,256]{1,0:T(8,128)(2,1)}, bf16[1024,256]{1,0:T(8,128)(2,1)}, u32[]{:S(2)}, u32[]{:S(2)}) collective-permute-start(bf16[1024,256]{1,0:T(8,128)(2,1)} %get-tuple-element.133), channel_id=1, source_target_pairs={{0,16},{4,20},{8,24},{12,28},{16,0},{20,4},{24,8},{28,12},{1,17},{... | collective-permute-start | bytes 1572872 | tf_op jit(solution)/shard_map/ppermute | solution.py:609
  137.4 32.4 %collective-permute-start.5 = (bf16[1024,256]{1,0:T(8,128)(2,1)S(1)}, bf16[1024,256]{1,0:T(8,128)(2,1)S(1)}, u32[]{:S(2)}, u32[]{:S(2)}) collective-permute-start(bf16[1024,256]{1,0:T(8,128)(2,1)S(1)} %copy-done.50), channel_id=1, source_target_pairs={{2,0},{3,1},{0,2},{1,3},{6,4},{7,5},{4,6},{5,7},{10,8},{11,9},{8,1... | collective-permute-start | bytes 1572872 | tf_op jit(solution)/shard_map/ppermute | solution.py:606
  138.4 34.1 %collective-permute-start.6 = (bf16[1024,256]{1,0:T(8,128)(2,1)S(1)}, bf16[1024,256]{1,0:T(8,128)(2,1)S(1)}, u32[]{:S(2)}, u32[]{:S(2)}) collective-permute-start(bf16[1024,256]{1,0:T(8,128)(2,1)S(1)} %copy-done.50), channel_id=1, source_target_pairs={{3,0},{0,1},{1,2},{2,3},{7,4},{4,5},{5,6},{6,7},{11,8},{8,9},{9,10... | collective-permute-start | bytes 1572872 | tf_op jit(solution)/shard_map/ppermute | solution.py:606
  139.8 33.3 %collective-permute-start = (bf16[1024,256]{1,0:T(8,128)(2,1)S(1)}, bf16[1024,256]{1,0:T(8,128)(2,1)S(1)}, u32[]{:S(2)}, u32[]{:S(2)}) collective-permute-start(bf16[1024,256]{1,0:T(8,128)(2,1)S(1)} %copy-done.50), channel_id=1, source_target_pairs={{1,0},{2,1},{3,2},{0,3},{5,4},{6,5},{7,6},{4,7},{9,8},{10,9},{11,1... | collective-permute-start | bytes 1572872 | tf_op jit(solution)/shard_map/ppermute | solution.py:606
  169.8 24.7 %collective-permute-start.12 = (bf16[2,1024,256]{2,1,0:T(8,128)(2,1)S(1)}, bf16[2,1024,256]{2,1,0:T(8,128)(2,1)S(1)}, u32[]{:S(2)}, u32[]{:S(2)}) collective-permute-start(bf16[2,1024,256]{2,1,0:T(8,128)(2,1)S(1)} %bitcast.219), channel_id=1, source_target_pairs={{3,0},{0,1},{1,2},{2,3},{7,4},{4,5},{5,6},{6,7},{11,8},{8,9},{9,10... | collective-permute-start | bytes 3145736 | tf_op jit(solution)/shard_map/ppermute | solution.py:606
  172.5 24.7 %collective-permute-start.40 = (bf16[2,1024,256]{2,1,0:T(8,128)(2,1)S(1)}, bf16[2,1024,256]{2,1,0:T(8,128)(2,1)}, u32[]{:S(2)}, u32[]{:S(2)}) collective-permute-start(bf16[2,1024,256]{2,1,0:T(8,128)(2,1)S(1)} %pad_maximum_fusion.15.refs_0_.refs_2_), channel_id=1, source_target_pairs={{0,16},{4,20},{8,24},{12,28},{16,0},{20,4},{24,8},{28,12},{1,17},{... | collective-permute-start | bytes 3145736 | tf_op jit(solution)/shard_map/ppermute | solution.py:609
  173.1 24.7 %collective-permute-start.44 = (bf16[2,1024,256]{2,1,0:T(8,128)(2,1)S(1)}, bf16[2,1024,256]{2,1,0:T(8,128)(2,1)}, u32[]{:S(2)}, u32[]{:S(2)}) collective-permute-start(bf16[2,1024,256]{2,1,0:T(8,128)(2,1)S(1)} %pad_maximum_fusion.16.refs_4_.refs_6_), channel_id=1, source_target_pairs={{0,8},{4,12},{8,0},{12,4},{16,24},{20,28},{24,16},{28,20},{1,9},{5... | collective-permute-start | bytes 3145736 | tf_op jit(solution)/shard_map/ppermute | solution.py:609
  173.6 26.7 %collective-permute-start.41 = (bf16[2,1024,256]{2,1,0:T(8,128)(2,1)S(1)}, bf16[2,1024,256]{2,1,0:T(8,128)(2,1)S(1)}, u32[]{:S(2)}, u32[]{:S(2)}) collective-permute-start(bf16[2,1024,256]{2,1,0:T(8,128)(2,1)S(1)} %pad_maximum_fusion.15.refs_0_.refs_2_), channel_id=1, source_target_pairs={{0,4},{4,0},{8,12},{12,8},{16,20},{20,16},{24,28},{28,24},{1,5},{5... | collective-permute-start | bytes 3145736 | tf_op jit(solution)/shard_map/ppermute | solution.py:609
  173.7 28.1 %collective-permute-start.45 = (bf16[2,1024,256]{2,1,0:T(8,128)(2,1)S(1)}, bf16[2,1024,256]{2,1,0:T(8,128)(2,1)S(1)}, u32[]{:S(2)}, u32[]{:S(2)}) collective-permute-start(bf16[2,1024,256]{2,1,0:T(8,128)(2,1)S(1)} %pad_maximum_fusion.16.refs_4_.refs_6_), channel_id=1, source_target_pairs={{0,4},{4,0},{8,12},{12,8},{16,20},{20,16},{24,28},{28,24},{1,5},{5... | collective-permute-start | bytes 3145736 | tf_op jit(solution)/shard_map/ppermute | solution.py:609
  200.4 53.0 %collective-permute-start.7 = (bf16[2,1024,256]{2,1,0:T(8,128)(2,1)S(1)}, bf16[2,1024,256]{2,1,0:T(8,128)(2,1)S(1)}, u32[]{:S(2)}, u32[]{:S(2)}) collective-permute-start(bf16[2,1024,256]{2,1,0:T(8,128)(2,1)S(1)} %get-tuple-element.151), channel_id=1, source_target_pairs={{0,16},{4,20},{8,24},{12,28},{16,0},{20,4},{24,8},{28,12},{1,17},{... | collective-permute-start | bytes 3145736 | tf_op jit(solution)/shard_map/ppermute | solution.py:609
  201.8 53.3 %collective-permute-start.1 = (bf16[2,1024,256]{2,1,0:T(8,128)(2,1)S(1)}, bf16[2,1024,256]{2,1,0:T(8,128)(2,1)S(1)}, u32[]{:S(2)}, u32[]{:S(2)}) collective-permute-start(bf16[2,1024,256]{2,1,0:T(8,128)(2,1)S(1)} %get-tuple-element.153), channel_id=1, source_target_pairs={{0,8},{4,12},{8,0},{12,4},{16,24},{20,28},{24,16},{28,20},{1,9},{5... | collective-permute-start | bytes 3145736 | tf_op jit(solution)/shard_map/ppermute | solution.py:609
  209.4 36.4 %collective-permute-start.26 = (bf16[1024,256]{1,0:T(8,128)(2,1)S(1)}, bf16[1024,256]{1,0:T(8,128)(2,1)S(1)}, u32[]{:S(2)}, u32[]{:S(2)}) collective-permute-start(bf16[1024,256]{1,0:T(8,128)(2,1)S(1)} %get-tuple-element.141), channel_id=1, source_target_pairs={{0,16},{4,20},{8,24},{12,28},{16,0},{20,4},{24,8},{28,12},{1,17},{... | collective-permute-start | bytes 1572872 | tf_op jit(solution)/shard_map/ppermute | solution.py:609
  212.1 39.8 %collective-permute-start.13 = (bf16[1024,256]{1,0:T(8,128)(2,1)S(1)}, bf16[1024,256]{1,0:T(8,128)(2,1)S(1)}, u32[]{:S(2)}, u32[]{:S(2)}) collective-permute-start(bf16[1024,256]{1,0:T(8,128)(2,1)S(1)} %get-tuple-element.147), channel_id=1, source_target_pairs={{0,8},{4,12},{8,0},{12,4},{16,24},{20,28},{24,16},{28,20},{1,9},{5... | collective-permute-start | bytes 1572872 | tf_op jit(solution)/shard_map/ppermute | solution.py:609
  220.6 32.7 %collective-permute-start.17 = (bf16[1024,256]{1,0:T(8,128)(2,1)S(1)}, bf16[1024,256]{1,0:T(8,128)(2,1)S(1)}, u32[]{:S(2)}, u32[]{:S(2)}) collective-permute-start(bf16[1024,256]{1,0:T(8,128)(2,1)S(1)} %get-tuple-element.148), channel_id=1, source_target_pairs={{0,16},{4,20},{8,24},{12,28},{16,0},{20,4},{24,8},{28,12},{1,17},{... | collective-permute-start | bytes 1572872 | tf_op jit(solution)/shard_map/ppermute | solution.py:609
  245.8 25.4 %collective-permute-start.42 = (bf16[2,1024,256]{2,1,0:T(8,128)(2,1)}, bf16[2,1024,256]{2,1,0:T(8,128)(2,1)}, u32[]{:S(2)}, u32[]{:S(2)}) collective-permute-start(bf16[2,1024,256]{2,1,0:T(8,128)(2,1)} %collective-permute-done.40.refs_1_.refs_3_), channel_id=1, source_target_pairs={{0,4},{4,0},{8,12},{12,8},{16,20},{20,16},{24,28},{28,24},{1,5},{5... | collective-permute-start | bytes 3145736 | tf_op jit(solution)/shard_map/ppermute | solution.py:609
  251.9 23.3 %collective-permute-start.32 = (bf16[2,1024,256]{2,1,0:T(8,128)(2,1)}, bf16[2,1024,256]{2,1,0:T(8,128)(2,1)}, u32[]{:S(2)}, u32[]{:S(2)}) collective-permute-start(bf16[2,1024,256]{2,1,0:T(8,128)(2,1)} %pad_maximum_fusion.13.refs_0_.refs_10_), channel_id=1, source_target_pairs={{0,16},{4,20},{8,24},{12,28},{16,0},{20,4},{24,8},{28,12},{1,17},{... | collective-permute-start | bytes 3145736 | tf_op jit(solution)/shard_map/ppermute | solution.py:609
  253.3 27.6 %collective-permute-start.33 = (bf16[2,1024,256]{2,1,0:T(8,128)(2,1)}, bf16[2,1024,256]{2,1,0:T(8,128)(2,1)}, u32[]{:S(2)}, u32[]{:S(2)}) collective-permute-start(bf16[2,1024,256]{2,1,0:T(8,128)(2,1)} %pad_maximum_fusion.13.refs_0_.refs_10_), channel_id=1, source_target_pairs={{0,4},{4,0},{8,12},{12,8},{16,20},{20,16},{24,28},{28,24},{1,5},{5... | collective-permute-start | bytes 3145736 | tf_op jit(solution)/shard_map/ppermute | solution.py:609
  253.4 25.9 %collective-permute-start.36 = (bf16[2,1024,256]{2,1,0:T(8,128)(2,1)}, bf16[2,1024,256]{2,1,0:T(8,128)(2,1)}, u32[]{:S(2)}, u32[]{:S(2)}) collective-permute-start(bf16[2,1024,256]{2,1,0:T(8,128)(2,1)} %pad_maximum_fusion.14.refs_4_.refs_14_), channel_id=1, source_target_pairs={{0,8},{4,12},{8,0},{12,4},{16,24},{20,28},{24,16},{28,20},{1,9},{5... | collective-permute-start | bytes 3145736 | tf_op jit(solution)/shard_map/ppermute | solution.py:609
  273.5 26.3 %collective-permute-start.23 = (bf16[2,1024,256]{2,1,0:T(8,128)(2,1)}, bf16[2,1024,256]{2,1,0:T(8,128)(2,1)}, u32[]{:S(2)}, u32[]{:S(2)}) collective-permute-start(bf16[2,1024,256]{2,1,0:T(8,128)(2,1)} %pad_maximum_fusion.11.refs_0_.refs_18_), channel_id=1, source_target_pairs={{0,16},{4,20},{8,24},{12,28},{16,0},{20,4},{24,8},{28,12},{1,17},{... | collective-permute-start | bytes 3145736 | tf_op jit(solution)/shard_map/ppermute | solution.py:609
  275.2 30.5 %collective-permute-start.24 = (bf16[2,1024,256]{2,1,0:T(8,128)(2,1)}, bf16[2,1024,256]{2,1,0:T(8,128)(2,1)}, u32[]{:S(2)}, u32[]{:S(2)}) collective-permute-start(bf16[2,1024,256]{2,1,0:T(8,128)(2,1)} %pad_maximum_fusion.11.refs_0_.refs_18_), channel_id=1, source_target_pairs={{0,4},{4,0},{8,12},{12,8},{16,20},{20,16},{24,28},{28,24},{1,5},{5... | collective-permute-start | bytes 3145736 | tf_op jit(solution)/shard_map/ppermute | solution.py:609
  279.2 26.4 %collective-permute-start.27 = (bf16[2,1024,256]{2,1,0:T(8,128)(2,1)}, bf16[2,1024,256]{2,1,0:T(8,128)(2,1)}, u32[]{:S(2)}, u32[]{:S(2)}) collective-permute-start(bf16[2,1024,256]{2,1,0:T(8,128)(2,1)} %pad_maximum_fusion.12.refs_4_.refs_22_), channel_id=1, source_target_pairs={{0,8},{4,12},{8,0},{12,4},{16,24},{20,28},{24,16},{28,20},{1,9},{5... | collective-permute-start | bytes 3145736 | tf_op jit(solution)/shard_map/ppermute | solution.py:609
  281.0 25.2 %collective-permute-start.28 = (bf16[2,1024,256]{2,1,0:T(8,128)(2,1)}, bf16[2,1024,256]{2,1,0:T(8,128)(2,1)}, u32[]{:S(2)}, u32[]{:S(2)}) collective-permute-start(bf16[2,1024,256]{2,1,0:T(8,128)(2,1)} %pad_maximum_fusion.12.refs_4_.refs_22_), channel_id=1, source_target_pairs={{0,4},{4,0},{8,12},{12,8},{16,20},{20,16},{24,28},{28,24},{1,5},{5... | collective-permute-start | bytes 3145736 | tf_op jit(solution)/shard_map/ppermute | solution.py:609
  284.4 37.3 %collective-permute-start.14 = (bf16[2,1024,256]{2,1,0:T(8,128)(2,1)}, bf16[2,1024,256]{2,1,0:T(8,128)(2,1)}, u32[]{:S(2)}, u32[]{:S(2)}) collective-permute-start(bf16[2,1024,256]{2,1,0:T(8,128)(2,1)} %pad_maximum_fusion.7.refs_0_.refs_26_), channel_id=1, source_target_pairs={{0,16},{4,20},{8,24},{12,28},{16,0},{20,4},{24,8},{28,12},{1,17},{... | collective-permute-start | bytes 3145736 | tf_op jit(solution)/shard_map/ppermute | solution.py:609
  299.8 28.3 %collective-permute-start.18 = (bf16[2,1024,256]{2,1,0:T(8,128)(2,1)S(1)}, bf16[2,1024,256]{2,1,0:T(8,128)(2,1)}, u32[]{:S(2)}, u32[]{:S(2)}) collective-permute-start(bf16[2,1024,256]{2,1,0:T(8,128)(2,1)S(1)} %copy-done.20), channel_id=1, source_target_pairs={{0,8},{4,12},{8,0},{12,4},{16,24},{20,28},{24,16},{28,20},{1,9},{5... | collective-permute-start | bytes 3145736 | tf_op jit(solution)/shard_map/ppermute | solution.py:609
  321.7 35.4 %collective-permute-start.29 = (bf16[2,1024,256]{2,1,0:T(8,128)(2,1)}, bf16[2,1024,256]{2,1,0:T(8,128)(2,1)}, u32[]{:S(2)}, u32[]{:S(2)}) collective-permute-start(bf16[2,1024,256]{2,1,0:T(8,128)(2,1)} %collective-permute-done.27.refs_5_.refs_23_), channel_id=1, source_target_pairs={{0,4},{4,0},{8,12},{12,8},{16,20},{20,16},{24,28},{28,24},{1,5},{5... | collective-permute-start | bytes 3145736 | tf_op jit(solution)/shard_map/ppermute | solution.py:609
  328.1 43.6 %collective-permute-start.15 = (bf16[2,1024,256]{2,1,0:T(8,128)(2,1)}, bf16[2,1024,256]{2,1,0:T(8,128)(2,1)}, u32[]{:S(2)}, u32[]{:S(2)}) collective-permute-start(bf16[2,1024,256]{2,1,0:T(8,128)(2,1)} %pad_maximum_fusion.7.refs_0_.refs_26_), channel_id=1, source_target_pairs={{0,4},{4,0},{8,12},{12,8},{16,20},{20,16},{24,28},{28,24},{1,5},{5... | collective-permute-start | bytes 3145736 | tf_op jit(solution)/shard_map/ppermute | solution.py:609
  328.6 43.6 %collective-permute-start.19 = (bf16[2,1024,256]{2,1,0:T(8,128)(2,1)S(1)}, bf16[2,1024,256]{2,1,0:T(8,128)(2,1)}, u32[]{:S(2)}, u32[]{:S(2)}) collective-permute-start(bf16[2,1024,256]{2,1,0:T(8,128)(2,1)S(1)} %copy-done.20), channel_id=1, source_target_pairs={{0,4},{4,0},{8,12},{12,8},{16,20},{20,16},{24,28},{28,24},{1,5},{5... | collective-permute-start | bytes 3145736 | tf_op jit(solution)/shard_map/ppermute | solution.py:609
  328.7 43.6 %collective-permute-start.16 = (bf16[2,1024,256]{2,1,0:T(8,128)(2,1)}, bf16[2,1024,256]{2,1,0:T(8,128)(2,1)}, u32[]{:S(2)}, u32[]{:S(2)}) collective-permute-start(bf16[2,1024,256]{2,1,0:T(8,128)(2,1)} %collective-permute-done.14.refs_1_.refs_27_), channel_id=1, source_target_pairs={{0,4},{4,0},{8,12},{12,8},{16,20},{20,16},{24,28},{28,24},{1,5},{5... | collective-permute-start | bytes 3145736 | tf_op jit(solution)/shard_map/ppermute | solution.py:609
  329.1 43.1 %collective-permute-start.20 = (bf16[2,1024,256]{2,1,0:T(8,128)(2,1)}, bf16[2,1024,256]{2,1,0:T(8,128)(2,1)}, u32[]{:S(2)}, u32[]{:S(2)}) collective-permute-start(bf16[2,1024,256]{2,1,0:T(8,128)(2,1)} %collective-permute-done.18.refs_5_.refs_31_), channel_id=1, source_target_pairs={{0,4},{4,0},{8,12},{12,8},{16,20},{20,16},{24,28},{28,24},{1,5},{5... | collective-permute-start | bytes 3145736 | tf_op jit(solution)/shard_map/ppermute | solution.py:609
  357.1 98.0 %collective-permute-start.8 = (bf16[2,2,1024,256]{3,2,1,0:T(8,128)(2,1)}, bf16[2,2,1024,256]{3,2,1,0:T(8,128)(2,1)}, u32[]{:S(2)}, u32[]{:S(2)}) collective-permute-start(bf16[2,2,1024,256]{3,2,1,0:T(8,128)(2,1)} %pad_maximum_fusion.3.refs_4_.refs_5_), channel_id=1, source_target_pairs={{0,8},{4,12},{8,0},{12,4},{16,24},{20,28},{24,16},{28,20},{1,9},{5... | collective-permute-start | bytes 6291464 | tf_op jit(solution)/shard_map/ppermute | solution.py:609
  371.7 83.4 %collective-permute-start.2 = (bf16[2,2,1024,256]{3,2,1,0:T(8,128)(2,1)}, bf16[2,2,1024,256]{3,2,1,0:T(8,128)(2,1)}, u32[]{:S(2)}, u32[]{:S(2)}) collective-permute-start(bf16[2,2,1024,256]{3,2,1,0:T(8,128)(2,1)} %pad_maximum_fusion.2.refs_0_.refs_1_), channel_id=1, source_target_pairs={{0,16},{4,20},{8,24},{12,28},{16,0},{20,4},{24,8},{28,12},{1,17},{... | collective-permute-start | bytes 6291464 | tf_op jit(solution)/shard_map/ppermute | solution.py:609
  389.1 56.0 %collective-permute-start.47 = (bf16[4,1024,128]{2,1,0:T(8,128)(2,1)}, bf16[4,1024,128]{2,1,0:T(8,128)(2,1)}, u32[]{:S(2)}, u32[]{:S(2)}) collective-permute-start(bf16[4,1024,128]{2,1,0:T(8,128)(2,1)} %add_convert_fusion.5), channel_id=1, source_target_pairs={{0,1},{1,2},{2,3},{4,5},{5,6},{6,7},{8,9},{9,10},{10,11},{12,13},{... | collective-permute-start | bytes 3145736 | tf_op jit(solution)/shard_map/ppermute | solution.py:751
  449.0 26.4 %collective-permute-start.48 = (bf16[4,1024,128]{2,1,0:T(8,128)(2,1)}, bf16[4,1024,128]{2,1,0:T(8,128)(2,1)}, u32[]{:S(2)}, u32[]{:S(2)}) collective-permute-start(bf16[4,1024,128]{2,1,0:T(8,128)(2,1)} %add_convert_fusion.4), channel_id=1, source_target_pairs={{0,1},{1,2},{2,3},{4,5},{5,6},{6,7},{8,9},{9,10},{10,11},{12,13},{... | collective-permute-start | bytes 3145736 | tf_op jit(solution)/shard_map/ppermute | solution.py:751
  454.6 56.0 %collective-permute-start.9 = (bf16[2,2,1024,256]{3,2,1,0:T(8,128)(2,1)}, bf16[2,2,1024,256]{3,2,1,0:T(8,128)(2,1)}, u32[]{:S(2)}, u32[]{:S(2)}) collective-permute-start(bf16[2,2,1024,256]{3,2,1,0:T(8,128)(2,1)} %pad_maximum_fusion.3.refs_4_.refs_5_), channel_id=1, source_target_pairs={{0,4},{4,0},{8,12},{12,8},{16,20},{20,16},{24,28},{28,24},{1,5},{5... | collective-permute-start | bytes 6291464 | tf_op jit(solution)/shard_map/ppermute | solution.py:609
  454.6 56.0 %collective-permute-start.3 = (bf16[2,2,1024,256]{3,2,1,0:T(8,128)(2,1)}, bf16[2,2,1024,256]{3,2,1,0:T(8,128)(2,1)}, u32[]{:S(2)}, u32[]{:S(2)}) collective-permute-start(bf16[2,2,1024,256]{3,2,1,0:T(8,128)(2,1)} %pad_maximum_fusion.2.refs_0_.refs_1_), channel_id=1, source_target_pairs={{0,4},{4,0},{8,12},{12,8},{16,20},{20,16},{24,28},{28,24},{1,5},{5... | collective-permute-start | bytes 6291464 | tf_op jit(solution)/shard_map/ppermute | solution.py:609
  455.1 55.5 %collective-permute-start.10 = (bf16[2,2,1024,256]{3,2,1,0:T(8,128)(2,1)}, bf16[2,2,1024,256]{3,2,1,0:T(8,128)(2,1)}, u32[]{:S(2)}, u32[]{:S(2)}) collective-permute-start(bf16[2,2,1024,256]{3,2,1,0:T(8,128)(2,1)} %collective-permute-done.8.refs_5_.refs_6_), channel_id=1, source_target_pairs={{0,4},{4,0},{8,12},{12,8},{16,20},{20,16},{24,28},{28,24},{1,5},{5... | collective-permute-start | bytes 6291464 | tf_op jit(solution)/shard_map/ppermute | solution.py:609
  455.1 55.4 %collective-permute-start.4 = (bf16[2,2,1024,256]{3,2,1,0:T(8,128)(2,1)}, bf16[2,2,1024,256]{3,2,1,0:T(8,128)(2,1)}, u32[]{:S(2)}, u32[]{:S(2)}) collective-permute-start(bf16[2,2,1024,256]{3,2,1,0:T(8,128)(2,1)} %collective-permute-done.2.refs_1_.refs_2_), channel_id=1, source_target_pairs={{0,4},{4,0},{8,12},{12,8},{16,20},{20,16},{24,28},{28,24},{1,5},{5... | collective-permute-start | bytes 6291464 | tf_op jit(solution)/shard_map/ppermute | solution.py:609
  479.1 28.2 %collective-permute-start.49 = (bf16[4,1024,128]{2,1,0:T(8,128)(2,1)}, bf16[4,1024,128]{2,1,0:T(8,128)(2,1)}, u32[]{:S(2)}, u32[]{:S(2)}) collective-permute-start(bf16[4,1024,128]{2,1,0:T(8,128)(2,1)} %add_convert_fusion.3), channel_id=1, source_target_pairs={{0,1},{1,2},{2,3},{4,5},{5,6},{6,7},{8,9},{9,10},{10,11},{12,13},{... | collective-permute-start | bytes 3145736 | tf_op jit(solution)/shard_map/ppermute | solution.py:751
  554.3 73.0 %collective-permute-start.50 = (bf16[4,1024,128]{2,1,0:T(8,128)(2,1)S(1)}, bf16[4,1024,128]{2,1,0:T(8,128)(2,1)}, u32[]{:S(2)}, u32[]{:S(2)}) collective-permute-start(bf16[4,1024,128]{2,1,0:T(8,128)(2,1)S(1)} %add_convert_fusion.2), channel_id=1, source_target_pairs={{1,0},{2,1},{3,2},{5,4},{6,5},{7,6},{9,8},{10,9},{11,10},{13,12},{... | collective-permute-start | bytes 3145736 | tf_op jit(solution)/shard_map/ppermute | solution.py:761
  630.2 26.1 %collective-permute-start.51 = (bf16[4,1024,128]{2,1,0:T(8,128)(2,1)S(1)}, bf16[4,1024,128]{2,1,0:T(8,128)(2,1)S(1)}, u32[]{:S(2)}, u32[]{:S(2)}) collective-permute-start(bf16[4,1024,128]{2,1,0:T(8,128)(2,1)S(1)} %add_convert_fusion.1), channel_id=1, source_target_pairs={{1,0},{2,1},{3,2},{5,4},{6,5},{7,6},{9,8},{10,9},{11,10},{13,12},{... | collective-permute-start | bytes 3145736 | tf_op jit(solution)/shard_map/ppermute | solution.py:761
  657.9 24.6 %collective-permute-start.52 = (bf16[4,1024,128]{2,1,0:T(8,128)(2,1)}, bf16[4,1024,128]{2,1,0:T(8,128)(2,1)}, u32[]{:S(2)}, u32[]{:S(2)}) collective-permute-start(bf16[4,1024,128]{2,1,0:T(8,128)(2,1)} %add_convert_fusion), channel_id=1, source_target_pairs={{1,0},{2,1},{3,2},{5,4},{6,5},{7,6},{9,8},{10,9},{11,10},{13,12},{... | collective-permute-start | bytes 3145736 | tf_op jit(solution)/shard_map/ppermute | solution.py:761
  788.1 80.6 %all-gather.12.cloned.1.call-start = ((), (), s32[]{:S(2)}) async-start(), calls=%async_computation.2 | async-start | bytes 1310720 | tf_op jit(solution)/shard_map/all_gather | solution.py:862
  (109 other events, 2733.9 us)
Sparse Core Ops, SparseCore 0:
  93.4 26.5 all-gather.7
  788.2 23.3 all-gather.9
  840.8 27.7 all-gather.11

commit v2 on v1

v2 whole, which is shorter than its diff:
```python
import functools

import jax
import jax.numpy as jnp
from jax import lax
from jax.experimental import pallas as pl
from jax.experimental.pallas import tpu as pltpu
from jax.sharding import PartitionSpec as P

f32 = jnp.float32
bf16 = jnp.bfloat16
epsilon = 1e-05
highest = lax.Precision.HIGHEST
LOG2E = 1.4426950408889634
HEAD = 64
HALO = 128
SUB = 256
CB = 256

NN = ((1,), (0,))
NT = ((1,), (1,))
TN = ((0,), (0,))


def dot(a, b, dims=NN):
    return lax.dot_general(a, b, (dims, ((), ())), preferred_element_type=f32)


def compiler_params(grid_rank):
    return pltpu.CompilerParams(
        dimension_semantics=("arbitrary",) * grid_rank, vmem_limit_bytes=60 * 2**20
    )


def cost(flops, size):
    return pl.CostEstimate(
        flops=int(flops) // 8, bytes_accessed=int(size) // 8, transcendentals=0
    )


def sigmoid(v):
    return 0.5 + 0.5 * jnp.tanh(0.5 * v)


def conv_values(raw, chan):
    out = raw * chan[:, 3:4]
    for k in range(3):
        out = out + pltpu.roll(raw, 3 - k, 1) * chan[:, k : k + 1]
    return out[:, HALO:]


def per_head(values, rows):
    hb = rows.shape[0]
    parts = [values[h * HEAD : (h + 1) * HEAD] * rows[h : h + 1] for h in range(hb)]
    return jnp.concatenate(parts, axis=0)


def head_sums(values, hb):
    parts = [
        jnp.sum(values[h * HEAD : (h + 1) * HEAD], axis=0, keepdims=True) for h in range(hb)
    ]
    return jnp.concatenate(parts, axis=0)


def joined(refs, picks):
    parts = [refs[k][b] for k, b in picks]
    return parts[0] if len(parts) == 1 else jnp.concatenate(parts, axis=1)


def block_at(mine, m, quick):
    return pl.multiple_of((mine ^ m) * CB, CB) if quick else m * CB


def turn_kernel(flat, quick, *refs):
    (sc, tok_r, bef_r, cot_r, gain, down, up) = refs[:7]
    normed_o, masked_o, root_o, low_o, back_o, nt_o, gt_o, tok_o, halo_sc = refs[-9:]
    tok_o[...] = jnp.zeros_like(tok_o)
    width = tok_r.shape[1]
    length = tok_r.shape[0]

    def norm(v):
        v = v.astype(f32)
        root = lax.rsqrt(jnp.sum(v * v, axis=1, keepdims=True) * (1.0 / width) + epsilon)
        return (v * root * gain[...]).astype(bf16), root

    normed, root = norm(tok_r[...])
    normed_o[...] = normed
    root_o[...] = root
    halo_sc[...] = jnp.zeros_like(halo_sc)
    halo_sc[HALO - 16 :, :] = norm(bef_r[...])[0]
    rows = lax.broadcasted_iota(jnp.int32, (length, 1), 0)
    masked_o[...] = jnp.where(rows < sc[1], cot_r[...].astype(f32), 0.0).astype(bf16)
    low = back = None
    for i, m in enumerate(flat):
        at = pl.ds(block_at(sc[0], m, quick), CB)
        nt = jnp.concatenate(
            [jnp.transpose(halo_sc[:, at]), jnp.transpose(normed_o[:, at])], axis=1
        )
        gt = jnp.transpose(masked_o[:, at])
        nt_o[i * CB : (i + 1) * CB, :] = nt
        gt_o[i * CB : (i + 1) * CB, :] = gt
        low_m = dot(down[at, :], nt, TN)
        back_m = dot(up[:, at], gt)
        low = low_m if low is None else low + low_m
        back = back_m if back is None else back + back_m
    for out, v in ((low_o, low), (back_o, back)):
        hi = v.astype(bf16)
        out[...] = jnp.concatenate([hi, (v - hi.astype(f32)).astype(bf16)], axis=0)


def turn_call(sc, tokens, before, cot, gain, down, up, flat, quick, later):
    length, width = tokens.shape
    rank = up.shape[0]
    ext = length + HALO
    vm = pl.BlockSpec(memory_space=pltpu.VMEM)
    return pl.pallas_call(
        functools.partial(turn_kernel, flat, quick),
        in_specs=[pl.BlockSpec(memory_space=pltpu.SMEM)] + [vm] * 6
        + [pl.BlockSpec(memory_space=pl.ANY)] * len(later),
        out_specs=[vm] * 8,
        out_shape=[
            jax.ShapeDtypeStruct((length, width), bf16),
            jax.ShapeDtypeStruct((length, width), bf16),
            jax.ShapeDtypeStruct((length, 1), f32),
            jax.ShapeDtypeStruct((2 * rank, ext), bf16),
            jax.ShapeDtypeStruct((2 * rank, length), bf16),
            jax.ShapeDtypeStruct((width, ext), bf16),
            jax.ShapeDtypeStruct((width, length), bf16),
            jax.ShapeDtypeStruct((8, 128), f32),
        ],
        scratch_shapes=[pltpu.VMEM((HALO, width), bf16)],
        compiler_params=compiler_params(0),
        cost_estimate=cost(length * width * 200, length * width * 16),
        name="turn",
    )(sc, tokens, before, cot, gain, down, up, *later)


def row_specs(paths, first, rows):
    ops, specs = [], []
    for arrays in paths:
        for a in arrays:
            ops.append(a)
            specs.append(
                pl.BlockSpec((a.shape[0], rows, a.shape[2]), lambda i: (0, first // rows, 0))
            )
    return ops, specs


def maps_kernel(n_w, picks, sub, *refs):
    nt, taps = refs[n_w : n_w + 2]
    bt_o, ct_o, bn_o, cn_o, cbt_o, pre_o, w_o = refs[-7:]
    length = bt_o.shape[1]
    state_w = bt_o.shape[0]
    per = n_w // len(picks)
    w = jnp.concatenate(
        [joined(refs[p * per : (p + 1) * per], order) for p, order in enumerate(picks)], axis=0
    )
    w_o[...] = w
    maps_pre = conv_values(dot(w, nt[...]), taps[...])
    pre_o[...] = maps_pre
    maps = (maps_pre * sigmoid(maps_pre)).astype(bf16)
    bt, ct = maps[:state_w], maps[state_w:]
    bt_o[...] = bt
    ct_o[...] = ct
    bn = jnp.transpose(bt)
    bn_o[...] = bn
    cn_o[...] = jnp.transpose(ct)
    row = lax.broadcasted_iota(jnp.int32, (sub, sub), 0)
    col = lax.broadcasted_iota(jnp.int32, (sub, sub), 1)
    upto = jnp.where(row <= col, 1.0, 0.0)
    for s in range(length // sub):
        cols = slice(s * sub, (s + 1) * sub)
        cbt_o[s] = upto * dot(bn[cols, :], ct[:, cols])


def maps_call(paths, first, rows, picks, nt, taps, length, later):
    ops, specs = row_specs(paths, first, rows)
    state_w = rows * len(picks) // 2
    vm = pl.BlockSpec(memory_space=pltpu.VMEM)
    n_w = len(ops)
    return pl.pallas_call(
        functools.partial(maps_kernel, n_w, picks, SUB),
        grid=(1,),
        in_specs=specs + [vm, vm] + [pl.BlockSpec(memory_space=pl.ANY)] * len(later),
        out_specs=[vm] * 7,
        out_shape=[
            jax.ShapeDtypeStruct((state_w, length), bf16),
            jax.ShapeDtypeStruct((state_w, length), bf16),
            jax.ShapeDtypeStruct((length, state_w), bf16),
            jax.ShapeDtypeStruct((length, state_w), bf16),
            jax.ShapeDtypeStruct((length // SUB, SUB, SUB), f32),
            jax.ShapeDtypeStruct((2 * state_w, length), f32),
            jax.ShapeDtypeStruct((2 * state_w, nt.shape[0]), bf16),
        ],
        compiler_params=compiler_params(1),
        cost_estimate=cost(nt.shape[0] * nt.shape[1] * 512, nt.size * 2 + nt.shape[0] * 1024),
        name="maps",
    )(*ops, nt, taps, *later)


def steps_kernel(n_w, order, hb, sub, *refs):
    nt, bias, speed = refs[n_w : n_w + 3]
    hp_o, sig_o, w_o = refs[-3:]
    length = sig_o.shape[1]
    heads = sig_o.shape[0]
    w = joined(refs[:n_w], order)
    w_o[...] = w
    steps = dot(w, nt[:, HALO:]) + bias[...]
    sig_o[...] = sigmoid(steps)
    delta = jnp.maximum(steps, 0.0) + jnp.log1p(jnp.exp(-jnp.abs(steps)))
    rates = -delta * speed[...]
    row = lax.broadcasted_iota(jnp.int32, (sub, sub), 0)
    col = lax.broadcasted_iota(jnp.int32, (sub, sub), 1)
    upto = jnp.where(row <= col, 1.0, 0.0)
    before = None
    for s in range(length // sub):
        cols = slice(s * sub, (s + 1) * sub)
        cum = (
            lax.dot_general(
                rates[:, cols], upto, (NN, ((), ())), precision=highest,
                preferred_element_type=f32,
            )
            * LOG2E
        )
        cum_all = cum if before is None else cum + before
        before = cum_all[:, sub - 1 : sub]
        for b in range(heads // hb):
            mine = slice(b * hb, (b + 1) * hb)
            hp_o[b, :hb, cols] = cum[mine]
            hp_o[b, hb : 2 * hb, cols] = cum_all[mine]
            hp_o[b, 2 * hb :, cols] = delta[mine, cols]


def steps_call(arrays, first, order, nt, bias, speed, length, later):
    heads = bias.shape[0]
    hb = CB // HEAD
    ops, specs = row_specs([arrays], first, heads)
    vm = pl.BlockSpec(memory_space=pltpu.VMEM)
    return pl.pallas_call(
        functools.partial(steps_kernel, len(ops), order, hb, SUB),
        grid=(1,),
        in_specs=specs + [vm] * 3 + [pl.BlockSpec(memory_space=pl.ANY)] * len(later),
        out_specs=[vm] * 3,
        out_shape=[
            jax.ShapeDtypeStruct((heads // hb, 3 * hb, length), f32),
            jax.ShapeDtypeStruct((heads, length), f32),
            jax.ShapeDtypeStruct((heads, nt.shape[0]), bf16),
        ],
        compiler_params=compiler_params(1),
        cost_estimate=cost(nt.shape[0] * nt.shape[1] * 128, nt.size * 2),
        name="steps",
    )(*ops, nt, bias, speed, *later)


def hop_kernel(hb, ncb, got, own, hp, *rest):
    out = rest[-1]
    length = hp.shape[2]
    for c in range(ncb):
        rows = slice(c * CB, (c + 1) * CB)
        total = jnp.exp2(hp[c, hb : 2 * hb, length - 1 : length])
        out[rows, :] = (per_head(got[rows, :].astype(f32), total) + own[rows, :]).astype(bf16)


def hop_call(got, shift, own, hp, later=()):
    slots, ch, state_w = own.shape
    ncb = ch // CB
    return pl.pallas_call(
        functools.partial(hop_kernel, CB // HEAD, ncb),
        grid=(slots,),
        in_specs=[
            pl.BlockSpec((None, ch, state_w), lambda s: ((s + shift) % slots, 0, 0)),
            pl.BlockSpec((None, ch, state_w), lambda s: (s, 0, 0)),
            pl.BlockSpec((ncb,) + hp.shape[1:], lambda s: (s, 0, 0)),
        ]
        + [pl.BlockSpec(memory_space=pl.ANY)] * len(later),
        out_specs=pl.BlockSpec((None, ch, state_w), lambda s: (s, 0, 0)),
        out_shape=jax.ShapeDtypeStruct((slots, ch, state_w), bf16),
        compiler_params=compiler_params(1),
        cost_estimate=cost(own.size * 4, own.size * 8),
        name="hop",
    )(got, own, hp, *later)


def hold_kernel(*refs):
    refs[-1][...] = jnp.zeros_like(refs[-1])


def hold(deps, passed=()):
    anywhere = pl.BlockSpec(memory_space=pl.ANY)
    deps, passed = list(deps), list(passed)
    out = pl.pallas_call(
        hold_kernel,
        in_specs=[anywhere] * (len(deps) + len(passed)),
        out_specs=[anywhere] * len(passed) + [pl.BlockSpec(memory_space=pltpu.VMEM)],
        out_shape=[jax.ShapeDtypeStruct(v.shape, v.dtype) for v in passed]
        + [jax.ShapeDtypeStruct((8, 128), f32)],
        input_output_aliases={len(deps) + k: k for k in range(len(passed))},
        cost_estimate=cost(8, 8),
        name="hold",
    )(*deps, *passed)
    return out[-1][0, 0].astype(bf16), out[-1], list(out[:-1])


def path_dots(out, refs, picks, right, step, blocks):
    per = len(refs) // len(picks)
    for p, order in enumerate(picks):
        mine = refs[p * per : (p + 1) * per]

        @pl.when(step // (blocks // len(picks)) == p)
        def _(mine=mine, order=order):
            out[...] = dot(joined(mine, order), right)


def scan_kernel(nx, picks, ncb, hb, sub, *refs):
    xrefs = refs[:nx]
    (nt, low, upx, chan_r, hp_r, ct, bn, cbt) = refs[nx : nx + 8]
    xc_out, mix_out, ent_out, st_out, sent_out, tok_out, raw_sc = refs[-7:]
    tok_out[...] = jnp.zeros_like(tok_out)
    chan = chan_r[...]
    hp = hp_r[...]
    length = ct.shape[1]
    path_dots(raw_sc, xrefs, picks, nt[...], pl.program_id(1), ncb)
    xr = raw_sc[...] + dot(upx[...], low[...])
    xc = conv_values(xr, chan)
    xc_out[...] = xc.astype(bf16)
    x = xc * sigmoid(xc)
    xs = per_head(x, hp[2 * hb : 3 * hb])
    xs_low = xs.astype(bf16)
    state = None
    for s in range(length // sub):
        cols = slice(s * sub, (s + 1) * sub)
        cum = hp[:hb, cols]
        rows_n = jnp.transpose(jnp.concatenate([cum, cum], axis=0))
        within = []
        for h in range(hb):
            gap = jnp.minimum(cum[h : h + 1] - rows_n[:, h : h + 1], 0.0)
            weight = (jnp.exp2(gap) * cbt[s]).astype(bf16)
            within.append(dot(xs_low[h * HEAD : (h + 1) * HEAD, cols], weight))
        y = jnp.concatenate(within, axis=0)
        last = cum[:, sub - 1 : sub]
        ends = jnp.exp2(last - cum)
        add = dot(per_head(xs[:, cols], ends).astype(bf16), bn[cols, :])
        if s > 0:
            ent_out[s - 1] = state
            y = y + per_head(dot(state.astype(bf16), ct[:, cols]), jnp.exp2(cum))
            state = per_head(state, jnp.exp2(last)) + add
        else:
            state = add
        mix_out[:, cols] = y + x[:, cols] * chan[:, 4:5]
    if length // sub == 1:
        ent_out[0] = state
    st_out[...] = state
    sent_out[...] = state.astype(bf16)


def range_specs(lo, ncb):
    full = lambda a: pl.BlockSpec(a.shape, lambda s, c: (0,) * a.ndim)
    per_chan = lambda a: pl.BlockSpec((None, CB, a.shape[2]), lambda s, c: (s + lo, c, 0))
    per_blk = lambda a: pl.BlockSpec(
        (None,) + a.shape[1:], lambda s, c: ((s + lo) * ncb + c, 0, 0)
    )
    return full, per_chan, per_blk


def weight_specs(weight, ncb):
    paths, base = weight
    per = ncb // len(paths)
    ops, specs = [], []
    for p, arrays in enumerate(paths):
        for a in arrays:
            ops.append(a)
            index = lambda s, c, p=p: (0, (s + base) * per + jnp.clip(c - p * per, 0, per - 1), 0)
            specs.append(pl.BlockSpec((a.shape[0], CB, a.shape[2]), index))
    return ops, specs


def scan_call(lo, hi, xw, picks, nt, low, upx, chan, hp, ct, bn, cbt, bufs, later=()):
    slots, ch = upx.shape[0], upx.shape[1]
    length = ct.shape[1]
    ext = low.shape[1]
    hb = CB // HEAD
    ncb = ch // CB
    nsub = length // SUB
    full, per_chan, per_blk = range_specs(lo, ncb)
    ops, specs = weight_specs(xw, ncb)
    nx = len(ops)
    ops += [nt, low, upx, chan, hp, ct, bn, cbt]
    specs += [full(nt), full(low), per_chan(upx), per_chan(chan)]
    specs += [per_blk(hp), full(ct), full(bn), full(cbt)]
    inner_states = max(nsub - 1, 1)
    shapes = [
        jax.ShapeDtypeStruct((slots, ch, length), bf16),
        jax.ShapeDtypeStruct((slots, ch, length), f32),
        jax.ShapeDtypeStruct((slots, inner_states, ch, 128), f32),
        jax.ShapeDtypeStruct((slots, ch, 128), f32),
        jax.ShapeDtypeStruct((slots, ch, 128), bf16),
        jax.ShapeDtypeStruct((8, 128), f32),
    ]
    chan_out = lambda w: pl.BlockSpec((None, CB, w), lambda s, c: (s + lo, c, 0))
    outs = [
        chan_out(length),
        chan_out(length),
        pl.BlockSpec((None, inner_states, CB, 128), lambda s, c: (s + lo, 0, c, 0)),
        chan_out(128),
        chan_out(128),
        pl.BlockSpec((8, 128), lambda s, c: (0, 0)),
    ]
    aliases = {}
    if bufs is not None:
        aliases = {len(ops) + k: k for k in range(5)}
        ops += list(bufs)
        specs += [pl.BlockSpec(memory_space=pl.ANY)] * 5
    ops += list(later)
    specs += [pl.BlockSpec(memory_space=pl.ANY)] * len(later)
    n = hi - lo
    out = pl.pallas_call(
        functools.partial(scan_kernel, nx, picks, ncb, hb, SUB),
        grid=(n, ncb),
        in_specs=specs,
        out_specs=outs,
        out_shape=shapes,
        scratch_shapes=[pltpu.VMEM((CB, ext), f32)],
        input_output_aliases=aliases,
        compiler_params=compiler_params(2),
        cost_estimate=cost(4 * n * ch * 2048 * ext, n * ch * (4096 + length * 8)),
        name="scan_slots",
    )(*ops)
    return out[:5], out[5]


def proj_kernel(n, picks, ncb, cut, gain, *refs):
    (right, low, up) = refs[n : n + 3]
    chan_r = refs[n + 3]
    out, tok_o, sc = refs[-3:]
    tok_o[...] = jnp.zeros_like(tok_o)
    path_dots(sc, refs[:n], picks, right[:, cut:], pl.program_id(1), ncb)
    value = sc[...] + dot(up[...], low[:, cut:])
    if gain:
        value = value * chan_r[:, 5:6]
    out[...] = value.astype(bf16)


def proj_call(lo, hi, weight, picks, right, low, up, chan, cut, gain, buf, later=()):
    slots, ch = up.shape[0], up.shape[1]
    length = right.shape[1] - cut
    ncb = ch // CB
    full, per_chan, _ = range_specs(lo, ncb)
    ops, specs = weight_specs(weight, ncb)
    n_w = len(ops)
    ops += [right, low, up, chan]
    specs += [full(right), full(low), per_chan(up), per_chan(chan)]
    aliases = {}
    if buf is not None:
        aliases = {len(ops): 0}
        ops.append(buf)
        specs.append(pl.BlockSpec(memory_space=pl.ANY))
    ops += list(later)
    specs += [pl.BlockSpec(memory_space=pl.ANY)] * len(later)
    n = hi - lo
    return pl.pallas_call(
        functools.partial(proj_kernel, n_w, picks, ncb, cut, gain),
        grid=(n, ncb),
        in_specs=specs,
        out_specs=[
            pl.BlockSpec((None, CB, length), lambda s, c: (s + lo, c, 0)),
            pl.BlockSpec((8, 128), lambda s, c: (0, 0)),
        ],
        out_shape=[
            jax.ShapeDtypeStruct((slots, ch, length), bf16),
            jax.ShapeDtypeStruct((8, 128), f32),
        ],
        scratch_shapes=[pltpu.VMEM((CB, length), f32)],
        input_output_aliases=aliases,
        compiler_params=compiler_params(2),
        cost_estimate=cost(2 * n * ch * 2048 * length, n * ch * (4096 + length * 2)),
        name="proj_slots",
    )(*ops)


def gate_kernel(hb, inner, *refs):
    (z_r, mix_r, wgt_r, ent_r, chan_r, hp_r, ct, cn) = refs[:8]
    nout_o, dmix_o, dz_o, sl_o, sent_o = refs[8:13]
    mix_sc, sq_sc, dot_sc = refs[13:]
    phase = pl.program_id(0)
    blk = pl.program_id(1) * pl.num_programs(2) + pl.program_id(2)
    length = ct.shape[1]
    z = z_r[...].astype(f32)
    sig = sigmoid(z)
    silu = z * sig
    weighted = wgt_r[...].astype(f32)
    cum = jnp.exp2(hp_r[hb : 2 * hb])

    @pl.when((phase == 0) & (blk == 0))
    def _():
        sq_sc[...] = jnp.zeros_like(sq_sc)
        dot_sc[...] = jnp.zeros_like(dot_sc)

    @pl.when(phase == 0)
    def _():
        mix = mix_r[...] + per_head(dot(ent_r[...], ct[...]), cum)
        mix_sc[blk] = mix
        gated = mix * silu
        sq_sc[...] += jnp.sum((gated * gated).reshape(CB // 8, 8, length), axis=0)
        dot_sc[...] += jnp.sum((gated * weighted).reshape(CB // 8, 8, length), axis=0)

    @pl.when(phase == 1)
    def _():
        r = lax.rsqrt(jnp.sum(sq_sc[...], axis=0, keepdims=True) * (1.0 / inner) + epsilon)
        coef = r * r * r * (jnp.sum(dot_sc[...], axis=0, keepdims=True) * (1.0 / inner))
        mix = mix_sc[blk]
        gated = mix * silu
        nout_o[...] = (gated * (r * chan_r[:, 5:6])).astype(bf16)
        d_gated = r * weighted - gated * coef
        d_mix = d_gated * silu
        dmix_o[...] = d_mix.astype(bf16)
        dz_o[...] = (d_gated * mix * (sig + silu * (1.0 - sig))).astype(bf16)
        adj = dot(per_head(d_mix, cum).astype(bf16), cn[...])
        sl_o[...] = adj
        sent_o[...] = adj.astype(bf16)


def gate_call(z, mix, wgt, ent, chan, hp, ct, cn, inner):
    slots, ch, length = mix.shape
    ncb = ch // CB
    hb = CB // HEAD
    full = lambda a: pl.BlockSpec(a.shape, lambda p, s, c: (0,) * a.ndim)
    per_chan = lambda a: pl.BlockSpec((None, CB, a.shape[2]), lambda p, s, c: (s, c, 0))
    per_blk = lambda a: pl.BlockSpec((None,) + a.shape[1:], lambda p, s, c: (s * ncb + c, 0, 0))
    held = lambda p, s, c, k: (
        jnp.where(p == 0, (s + k) % slots, (slots - 1 + k) % slots),
        jnp.where(p == 0, c, ncb - 1),
        0,
    )
    first = lambda a, k: pl.BlockSpec((None, CB, a.shape[2]), lambda p, s, c: held(p, s, c, k))
    later = lambda w: pl.BlockSpec(
        (None, CB, w), lambda p, s, c: (jnp.where(p == 1, s, 0), jnp.where(p == 1, c, 0), 0)
    )
    return pl.pallas_call(
        functools.partial(gate_kernel, hb, inner),
        grid=(2, slots, ncb),
        in_specs=[per_chan(z), first(mix, 0), per_chan(wgt), first(ent, 1), per_chan(chan)]
        + [per_blk(hp), full(ct), full(cn)],
        out_specs=[later(length), later(length), later(length), later(128), later(128)],
        out_shape=[
            jax.ShapeDtypeStruct((slots, ch, length), bf16),
            jax.ShapeDtypeStruct((slots, ch, length), bf16),
            jax.ShapeDtypeStruct((slots, ch, length), bf16),
            jax.ShapeDtypeStruct((slots, ch, 128), f32),
            jax.ShapeDtypeStruct((slots, ch, 128), bf16),
        ],
        scratch_shapes=[
            pltpu.VMEM((slots * ncb, CB, length), f32),
            pltpu.VMEM((8, length), f32),
            pltpu.VMEM((8, length), f32),
        ],
        compiler_params=compiler_params(3),
        cost_estimate=cost(slots * ch * length * 600, slots * ch * length * 22),
        name="gate",
    )(z, mix, wgt, ent, chan, hp, ct, cn)


def grid_specs(ncb):
    full = lambda a: pl.BlockSpec(a.shape, lambda s, c: (0,) * a.ndim)
    per_chan = lambda a: pl.BlockSpec((None, CB, a.shape[2]), lambda s, c: (s, c, 0))
    per_blk = lambda a: pl.BlockSpec((None,) + a.shape[1:], lambda s, c: (s * ncb + c, 0, 0))
    return full, per_chan, per_blk


def back_kernel(hb, sub, *refs):
    (dy_r, xc_r, hp_r, ent_r, loc_r, ct, cn, bt, cbt) = refs[:9]
    dxs_o, u1_o, u2_o, kl_o, dcb_o, db_o, dc_o = refs[-7:]
    blk = pl.program_id(0) * pl.num_programs(1) + pl.program_id(1)
    hp = hp_r[...]
    length = ct.shape[1]
    nsub = length // sub

    @pl.when(blk == 0)
    def _():
        dcb_o[...] = jnp.zeros_like(dcb_o)
        db_o[...] = jnp.zeros_like(db_o)
        dc_o[...] = jnp.zeros_like(dc_o)

    xc = xc_r[...].astype(f32)
    x = xc * sigmoid(xc)
    xs = per_head(x, hp[2 * hb : 3 * hb])
    xs_low = xs.astype(bf16)
    adj = None
    kl = []
    for s in reversed(range(nsub)):
        cols = slice(s * sub, (s + 1) * sub)
        cum = hp[:hb, cols]
        rows_n = jnp.transpose(jnp.concatenate([cum, cum], axis=0))
        ecum = jnp.exp2(cum)
        last = cum[:, sub - 1 : sub]
        state = ent_r[...].astype(f32)
        if s > 0:
            before = hp[hb : 2 * hb, s * sub - 1 : s * sub]
            state = loc_r[s - 1] + per_head(state, jnp.exp2(before))
        state_low = state.astype(bf16)
        dy_low = dy_r[:, cols]
        dy = dy_low.astype(f32)
        y_in = per_head(dot(state_low, ct[:, cols]), ecum)
        ed = per_head(dy, ecum).astype(bf16)
        dc_o[:, cols] += dot(state_low, ed, TN)
        dxw, yw = [], []
        for h in range(hb):
            hs = slice(h * HEAD, (h + 1) * HEAD)
            gap = jnp.minimum(cum[h : h + 1] - rows_n[:, h : h + 1], 0.0)
            decay = jnp.exp2(gap)
            weight = (decay * cbt[s]).astype(bf16)
            yw.append(dot(xs_low[hs, cols], weight))
            dxw.append(dot(dy_low[hs], weight, NT))
            dcb_o[s] += decay * dot(xs_low[hs, cols], dy_low[hs], TN)
        yw = jnp.concatenate(yw, axis=0)
        dxs = jnp.concatenate(dxw, axis=0)
        u1_o[:, cols] = head_sums(dy * (yw + y_in) - xs_low[:, cols].astype(f32) * dxs, hb)
        add = dot(ed, cn[cols, :])
        if adj is None:
            u2_o[:, cols] = jnp.zeros((hb, sub), f32)
            kl.append(jnp.zeros((hb, 128), f32))
            adj = add
        else:
            ends = jnp.exp2(last - cum)
            adj_low = adj.astype(bf16)
            dxi = per_head(dot(adj_low, bt[:, cols]), ends)
            xs_s = xs[:, cols]
            u2_o[:, cols] = head_sums(xs_s * dxi, hb)
            kl.append(head_sums(adj * state, hb) * jnp.exp2(last))
            db_o[:, cols] += dot(adj_low, per_head(xs_s, ends).astype(bf16), TN)
            dxs = dxs + dxi
            adj = per_head(adj, jnp.exp2(last)) + add
        dxs_o[:, cols] = dxs
    for s in range(nsub):
        kl_o[:, s * 128 : (s + 1) * 128] = kl[nsub - 1 - s]


def back_call(lo, hi, dy, xc, hp, ent, loc, ct, cn, bt, cbt, bufs, later=()):
    slots, ch, length = dy.shape
    ncb = ch // CB
    hb = CB // HEAD
    nsub = length // SUB
    full = lambda a: pl.BlockSpec(a.shape, lambda s, c: (0,) * a.ndim)
    per_chan = lambda a: pl.BlockSpec((None, CB, a.shape[2]), lambda s, c: (s + lo, c, 0))
    per_blk = lambda a: pl.BlockSpec(
        (None,) + a.shape[1:], lambda s, c: ((s + lo) * ncb + c, 0, 0)
    )
    blk_out = lambda w: pl.BlockSpec((None, hb, w), lambda s, c: ((s + lo) * ncb + c, 0, 0))
    loc_spec = pl.BlockSpec((None, loc.shape[1], CB, 128), lambda s, c: (s + lo, 0, c, 0))
    blocks = slots * ncb
    ops = [dy, xc, hp, ent, loc, ct, cn, bt, cbt]
    entered = pl.BlockSpec((None, CB, 128), lambda s, c: ((s + lo + 1) % slots, c, 0))
    specs = [per_chan(dy), per_chan(xc), per_blk(hp), entered, loc_spec]
    specs += [full(ct), full(cn), full(bt), full(cbt)]
    aliases = {}
    if bufs is not None:
        aliases = {len(ops) + k: k for k in range(4)}
        ops += list(bufs)
        specs += [pl.BlockSpec(memory_space=pl.ANY)] * 4
    ops += list(later)
    specs += [pl.BlockSpec(memory_space=pl.ANY)] * len(later)
    return pl.pallas_call(
        functools.partial(back_kernel, hb, SUB),
        grid=(hi - lo, ncb),
        in_specs=specs,
        out_specs=[
            pl.BlockSpec((None, CB, length), lambda s, c: (s + lo, c, 0)),
            blk_out(length),
            blk_out(length),
            blk_out(128 * nsub),
            pl.BlockSpec((nsub, SUB, SUB), lambda s, c: (0, 0, 0)),
            pl.BlockSpec((128, length), lambda s, c: (0, 0)),
            pl.BlockSpec((128, length), lambda s, c: (0, 0)),
        ],
        out_shape=[
            jax.ShapeDtypeStruct((slots, ch, length), f32),
            jax.ShapeDtypeStruct((blocks, hb, length), f32),
            jax.ShapeDtypeStruct((blocks, hb, length), f32),
            jax.ShapeDtypeStruct((blocks, hb, 128 * nsub), f32),
            jax.ShapeDtypeStruct((nsub, SUB, SUB), f32),
            jax.ShapeDtypeStruct((128, length), f32),
            jax.ShapeDtypeStruct((128, length), f32),
        ],
        input_output_aliases=aliases,
        compiler_params=compiler_params(2),
        cost_estimate=cost((hi - lo) * ch * length * SUB * 20, (hi - lo) * ch * length * 8),
        name="state_back",
    )(*ops)


def finish_kernel(hb, *refs):
    (dxs_r, dy_r, xc_r, dz_r, chan_r, hp_r, ent_r, adj_r, bt, upz, upx, low) = refs[:12]
    dx_o, tail_o, head_o, gz_o, gx_o, dl_o, dd_o, u2_o, kf_o, db_o = refs[-10:]
    blk = pl.program_id(0) * pl.num_programs(1) + pl.program_id(1)
    chan = chan_r[...]
    hp = hp_r[...]
    length = bt.shape[1]

    @pl.when(blk == 0)
    def _():
        db_o[...] = jnp.zeros_like(db_o)
        dl_o[...] = jnp.zeros_like(dl_o)

    xc = xc_r[...].astype(f32)
    sig = sigmoid(xc)
    x = xc * sig
    delta = hp[2 * hb : 3 * hb]
    xs = per_head(x, delta)
    total = hp[hb : 2 * hb]
    last = total[:, length - 1 : length]
    ends = jnp.exp2(last - total)
    adj_low = adj_r[...]
    extra = per_head(dot(adj_low, bt[...]), ends)
    u2_o[...] = head_sums(xs * extra, hb)
    kf_o[...] = head_sums(adj_low.astype(f32) * ent_r[...].astype(f32), hb) * jnp.exp2(last)
    db_o[...] += dot(adj_low, per_head(xs, ends).astype(bf16), TN)
    dxs = dxs_r[...] + extra
    dd_o[...] = head_sums(x * dxs, hb)
    dx = per_head(dxs, delta) + dy_r[...].astype(f32) * chan[:, 4:5]
    dconv = dx * (sig + x * (1.0 - sig))
    head_o[...] = jnp.transpose(dconv[:, :HALO])[:8]
    ext = jnp.concatenate([dconv, jnp.zeros((CB, HALO), f32)], axis=1)
    width = ext.shape[1]
    out = ext * chan[:, 3:4]
    for k in range(3):
        out = out + pltpu.roll(ext, width - (3 - k), 1) * chan[:, k : k + 1]
    out = out[:, :length]
    tail_o[...] = out[:, length - HALO :]
    dx_low = out.astype(bf16)
    dx_o[...] = dx_low
    dz = dz_r[...]
    gz_o[...] = dot(low[...], dz, NT)
    gx_o[...] = dot(low[...], dx_low, NT)
    dl_o[...] += dot(upz[...], dz, TN) + dot(upx[...], dx_low, TN)


def finish_call(dxs, dy, xc, dz, chan, hp, ent, adj, bt, upz, upx, low, later):
    slots, ch, length = dy.shape
    ncb = ch // CB
    hb = CB // HEAD
    rank2 = low.shape[0]
    full, per_chan, per_blk = grid_specs(ncb)
    blk_out = lambda w: pl.BlockSpec((None, hb, w), lambda s, c: (s * ncb + c, 0, 0))
    chan_out = lambda w: pl.BlockSpec((None, CB, w), lambda s, c: (s, c, 0))
    turned = lambda w: pl.BlockSpec((None, w, CB), lambda s, c: (s, 0, c))
    moved = lambda k: pl.BlockSpec((None, CB, 128), lambda s, c: ((s + k) % slots, c, 0))
    blocks = slots * ncb
    return pl.pallas_call(
        functools.partial(finish_kernel, hb),
        grid=(slots, ncb),
        in_specs=[per_chan(dxs), per_chan(dy), per_chan(xc), per_chan(dz), per_chan(chan)]
        + [per_blk(hp), moved(1), moved(slots - 1), full(bt), per_chan(upz), per_chan(upx)]
        + [full(low)] + [pl.BlockSpec(memory_space=pl.ANY)] * len(later),
        out_specs=[
            chan_out(length),
            chan_out(HALO),
            turned(8),
            turned(rank2),
            turned(rank2),
            pl.BlockSpec((rank2, length), lambda s, c: (0, 0)),
            blk_out(length),
            blk_out(length),
            blk_out(128),
            pl.BlockSpec((128, length), lambda s, c: (0, 0)),
        ],
        out_shape=[
            jax.ShapeDtypeStruct((slots, ch, length), bf16),
            jax.ShapeDtypeStruct((slots, ch, HALO), f32),
            jax.ShapeDtypeStruct((slots, 8, ch), f32),
            jax.ShapeDtypeStruct((slots, rank2, ch), f32),
            jax.ShapeDtypeStruct((slots, rank2, ch), f32),
            jax.ShapeDtypeStruct((rank2, length), f32),
            jax.ShapeDtypeStruct((blocks, hb, length), f32),
            jax.ShapeDtypeStruct((blocks, hb, length), f32),
            jax.ShapeDtypeStruct((blocks, hb, 128), f32),
            jax.ShapeDtypeStruct((128, length), f32),
        ],
        compiler_params=compiler_params(2),
        cost_estimate=cost(slots * ch * length * 700, slots * ch * length * 14),
        name="finish_back",
    )(dxs, dy, xc, dz, chan, hp, ent, adj, bt, upz, upx, low, *later)


def glue_kernel(hb, sub, *refs):
    (dcb_r, db1, db2, dc1, bt, ct, pre_r, u1, u2, kl, dd, u2f, kf) = refs[:13]
    (sig_r, speed, taps) = refs[13:16]
    left_o, tail_o, head_o = refs[16:]
    state_w, length = bt.shape
    nsub = length // sub
    blocks = u1.shape[0]
    row = lax.broadcasted_iota(jnp.int32, (sub, sub), 0)
    col = lax.broadcasted_iota(jnp.int32, (sub, sub), 1)
    below = jnp.where(row >= col, 1.0, 0.0)
    keep = jnp.where(row <= col, 1.0, 0.0)

    def exact(p, q):
        return lax.dot_general(
            p, q, (NN, ((), ())), precision=highest, preferred_element_type=f32
        )

    def flat(ref, cols=slice(None)):
        return jnp.concatenate([ref[b, :, cols] for b in range(blocks)], axis=0)

    d_b, d_c, rate_in = [], [], []
    for s in range(nsub):
        cols = slice(s * sub, (s + 1) * sub)
        dcb = (dcb_r[s] * keep).astype(bf16)
        d_b.append(dot(ct[:, cols], dcb, NT))
        d_c.append(dot(bt[:, cols], dcb))
        lane = slice(s * 128, (s + 1) * 128)
        rate_in.append(
            exact(flat(u1, cols), below)
            + exact(flat(u2, cols), 1.0 - below)
            + jnp.sum(flat(kl, lane), axis=1, keepdims=True)
        )
    d_b = jnp.concatenate(d_b, axis=1) + db1[...] + db2[...]
    d_c = jnp.concatenate(d_c, axis=1) + dc1[...]
    pre = pre_r[...]
    sig = sigmoid(pre)
    d_pre = jnp.concatenate([d_b, d_c], axis=0) * (sig + pre * sig * (1.0 - sig))
    head_o[...] = jnp.transpose(d_pre[:, :HALO])[:8]
    ext = jnp.concatenate([d_pre, jnp.zeros((2 * state_w, HALO), f32)], axis=1)
    out = ext * taps[:, 3:4]
    for k in range(3):
        out = out + pltpu.roll(ext, ext.shape[1] - (3 - k), 1) * taps[:, k : k + 1]
    tail_o[...] = out[:, length - HALO : length]
    left_o[: 2 * state_w, :] = out[:, :length].astype(bf16)
    rate = jnp.concatenate(rate_in, axis=1) + jnp.sum(flat(kf), axis=1, keepdims=True)
    first = flat(u2f)
    run = None
    parts = []
    for s in range(nsub):
        piece = first[:, s * sub : (s + 1) * sub]
        here = exact(piece, 1.0 - below)
        parts.append(here if run is None else here + run)
        ends = jnp.sum(piece, axis=1, keepdims=True)
        run = ends if run is None else run + ends
    rate = rate + jnp.concatenate(parts, axis=1)
    left_o[2 * state_w :, :] = ((flat(dd) - speed[...] * rate) * sig_r[...]).astype(bf16)


def glue_call(args, state_w, length, heads):
    vm = pl.BlockSpec(memory_space=pltpu.VMEM)
    return pl.pallas_call(
        functools.partial(glue_kernel, CB // HEAD, SUB),
        in_specs=[vm] * len(args),
        out_specs=[vm] * 3,
        out_shape=[
            jax.ShapeDtypeStruct((2 * state_w + heads, length), bf16),
            jax.ShapeDtypeStruct((2 * state_w, HALO), f32),
            jax.ShapeDtypeStruct((8, 2 * state_w), f32),
        ],
        compiler_params=compiler_params(0),
        cost_estimate=cost(1e8, 4e6),
        name="glue",
    )(*args)


def add_products(acc, turned, sets, picks, n_left, refs, slot, c):
    at = 0
    for lo, hi, per in sets:
        for p, order in enumerate(picks):
            groups = [refs[at + g * per : at + (g + 1) * per] for g in range(n_left)]
            at += n_left * per

            @pl.when((slot >= lo) & (slot < hi) & (c == p))
            def _(groups=groups, order=order):
                off = 0
                for k, b in order:
                    parts = [g[k][b] for g in groups]
                    w = parts[0] if n_left == 1 else jnp.concatenate(parts, axis=0)
                    acc[:, off : off + w.shape[1]] += dot(turned, w)
                    off += w.shape[1]


def product_specs(weights, paths, block):
    ops, specs, sets = [], [], []
    for (lo, hi), groups in weights:
        sets.append((lo, hi, len(groups[0][0][0])))
        for p in range(paths):
            for arrays, base in groups:
                for a in arrays[p]:
                    ops.append(a)

                    def index(s, c, lo=lo, hi=hi, base=base):
                        return (0, base + jnp.clip(s, lo, hi - 1) - lo, 0)

                    specs.append(pl.BlockSpec((a.shape[0], block, a.shape[2]), index))
    return ops, specs, sets


def output_kernel(sets, picks, flat, quick, n_w, *refs):
    (sc, nout, dn, bh, up, tok, masked) = refs[:7]
    wrefs = refs[7 : 7 + n_w]
    mixed_o, gdo_o, guo_o, acc, hid = refs[-5:]
    slot, c = pl.program_id(0), pl.program_id(1)
    rank = up.shape[0]
    length, width = tok.shape

    @pl.when((slot == 0) & (c == 0))
    def _():
        acc[...] = jnp.zeros_like(acc)
        hid[...] = jnp.zeros_like(hid)

    values = nout[...]
    gdo_o[...] = dot(bh[:rank, :], values, NT)
    hid[...] += dot(dn[:, :rank], values, TN)
    add_products(acc, jnp.transpose(values), sets, picks, 1, wrefs, slot, c)

    @pl.when((slot == pl.num_programs(0) - 1) & (c == pl.num_programs(1) - 1))
    def _():
        low = hid[...].astype(bf16)
        guo_o[...] = dot(low, masked[...])
        rows = lax.broadcasted_iota(jnp.int32, (length, 1), 0) < sc[1]
        for i, m in enumerate(flat):
            at = pl.ds(block_at(sc[0], m, quick), CB)
            total = acc[:, i * CB : (i + 1) * CB] + dot(low, up[:, at], TN)
            total = total + tok[:, at].astype(f32)
            mixed_o[:, at] = jnp.where(rows, total, 0.0).astype(bf16)


def output_call(sc, nout, dn, bh, up, tok, masked, weights, picks, flat, quick):
    slots, ch, length = nout.shape
    rank, width = up.shape
    paths = len(picks)
    block = ch // paths
    full = lambda a: pl.BlockSpec(a.shape, lambda s, c: (0,) * a.ndim)
    chan = lambda a: pl.BlockSpec((None, block, a.shape[2]), lambda s, c: (s, c, 0))
    w_ops, w_specs, sets = product_specs(weights, paths, block)
    return pl.pallas_call(
        functools.partial(output_kernel, sets, picks, flat, quick, len(w_ops)),
        grid=(slots, paths),
        in_specs=[pl.BlockSpec(memory_space=pltpu.SMEM), chan(nout), chan(dn), full(bh)]
        + [full(up), full(tok), full(masked)] + w_specs,
        out_specs=[
            pl.BlockSpec((length, width), lambda s, c: (0, 0)),
            pl.BlockSpec((None, rank, block), lambda s, c: (s, 0, c)),
            pl.BlockSpec((rank, width), lambda s, c: (0, 0)),
        ],
        out_shape=[
            jax.ShapeDtypeStruct((length, width), bf16),
            jax.ShapeDtypeStruct((slots, rank, ch), f32),
            jax.ShapeDtypeStruct((rank, width), f32),
        ],
        scratch_shapes=[pltpu.VMEM((length, width), f32), pltpu.VMEM((rank, length), f32)],
        compiler_params=compiler_params(2),
        cost_estimate=cost(2 * slots * ch * length * width, slots * ch * width * 2),
        name="output",
    )(sc, nout, dn, bh, up, tok, masked, *w_ops)


def gate_back_kernel(sets, picks, n_w, *refs):
    dz = refs[0]
    acc = refs[-1]
    slot, c = pl.program_id(0), pl.program_id(1)

    @pl.when((slot == 0) & (c == 0))
    def _():
        acc[...] = jnp.zeros_like(acc)

    add_products(acc, jnp.transpose(dz[...]), sets, picks, 1, refs[1 : 1 + n_w], slot, c)


def gate_back_call(dz, weights, picks, width, later=()):
    slots, ch, length = dz.shape
    paths = len(picks)
    block = ch // paths
    w_ops, w_specs, sets = product_specs(weights, paths, block)
    return pl.pallas_call(
        functools.partial(gate_back_kernel, sets, picks, len(w_ops)),
        grid=(slots, paths),
        in_specs=[pl.BlockSpec((None, block, length), lambda s, c: (s, c, 0))] + w_specs
        + [pl.BlockSpec(memory_space=pl.ANY)] * len(later),
        out_specs=pl.BlockSpec((length, width), lambda s, c: (0, 0)),
        out_shape=jax.ShapeDtypeStruct((length, width), f32),
        compiler_params=compiler_params(2),
        cost_estimate=cost(2 * slots * ch * length * width, 2 * slots * ch * width),
        name="gate_back",
    )(dz, *w_ops, *later)


def input_kernel(sets, picks, flat, quick, n_w, n_small, *refs):
    (sc, dx, tail, left, d_low, down, root_r, gain, tok, masked, start) = refs[:11]
    smalls = refs[11 : 11 + n_small]
    wrefs = refs[11 + n_small : 11 + n_small + n_w]
    out, acc = refs[-2:]
    slot, c = pl.program_id(0), pl.program_id(1)
    length, width = tok.shape

    @pl.when((slot == 0) & (c == 0))
    def _():
        low = jnp.transpose(d_low[...])
        total = start[...]
        row = 0
        for w in smalls:
            total = total + dot(left[row : row + w.shape[0], :], w[...], TN)
            row += w.shape[0]
        acc[...] = total
        for i, m in enumerate(flat):
            at = pl.ds(block_at(sc[0], m, quick), CB)
            acc[:, i * CB : (i + 1) * CB] += dot(low, down[at, :], NT)

    dx_all = jnp.concatenate([dx[:, : length - HALO], tail[...]], axis=1)
    add_products(acc, jnp.transpose(dx_all), sets, picks, 1, wrefs, slot, c)

    @pl.when((slot == pl.num_programs(0) - 1) & (c == pl.num_programs(1) - 1))
    def _():
        root = root_r[...]
        mean = None
        for i, m in enumerate(flat):
            at = pl.ds(block_at(sc[0], m, quick), CB)
            cols = slice(i * CB, (i + 1) * CB)
            scaled = acc[:, cols] * gain[:, at]
            acc[:, cols] = scaled
            part = jnp.sum(scaled * tok[:, at].astype(f32), axis=1, keepdims=True)
            mean = part if mean is None else mean + part
        coef = root * root * root * (mean * (1.0 / width))
        for i, m in enumerate(flat):
            at = pl.ds(block_at(sc[0], m, quick), CB)
            d_resid = root * acc[:, i * CB : (i + 1) * CB] - tok[:, at].astype(f32) * coef
            out[:, at] = (masked[:, at].astype(f32) + d_resid).astype(bf16)


def input_call(
    sc, dx, tail, left, d_low, down, root, gain, tok, masked, start, smalls, weights, picks,
    flat, quick,
):
    slots, ch, length = dx.shape
    width = tok.shape[1]
    paths = len(picks)
    block = ch // paths
    once = pl.Buffered(1)
    full = lambda a: pl.BlockSpec(a.shape, lambda s, c: (0,) * a.ndim, pipeline_mode=once)
    chan = lambda a: pl.BlockSpec((None, block, a.shape[2]), lambda s, c: (s, c, 0))
    w_ops, w_specs, sets = product_specs(weights, paths, block)
    return pl.pallas_call(
        functools.partial(input_kernel, sets, picks, flat, quick, len(w_ops), len(smalls)),
        grid=(slots, paths),
        in_specs=[pl.BlockSpec(memory_space=pltpu.SMEM), chan(dx), chan(tail)]
        + [full(a) for a in [left, d_low, down, root, gain, tok, masked, start] + list(smalls)]
        + w_specs,
        out_specs=pl.BlockSpec((length, width), lambda s, c: (0, 0)),
        out_shape=jax.ShapeDtypeStruct((length, width), bf16),
        scratch_shapes=[pltpu.VMEM((length, width), f32)],
        compiler_params=compiler_params(2),
        cost_estimate=cost(2 * slots * ch * length * width, 2 * slots * ch * width),
        name="input_back",
    )(sc, dx, tail, left, d_low, down, root, gain, tok, masked, start, *smalls, *w_ops)


def body(
    tokens,
    cotangent,
    lengths,
    adapter_ids,
    pre_gain,
    in_inner,
    in_maps,
    in_steps,
    conv_inner,
    conv_maps,
    step_bias,
    decay_log,
    skip_gain,
    norm_gain,
    out_weight,
    adapter_in_down,
    adapter_in_up,
    adapter_out_down,
    adapter_out_up,
):
    planes = lax.axis_size("tensor")
    seqs = lax.axis_size("dp")
    place = lax.axis_index("tensor")
    mine = lax.axis_index("dp")
    length = tokens.shape[1]
    width = tokens.shape[2]
    rows_here = in_inner.shape[0]
    ch = in_inner.shape[2]
    inner = ch * planes
    hs = in_steps.shape[1]
    heads = hs * planes
    rank = adapter_in_down.shape[2]
    adapters = adapter_in_down.shape[0]
    state_w = in_maps.shape[1] // 2
    hb = CB // HEAD
    ncb = ch // CB
    nblk = planes * ncb
    nsub = length // SUB
    quick = seqs == 8 and planes == 4

    def from_plane(v, j):
        return lax.ppermute(v, "tensor", [((s + j) % planes, s) for s in range(planes)])

    def flip(v, bit):
        return lax.ppermute(v, "dp", [(i, i ^ bit) for i in range(seqs)])

    def slot_order(v, first=0):
        return jnp.stack(
            [
                lax.dynamic_index_in_dim(v, (place + j) % planes, 0, keepdims=False)
                for j in range(first, planes)
            ]
        )

    def by_slot(v):
        return slot_order(lax.all_gather(v, "tensor", axis=0))

    def to_slots(v):
        total = v[0]
        for j in range(1, planes):
            total = total + lax.ppermute(
                v[j].astype(bf16), "tensor", [(s, (s + j) % planes) for s in range(planes)]
            ).astype(f32)
        return total

    flat = [0, 2, 4, 6, 1, 3, 5, 7] if quick else list(range(width // CB))
    if quick:
        picks = [
            [(0, 0), (0, 1), (1, 0), (1, 1), (2, 0), (2, 1), (3, 0), (3, 1)],
            [(0, 0), (1, 0), (0, 1), (1, 1), (2, 0), (3, 0), (2, 1), (3, 1)],
        ]
    else:
        picks = [[(0, 0)]]
    half = planes // 2

    def halves(parts, more=((), ())):
        cut = ch // 2
        return [
            jnp.concatenate([v[:cut] for v in parts] + list(more[0]), axis=0),
            jnp.concatenate([v[cut:] for v in parts] + list(more[1]), axis=0),
        ]

    def pass_one(ab):
        return [flip(ab[0], 2), flip(ab[1], 4)]

    def with_first(ab, got, token):
        return [jnp.stack([v, w]) + token for v, w in zip(ab, got)]

    def pass_two(ab):
        return [flip(ab[0], 4), flip(ab[1], 2)]

    def pass_core(arrays):
        return [flip(v, 1) for v in arrays]

    def as_paths(arrays, swapped):
        return [[arrays[k], arrays[k + 2], swapped[k], swapped[k + 2]] for k in range(2)]

    pick = adapter_ids[0]
    down_in = lax.dynamic_index_in_dim(adapter_in_down, pick, 0, keepdims=False)
    up_here = lax.dynamic_index_in_dim(adapter_in_up, pick, 0, keepdims=False)
    down_here = lax.dynamic_index_in_dim(adapter_out_down, pick, 0, keepdims=False)
    up_out = lax.dynamic_index_in_dim(adapter_out_up, pick, 0, keepdims=False)
    step_rows = rows_here * hs // ch
    halo_rows = 16 * width // ch
    numbers = jnp.concatenate(
        [
            conv_inner,
            jnp.repeat(skip_gain, HEAD)[None],
            norm_gain[None],
            jnp.pad(jnp.stack([step_bias, decay_log]), ((0, 0), (0, ch - hs))),
        ],
        axis=0,
    )
    coarse = lax.optimization_barrier(numbers.astype(bf16))
    fine = lax.optimization_barrier((numbers - coarse.astype(f32)).astype(bf16))
    packed = jnp.concatenate(
        [
            jnp.transpose(up_here, (1, 0, 2)).reshape(2 * rank, ch),
            down_here.T,
            in_steps.T.reshape(step_rows, ch),
            tokens[0, -16:].reshape(halo_rows, ch),
            coarse,
            fine,
        ],
        axis=0,
    )
    halo = [(s, s + 1) for s in range(planes - 1)]
    wt = jnp.transpose(in_inner, (1, 2, 0))
    maps_w = in_maps.T
    own_rows = 3 * ch // 2
    if quick:
        own = halves(
            [wt[0], wt[1], out_weight],
            ([maps_w[:state_w], in_steps.T], [maps_w[state_w:]]),
        )
        got = pass_one(own)
        packed = jnp.stack([packed] + [from_plane(packed, j) for j in range(1, planes)])
        all_x = lax.all_gather(wt[1], "tensor", axis=0)
        all_z = lax.all_gather(wt[0], "tensor", axis=0)
        all_o = lax.all_gather(out_weight, "tensor", axis=0)
    else:
        packed = by_slot(packed)
    step_at, halo_at = 3 * rank, 3 * rank + step_rows
    number_at = halo_at + halo_rows
    before = packed[planes - 1, halo_at:number_at].reshape(16, width)
    before = jnp.where(place > 0, before, jnp.zeros_like(before))
    numbers = packed[:, number_at : number_at + 8].astype(f32) + packed[
        :, number_at + 8 :
    ].astype(f32)
    steps_w = packed[:, step_at:halo_at].reshape(planes, hs, rows_here)
    held = []
    if quick:
        token, held, _ = hold(got + [before])
        own = with_first(own, got, token)
        two = pass_two(own)
        swapped = pass_core(own)
        far_x = halves(slot_order(all_x, 1), ([steps_w[1:].reshape(-1, rows_here)], ()))
        held = [held]

    up_z = jnp.swapaxes(packed[:, :rank], 1, 2)
    up_x = jnp.swapaxes(packed[:, rank : 2 * rank], 1, 2)
    down_out = jnp.swapaxes(packed[:, 2 * rank : 3 * rank], 1, 2)
    taps = numbers[:, :4]
    chan = jnp.swapaxes(jnp.pad(numbers[:, :6], ((0, 0), (0, 2), (0, 0))), 1, 2)
    bias = numbers[:, 6, :hs].reshape(heads)
    speed = jnp.exp(numbers[:, 7, :hs].reshape(heads))
    up_z2 = jnp.concatenate([up_z, up_z], axis=2)
    up_x2 = jnp.concatenate([up_x, up_x], axis=2)
    down_out2 = jnp.concatenate([down_out, down_out], axis=2)

    sc = jnp.stack([mine, lengths[0] - place * length]).astype(jnp.int32)
    normed, masked, root, low2, back2, nt, gt, turned = turn_call(
        sc, tokens[0], before, cotangent[0], pre_gain[None], down_in, up_out, flat, quick, held
    )
    map_taps = jnp.pad(conv_maps.T, ((0, 0), (0, 4)))
    if quick:
        token, held, passed = hold([turned] + swapped, two + far_x)
        two, far_x = passed[:2], passed[2:]
        own = own + two
        swapped = swapped + pass_core(two)
        got = pass_one(far_x)
        own = as_paths(own, swapped)
        token, held, _ = hold(got + own[0] + own[1])
        held = [held]
        all_maps, all_steps = own, own[0]
        maps_at, maps_rows = own_rows, state_w
        steps_at, mine_heads = own_rows + state_w, hs
    else:
        all_maps = [[lax.all_gather(maps_w, "dp", axis=1, tiled=True)[None]]]
        all_steps = steps_w.reshape(heads, rows_here)
        all_steps = [lax.all_gather(all_steps, "dp", axis=1, tiled=True)[None]]
        maps_at, maps_rows = 0, 2 * state_w
        steps_at, mine_heads = 0, heads
    bt, ct, b_low, c_low, cbt, maps_pre, maps_w = maps_call(
        all_maps, maps_at, maps_rows, picks, nt, map_taps, length, held
    )
    hp, step_sig, mine_w = steps_call(
        all_steps, steps_at, picks[0], nt, bias[:mine_heads, None], speed[:mine_heads, None],
        length, held,
    )
    small_w = [maps_w, mine_w]

    x_args = (picks, nt, low2, up_x2, chan)
    z_args = (picks, nt, low2, up_z2, chan, HALO, False)
    o_args = (picks, gt, back2, down_out2, chan, 0, True)
    if quick:
        far_x = with_first(far_x, got, token)
        two = pass_two(far_x)
        swapped = pass_core(far_x)
        far_z = halves(slot_order(all_z, 1))
        bufs, done = scan_call(0, 1, (own, 1), *x_args, hp, ct, b_low, cbt, None, held)

        token, held, passed = hold([done] + swapped, two + far_z)
        two, far_z = passed[:2], passed[2:]
        far_x = as_paths(far_x + two, swapped + pass_core(two))
        got = pass_one(far_z)
        z, done = proj_call(0, 1, (own, 0), *z_args, None, [held])
        wgt, beside = proj_call(0, 1, (own, 2), *o_args, None, [done])

        token, held, _ = hold(got + far_x[0] + far_x[1] + [beside])
        far_z = with_first(far_z, got, token)
        two = pass_two(far_z)
        swapped = pass_core(far_z)
        far_o = halves(slot_order(all_o, 1))
        hp_far, sig_far, far_w = steps_call(
            far_x[0], own_rows, picks[0], nt, bias[hs:, None], speed[hs:, None], length, [held]
        )
        hp = jnp.concatenate([hp, hp_far], axis=0)
        step_sig = jnp.concatenate([step_sig, sig_far], axis=0)
        small_w.append(far_w)
        bufs, done = scan_call(
            1, planes, (far_x, 0), *x_args, hp, ct, b_low, cbt, bufs, [held]
        )

        token, held, passed = hold([done] + swapped, two + far_o)
        two, far_o = passed[:2], passed[2:]
        far_z = as_paths(far_z + two, swapped + pass_core(two))
        got = pass_one(far_o)
        ent = lax.ppermute(bufs[4], "tensor", halo)

        token, held, (ent,) = hold(got + far_z[0] + far_z[1], [ent])
        far_o = with_first(far_o, got, token)
        two = pass_two(far_o)
        swapped = pass_core(far_o)
        ent = lax.ppermute(hop_call(ent, 1, bufs[3], hp), "tensor", halo)
        z, done = proj_call(1, planes, (far_z, 0), *z_args, z, [held])

        token, held, passed = hold([done] + swapped, two + [ent])
        two, ent = passed[:2], passed[2]
        far_o = as_paths(far_o + two, swapped + pass_core(two))
        ent = lax.ppermute(hop_call(ent, 1, bufs[3], hp), "tensor", halo)
        wgt, _ = proj_call(1, planes, (far_o, 0), *o_args, wgt, [held])
        z_sets = [((0, 1), [(own, 0)]), ((1, planes), [(far_z, 0)])]
        x_sets = [((0, 1), [(own, 1)]), ((1, planes), [(far_x, 0)])]
        o_sets = [((0, 1), [(own, 2)]), ((1, planes), [(far_o, 0)])]
    else:
        w = lax.all_gather(wt, "dp", axis=2, tiled=True)
        w = slot_order(lax.all_gather(w, "tensor", axis=0))
        o = lax.all_gather(out_weight, "dp", axis=1, tiled=True)
        flat_rows = lambda v: [[v.reshape(1, inner, width)]]
        wz, wx = flat_rows(w[:, 0]), flat_rows(w[:, 1])
        o = flat_rows(slot_order(lax.all_gather(o, "tensor", axis=0)))
        bufs, _ = scan_call(0, planes, (wx, 0), *x_args, hp, ct, b_low, cbt, None)
        z, _ = proj_call(0, planes, (wz, 0), *z_args, None)
        wgt, _ = proj_call(0, planes, (o, 0), *o_args, None)
        ent = lax.ppermute(bufs[4], "tensor", halo)
        for _ in range(planes - 2):
            ent = lax.ppermute(hop_call(ent, 1, bufs[3], hp), "tensor", halo)
        z_sets = [((0, planes), [(wz, 0)])]
        x_sets = [((0, planes), [(wx, 0)])]
        o_sets = [((0, planes), [(o, 0)])]
    xc, mix, loc, s_end, _ = bufs
    left = [(s + 1, s) for s in range(planes - 1)]

    nout, dy, dz, sl, sl_sent = gate_call(z, mix, wgt, ent, chan, hp, ct, c_low, inner)

    adj = lax.ppermute(sl_sent, "tensor", left)
    mixed, grad_down_out, grad_up_out = output_call(
        sc, nout, down_out2, back2, up_out, tokens[0], masked, o_sets, picks, flat, quick
    )
    adj = lax.ppermute(hop_call(adj, planes - 1, sl, hp, [mixed]), "tensor", left)
    d_normed = gate_back_call(dz, z_sets, picks, width, [mixed])
    adj = lax.ppermute(hop_call(adj, planes - 1, sl, hp, [d_normed]), "tensor", left)
    for _ in range(planes - 4):
        adj = lax.ppermute(hop_call(adj, planes - 1, sl, hp), "tensor", left)
    dxs, u1, u2, kl, dcb, db1, dc1 = back_call(
        0, planes, dy, xc, hp, ent, loc, ct, c_low, bt, cbt, None, [d_normed]
    )

    (dx, tail, head, grad_z, grad_x, d_low2, ddelta, u2f, kf, db3) = finish_call(
        dxs, dy, xc, dz, chan, hp, ent, adj, bt, up_z2, up_x2, low2[:, HALO:], [mixed]
    )
    small_left, maps_tail, maps_head = glue_call(
        [dcb, db1, db3, dc1, bt, ct, maps_pre]
        + [u1, u2, kl, ddelta, u2f, kf, step_sig, speed[:, None], map_taps],
        state_w, length, heads,
    )

    near = lax.ppermute(
        jnp.concatenate(
            [head[:, :4].reshape(planes * 4 * ch), maps_head[:4].reshape(8 * state_w)]
        ),
        "tensor",
        left,
    )

    def beyond(values, taps_of):
        return [sum(taps_of(k) * values(i - k) for k in range(i + 1)) for i in range(3)]

    near_x = jnp.roll(near[: planes * 4 * ch].reshape(planes, 4, ch), 1, axis=0)
    more = jnp.stack(beyond(lambda n: near_x[:, n], lambda k: taps[:, k]), axis=1)
    tail = (
        tail + jnp.pad(jnp.swapaxes(more, 1, 2), ((0, 0), (0, 0), (HALO - 3, 0)))
    ).astype(bf16)
    low_last = low2[:rank, -3:].astype(f32)
    grad_x = grad_x[:, :rank] + grad_x[:, rank:]
    grad_x += sum(low_last[None, :, i, None] * more[:, i, None, :] for i in range(3))
    grad_z = grad_z[:, :rank] + grad_z[:, rank:]
    d_low_more = jnp.einsum("jrk,jik->ri", packed[:, rank : 2 * rank].astype(f32), more)
    d_low = d_low2[:rank] + jnp.pad(d_low_more, ((0, 0), (length - 3, 0)))
    d_low = d_low.astype(bf16)
    near_maps = near[planes * 4 * ch :].reshape(4, 2 * state_w)
    maps_more = jnp.stack(beyond(lambda n: near_maps[n], lambda k: conv_maps[k]), axis=1)
    maps_tail = maps_tail + jnp.pad(maps_more, ((0, 0), (HALO - 3, 0)))
    small_left = lax.dynamic_update_slice(
        small_left, maps_tail.astype(bf16), (0, length - HALO)
    )

    grad_down = dot(d_low, normed)
    quarters = lambda v: slot_order(
        jnp.swapaxes(v.reshape(rank, planes, width // planes), 0, 1)
    )
    mine_sum = to_slots(
        jnp.concatenate(
            [grad_z, grad_x, grad_down_out, quarters(grad_down), quarters(grad_up_out)], axis=2
        )
    ).astype(bf16)
    head_part = 3 * ch
    shared = by_slot(mine_sum[:, head_part:])
    sent = jnp.concatenate(
        [
            mine_sum[:, :head_part],
            jnp.swapaxes(shared, 0, 1).reshape(rank, -1),
            jnp.full((rank, 128), pick).astype(bf16),
        ],
        axis=1,
    )
    if quick:
        by_seq = sent[None]
        for bit in (2, 4, 1):
            by_seq = jnp.concatenate([by_seq, flip(by_seq, bit)], axis=0)
    else:
        by_seq = lax.all_gather(sent, "dp", axis=0)
    ids = by_seq[:, 0, -1].astype(jnp.int32)
    chosen = (ids[None, :] == jnp.arange(adapters)[:, None]).astype(bf16)
    grads = jnp.einsum("as,srk->ark", chosen, by_seq[..., :-128], preferred_element_type=f32)
    g_up = grads[:, :, : 2 * ch].reshape(adapters, rank, 2, ch)
    g_down_out = jnp.swapaxes(grads[:, :, 2 * ch : 3 * ch], 1, 2)
    common = grads[:, :, 3 * ch :].reshape(adapters, rank, planes, 2, width // planes)
    twice = jnp.concatenate([common, common], axis=2)
    common = lax.dynamic_slice_in_dim(twice, (planes - place) % planes, planes, 2)
    g_down = jnp.swapaxes(common[:, :, :, 0].reshape(adapters, rank, width), 1, 2)
    g_up_out = common[:, :, :, 1].reshape(adapters, rank, width)

    tokens_grad = input_call(
        sc, dx, tail, small_left, d_low, down_in, root, pre_gain[None], tokens[0], masked,
        d_normed, small_w, x_sets, picks, flat, quick,
    )
    return (mixed[None], tokens_grad[None], g_down, g_up, g_down_out, g_up_out)


def solution(mesh):
    placed = (
        P("dp", "tensor", None),
        P("dp", "tensor", None),
        P("dp"),
        P("dp"),
        P(),
        P("dp", None, "tensor"),
        P("dp", None),
        P("dp", "tensor"),
        P(None, "tensor"),
        P(),
        P("tensor"),
        P("tensor"),
        P("tensor"),
        P("tensor"),
        P("tensor", "dp"),
        P(),
        P(None, None, None, "tensor"),
        P(None, "tensor", None),
        P(),
    )
    return jax.shard_map(
        body,
        mesh=mesh,
        in_specs=placed,
        out_specs=(
            P("dp", "tensor", None),
            P("dp", "tensor", None),
            P(),
            P(None, None, None, "tensor"),
            P(None, "tensor", None),
            P(),
        ),
        check_vma=False,
    )
```

time: 903 us -> 675 us (0.75)
  local copies, waits for them, and re-layouts: 177 us -> 67.8 us
  blocking collectives: 101 us -> 13.7 us
  Pallas kernels: 231 us -> 307 us
  waiting for transfers between devices: 176 us -> 135 us
  starting transfers between devices: 93 us -> 61.6 us
  matrix products: 30.3 us -> 5.05 us
    all_gather x2 -> x1, blocking collectives: 93.6 us -> 13.7 us  [by_slot(): return slot_order(lax.all_gather(v, 'tensor', axis=0))]
    pallas_call x9 -> x28, Pallas kernels: 208 us -> 281 us  [the longest x2 55.1 us: scan_call(): pl.pallas_call(functools.partial(scan_kernel, nx, picks, ncb, hb, SUB), g...]
    ppermute x40 -> x35, waiting for transfers between devices: 76.2 us -> 30.7 us  [flip(): return lax.ppermute(v, 'dp', [(i, i ^ bit) for i in range(seqs)])]
    ppermute x11 -> x10, starting transfers between devices: 59.1 us -> 22.5 us  [the longest x2 9.61 us: body(): ent = lax.ppermute(hop_call(ent, 1, bufs[3], hp), 'tensor', halo)]
    unnamed x228 -> x172, local copies, waits for them, and re-layouts: 64.6 us -> 30.1 us
    reshape x18 -> x7, local copies, waits for them, and re-layouts: 31.2 us -> 0.62 us  [the longest x2 0.22 us: body(): in_steps.T.reshape(step_rows, ch)]
    add x2 -> x10, other arithmetic: 1.9 us -> 22.4 us  [the longest x8 19.7 us: with_first(): return [jnp.stack([v, w]) + token for v, w in zip(ab, got)]]
    dot_general x9 -> x1, matrix products: 19.7 us -> 0.38 us  [dot(): return lax.dot_general(a, b, (dims, ((), ())), preferred_element_type=f32)]
  transfers between devices with their start and end apart: 60 -> 51, of which waited for: 17 -> 17; matrix products, arithmetic and copies ran while one was open for 22% -> 10% of each run, Pallas kernels for 17% -> 35%
where the time goes in v2:
time: 675 us; the launch traced here: 669 us
  Pallas kernels  307 us (45%)
  waiting for transfers between devices  135 us (20%)
  local copies, waits for them, and re-layouts  67.8 us (10%)
  other arithmetic  62.5 us (9%)
  starting transfers between devices  61.6 us (9%)
  between operations  16.7 us (2%)
  blocking collectives  13.7 us (2%)
    pallas_call x2, Pallas kernels, scan_call(): pl.pallas_call(functools.partial(scan_kernel, nx, picks, ncb, hb, SUB), g...  55.1 us
    pallas_call x4, Pallas kernels, proj_call(): pl.pallas_call(functools.partial(proj_kernel, n_w, picks, ncb, cut, gain)...  51.2 us
    ppermute x3, waiting for transfers between devices, from_plane(): lax.ppermute(v, 'tensor', [((s + j) % planes, s) for s in range(planes)])  40 us
    pallas_call x1, Pallas kernels, gate_call(): pl.pallas_call(functools.partial(gate_kernel, hb, inner), grid=(2, slots,...  32.3 us
    ppermute x35, waiting for transfers between devices, flip(): return lax.ppermute(v, 'dp', [(i, i ^ bit) for i in range(seqs)])  30.7 us
    unnamed x172, local copies, waits for them, and re-layouts  30.1 us
    pallas_call x1, Pallas kernels, input_call(): pl.pallas_call(functools.partial(input_kernel, sets, picks, flat, quick,...  27.2 us
    ppermute x35, starting transfers between devices, flip(): return lax.ppermute(v, 'dp', [(i, i ^ bit) for i in range(seqs)])  27 us
  transfers between devices with their start and end apart: 51, of which 17 were waited for; matrix products, arithmetic and copies ran while one was open for 10% of the time, Pallas kernels for 35%

profile of v2, /device:TPU:0, one launch (start us, length us, event | category | flops | bytes accessed | tf_op | source)
XLA Modules:
  0.0 669.0 jit_solution(3433652181983301536)
XLA Ops:
  13.4 3.0 collective-permute-start.1
  24.3 14.5 %collective-permute-done.2 = bf16[100,1024]{0,1:T(8,128)(2,1)S(1)} collective-permute-done((bf16[100,1024]{0,1:T(8,128)(2,1)}, bf16[100,1024]{0,1:T(8,128)(2,1)S(1)}, u32[]{:S(2)}, u32[]{:S(2)}) %collective-permute-start.2) | collective-permute-done | bytes 204832 | tf_op jit(solution)/shard_map/ppermute | solution.py:1092
  48.7 8.3 %collective-permute-start.7 = (bf16[100,1024]{0,1:T(8,128)(2,1)}, bf16[100,1024]{0,1:T(8,128)(2,1)}, u32[]{:S(2)}, u32[]{:S(2)}) collective-permute-start(bf16[100,1024]{0,1:T(8,128)(2,1)} %concatenate.76), channel_id=1, source_target_pairs={{1,0},{2,1},{3,2},{0,3},{5,4},{6,5},{7,6},{4,7},{9,8},{10,9},{11,1... | collective-permute-start | bytes 614408 | tf_op jit(solution)/shard_map/ppermute | solution.py:1092
  60.2 9.0 %collective-permute-done.7 = bf16[100,1024]{0,1:T(8,128)(2,1)} collective-permute-done((bf16[100,1024]{0,1:T(8,128)(2,1)}, bf16[100,1024]{0,1:T(8,128)(2,1)}, u32[]{:S(2)}, u32[]{:S(2)}) %collective-permute-start.7) | collective-permute-done | bytes 204832 | tf_op jit(solution)/shard_map/ppermute | solution.py:1092
  72.7 16.5 %collective-permute-done.8 = bf16[100,1024]{0,1:T(8,128)(2,1)S(1)} collective-permute-done((bf16[100,1024]{0,1:T(8,128)(2,1)}, bf16[100,1024]{0,1:T(8,128)(2,1)S(1)}, u32[]{:S(2)}, u32[]{:S(2)}) %collective-permute-start.8) | collective-permute-done | bytes 204832 | tf_op jit(solution)/shard_map/ppermute | solution.py:1092
  93.6 9.1 %turn.1 = (bf16[512,2048]{1,0:T(8,128)(2,1)}, bf16[512,2048]{1,0:T(8,128)(2,1)}, f32[512,1]{1,0:T(8,128)}, bf16[32,640]{1,0:T(8,128)(2,1)}, bf16[32,512]{1,0:T(8...) custom-call(s32[2]{0:T(128)} %pad_add_fusion.refs_0_, ...), custom_call_target="tpu_custom_call" | custom-call | flops 26214400 | bytes 2097152 | tf_op jit(solution)/shard_map/turn/pallas_call | solution.py:116
  119.0 11.3 %collective-permute-done.12.refs_1_ = bf16[1536,256]{1,0:T(8,128)(2,1)} collective-permute-done((bf16[1536,256]{1,0:T(8,128)(2,1)}, bf16[1536,256]{1,0:T(8,128)(2,1)}, u32[]{:S(2)}, u32[]{:S(2)}) %collective-permute-start.12) | collective-permute-done | bytes 786464 | tf_op jit(solution)/shard_map/ppermute | solution.py:1095
  134.5 3.3 maximum_add_fusion.2.refs_2_.refs_0_.refs_22_
  139.7 3.0 maximum_add_fusion.3.refs_6_.refs_4_.refs_26_
  147.6 18.1 %all-gather.10.cloned.1.call-done = bf16[4096,256]{1,0:T(8,128)(2,1)} async-done(((bf16[1024,256]{1,0:T(8,128)(2,1)}), bf16[4096,256]{1,0:T(8,128)(2,1)}) %all-gather.10.cloned.1.call-update) | async-done | bytes 2097168 | tf_op jit(solution)/shard_map/all_gather | solution.py:1190
  165.7 3.0 dynamic-slice_bitcast_fusion.2
  170.5 3.3 steps.2
  173.8 4.9 maps.1
  178.7 15.5 %scan_slots.2 = (bf16[4,1024,512]{2,1,0:T(8,128)(2,1)}, f32[4,1024,512]{2,1,0:T(8,128)}, f32[4,1,1024,128]{3,2,1,0:T(8,128)}, f32[4,1024,128]{2,1,0:T(8,128)}, b...) custom-call(bf16[2,1680,256]{2,1,0:T(8,128)(2,1)} %copy-done.2, ...), custom_call_target="tpu_custom_call" | custom-call | flops 671088640 | bytes 1048576 | tf_op jit(solution)/shard_map/scan_slots/pallas_call | solution.py:416
  199.4 3.2 pad_maximum_fusion.10.refs_10_.refs_9_
  204.1 7.8 %proj_slots.4 = (bf16[4,1024,512]{2,1,0:T(8,128)(2,1)}, f32[8,128]{1,0:T(8,128)}) custom-call(bf16[2,1680,256]{2,1,0:T(8,128)(2,1)} %copy-done.2, bf16[2,1680,256]{2,1,0:T(8,128)(2,1)} %get-tuple-element.94.refs_3_.refs_1_.refs_8_.refs_2_.refs_15_, bf16[2,1680,256]{2,1,0:T(8,128)(2,1)} %copy-done.3, bf16[2,1680,256]{2,1,0:T(8,128)(2,1)} %copy-done.4, ...), custom_call_target="tpu_custom_call" | custom-call | flops 268435456 | bytes 655360 | tf_op jit(solution)/shard_map/proj_slots/pallas_call | solution.py:460
  211.9 7.7 %proj_slots.5 = (bf16[4,1024,512]{2,1,0:T(8,128)(2,1)}, f32[8,128]{1,0:T(8,128)}) custom-call(bf16[2,1680,256]{2,1,0:T(8,128)(2,1)} %copy-done.2, bf16[2,1680,256]{2,1,0:T(8,128)(2,1)} %get-tuple-element.94.refs_3_.refs_1_.refs_8_.refs_2_.refs_15_, bf16[2,1680,256]{2,1,0:T(8,128)(2,1)} %copy-done.3, bf16[2,1680,256]{2,1,0:T(8,128)(2,1)} %copy-done.4, ...), custom_call_target="tpu_custom_call" | custom-call | flops 268435456 | bytes 655360 | tf_op jit(solution)/shard_map/proj_slots/pallas_call | solution.py:460
  225.7 3.2 maximum_add_fusion.4.refs_2_.refs_0_.refs_9_
  233.6 3.6 steps.3
  239.0 39.6 %scan_slots.3 = (bf16[4,1024,512]{2,1,0:T(8,128)(2,1)}, f32[4,1024,512]{2,1,0:T(8,128)}, f32[4,1,1024,128]{3,2,1,0:T(8,128)}, f32[4,1024,128]{2,1,0:T(8,128)}, b...) custom-call(bf16[2,1584,256]{2,1,0:T(8,128)(2,1)} %maximum_add_fusio, ...), custom_call_target="tpu_custom_call", output_to_operand_aliasing={{0}: (16, {}), {1}: (17, {}), {2}: (18, {}), {3}: (19, {}),... | custom-call | flops 2013265920 | bytes 3145728 | tf_op jit(solution)/shard_map/scan_slots/pallas_call | solution.py:416
  284.6 19.9 %collective-permute-done.29.refs_10_ = bf16[4,1024,128]{2,1,0:T(8,128)(2,1)S(1)} collective-permute-done((bf16[4,1024,128]{2,1,0:T(8,128)(2,1)}, bf16[4,1024,128]{2,1,0:T(8,128)(2,1)S(1)}, u32[]{:S(2)}, u32[]{:S(2)}) %collective-permute-start.29) | collective-permute-done | bytes 1048608 | tf_op jit(solution)/shard_map/ppermute | solution.py:1289
  316.1 4.1 hop.4
  320.3 5.3 collective-permute-start.34
  325.5 17.9 %proj_slots.6 = (bf16[4,1024,512]{2,1,0:T(8,128)(2,1)}, f32[8,128]{1,0:T(8,128)}) custom-call(bf16[2,1536,256]{2,1,0:T(8,128)(2,1)} %maximum_add_fusion.4.refs_2_.refs_0_.refs_9_, bf16[2,1536,256]{2,1,0:T(8,128)(2,1)} %get-tuple-element.121.refs_3_.refs_1_.refs_10_, ...), custom_call_target="tpu_custom_call", output_to_operand_aliasing={{0}: (12, {})} | custom-call | flops 805306368 | bytes 1966080 | tf_op jit(solution)/shard_map/proj_slots/pallas_call | solution.py:460
  343.4 4.1 collective-permute-done.34.refs_5_
  348.0 3.6 collective-permute-done.32.refs_3_
  352.7 4.1 hop.5
  356.8 4.3 collective-permute-start.37
  361.2 17.8 %proj_slots.7 = (bf16[4,1024,512]{2,1,0:T(8,128)(2,1)}, f32[8,128]{1,0:T(8,128)}) custom-call(bf16[2,1536,256]{2,1,0:T(8,128)(2,1)} %maximum_add_fusion.6.refs_0_.refs_15_, bf16[2,1536,256]{2,1,0:T(8,128)(2,1)} %get-tuple-element.133.refs_1_.refs_16_, ...), custom_call_target="tpu_custom_call", output_to_operand_aliasing={{0}: (12, {})} | custom-call | flops 805306368 | bytes 1966080 | tf_op jit(solution)/shard_map/proj_slots/pallas_call | solution.py:460
  379.0 5.0 collective-permute-done.37.refs_3_.refs_6_
  384.9 32.3 %gate.1 = (bf16[4,1024,512]{2,1,0:T(8,128)(2,1)}, bf16[4,1024,512]{2,1,0:T(8,128)(2,1)}, bf16[4,1024,512]{2,1,0:T(8,128)(2,1)}, f32[4,1024,128]{2,1,0:T(8,128)}, bf16[4,1024,128]{2,1,0:T(8,128)(2,1)}) custom-call(bf16[4,1024,512]{2,1,0:T(8,128)(2,1)} %get-tuple-element.128.refs_0_, f32[4,1024,512]{2,1,0:T(8,128)} %get-tuple-element.129.refs_1_, ...), custom_call_target="tpu_custom_call" | custom-call | flops 157286400 | bytes 5767168 | tf_op jit(solution)/shard_map/gate/pallas_call | solution.py:538
  418.5 23.4 %output.1 = (bf16[512,2048]{1,0:T(8,128)(2,1)}, f32[4,16,1024]{2,1,0:T(8,128)}, f32[16,2048]{1,0:T(8,128)}) custom-call(s32[2]{0:T(128)} %pad_add_fusion.refs_0_, bf16[4,1024,512]{2,1,0:T(8,128)(2,1)} %get-tuple-element.140.refs_1_, bf16[4,1024,32]{2,1,0:T(8,128)(2,1)} %pad_maximum_fusion.9.refs_10_.refs_2_, ...), custom_call_target="tpu_custom_call" | custom-call | flops 1073741824 | bytes 2097152 | tf_op jit(solution)/shard_map/output/pallas_call | solution.py:929
  445.2 4.1 hop.6
  450.6 19.8 %gate_back.1.refs_9_.rest_0_.refs_10_ = f32[512,2048]{1,0:T(8,128)} custom-call(bf16[4,1024,512]{2,1,0:T(8,128)(2,1)} %get-tuple-element.147.refs_0_.refs_3_, bf16[2,1680,256]{2,1,0:T(8,128)(2,1)} %copy-done.2, bf16[2,1680,256]{2,1,0:T(8,128)(2,1)} %get-tuple-element.94.refs_3_.refs_1_.refs_8_.refs_2_.refs_15_, bf16[2,1680,256]{2,1,0:T(8,128)(2,1)} %copy-done.3, ...), custom_call_target="tpu_custom_call" | custom-call | flops 1073741824 | bytes 2097152 | tf_op jit(solution)/shard_map/gate_back/pallas_call | solution.py:968
  470.4 4.6 collective-permute-done.39.got
  475.9 4.1 hop.7
  483.2 26.0 %state_back.1 = (f32[4,1024,512]{2,1,0:T(8,128)}, f32[16,4,512]{2,1,0:T(4,128)}, f32[16,4,512]{2,1,0:T(4,128)}, f32[16,4,256]{2,1,0:T(4,128)}, f32[2,256,256]{2,...) custom-call(bf16[4,1024,512]{2,1,0:T(8,128)(2,1)} %get-tuple-element.143.refs_0_.refs_1_, ...), custom_call_target="tpu_custom_call" | custom-call | flops 1342177280 | bytes 2097152 | tf_op jit(solution)/shard_map/state_back/pallas_call | solution.py:661
  510.2 26.0 %finish_back.1 = (bf16[4,1024,512]{2,1,0:T(8,128)(2,1)}, f32[4,1024,128]{2,1,0:T(8,128)}, f32[4,8,1024]{2,1,0:T(8,128)}, f32[4,32,1024]{2,1,0:T(8,128)}, f32[4,3...) custom-call(f32[4,1024,512]{2,1,0:T(8,128)} %get-tuple-element.148.r, ...), custom_call_target="tpu_custom_call" | custom-call | flops 183500800 | bytes 3670016 | tf_op jit(solution)/shard_map/finish_back/pallas_call | solution.py:747
  536.2 3.8 glue.1
  542.8 4.8 collective-permute-done.41
  553.7 5.7 fusion.21
  570.9 3.8 collective-permute-done.43
  574.8 13.7 %all-gather.1 = bf16[64,1024]{1,0:T(8,128)(2,1)S(1)} all-gather(bf16[16,1024]{1,0:T(8,128)(2,1)S(1)} %slice.529), channel_id=3, replica_groups=mesh['dp'=8,'tensor'=4] {'tensor'}, dimensions={0}, use_global_device_ids=true | all-gather | bytes 163840 | tf_op jit(solution)/shard_map/all_gather | solution.py:1106
  589.6 8.0 %collective-permute-done.45 = bf16[1,16,7296]{2,0,1:T(2,128)(2,1)S(1)} collective-permute-done((bf16[1,16,7296]{2,0,1:T(2,128)(2,1)S(1)}, bf16[1,16,7296]{2,0,1:T(2,128)(2,1)S(1)}, u32[]{:S(2)}, u32[]{:S(2)}) %collective-permute-start.45) | collective-permute-done | bytes 233504 | tf_op jit(solution)/shard_map/ppermute | solution.py:1095
  601.0 7.3 %collective-permute-done.46 = bf16[2,16,7296]{2,0,1:T(2,128)(2,1)S(1)} collective-permute-done((bf16[2,16,7296]{2,0,1:T(2,128)(2,1)}, bf16[2,16,7296]{2,0,1:T(2,128)(2,1)S(1)}, u32[]{:S(2)}, u32[]{:S(2)}) %collective-permute-start.46) | collective-permute-done | bytes 466976 | tf_op jit(solution)/shard_map/ppermute | solution.py:1095
  612.3 3.5 fusion.19
  618.2 27.2 %input_back.1 = bf16[512,2048]{1,0:T(8,128)(2,1)} custom-call(s32[2]{0:T(128)} %pad_add_fusion.refs_0_, bf16[4,1024,512]{2,1,0:T(8,128)(2,1)} %get-tuple-element.151.refs_1_, bf16[4,1024,128]{2,1,0:T(8,128)(2,1)} %add_convert_fusion.refs_2_, bf16[320,512]{1,0:T(8,128)(2,1)} %fusion.11.refs_3_, bf16[16,512]{1,0:T(8,128)(2,1)} %copy-done.57, ...), custom_call_target="tpu_custom_call" | custom-call | flops 1073741824 | bytes 2097152 | tf_op jit(solution)/shard_map/input_back/pallas_call | solution.py:1035
  646.3 3.3 fusion.2
  (387 shorter events, 157.3 us)
Async XLA Ops:
  7.2 95.5 %all-gather.6.cloned.1.call-start = ((), (), s32[]{:S(2)}) async-start(), calls=%async_computation | async-start | bytes 2621440 | tf_op jit(solution)/shard_map/all_gather | solution.py:1188
  10.9 136.7 %all-gather.8.cloned.1.call-start = ((), (), s32[]{:S(2)}) async-start(), calls=%async_computation.1 | async-start | bytes 2621440 | tf_op jit(solution)/shard_map/all_gather | solution.py:1189
  11.6 154.0 %all-gather.10.cloned.1.call-start = ((), (), s32[]{:S(2)}) async-start(), calls=%async_computation.2 | async-start | bytes 2621440 | tf_op jit(solution)/shard_map/all_gather | solution.py:1190
  13.4 26.4 %collective-permute-start.1 = (bf16[1664,256]{1,0:T(8,128)(2,1)}, bf16[1664,256]{1,0:T(8,128)(2,1)S(1)}, u32[]{:S(2)}, u32[]{:S(2)}) collective-permute-start(bf16[1664,256]{1,0:T(8,128)(2,1)} %get-tuple-element.261), channel_id=1, source_target_pairs={{0,16},{4,20},{8,24},{12,28},{16,0},{20,4},{24,8},{28,12},{1,17},{... | collective-permute-start | bytes 2555912 | tf_op jit(solution)/shard_map/ppermute | solution.py:1095
  16.9 22.9 %collective-permute-start = (bf16[1680,256]{1,0:T(8,128)(2,1)}, bf16[1680,256]{1,0:T(8,128)(2,1)S(1)}, u32[]{:S(2)}, u32[]{:S(2)}) collective-permute-start(bf16[1680,256]{1,0:T(8,128)(2,1)} %constant_dynamic-update-slice_fusion), channel_id=1, source_target_pairs={{0,8},{4,12},{8,0},{12,4},{16,24},{20,28},{24,16},{28,20},{1,9},{5... | collective-permute-start | bytes 2580488 | tf_op jit(solution)/shard_map/ppermute | solution.py:1095
  22.7 16.1 %collective-permute-start.2 = (bf16[100,1024]{0,1:T(8,128)(2,1)}, bf16[100,1024]{0,1:T(8,128)(2,1)S(1)}, u32[]{:S(2)}, u32[]{:S(2)}) collective-permute-start(bf16[100,1024]{0,1:T(8,128)(2,1)} %concatenate.76), channel_id=1, source_target_pairs={{3,0},{0,1},{1,2},{2,3},{7,4},{4,5},{5,6},{6,7},{11,8},{8,9},{9,10... | collective-permute-start | bytes 614408 | tf_op jit(solution)/shard_map/ppermute | solution.py:1092
  45.8 60.3 %collective-permute-start.3 = (bf16[2,1680,256]{2,1,0:T(8,128)(2,1)S(1)}, bf16[2,1680,256]{2,1,0:T(8,128)(2,1)S(1)}, u32[]{:S(2)}, u32[]{:S(2)}) collective-permute-start(bf16[2,1680,256]{2,1,0:T(8,128)(2,1)S(1)} %maximum_add_fusion.refs_2_.refs_0_.refs_7_.refs_1_.refs_14_), channel_id=1, source_target_pairs={{0,4},{4,0},{8,12},{12,8},{16,20},{20,16},{24,28},{28,24},{1,5},{5... | collective-permute-start | bytes 5160968 | tf_op jit(solution)/shard_map/ppermute | solution.py:1095
  45.8 60.3 %collective-permute-start.5 = (bf16[2,1680,256]{2,1,0:T(8,128)(2,1)S(1)}, bf16[2,1680,256]{2,1,0:T(8,128)(2,1)}, u32[]{:S(2)}, u32[]{:S(2)}) collective-permute-start(bf16[2,1680,256]{2,1,0:T(8,128)(2,1)S(1)} %maximum_add_fusion.refs_2_.refs_0_.refs_7_.refs_1_.refs_14_), channel_id=1, source_target_pairs={{0,16},{4,20},{8,24},{12,28},{16,0},{20,4},{24,8},{28,12},{1,17},{... | collective-permute-start | bytes 5160968 | tf_op jit(solution)/shard_map/ppermute | solution.py:1095
  48.2 57.8 %collective-permute-start.4 = (bf16[2,1664,256]{2,1,0:T(8,128)(2,1)}, bf16[2,1664,256]{2,1,0:T(8,128)(2,1)}, u32[]{:S(2)}, u32[]{:S(2)}) collective-permute-start(bf16[2,1664,256]{2,1,0:T(8,128)(2,1)} %maximum_add_fusion.1.refs_6_.refs_4_.refs_11_.refs_5_.refs_18_), channel_id=1, source_target_pairs={{0,4},{4,0},{8,12},{12,8},{16,20},{20,16},{24,28},{28,24},{1,5},{5... | collective-permute-start | bytes 5111816 | tf_op jit(solution)/shard_map/ppermute | solution.py:1095
  48.4 57.7 %collective-permute-start.6 = (bf16[2,1664,256]{2,1,0:T(8,128)(2,1)}, bf16[2,1664,256]{2,1,0:T(8,128)(2,1)}, u32[]{:S(2)}, u32[]{:S(2)}) collective-permute-start(bf16[2,1664,256]{2,1,0:T(8,128)(2,1)} %maximum_add_fusion.1.refs_6_.refs_4_.refs_11_.refs_5_.refs_18_), channel_id=1, source_target_pairs={{0,8},{4,12},{8,0},{12,4},{16,24},{20,28},{24,16},{28,20},{1,9},{5... | collective-permute-start | bytes 5111816 | tf_op jit(solution)/shard_map/ppermute | solution.py:1095
  48.7 20.5 %collective-permute-start.7 = (bf16[100,1024]{0,1:T(8,128)(2,1)}, bf16[100,1024]{0,1:T(8,128)(2,1)}, u32[]{:S(2)}, u32[]{:S(2)}) collective-permute-start(bf16[100,1024]{0,1:T(8,128)(2,1)} %concatenate.76), channel_id=1, source_target_pairs={{1,0},{2,1},{3,2},{0,3},{5,4},{6,5},{7,6},{4,7},{9,8},{10,9},{11,1... | collective-permute-start | bytes 614408 | tf_op jit(solution)/shard_map/ppermute | solution.py:1092
  69.2 20.0 %collective-permute-start.8 = (bf16[100,1024]{0,1:T(8,128)(2,1)}, bf16[100,1024]{0,1:T(8,128)(2,1)S(1)}, u32[]{:S(2)}, u32[]{:S(2)}) collective-permute-start(bf16[100,1024]{0,1:T(8,128)(2,1)} %concatenate.76), channel_id=1, source_target_pairs={{2,0},{3,1},{0,2},{1,3},{6,4},{7,5},{4,6},{5,7},{10,8},{11,9},{8,1... | collective-permute-start | bytes 614408 | tf_op jit(solution)/shard_map/ppermute | solution.py:1092
  107.9 22.4 %collective-permute-start.9 = (bf16[2,1680,256]{2,1,0:T(8,128)(2,1)}, bf16[2,1680,256]{2,1,0:T(8,128)(2,1)S(1)}, u32[]{:S(2)}, u32[]{:S(2)}) collective-permute-start(bf16[2,1680,256]{2,1,0:T(8,128)(2,1)} %get-tuple-element.94.refs_3_.refs_1_.refs_8_.refs_2_.refs_15_), channel_id=1, source_target_pairs={{0,4},{4,0},{8,12},{12,8},{16,20},{20,16},{24,28},{28,24},{1,5},{5... | collective-permute-start | bytes 5160968 | tf_op jit(solution)/shard_map/ppermute | solution.py:1095
  107.9 22.4 %collective-permute-start.10 = (bf16[2,1664,256]{2,1,0:T(8,128)(2,1)}, bf16[2,1664,256]{2,1,0:T(8,128)(2,1)S(1)}, u32[]{:S(2)}, u32[]{:S(2)}) collective-permute-start(bf16[2,1664,256]{2,1,0:T(8,128)(2,1)} %get-tuple-element.95.refs_7_.refs_5_.refs_12_.refs_6_.refs_19_), channel_id=1, source_target_pairs={{0,4},{4,0},{8,12},{12,8},{16,20},{20,16},{24,28},{28,24},{1,5},{5... | collective-permute-start | bytes 5111816 | tf_op jit(solution)/shard_map/ppermute | solution.py:1095
  108.4 21.9 %collective-permute-start.11 = (bf16[1584,256]{1,0:T(8,128)(2,1)}, bf16[1584,256]{1,0:T(8,128)(2,1)}, u32[]{:S(2)}, u32[]{:S(2)}) collective-permute-start(bf16[1584,256]{1,0:T(8,128)(2,1)} %get-tuple-element.98), channel_id=1, source_target_pairs={{0,8},{4,12},{8,0},{12,4},{16,24},{20,28},{24,16},{28,20},{1,9},{5... | collective-permute-start | bytes 2433032 | tf_op jit(solution)/shard_map/ppermute | solution.py:1095
  109.9 20.4 %collective-permute-start.12 = (bf16[1536,256]{1,0:T(8,128)(2,1)}, bf16[1536,256]{1,0:T(8,128)(2,1)}, u32[]{:S(2)}, u32[]{:S(2)}) collective-permute-start(bf16[1536,256]{1,0:T(8,128)(2,1)} %get-tuple-element.99), channel_id=1, source_target_pairs={{0,16},{4,20},{8,24},{12,28},{16,0},{20,4},{24,8},{28,12},{1,17},{... | collective-permute-start | bytes 2359304 | tf_op jit(solution)/shard_map/ppermute | solution.py:1095
  137.9 56.3 %collective-permute-start.13 = (bf16[2,1584,256]{2,1,0:T(8,128)(2,1)}, bf16[2,1584,256]{2,1,0:T(8,128)(2,1)S(1)}, u32[]{:S(2)}, u32[]{:S(2)}) collective-permute-start(bf16[2,1584,256]{2,1,0:T(8,128)(2,1)} %maximum_add_fusion.2.refs_2_.refs_0_.refs_22_), channel_id=1, source_target_pairs={{0,4},{4,0},{8,12},{12,8},{16,20},{20,16},{24,28},{28,24},{1,5},{5... | collective-permute-start | bytes 4866056 | tf_op jit(solution)/shard_map/ppermute | solution.py:1095
  137.9 56.3 %collective-permute-start.15 = (bf16[2,1584,256]{2,1,0:T(8,128)(2,1)}, bf16[2,1584,256]{2,1,0:T(8,128)(2,1)}, u32[]{:S(2)}, u32[]{:S(2)}) collective-permute-start(bf16[2,1584,256]{2,1,0:T(8,128)(2,1)} %maximum_add_fusion.2.refs_2_.refs_0_.refs_22_), channel_id=1, source_target_pairs={{0,16},{4,20},{8,24},{12,28},{16,0},{20,4},{24,8},{28,12},{1,17},{... | collective-permute-start | bytes 4866056 | tf_op jit(solution)/shard_map/ppermute | solution.py:1095
  142.7 51.5 %collective-permute-start.14 = (bf16[2,1536,256]{2,1,0:T(8,128)(2,1)}, bf16[2,1536,256]{2,1,0:T(8,128)(2,1)}, u32[]{:S(2)}, u32[]{:S(2)}) collective-permute-start(bf16[2,1536,256]{2,1,0:T(8,128)(2,1)} %maximum_add_fusion.3.refs_6_.refs_4_.refs_26_), channel_id=1, source_target_pairs={{0,4},{4,0},{8,12},{12,8},{16,20},{20,16},{24,28},{28,24},{1,5},{5... | collective-permute-start | bytes 4718600 | tf_op jit(solution)/shard_map/ppermute | solution.py:1095
  142.9 51.3 %collective-permute-start.16 = (bf16[2,1536,256]{2,1,0:T(8,128)(2,1)}, bf16[2,1536,256]{2,1,0:T(8,128)(2,1)}, u32[]{:S(2)}, u32[]{:S(2)}) collective-permute-start(bf16[2,1536,256]{2,1,0:T(8,128)(2,1)} %maximum_add_fusion.3.refs_6_.refs_4_.refs_26_), channel_id=1, source_target_pairs={{0,8},{4,12},{8,0},{12,4},{16,24},{20,28},{24,16},{28,20},{1,9},{5... | collective-permute-start | bytes 4718600 | tf_op jit(solution)/shard_map/ppermute | solution.py:1095
  195.9 23.7 %collective-permute-start.19 = (bf16[2,1584,256]{2,1,0:T(8,128)(2,1)}, bf16[2,1584,256]{2,1,0:T(8,128)(2,1)S(1)}, u32[]{:S(2)}, u32[]{:S(2)}) collective-permute-start(bf16[2,1584,256]{2,1,0:T(8,128)(2,1)} %get-tuple-element.107.refs_3_.refs_1_.refs_23_), channel_id=1, source_target_pairs={{0,4},{4,0},{8,12},{12,8},{16,20},{20,16},{24,28},{28,24},{1,5},{5... | collective-permute-start | bytes 4866056 | tf_op jit(solution)/shard_map/ppermute | solution.py:1095
  195.9 23.7 %collective-permute-start.20 = (bf16[2,1536,256]{2,1,0:T(8,128)(2,1)}, bf16[2,1536,256]{2,1,0:T(8,128)(2,1)}, u32[]{:S(2)}, u32[]{:S(2)}) collective-permute-start(bf16[2,1536,256]{2,1,0:T(8,128)(2,1)} %get-tuple-element.108.refs_7_.refs_5_.refs_27_), channel_id=1, source_target_pairs={{0,4},{4,0},{8,12},{12,8},{16,20},{20,16},{24,28},{28,24},{1,5},{5... | collective-permute-start | bytes 4718600 | tf_op jit(solution)/shard_map/ppermute | solution.py:1095
  196.4 23.2 %collective-permute-start.17 = (bf16[1536,256]{1,0:T(8,128)(2,1)}, bf16[1536,256]{1,0:T(8,128)(2,1)}, u32[]{:S(2)}, u32[]{:S(2)}) collective-permute-start(bf16[1536,256]{1,0:T(8,128)(2,1)} %get-tuple-element.105), channel_id=1, source_target_pairs={{0,8},{4,12},{8,0},{12,4},{16,24},{20,28},{24,16},{28,20},{1,9},{5... | collective-permute-start | bytes 2359304 | tf_op jit(solution)/shard_map/ppermute | solution.py:1095
  197.9 21.7 %collective-permute-start.18 = (bf16[1536,256]{1,0:T(8,128)(2,1)}, bf16[1536,256]{1,0:T(8,128)(2,1)}, u32[]{:S(2)}, u32[]{:S(2)}) collective-permute-start(bf16[1536,256]{1,0:T(8,128)(2,1)} %get-tuple-element.106), channel_id=1, source_target_pairs={{0,16},{4,20},{8,24},{12,28},{16,0},{20,4},{24,8},{28,12},{1,17},{... | collective-permute-start | bytes 2359304 | tf_op jit(solution)/shard_map/ppermute | solution.py:1095
  224.9 53.7 %collective-permute-start.22 = (bf16[2,1536,256]{2,1,0:T(8,128)(2,1)S(1)}, bf16[2,1536,256]{2,1,0:T(8,128)(2,1)}, u32[]{:S(2)}, u32[]{:S(2)}) collective-permute-start(bf16[2,1536,256]{2,1,0:T(8,128)(2,1)S(1)} %maximum_add_fusion.5.refs_6_.refs_4_.refs_13_), channel_id=1, source_target_pairs={{0,4},{4,0},{8,12},{12,8},{16,20},{20,16},{24,28},{28,24},{1,5},{5... | collective-permute-start | bytes 4718600 | tf_op jit(solution)/shard_map/ppermute | solution.py:1095
  225.0 53.6 %collective-permute-start.24 = (bf16[2,1536,256]{2,1,0:T(8,128)(2,1)S(1)}, bf16[2,1536,256]{2,1,0:T(8,128)(2,1)}, u32[]{:S(2)}, u32[]{:S(2)}) collective-permute-start(bf16[2,1536,256]{2,1,0:T(8,128)(2,1)S(1)} %maximum_add_fusion.5.refs_6_.refs_4_.refs_13_), channel_id=1, source_target_pairs={{0,8},{4,12},{8,0},{12,4},{16,24},{20,28},{24,16},{28,20},{1,9},{5... | collective-permute-start | bytes 4718600 | tf_op jit(solution)/shard_map/ppermute | solution.py:1095
  228.9 49.8 %collective-permute-start.21 = (bf16[2,1536,256]{2,1,0:T(8,128)(2,1)}, bf16[2,1536,256]{2,1,0:T(8,128)(2,1)}, u32[]{:S(2)}, u32[]{:S(2)}) collective-permute-start(bf16[2,1536,256]{2,1,0:T(8,128)(2,1)} %maximum_add_fusion.4.refs_2_.refs_0_.refs_9_), channel_id=1, source_target_pairs={{0,4},{4,0},{8,12},{12,8},{16,20},{20,16},{24,28},{28,24},{1,5},{5... | collective-permute-start | bytes 4718600 | tf_op jit(solution)/shard_map/ppermute | solution.py:1095
  229.0 49.6 %collective-permute-start.23 = (bf16[2,1536,256]{2,1,0:T(8,128)(2,1)}, bf16[2,1536,256]{2,1,0:T(8,128)(2,1)}, u32[]{:S(2)}, u32[]{:S(2)}) collective-permute-start(bf16[2,1536,256]{2,1,0:T(8,128)(2,1)} %maximum_add_fusion.4.refs_2_.refs_0_.refs_9_), channel_id=1, source_target_pairs={{0,16},{4,20},{8,24},{12,28},{16,0},{20,4},{24,8},{28,12},{1,17},{... | collective-permute-start | bytes 4718600 | tf_op jit(solution)/shard_map/ppermute | solution.py:1095
  279.2 25.3 %collective-permute-start.25 = (bf16[2,1536,256]{2,1,0:T(8,128)(2,1)}, bf16[2,1536,256]{2,1,0:T(8,128)(2,1)S(1)}, u32[]{:S(2)}, u32[]{:S(2)}) collective-permute-start(bf16[2,1536,256]{2,1,0:T(8,128)(2,1)} %get-tuple-element.121.refs_3_.refs_1_.refs_10_), channel_id=1, source_target_pairs={{0,4},{4,0},{8,12},{12,8},{16,20},{20,16},{24,28},{28,24},{1,5},{5... | collective-permute-start | bytes 4718600 | tf_op jit(solution)/shard_map/ppermute | solution.py:1095
  279.3 26.7 %collective-permute-start.26 = (bf16[2,1536,256]{2,1,0:T(8,128)(2,1)}, bf16[2,1536,256]{2,1,0:T(8,128)(2,1)}, u32[]{:S(2)}, u32[]{:S(2)}) collective-permute-start(bf16[2,1536,256]{2,1,0:T(8,128)(2,1)} %get-tuple-element.122.refs_7_.refs_5_.refs_14_), channel_id=1, source_target_pairs={{0,4},{4,0},{8,12},{12,8},{16,20},{20,16},{24,28},{28,24},{1,5},{5... | collective-permute-start | bytes 4718600 | tf_op jit(solution)/shard_map/ppermute | solution.py:1095
  279.7 24.7 %collective-permute-start.29 = (bf16[4,1024,128]{2,1,0:T(8,128)(2,1)}, bf16[4,1024,128]{2,1,0:T(8,128)(2,1)S(1)}, u32[]{:S(2)}, u32[]{:S(2)}) collective-permute-start(bf16[4,1024,128]{2,1,0:T(8,128)(2,1)} %get-tuple-element.126), channel_id=1, source_target_pairs={{0,1},{1,2},{2,3},{4,5},{5,6},{6,7},{8,9},{9,10},{10,11},{12,13},{... | collective-permute-start | bytes 3145736 | tf_op jit(solution)/shard_map/ppermute | solution.py:1289
  281.6 22.9 %collective-permute-start.27 = (bf16[1536,256]{1,0:T(8,128)(2,1)}, bf16[1536,256]{1,0:T(8,128)(2,1)S(1)}, u32[]{:S(2)}, u32[]{:S(2)}) collective-permute-start(bf16[1536,256]{1,0:T(8,128)(2,1)} %get-tuple-element.124), channel_id=1, source_target_pairs={{0,8},{4,12},{8,0},{12,4},{16,24},{20,28},{24,16},{28,20},{1,9},{5... | collective-permute-start | bytes 2359304 | tf_op jit(solution)/shard_map/ppermute | solution.py:1095
  283.1 21.4 %collective-permute-start.28 = (bf16[1536,256]{1,0:T(8,128)(2,1)}, bf16[1536,256]{1,0:T(8,128)(2,1)S(1)}, u32[]{:S(2)}, u32[]{:S(2)}) collective-permute-start(bf16[1536,256]{1,0:T(8,128)(2,1)} %get-tuple-element.125), channel_id=1, source_target_pairs={{0,16},{4,20},{8,24},{12,28},{16,0},{20,4},{24,8},{28,12},{1,17},{... | collective-permute-start | bytes 2359304 | tf_op jit(solution)/shard_map/ppermute | solution.py:1095
  311.0 36.5 %collective-permute-start.31 = (bf16[2,1536,256]{2,1,0:T(8,128)(2,1)S(1)}, bf16[2,1536,256]{2,1,0:T(8,128)(2,1)}, u32[]{:S(2)}, u32[]{:S(2)}) collective-permute-start(bf16[2,1536,256]{2,1,0:T(8,128)(2,1)S(1)} %maximum_add_fusion.7.refs_4_.refs_19_), channel_id=1, source_target_pairs={{0,4},{4,0},{8,12},{12,8},{16,20},{20,16},{24,28},{28,24},{1,5},{5... | collective-permute-start | bytes 4718600 | tf_op jit(solution)/shard_map/ppermute | solution.py:1095
  311.1 36.9 %collective-permute-start.33 = (bf16[2,1536,256]{2,1,0:T(8,128)(2,1)S(1)}, bf16[2,1536,256]{2,1,0:T(8,128)(2,1)}, u32[]{:S(2)}, u32[]{:S(2)}) collective-permute-start(bf16[2,1536,256]{2,1,0:T(8,128)(2,1)S(1)} %maximum_add_fusion.7.refs_4_.refs_19_), channel_id=1, source_target_pairs={{0,8},{4,12},{8,0},{12,4},{16,24},{20,28},{24,16},{28,20},{1,9},{5... | collective-permute-start | bytes 4718600 | tf_op jit(solution)/shard_map/ppermute | solution.py:1095
  314.5 33.5 %collective-permute-start.30 = (bf16[2,1536,256]{2,1,0:T(8,128)(2,1)}, bf16[2,1536,256]{2,1,0:T(8,128)(2,1)}, u32[]{:S(2)}, u32[]{:S(2)}) collective-permute-start(bf16[2,1536,256]{2,1,0:T(8,128)(2,1)} %maximum_add_fusion.6.refs_0_.refs_15_), channel_id=1, source_target_pairs={{0,4},{4,0},{8,12},{12,8},{16,20},{20,16},{24,28},{28,24},{1,5},{5... | collective-permute-start | bytes 4718600 | tf_op jit(solution)/shard_map/ppermute | solution.py:1095
  314.6 37.0 %collective-permute-start.32 = (bf16[2,1536,256]{2,1,0:T(8,128)(2,1)}, bf16[2,1536,256]{2,1,0:T(8,128)(2,1)}, u32[]{:S(2)}, u32[]{:S(2)}) collective-permute-start(bf16[2,1536,256]{2,1,0:T(8,128)(2,1)} %maximum_add_fusion.6.refs_0_.refs_15_), channel_id=1, source_target_pairs={{0,16},{4,20},{8,24},{12,28},{16,0},{20,4},{24,8},{28,12},{1,17},{... | collective-permute-start | bytes 4718600 | tf_op jit(solution)/shard_map/ppermute | solution.py:1095
  320.3 27.2 %collective-permute-start.34 = (bf16[4,1024,128]{2,1,0:T(8,128)(2,1)}, bf16[4,1024,128]{2,1,0:T(8,128)(2,1)}, u32[]{:S(2)}, u32[]{:S(2)}) collective-permute-start(bf16[4,1024,128]{2,1,0:T(8,128)(2,1)} %hop.4), channel_id=1, source_target_pairs={{0,1},{1,2},{2,3},{4,5},{5,6},{6,7},{8,9},{9,10},{10,11},{12,13},{... | collective-permute-start | bytes 3145736 | tf_op jit(solution)/shard_map/ppermute | solution.py:1295
  352.2 9.0 %collective-permute-start.35 = (bf16[2,1536,256]{2,1,0:T(8,128)(2,1)}, bf16[2,1536,256]{2,1,0:T(8,128)(2,1)}, u32[]{:S(2)}, u32[]{:S(2)}) collective-permute-start(bf16[2,1536,256]{2,1,0:T(8,128)(2,1)} %get-tuple-element.133.refs_1_.refs_16_), channel_id=1, source_target_pairs={{0,4},{4,0},{8,12},{12,8},{16,20},{20,16},{24,28},{28,24},{1,5},{5... | collective-permute-start | bytes 4718600 | tf_op jit(solution)/shard_map/ppermute | solution.py:1095
  352.2 9.0 %collective-permute-start.36 = (bf16[2,1536,256]{2,1,0:T(8,128)(2,1)}, bf16[2,1536,256]{2,1,0:T(8,128)(2,1)}, u32[]{:S(2)}, u32[]{:S(2)}) collective-permute-start(bf16[2,1536,256]{2,1,0:T(8,128)(2,1)} %get-tuple-element.134.refs_5_.refs_20_), channel_id=1, source_target_pairs={{0,4},{4,0},{8,12},{12,8},{16,20},{20,16},{24,28},{28,24},{1,5},{5... | collective-permute-start | bytes 4718600 | tf_op jit(solution)/shard_map/ppermute | solution.py:1095
  356.8 27.2 %collective-permute-start.37 = (bf16[4,1024,128]{2,1,0:T(8,128)(2,1)}, bf16[4,1024,128]{2,1,0:T(8,128)(2,1)S(1)}, u32[]{:S(2)}, u32[]{:S(2)}) collective-permute-start(bf16[4,1024,128]{2,1,0:T(8,128)(2,1)} %hop.5), channel_id=1, source_target_pairs={{0,1},{1,2},{2,3},{4,5},{5,6},{6,7},{8,9},{9,10},{10,11},{12,13},{... | collective-permute-start | bytes 3145736 | tf_op jit(solution)/shard_map/ppermute | solution.py:1301
  417.2 27.0 %collective-permute-start.38 = (bf16[4,1024,128]{2,1,0:T(8,128)(2,1)}, bf16[4,1024,128]{2,1,0:T(8,128)(2,1)S(1)}, u32[]{:S(2)}, u32[]{:S(2)}) collective-permute-start(bf16[4,1024,128]{2,1,0:T(8,128)(2,1)} %get-tuple-element.149), channel_id=1, source_target_pairs={{1,0},{2,1},{3,2},{5,4},{6,5},{7,6},{9,8},{10,9},{11,10},{13,12},{... | collective-permute-start | bytes 3145736 | tf_op jit(solution)/shard_map/ppermute | solution.py:1327
  449.3 25.7 %collective-permute-start.39 = (bf16[4,1024,128]{2,1,0:T(8,128)(2,1)}, bf16[4,1024,128]{2,1,0:T(8,128)(2,1)S(1)}, u32[]{:S(2)}, u32[]{:S(2)}) collective-permute-start(bf16[4,1024,128]{2,1,0:T(8,128)(2,1)} %hop.6), channel_id=1, source_target_pairs={{1,0},{2,1},{3,2},{5,4},{6,5},{7,6},{9,8},{10,9},{11,10},{13,12},{... | collective-permute-start | bytes 3145736 | tf_op jit(solution)/shard_map/ppermute | solution.py:1331
  480.0 29.1 %collective-permute-start.40 = (bf16[4,1024,128]{2,1,0:T(8,128)(2,1)}, bf16[4,1024,128]{2,1,0:T(8,128)(2,1)S(1)}, u32[]{:S(2)}, u32[]{:S(2)}) collective-permute-start(bf16[4,1024,128]{2,1,0:T(8,128)(2,1)} %hop.7), channel_id=1, source_target_pairs={{1,0},{2,1},{3,2},{5,4},{6,5},{7,6},{9,8},{10,9},{11,10},{13,12},{... | collective-permute-start | bytes 3145736 | tf_op jit(solution)/shard_map/ppermute | solution.py:1333
  566.0 8.6 %collective-permute-start.43 = (bf16[16,4096]{1,0:T(8,128)(2,1)S(1)}, bf16[16,4096]{1,0:T(8,128)(2,1)S(1)}, u32[]{:S(2)}, u32[]{:S(2)}) collective-permute-start(bf16[16,4096]{1,0:T(8,128)(2,1)S(1)} %get-tuple-element.264), channel_id=1, source_target_pairs={{0,2},{1,3},{2,0},{3,1},{4,6},{5,7},{6,4},{7,5},{8,10},{9,11},{10,... | collective-permute-start | bytes 393224 | tf_op jit(solution)/shard_map/ppermute | solution.py:1111
  589.0 8.6 %collective-permute-start.45 = (bf16[1,16,7296]{2,0,1:T(2,128)(2,1)S(1)}, bf16[1,16,7296]{2,0,1:T(2,128)(2,1)S(1)}, u32[]{:S(2)}, u32[]{:S(2)}) collective-permute-start(bf16[1,16,7296]{2,0,1:T(2,128)(2,1)S(1)} %copy.332), channel_id=1, source_target_pairs={{0,8},{4,12},{8,0},{12,4},{16,24},{20,28},{24,16},{28,20},{1,9},{5... | collective-permute-start | bytes 700424 | tf_op jit(solution)/shard_map/ppermute | solution.py:1095
  599.5 8.8 %collective-permute-start.46 = (bf16[2,16,7296]{2,0,1:T(2,128)(2,1)}, bf16[2,16,7296]{2,0,1:T(2,128)(2,1)S(1)}, u32[]{:S(2)}, u32[]{:S(2)}) collective-permute-start(bf16[2,16,7296]{2,0,1:T(2,128)(2,1)} %pad_maximum_fusion.21), channel_id=1, source_target_pairs={{0,16},{4,20},{8,24},{12,28},{16,0},{20,4},{24,8},{28,12},{1,17},{... | collective-permute-start | bytes 1400840 | tf_op jit(solution)/shard_map/ppermute | solution.py:1095
  610.7 34.7 %collective-permute-start.47 = (bf16[4,16,7296]{2,0,1:T(4,128)(2,1)}, bf16[4,16,7296]{2,0,1:T(4,128)(2,1)}, u32[]{:S(2)}, u32[]{:S(2)}) collective-permute-start(bf16[4,16,7296]{2,0,1:T(4,128)(2,1)} %pad_maximum_fusion.11), channel_id=1, source_target_pairs={{0,4},{4,0},{8,12},{12,8},{16,20},{20,16},{24,28},{28,24},{1,5},{5... | collective-permute-start | bytes 2801672 | tf_op jit(solution)/shard_map/ppermute | solution.py:1095
  (79 other events, 495.4 us)
Sparse Core Ops, SparseCore 0:
  11.0 57.7 all-gather.5
  70.4 48.0 all-gather.7
  120.0 45.6 all-gather.9

commit v3 on v2

--- a/solution.py
+++ b/solution.py
@@ -38,8 +38,25 @@
     )
 
 
+def packed_spec(kind, index):
+    def where(*grid):
+        slot, c = index(*grid)
+        return (slot, c * 4 + kind, 0)
+
+    return pl.BlockSpec((None, 16, CB), where)
+
+
 def sigmoid(v):
     return 0.5 + 0.5 * jnp.tanh(0.5 * v)
+
+
+def columns(numbers):
+    v = numbers[...].astype(f32)
+    return jnp.transpose(v[:8] + v[8:])
+
+
+def tall(rows):
+    return jnp.transpose(jnp.concatenate([rows, rows], axis=0))
 
 
 def conv_values(raw, chan):
@@ -73,8 +90,7 @@
 
 def turn_kernel(flat, quick, *refs):
     (sc, tok_r, bef_r, cot_r, gain, down, up) = refs[:7]
-    normed_o, masked_o, root_o, low_o, back_o, nt_o, gt_o, tok_o, halo_sc = refs[-9:]
-    tok_o[...] = jnp.zeros_like(tok_o)
+    normed_o, masked_o, root_o, low_o, back_o, nt_o, gt_o, halo_sc = refs[-8:]
     width = tok_r.shape[1]
     length = tok_r.shape[0]
 
@@ -103,9 +119,8 @@
         back_m = dot(up[:, at], gt)
         low = low_m if low is None else low + low_m
         back = back_m if back is None else back + back_m
-    for out, v in ((low_o, low), (back_o, back)):
-        hi = v.astype(bf16)
-        out[...] = jnp.concatenate([hi, (v - hi.astype(f32)).astype(bf16)], axis=0)
+    low_o[...] = low.astype(bf16)
+    back_o[...] = back.astype(bf16)
 
 
 def turn_call(sc, tokens, before, cot, gain, down, up, flat, quick, later):
@@ -117,16 +132,15 @@
         functools.partial(turn_kernel, flat, quick),
         in_specs=[pl.BlockSpec(memory_space=pltpu.SMEM)] + [vm] * 6
         + [pl.BlockSpec(memory_space=pl.ANY)] * len(later),
-        out_specs=[vm] * 8,
+        out_specs=[vm] * 7,
         out_shape=[
             jax.ShapeDtypeStruct((length, width), bf16),
             jax.ShapeDtypeStruct((length, width), bf16),
             jax.ShapeDtypeStruct((length, 1), f32),
-            jax.ShapeDtypeStruct((2 * rank, ext), bf16),
-            jax.ShapeDtypeStruct((2 * rank, length), bf16),
+            jax.ShapeDtypeStruct((rank, ext), bf16),
+            jax.ShapeDtypeStruct((rank, length), bf16),
             jax.ShapeDtypeStruct((width, ext), bf16),
             jax.ShapeDtypeStruct((width, length), bf16),
-            jax.ShapeDtypeStruct((8, 128), f32),
         ],
         scratch_shapes=[pltpu.VMEM((HALO, width), bf16)],
         compiler_params=compiler_params(0),
@@ -156,7 +170,7 @@
         [joined(refs[p * per : (p + 1) * per], order) for p, order in enumerate(picks)], axis=0
     )
     w_o[...] = w
-    maps_pre = conv_values(dot(w, nt[...]), taps[...])
+    maps_pre = conv_values(dot(w, nt[...]), tall(taps[...]))
     pre_o[...] = maps_pre
     maps = (maps_pre * sigmoid(maps_pre)).astype(bf16)
     bt, ct = maps[:state_w], maps[state_w:]
@@ -198,17 +212,21 @@
     )(*ops, nt, taps, *later)
 
 
-def steps_kernel(n_w, order, hb, sub, *refs):
-    nt, bias, speed = refs[n_w : n_w + 3]
-    hp_o, sig_o, w_o = refs[-3:]
+def steps_kernel(n_w, order, hb, sub, lo, hi, hs, *refs):
+    nt, numbers = refs[n_w : n_w + 2]
+    hp_o, sig_o, speed_o, w_o = refs[-4:]
     length = sig_o.shape[1]
     heads = sig_o.shape[0]
     w = joined(refs[:n_w], order)
     w_o[...] = w
-    steps = dot(w, nt[:, HALO:]) + bias[...]
+    cols = [columns(numbers.at[j])[:hs] for j in range(lo, hi)]
+    bias = jnp.concatenate([v[:, 6:7] for v in cols], axis=0)
+    speed = jnp.exp(jnp.concatenate([v[:, 7:8] for v in cols], axis=0))
+    speed_o[...] = jnp.broadcast_to(speed, (heads, 128))
+    steps = dot(w, nt[:, HALO:]) + bias
     sig_o[...] = sigmoid(steps)
     delta = jnp.maximum(steps, 0.0) + jnp.log1p(jnp.exp(-jnp.abs(steps)))
-    rates = -delta * speed[...]
+    rates = -delta * speed
     row = lax.broadcasted_iota(jnp.int32, (sub, sub), 0)
     col = lax.broadcasted_iota(jnp.int32, (sub, sub), 1)
     upto = jnp.where(row <= col, 1.0, 0.0)
@@ -231,74 +249,90 @@
             hp_o[b, 2 * hb :, cols] = delta[mine, cols]
 
 
-def steps_call(arrays, first, order, nt, bias, speed, length, later):
-    heads = bias.shape[0]
+def steps_call(arrays, first, order, nt, pk, lo, hi, hs, length, later):
+    heads = (hi - lo) * hs
     hb = CB // HEAD
     ops, specs = row_specs([arrays], first, heads)
     vm = pl.BlockSpec(memory_space=pltpu.VMEM)
     return pl.pallas_call(
-        functools.partial(steps_kernel, len(ops), order, hb, SUB),
+        functools.partial(steps_kernel, len(ops), order, hb, SUB, lo, hi, hs),
         grid=(1,),
-        in_specs=specs + [vm] * 3 + [pl.BlockSpec(memory_space=pl.ANY)] * len(later),
-        out_specs=[vm] * 3,
+        in_specs=specs
+        + [vm, pl.BlockSpec((pk.shape[0], 16, CB), lambda i: (0, 3, 0))]
+        + [pl.BlockSpec(memory_space=pl.ANY)] * len(later),
+        out_specs=[vm] * 4,
         out_shape=[
             jax.ShapeDtypeStruct((heads // hb, 3 * hb, length), f32),
             jax.ShapeDtypeStruct((heads, length), f32),
+            jax.ShapeDtypeStruct((heads, 128), f32),
             jax.ShapeDtypeStruct((heads, nt.shape[0]), bf16),
         ],
         compiler_params=compiler_params(1),
         cost_estimate=cost(nt.shape[0] * nt.shape[1] * 128, nt.size * 2),
         name="steps",
-    )(*ops, nt, bias, speed, *later)
-
-
-def hop_kernel(hb, ncb, got, own, hp, *rest):
+    )(*ops, nt, pk, *later)
+
+
+def hop_kernel(hb, got, own, hp, *rest):
     out = rest[-1]
     length = hp.shape[2]
-    for c in range(ncb):
+    for c in range(hp.shape[0]):
         rows = slice(c * CB, (c + 1) * CB)
         total = jnp.exp2(hp[c, hb : 2 * hb, length - 1 : length])
         out[rows, :] = (per_head(got[rows, :].astype(f32), total) + own[rows, :]).astype(bf16)
 
 
-def hop_call(got, shift, own, hp, later=()):
-    slots, ch, state_w = own.shape
-    ncb = ch // CB
+def hop_call(got, shift, own, hp, part=0, later=()):
+    slots, rows, state_w = got.shape
+    parts = own.shape[1] // rows
     return pl.pallas_call(
-        functools.partial(hop_kernel, CB // HEAD, ncb),
+        functools.partial(hop_kernel, CB // HEAD),
         grid=(slots,),
         in_specs=[
-            pl.BlockSpec((None, ch, state_w), lambda s: ((s + shift) % slots, 0, 0)),
-            pl.BlockSpec((None, ch, state_w), lambda s: (s, 0, 0)),
-            pl.BlockSpec((ncb,) + hp.shape[1:], lambda s: (s, 0, 0)),
+            pl.BlockSpec((None, rows, state_w), lambda s: ((s + shift) % slots, 0, 0)),
+            pl.BlockSpec((None, rows, state_w), lambda s: (s, part, 0)),
+            pl.BlockSpec((rows // CB,) + hp.shape[1:], lambda s: (s * parts + part, 0, 0)),
         ]
         + [pl.BlockSpec(memory_space=pl.ANY)] * len(later),
-        out_specs=pl.BlockSpec((None, ch, state_w), lambda s: (s, 0, 0)),
-        out_shape=jax.ShapeDtypeStruct((slots, ch, state_w), bf16),
+        out_specs=pl.BlockSpec((None, rows, state_w), lambda s: (s, 0, 0)),
+        out_shape=jax.ShapeDtypeStruct((slots, rows, state_w), bf16),
         compiler_params=compiler_params(1),
-        cost_estimate=cost(own.size * 4, own.size * 8),
+        cost_estimate=cost(got.size * 4, got.size * 8),
         name="hop",
     )(got, own, hp, *later)
 
 
-def hold_kernel(*refs):
-    refs[-1][...] = jnp.zeros_like(refs[-1])
-
-
-def hold(deps, passed=()):
+def hold_kernel(n_joined, *refs):
+    parts = refs[:n_joined]
+    outs = refs[-1 - n_joined :]
+    for part, out in zip(parts, outs):
+        out[...] = part[...]
+    outs[-1][...] = jnp.zeros((1, 1), bf16)
+
+
+def hold(deps, passed=(), joined_to=(), parts=()):
     anywhere = pl.BlockSpec(memory_space=pl.ANY)
-    deps, passed = list(deps), list(passed)
+    deps, passed, joined_to, parts = list(deps), list(passed), list(joined_to), list(parts)
+    kept = passed + joined_to
+    whole = lambda a: pl.BlockSpec(a.shape, lambda i: (0, 0))
+    second = lambda a: pl.BlockSpec((None,) + a.shape[1:], lambda i: (1, 0, 0))
+    first = len(parts) + len(deps)
     out = pl.pallas_call(
-        hold_kernel,
-        in_specs=[anywhere] * (len(deps) + len(passed)),
-        out_specs=[anywhere] * len(passed) + [pl.BlockSpec(memory_space=pltpu.VMEM)],
-        out_shape=[jax.ShapeDtypeStruct(v.shape, v.dtype) for v in passed]
-        + [jax.ShapeDtypeStruct((8, 128), f32)],
-        input_output_aliases={len(deps) + k: k for k in range(len(passed))},
+        functools.partial(hold_kernel, len(parts)),
+        grid=(1,),
+        in_specs=[whole(a) for a in parts] + [anywhere] * (len(deps) + len(kept)),
+        out_specs=[anywhere] * len(passed)
+        + [second(a) for a in joined_to]
+        + [pl.BlockSpec((1, 1), lambda i: (0, 0))],
+        out_shape=[jax.ShapeDtypeStruct(v.shape, v.dtype) for v in kept]
+        + [jax.ShapeDtypeStruct((1, 1), bf16)],
+        input_output_aliases={first + k: k for k in range(len(kept))},
+        compiler_params=compiler_params(1),
         cost_estimate=cost(8, 8),
         name="hold",
-    )(*deps, *passed)
-    return out[-1][0, 0].astype(bf16), out[-1], list(out[:-1])
+    )(*parts, *deps, *kept)
+    n = len(passed)
+    return out[-1], list(out[:n]), list(out[n:-1])
 
 
 def path_dots(out, refs, picks, right, step, blocks):
@@ -311,16 +345,15 @@
             out[...] = dot(joined(mine, order), right)
 
 
-def scan_kernel(nx, picks, ncb, hb, sub, *refs):
+def scan_kernel(nx, order, hb, sub, *refs):
     xrefs = refs[:nx]
-    (nt, low, upx, chan_r, hp_r, ct, bn, cbt) = refs[nx : nx + 8]
-    xc_out, mix_out, ent_out, st_out, sent_out, tok_out, raw_sc = refs[-7:]
+    (nt, low, upx, num_r, hp_r, ct, bn, cbt) = refs[nx : nx + 8]
+    xc_out, mix_out, ent_out, st_out, sent_out, tok_out = refs[-6:]
     tok_out[...] = jnp.zeros_like(tok_out)
-    chan = chan_r[...]
+    chan = columns(num_r)
     hp = hp_r[...]
     length = ct.shape[1]
-    path_dots(raw_sc, xrefs, picks, nt[...], pl.program_id(1), ncb)
-    xr = raw_sc[...] + dot(upx[...], low[...])
+    xr = dot(joined(xrefs, order), nt[...]) + dot(upx[...], low[...], TN)
     xc = conv_values(xr, chan)
     xc_out[...] = xc.astype(bf16)
     x = xc * sigmoid(xc)
@@ -374,81 +407,91 @@
     return ops, specs
 
 
-def scan_call(lo, hi, xw, picks, nt, low, upx, chan, hp, ct, bn, cbt, bufs, later=()):
-    slots, ch = upx.shape[0], upx.shape[1]
+def scan_call(lo, hi, xw, part, picks, nt, low, pk, ch, hp, ct, bn, cbt, bufs, later=()):
+    slots = pk.shape[0]
     length = ct.shape[1]
-    ext = low.shape[1]
     hb = CB // HEAD
+    paths, base = xw
     ncb = ch // CB
+    per = ncb // len(paths)
+    off = part * per
     nsub = length // SUB
-    full, per_chan, per_blk = range_specs(lo, ncb)
-    ops, specs = weight_specs(xw, ncb)
+    full = lambda a: pl.BlockSpec(a.shape, lambda s, c: (0,) * a.ndim)
+    per_chan = lambda w: pl.BlockSpec((None, CB, w), lambda s, c: (s + lo, c + off, 0))
+    ops = list(paths[part])
+    specs = [
+        pl.BlockSpec((a.shape[0], CB, a.shape[2]), lambda s, c: (0, (s + base) * per + c, 0))
+        for a in ops
+    ]
     nx = len(ops)
-    ops += [nt, low, upx, chan, hp, ct, bn, cbt]
-    specs += [full(nt), full(low), per_chan(upx), per_chan(chan)]
-    specs += [per_blk(hp), full(ct), full(bn), full(cbt)]
+    ops += [nt, low, pk, pk, hp, ct, bn, cbt]
+    here = lambda s, c: (s + lo, c + off)
+    specs += [full(nt), full(low), packed_spec(1, here), packed_spec(3, here)]
+    specs += [
+        pl.BlockSpec((None,) + hp.shape[1:], lambda s, c: ((s + lo) * ncb + c + off, 0, 0)),
+        full(ct), full(bn), full(cbt),
+    ]
     inner_states = max(nsub - 1, 1)
     shapes = [
         jax.ShapeDtypeStruct((slots, ch, length), bf16),
         jax.ShapeDtypeStruct((slots, ch, length), f32),
         jax.ShapeDtypeStruct((slots, inner_states, ch, 128), f32),
         jax.ShapeDtypeStruct((slots, ch, 128), f32),
-        jax.ShapeDtypeStruct((slots, ch, 128), bf16),
-        jax.ShapeDtypeStruct((8, 128), f32),
+        jax.ShapeDtypeStruct((slots, per * CB, 128), bf16),
+        jax.ShapeDtypeStruct((1, 1), bf16),
     ]
-    chan_out = lambda w: pl.BlockSpec((None, CB, w), lambda s, c: (s + lo, c, 0))
     outs = [
-        chan_out(length),
-        chan_out(length),
-        pl.BlockSpec((None, inner_states, CB, 128), lambda s, c: (s + lo, 0, c, 0)),
-        chan_out(128),
-        chan_out(128),
-        pl.BlockSpec((8, 128), lambda s, c: (0, 0)),
+        per_chan(length),
+        per_chan(length),
+        pl.BlockSpec((None, inner_states, CB, 128), lambda s, c: (s + lo, 0, c + off, 0)),
+        per_chan(128),
+        pl.BlockSpec((None, CB, 128), lambda s, c: (s + lo, c, 0)),
+        pl.BlockSpec((1, 1), lambda s, c: (0, 0)),
     ]
-    aliases = {}
-    if bufs is not None:
-        aliases = {len(ops) + k: k for k in range(5)}
-        ops += list(bufs)
-        specs += [pl.BlockSpec(memory_space=pl.ANY)] * 5
-    ops += list(later)
-    specs += [pl.BlockSpec(memory_space=pl.ANY)] * len(later)
+    aliases = {len(ops) + k: k for k in range(5) if bufs[k] is not None}
+    given = [v for v in bufs if v is not None]
+    aliases = {len(ops) + i: k for i, k in enumerate(k for k in range(5) if bufs[k] is not None)}
+    ops += given + list(later)
+    specs += [pl.BlockSpec(memory_space=pl.ANY)] * (len(given) + len(later))
     n = hi - lo
     out = pl.pallas_call(
-        functools.partial(scan_kernel, nx, picks, ncb, hb, SUB),
-        grid=(n, ncb),
+        functools.partial(scan_kernel, nx, picks[part], hb, SUB),
+        grid=(n, per),
         in_specs=specs,
         out_specs=outs,
         out_shape=shapes,
-        scratch_shapes=[pltpu.VMEM((CB, ext), f32)],
         input_output_aliases=aliases,
         compiler_params=compiler_params(2),
-        cost_estimate=cost(4 * n * ch * 2048 * ext, n * ch * (4096 + length * 8)),
+        cost_estimate=cost(
+            4 * n * per * CB * 2048 * length, n * per * CB * (4096 + length * 8)
+        ),
         name="scan_slots",
     )(*ops)
-    return out[:5], out[5]
+    return list(out[:5]), out[5]
 
 
 def proj_kernel(n, picks, ncb, cut, gain, *refs):
     (right, low, up) = refs[n : n + 3]
-    chan_r = refs[n + 3]
+    num_r = refs[n + 3]
     out, tok_o, sc = refs[-3:]
     tok_o[...] = jnp.zeros_like(tok_o)
     path_dots(sc, refs[:n], picks, right[:, cut:], pl.program_id(1), ncb)
-    value = sc[...] + dot(up[...], low[:, cut:])
+    value = sc[...] + dot(up[...], low[:, cut:], TN)
     if gain:
-        value = value * chan_r[:, 5:6]
+        value = value * columns(num_r)[:, 5:6]
     out[...] = value.astype(bf16)
 
 
-def proj_call(lo, hi, weight, picks, right, low, up, chan, cut, gain, buf, later=()):
-    slots, ch = up.shape[0], up.shape[1]
+def proj_call(lo, hi, weight, picks, right, low, pk, ch, cut, gain, buf, later=()):
+    slots = pk.shape[0]
     length = right.shape[1] - cut
     ncb = ch // CB
     full, per_chan, _ = range_specs(lo, ncb)
     ops, specs = weight_specs(weight, ncb)
     n_w = len(ops)
-    ops += [right, low, up, chan]
-    specs += [full(right), full(low), per_chan(up), per_chan(chan)]
+    ops += [right, low, pk, pk]
+    here = lambda s, c: (s + lo, c)
+    specs += [full(right), full(low), packed_spec(2 if gain else 0, here), packed_spec(3, here)]
     aliases = {}
     if buf is not None:
         aliases = {len(ops): 0}
@@ -463,11 +506,11 @@
         in_specs=specs,
         out_specs=[
             pl.BlockSpec((None, CB, length), lambda s, c: (s + lo, c, 0)),
-            pl.BlockSpec((8, 128), lambda s, c: (0, 0)),
+            pl.BlockSpec((1, 1), lambda s, c: (0, 0)),
         ],
         out_shape=[
             jax.ShapeDtypeStruct((slots, ch, length), bf16),
-            jax.ShapeDtypeStruct((8, 128), f32),
+            jax.ShapeDtypeStruct((1, 1), bf16),
         ],
         scratch_shapes=[pltpu.VMEM((CB, length), f32)],
         input_output_aliases=aliases,
@@ -478,7 +521,7 @@
 
 
 def gate_kernel(hb, inner, *refs):
-    (z_r, mix_r, wgt_r, ent_r, chan_r, hp_r, ct, cn) = refs[:8]
+    (z_r, mix_r, wgt_r, ent_r, num_r, hp_r, ct, cn) = refs[:8]
     nout_o, dmix_o, dz_o, sl_o, sent_o = refs[8:13]
     mix_sc, sq_sc, dot_sc = refs[13:]
     phase = pl.program_id(0)
@@ -509,7 +552,7 @@
         coef = r * r * r * (jnp.sum(dot_sc[...], axis=0, keepdims=True) * (1.0 / inner))
         mix = mix_sc[blk]
         gated = mix * silu
-        nout_o[...] = (gated * (r * chan_r[:, 5:6])).astype(bf16)
+        nout_o[...] = (gated * (r * columns(num_r)[:, 5:6])).astype(bf16)
         d_gated = r * weighted - gated * coef
         d_mix = d_gated * silu
         dmix_o[...] = d_mix.astype(bf16)
@@ -519,7 +562,7 @@
         sent_o[...] = adj.astype(bf16)
 
 
-def gate_call(z, mix, wgt, ent, chan, hp, ct, cn, inner):
+def gate_call(z, mix, wgt, ent, pk, hp, ct, cn, inner):
     slots, ch, length = mix.shape
     ncb = ch // CB
     hb = CB // HEAD
@@ -532,13 +575,20 @@
         0,
     )
     first = lambda a, k: pl.BlockSpec((None, CB, a.shape[2]), lambda p, s, c: held(p, s, c, k))
+    per = ncb // ent.shape[0]
+
+    def entered(p, s, c):
+        slot, block, _ = held(p, s, c, 1)
+        return (block // per, slot, block % per, 0)
+
     later = lambda w: pl.BlockSpec(
         (None, CB, w), lambda p, s, c: (jnp.where(p == 1, s, 0), jnp.where(p == 1, c, 0), 0)
     )
     return pl.pallas_call(
         functools.partial(gate_kernel, hb, inner),
         grid=(2, slots, ncb),
-        in_specs=[per_chan(z), first(mix, 0), per_chan(wgt), first(ent, 1), per_chan(chan)]
+        in_specs=[per_chan(z), first(mix, 0), per_chan(wgt)]
+        + [pl.BlockSpec((None, None, CB, 128), entered), packed_spec(3, lambda p, s, c: (s, c))]
         + [per_blk(hp), full(ct), full(cn)],
         out_specs=[later(length), later(length), later(length), later(128), later(128)],
         out_shape=[
@@ -556,7 +606,7 @@
         compiler_params=compiler_params(3),
         cost_estimate=cost(slots * ch * length * 600, slots * ch * length * 22),
         name="gate",
-    )(z, mix, wgt, ent, chan, hp, ct, cn)
+    )(z, mix, wgt, ent, pk, hp, ct, cn)
 
 
 def grid_specs(ncb):
@@ -648,7 +698,10 @@
     loc_spec = pl.BlockSpec((None, loc.shape[1], CB, 128), lambda s, c: (s + lo, 0, c, 0))
     blocks = slots * ncb
     ops = [dy, xc, hp, ent, loc, ct, cn, bt, cbt]
-    entered = pl.BlockSpec((None, CB, 128), lambda s, c: ((s + lo + 1) % slots, c, 0))
+    per = ncb // ent.shape[0]
+    entered = pl.BlockSpec(
+        (None, None, CB, 128), lambda s, c: (c // per, (s + lo + 1) % slots, c % per, 0)
+    )
     specs = [per_chan(dy), per_chan(xc), per_blk(hp), entered, loc_spec]
     specs += [full(ct), full(cn), full(bt), full(cbt)]
     aliases = {}
@@ -688,10 +741,10 @@
 
 
 def finish_kernel(hb, *refs):
-    (dxs_r, dy_r, xc_r, dz_r, chan_r, hp_r, ent_r, adj_r, bt, upz, upx, low) = refs[:12]
-    dx_o, tail_o, head_o, gz_o, gx_o, dl_o, dd_o, u2_o, kf_o, db_o = refs[-10:]
+    (dxs_r, dy_r, xc_r, dz_r, num_r, hp_r, ent_r, adj_r, bt, upz, upx, low) = refs[:12]
+    dx_o, tail_o, head_o, gx_o, dl_o, dd_o, u2_o, kf_o, db_o = refs[-9:]
     blk = pl.program_id(0) * pl.num_programs(1) + pl.program_id(1)
-    chan = chan_r[...]
+    chan = columns(num_r)
     hp = hp_r[...]
     length = bt.shape[1]
 
@@ -718,45 +771,50 @@
     dx = per_head(dxs, delta) + dy_r[...].astype(f32) * chan[:, 4:5]
     dconv = dx * (sig + x * (1.0 - sig))
     head_o[...] = jnp.transpose(dconv[:, :HALO])[:8]
-    ext = jnp.concatenate([dconv, jnp.zeros((CB, HALO), f32)], axis=1)
+    none = jnp.zeros((CB, HALO), f32)
+    ext = jnp.concatenate([none, dconv, none], axis=1)
     width = ext.shape[1]
     out = ext * chan[:, 3:4]
     for k in range(3):
         out = out + pltpu.roll(ext, width - (3 - k), 1) * chan[:, k : k + 1]
-    out = out[:, :length]
-    tail_o[...] = out[:, length - HALO :]
-    dx_low = out.astype(bf16)
-    dx_o[...] = dx_low
-    dz = dz_r[...]
-    gz_o[...] = dot(low[...], dz, NT)
-    gx_o[...] = dot(low[...], dx_low, NT)
-    dl_o[...] += dot(upz[...], dz, TN) + dot(upx[...], dx_low, TN)
-
-
-def finish_call(dxs, dy, xc, dz, chan, hp, ent, adj, bt, upz, upx, low, later):
+    out = out[:, : HALO + length]
+    tail_o[...] = out[:, length:]
+    all_low = out.astype(bf16)
+    dx_o[...] = all_low[:, HALO:]
+    gx_o[...] = dot(low[...], all_low, NT)
+    dl_o[...] += dot(upx[...], all_low)
+    dl_o[:, HALO:] += dot(upz[...], dz_r[...])
+
+
+def finish_call(dxs, dy, xc, dz, pk, hp, ent, adj, bt, low, later):
     slots, ch, length = dy.shape
     ncb = ch // CB
     hb = CB // HEAD
-    rank2 = low.shape[0]
+    rank = low.shape[0]
     full, per_chan, per_blk = grid_specs(ncb)
     blk_out = lambda w: pl.BlockSpec((None, hb, w), lambda s, c: (s * ncb + c, 0, 0))
     chan_out = lambda w: pl.BlockSpec((None, CB, w), lambda s, c: (s, c, 0))
     turned = lambda w: pl.BlockSpec((None, w, CB), lambda s, c: (s, 0, c))
     moved = lambda k: pl.BlockSpec((None, CB, 128), lambda s, c: ((s + k) % slots, c, 0))
+    per = ncb // ent.shape[0]
+    entered = pl.BlockSpec(
+        (None, None, CB, 128), lambda s, c: (c // per, (s + 1) % slots, c % per, 0)
+    )
+    here = lambda s, c: (s, c)
     blocks = slots * ncb
     return pl.pallas_call(
         functools.partial(finish_kernel, hb),
         grid=(slots, ncb),
-        in_specs=[per_chan(dxs), per_chan(dy), per_chan(xc), per_chan(dz), per_chan(chan)]
-        + [per_blk(hp), moved(1), moved(slots - 1), full(bt), per_chan(upz), per_chan(upx)]
-        + [full(low)] + [pl.BlockSpec(memory_space=pl.ANY)] * len(later),
+        in_specs=[per_chan(dxs), per_chan(dy), per_chan(xc), per_chan(dz), packed_spec(3, here)]
+        + [per_blk(hp), entered, moved(slots - 1), full(bt)]
+        + [packed_spec(0, here), packed_spec(1, here), full(low)]
+        + [pl.BlockSpec(memory_space=pl.ANY)] * len(later),
         out_specs=[
             chan_out(length),
             chan_out(HALO),
             turned(8),
-            turned(rank2),
-            turned(rank2),
-            pl.BlockSpec((rank2, length), lambda s, c: (0, 0)),
+            turned(rank),
+            pl.BlockSpec((rank, HALO + length), lambda s, c: (0, 0)),
             blk_out(length),
             blk_out(length),
             blk_out(128),
@@ -766,9 +824,8 @@
             jax.ShapeDtypeStruct((slots, ch, length), bf16),
             jax.ShapeDtypeStruct((slots, ch, HALO), f32),
             jax.ShapeDtypeStruct((slots, 8, ch), f32),
-            jax.ShapeDtypeStruct((slots, rank2, ch), f32),
-            jax.ShapeDtypeStruct((slots, rank2, ch), f32),
-            jax.ShapeDtypeStruct((rank2, length), f32),
+            jax.ShapeDtypeStruct((slots, rank, ch), f32),
+            jax.ShapeDtypeStruct((rank, HALO + length), f32),
             jax.ShapeDtypeStruct((blocks, hb, length), f32),
             jax.ShapeDtypeStruct((blocks, hb, length), f32),
             jax.ShapeDtypeStruct((blocks, hb, 128), f32),
@@ -777,13 +834,18 @@
         compiler_params=compiler_params(2),
         cost_estimate=cost(slots * ch * length * 700, slots * ch * length * 14),
         name="finish_back",
-    )(dxs, dy, xc, dz, chan, hp, ent, adj, bt, upz, upx, low, *later)
-
-
-def glue_kernel(hb, sub, *refs):
+    )(dxs, dy, xc, dz, pk, hp, ent, adj, bt, pk, pk, low, *later)
+
+
+def glue_kernel(flat_order, quick, sub, *refs):
     (dcb_r, db1, db2, dc1, bt, ct, pre_r, u1, u2, kl, dd, u2f, kf) = refs[:13]
-    (sig_r, speed, taps) = refs[13:16]
-    left_o, tail_o, head_o = refs[16:]
+    (sig_r, speed, taps_r, sc, dl, nt) = refs[13:19]
+    left_o, tail_o, head_o, gd_o = refs[19:]
+    taps = tall(taps_r[...])
+    low = dl[...].astype(bf16)
+    for i, m in enumerate(flat_order):
+        at = pl.ds(block_at(sc[0], m, quick), CB)
+        gd_o[:, at] = dot(low, nt[i * CB : (i + 1) * CB, :], NT)
     state_w, length = bt.shape
     nsub = length // sub
     blocks = u1.shape[0]
@@ -835,24 +897,25 @@
         ends = jnp.sum(piece, axis=1, keepdims=True)
         run = ends if run is None else run + ends
     rate = rate + jnp.concatenate(parts, axis=1)
-    left_o[2 * state_w :, :] = ((flat(dd) - speed[...] * rate) * sig_r[...]).astype(bf16)
-
-
-def glue_call(args, state_w, length, heads):
+    left_o[2 * state_w :, :] = ((flat(dd) - speed[:, :1] * rate) * sig_r[...]).astype(bf16)
+
+
+def glue_call(args, sc, dl, nt, state_w, length, heads, flat, quick):
     vm = pl.BlockSpec(memory_space=pltpu.VMEM)
     return pl.pallas_call(
-        functools.partial(glue_kernel, CB // HEAD, SUB),
-        in_specs=[vm] * len(args),
-        out_specs=[vm] * 3,
+        functools.partial(glue_kernel, flat, quick, SUB),
+        in_specs=[vm] * len(args) + [pl.BlockSpec(memory_space=pltpu.SMEM), vm, vm],
+        out_specs=[vm] * 4,
         out_shape=[
             jax.ShapeDtypeStruct((2 * state_w + heads, length), bf16),
             jax.ShapeDtypeStruct((2 * state_w, HALO), f32),
             jax.ShapeDtypeStruct((8, 2 * state_w), f32),
+            jax.ShapeDtypeStruct((dl.shape[0], nt.shape[0]), f32),
         ],
         compiler_params=compiler_params(0),
         cost_estimate=cost(1e8, 4e6),
         name="glue",
-    )(*args)
+    )(*args, sc, dl, nt)
 
 
 def add_products(acc, turned, sets, picks, n_left, refs, slot, c):
@@ -902,8 +965,10 @@
         hid[...] = jnp.zeros_like(hid)
 
     values = nout[...]
-    gdo_o[...] = dot(bh[:rank, :], values, NT)
-    hid[...] += dot(dn[:, :rank], values, TN)
+    gdo_o[...] = dot(bh[...], values, NT)
+    for part in range(dn.shape[0] // 64):
+        mine = slice(part * CB, (part + 1) * CB)
+        hid[...] += dot(dn[part * 64 + 32 : part * 64 + 48, :], values[mine])
     add_products(acc, jnp.transpose(values), sets, picks, 1, wrefs, slot, c)
 
     @pl.when((slot == pl.num_programs(0) - 1) & (c == pl.num_programs(1) - 1))
@@ -918,7 +983,7 @@
             mixed_o[:, at] = jnp.where(rows, total, 0.0).astype(bf16)
 
 
-def output_call(sc, nout, dn, bh, up, tok, masked, weights, picks, flat, quick):
+def output_call(sc, nout, pk, bh, up, tok, masked, weights, picks, flat, quick):
     slots, ch, length = nout.shape
     rank, width = up.shape
     paths = len(picks)
@@ -929,7 +994,8 @@
     return pl.pallas_call(
         functools.partial(output_kernel, sets, picks, flat, quick, len(w_ops)),
         grid=(slots, paths),
-        in_specs=[pl.BlockSpec(memory_space=pltpu.SMEM), chan(nout), chan(dn), full(bh)]
+        in_specs=[pl.BlockSpec(memory_space=pltpu.SMEM), chan(nout)]
+        + [pl.BlockSpec((None, block // 4, CB), lambda s, c: (s, c, 0)), full(bh)]
         + [full(up), full(tok), full(masked)] + w_specs,
         out_specs=[
             pl.BlockSpec((length, width), lambda s, c: (0, 0)),
@@ -945,53 +1011,83 @@
         compiler_params=compiler_params(2),
         cost_estimate=cost(2 * slots * ch * length * width, slots * ch * width * 2),
         name="output",
-    )(sc, nout, dn, bh, up, tok, masked, *w_ops)
+    )(sc, nout, pk, bh, up, tok, masked, *w_ops)
 
 
 def gate_back_kernel(sets, picks, n_w, *refs):
-    dz = refs[0]
-    acc = refs[-1]
+    dz, low = refs[:2]
+    acc, gz_o = refs[-2:]
     slot, c = pl.program_id(0), pl.program_id(1)
 
     @pl.when((slot == 0) & (c == 0))
     def _():
         acc[...] = jnp.zeros_like(acc)
 
-    add_products(acc, jnp.transpose(dz[...]), sets, picks, 1, refs[1 : 1 + n_w], slot, c)
-
-
-def gate_back_call(dz, weights, picks, width, later=()):
+    gz_o[...] = dot(low[:, HALO:], dz[...], NT)
+    add_products(acc, jnp.transpose(dz[...]), sets, picks, 1, refs[2 : 2 + n_w], slot, c)
+
+
+def gate_back_call(dz, low, weights, picks, width, later=()):
     slots, ch, length = dz.shape
+    rank = low.shape[0]
     paths = len(picks)
     block = ch // paths
     w_ops, w_specs, sets = product_specs(weights, paths, block)
     return pl.pallas_call(
         functools.partial(gate_back_kernel, sets, picks, len(w_ops)),
         grid=(slots, paths),
-        in_specs=[pl.BlockSpec((None, block, length), lambda s, c: (s, c, 0))] + w_specs
+        in_specs=[
+            pl.BlockSpec((None, block, length), lambda s, c: (s, c, 0)),
+            pl.BlockSpec(low.shape, lambda s, c: (0, 0)),
+        ]
+        + w_specs
         + [pl.BlockSpec(memory_space=pl.ANY)] * len(later),
-        out_specs=pl.BlockSpec((length, width), lambda s, c: (0, 0)),
-        out_shape=jax.ShapeDtypeStruct((length, width), f32),
+        out_specs=[
+            pl.BlockSpec((length, width), lambda s, c: (0, 0)),
+            pl.BlockSpec((None, rank, block), lambda s, c: (s, 0, c)),
+        ],
+        out_shape=[
+            jax.ShapeDtypeStruct((length, width), f32),
+            jax.ShapeDtypeStruct((slots, rank, ch), f32),
+        ],
         compiler_params=compiler_params(2),
         cost_estimate=cost(2 * slots * ch * length * width, 2 * slots * ch * width),
         name="gate_back",
-    )(dz, *w_ops, *later)
+    )(dz, low, *w_ops, *later)
+
+
+def beyond(near, taps, rows):
+    parts = [jnp.zeros((HALO - 3, rows), f32)]
+    for i in range(3):
+        total = near[i : i + 1] * taps[0:1]
+        for k in range(1, i + 1):
+            total = total + near[i - k : i - k + 1] * taps[k : k + 1]
+        parts.append(total)
+    return jnp.transpose(jnp.concatenate(parts, axis=0))
 
 
 def input_kernel(sets, picks, flat, quick, n_w, n_small, *refs):
-    (sc, dx, tail, left, d_low, down, root_r, gain, tok, masked, start) = refs[:11]
-    smalls = refs[11 : 11 + n_small]
-    wrefs = refs[11 + n_small : 11 + n_small + n_w]
+    (sc, dx, tail, near, num, left, maps_tail, maps_near, maps_taps) = refs[:9]
+    (dl, near_dl, down, root_r, gain, tok, masked, start) = refs[9:17]
+    smalls = refs[17 : 17 + n_small]
+    wrefs = refs[17 + n_small : 17 + n_small + n_w]
     out, acc = refs[-2:]
     slot, c = pl.program_id(0), pl.program_id(1)
     length, width = tok.shape
+    cut = length - HALO
 
     @pl.when((slot == 0) & (c == 0))
     def _():
-        low = jnp.transpose(d_low[...])
-        total = start[...]
-        row = 0
-        for w in smalls:
+        d_low = jnp.concatenate(
+            [dl[:, HALO:length], dl[:, length:] + near_dl[:, :HALO]], axis=1
+        ).astype(bf16)
+        low = jnp.transpose(d_low)
+        n_maps = maps_tail.shape[0]
+        maps_last = maps_tail[...] + beyond(maps_near[:, :n_maps], maps_taps, n_maps)
+        maps_left = jnp.concatenate([left[:n_maps, :cut], maps_last.astype(bf16)], axis=1)
+        total = start[...] + dot(maps_left, smalls[0][...], TN)
+        row = n_maps
+        for w in smalls[1:]:
             total = total + dot(left[row : row + w.shape[0], :], w[...], TN)
             row += w.shape[0]
         acc[...] = total
@@ -999,7 +1095,17 @@
             at = pl.ds(block_at(sc[0], m, quick), CB)
             acc[:, i * CB : (i + 1) * CB] += dot(low, down[at, :], NT)
 
-    dx_all = jnp.concatenate([dx[:, : length - HALO], tail[...]], axis=1)
+    block = dx.shape[0]
+    taps = jnp.concatenate(
+        [
+            num[b * 64 + 48 : b * 64 + 56, :].astype(f32)
+            + num[b * 64 + 56 : b * 64 + 64, :].astype(f32)
+            for b in range(block // CB)
+        ],
+        axis=1,
+    )
+    last = tail[...] + beyond(near[...], taps, block)
+    dx_all = jnp.concatenate([dx[:, :cut], last.astype(bf16)], axis=1)
     add_products(acc, jnp.transpose(dx_all), sets, picks, 1, wrefs, slot, c)
 
     @pl.when((slot == pl.num_programs(0) - 1) & (c == pl.num_programs(1) - 1))
@@ -1021,30 +1127,84 @@
 
 
 def input_call(
-    sc, dx, tail, left, d_low, down, root, gain, tok, masked, start, smalls, weights, picks,
-    flat, quick,
+    sc, dx, tail, near, pk, left, maps_tail, maps_taps, dl, down, root, gain, tok, masked, start,
+    smalls, weights, picks, flat, quick, later=(),
 ):
     slots, ch, length = dx.shape
     width = tok.shape[1]
     paths = len(picks)
     block = ch // paths
+    rank = dl.shape[0]
     once = pl.Buffered(1)
     full = lambda a: pl.BlockSpec(a.shape, lambda s, c: (0,) * a.ndim, pipeline_mode=once)
     chan = lambda a: pl.BlockSpec((None, block, a.shape[2]), lambda s, c: (s, c, 0))
     w_ops, w_specs, sets = product_specs(weights, paths, block)
+    near_rows = pl.BlockSpec((8, block), lambda s, c: ((s + slots - 1) % slots, c))
+    near_maps = pl.BlockSpec((8, ch), lambda s, c: (slots, 0), pipeline_mode=once)
+    near_low = pl.BlockSpec(
+        (rank, ch), lambda s, c: (((slots + 1) * 8 + rank - 1) // rank, 0), pipeline_mode=once
+    )
     return pl.pallas_call(
         functools.partial(input_kernel, sets, picks, flat, quick, len(w_ops), len(smalls)),
         grid=(slots, paths),
-        in_specs=[pl.BlockSpec(memory_space=pltpu.SMEM), chan(dx), chan(tail)]
-        + [full(a) for a in [left, d_low, down, root, gain, tok, masked, start] + list(smalls)]
-        + w_specs,
+        in_specs=[pl.BlockSpec(memory_space=pltpu.SMEM), chan(dx), chan(tail), near_rows]
+        + [pl.BlockSpec((None, block // 4, CB), lambda s, c: (s, c, 0))]
+        + [full(left), full(maps_tail), near_maps, full(maps_taps), full(dl), near_low]
+        + [full(a) for a in [down, root, gain, tok, masked, start] + list(smalls)]
+        + w_specs
+        + [pl.BlockSpec(memory_space=pl.ANY)] * len(later),
         out_specs=pl.BlockSpec((length, width), lambda s, c: (0, 0)),
         out_shape=jax.ShapeDtypeStruct((length, width), bf16),
         scratch_shapes=[pltpu.VMEM((length, width), f32)],
         compiler_params=compiler_params(2),
         cost_estimate=cost(2 * slots * ch * length * width, 2 * slots * ch * width),
         name="input_back",
-    )(sc, dx, tail, left, d_low, down, root, gain, tok, masked, start, *smalls, *w_ops)
+    )(
+        sc, dx, tail, near, pk, left, maps_tail, near, maps_taps, dl, near, down, root, gain, tok,
+        masked, start, *smalls, *w_ops, *later
+    )
+
+
+def assemble_kernel(n, planes, ch, *refs):
+    parts = refs[:n]
+    down_o, up_o, down_out_o, up_out_o = refs[n:]
+    which = pl.program_id(0).astype(f32)
+    total = None
+    for ref in parts:
+        for b in range(ref.shape[0]):
+            chosen = jnp.where(ref[b, :, -1:].astype(f32) == which, 1.0, 0.0)
+            term = ref[b, :, :-128].astype(f32) * chosen
+            total = term if total is None else total + term
+    up_o[:, 0, :] = total[:, :ch]
+    up_o[:, 1, :] = total[:, ch : 2 * ch]
+    down_out_o[...] = total[:, 2 * ch : 3 * ch]
+    width = down_o.shape[1]
+    down_o[...] = total[:, 3 * ch : 3 * ch + width]
+    up_out_o[...] = total[:, 3 * ch + width :]
+
+
+def assemble_call(parts, adapters, planes, ch, width):
+    rank = parts[0].shape[1]
+    return pl.pallas_call(
+        functools.partial(assemble_kernel, len(parts), planes, ch),
+        grid=(adapters,),
+        in_specs=[pl.BlockSpec(a.shape, lambda i: (0, 0, 0)) for a in parts],
+        out_specs=[
+            pl.BlockSpec((None, rank, width), lambda i: (i, 0, 0)),
+            pl.BlockSpec((None, rank, 2, ch), lambda i: (i, 0, 0, 0)),
+            pl.BlockSpec((None, rank, ch), lambda i: (i, 0, 0)),
+            pl.BlockSpec((None, rank, width), lambda i: (i, 0, 0)),
+        ],
+        out_shape=[
+            jax.ShapeDtypeStruct((adapters, rank, width), f32),
+            jax.ShapeDtypeStruct((adapters, rank, 2, ch), f32),
+            jax.ShapeDtypeStruct((adapters, rank, ch), f32),
+            jax.ShapeDtypeStruct((adapters, rank, width), f32),
+        ],
+        compiler_params=compiler_params(1),
+        cost_estimate=cost(1e7, 2e7),
+        name="assemble",
+    )(*parts)
 
 
 def body(
@@ -1094,22 +1254,21 @@
     def flip(v, bit):
         return lax.ppermute(v, "dp", [(i, i ^ bit) for i in range(seqs)])
 
-    def slot_order(v, first=0):
-        return jnp.stack(
-            [
-                lax.dynamic_index_in_dim(v, (place + j) % planes, 0, keepdims=False)
-                for j in range(first, planes)
-            ]
-        )
+    def slot_order(v, first=0, at=place):
+        return [
+            lax.dynamic_index_in_dim(v, (at + j) % planes, 0, keepdims=False)
+            for j in range(first, planes)
+        ]
 
     def by_slot(v):
-        return slot_order(lax.all_gather(v, "tensor", axis=0))
-
-    def to_slots(v):
-        total = v[0]
+        return jnp.stack(slot_order(lax.all_gather(v, "tensor", axis=0)))
+
+    def to_slots(rows, whole):
+        total = jnp.concatenate([rows[0], whole], axis=1)
         for j in range(1, planes):
+            part = jnp.concatenate([rows[j], whole], axis=1).astype(bf16)
             total = total + lax.ppermute(
-                v[j].astype(bf16), "tensor", [(s, (s + j) % planes) for s in range(planes)]
+                part, "tensor", [(s, (s + j) % planes) for s in range(planes)]
             ).astype(f32)
         return total
 
@@ -1133,8 +1292,8 @@
     def pass_one(ab):
         return [flip(ab[0], 2), flip(ab[1], 4)]
 
-    def with_first(ab, got, token):
-        return [jnp.stack([v, w]) + token for v, w in zip(ab, got)]
+    def room(ab):
+        return [jnp.stack([v, jnp.zeros_like(v)]) for v in ab]
 
     def pass_two(ab):
         return [flip(ab[0], 4), flip(ab[1], 2)]
@@ -1150,8 +1309,6 @@
     up_here = lax.dynamic_index_in_dim(adapter_in_up, pick, 0, keepdims=False)
     down_here = lax.dynamic_index_in_dim(adapter_out_down, pick, 0, keepdims=False)
     up_out = lax.dynamic_index_in_dim(adapter_out_up, pick, 0, keepdims=False)
-    step_rows = rows_here * hs // ch
-    halo_rows = 16 * width // ch
     numbers = jnp.concatenate(
         [
             conv_inner,
@@ -1164,258 +1321,239 @@
     coarse = lax.optimization_barrier(numbers.astype(bf16))
     fine = lax.optimization_barrier((numbers - coarse.astype(f32)).astype(bf16))
     packed = jnp.concatenate(
-        [
-            jnp.transpose(up_here, (1, 0, 2)).reshape(2 * rank, ch),
-            down_here.T,
-            in_steps.T.reshape(step_rows, ch),
-            tokens[0, -16:].reshape(halo_rows, ch),
-            coarse,
-            fine,
-        ],
+        [jnp.transpose(up_here, (1, 0, 2)).reshape(2 * rank, ch), down_here.T, coarse, fine],
         axis=0,
     )
+    packed = jnp.swapaxes(packed.reshape(64, ncb, CB), 0, 1).reshape(64 * ncb, CB)
+    last_rows = tokens[0, -16:].reshape(16 * width // CB, CB)
     halo = [(s, s + 1) for s in range(planes - 1)]
     wt = jnp.transpose(in_inner, (1, 2, 0))
     maps_w = in_maps.T
+    steps_w = in_steps.T
     own_rows = 3 * ch // 2
     if quick:
         own = halves(
             [wt[0], wt[1], out_weight],
-            ([maps_w[:state_w], in_steps.T], [maps_w[state_w:]]),
+            ([maps_w[:state_w], steps_w], [maps_w[state_w:]]),
         )
         got = pass_one(own)
-        packed = jnp.stack([packed] + [from_plane(packed, j) for j in range(1, planes)])
-        all_x = lax.all_gather(wt[1], "tensor", axis=0)
+        all_x = lax.all_gather(
+            jnp.concatenate([wt[1], packed, steps_w, last_rows], axis=0), "tensor", axis=0
+        )
         all_z = lax.all_gather(wt[0], "tensor", axis=0)
         all_o = lax.all_gather(out_weight, "tensor", axis=0)
-    else:
-        packed = by_slot(packed)
-    step_at, halo_at = 3 * rank, 3 * rank + step_rows
-    number_at = halo_at + halo_rows
-    before = packed[planes - 1, halo_at:number_at].reshape(16, width)
-    before = jnp.where(place > 0, before, jnp.zeros_like(before))
-    numbers = packed[:, number_at : number_at + 8].astype(f32) + packed[
-        :, number_at + 8 :
-    ].astype(f32)
-    steps_w = packed[:, step_at:halo_at].reshape(planes, hs, rows_here)
-    held = []
-    if quick:
-        token, held, _ = hold(got + [before])
-        own = with_first(own, got, token)
+        token, _, own = hold([], [], room(own), got)
         two = pass_two(own)
         swapped = pass_core(own)
-        far_x = halves(slot_order(all_x, 1), ([steps_w[1:].reshape(-1, rows_here)], ()))
-        held = [held]
-
-    up_z = jnp.swapaxes(packed[:, :rank], 1, 2)
-    up_x = jnp.swapaxes(packed[:, rank : 2 * rank], 1, 2)
-    down_out = jnp.swapaxes(packed[:, 2 * rank : 3 * rank], 1, 2)
-    taps = numbers[:, :4]
-    chan = jnp.swapaxes(jnp.pad(numbers[:, :6], ((0, 0), (0, 2), (0, 0))), 1, 2)
-    bias = numbers[:, 6, :hs].reshape(heads)
-    speed = jnp.exp(numbers[:, 7, :hs].reshape(heads))
-    up_z2 = jnp.concatenate([up_z, up_z], axis=2)
-    up_x2 = jnp.concatenate([up_x, up_x], axis=2)
-    down_out2 = jnp.concatenate([down_out, down_out], axis=2)
-
-    sc = jnp.stack([mine, lengths[0] - place * length]).astype(jnp.int32)
-    normed, masked, root, low2, back2, nt, gt, turned = turn_call(
-        sc, tokens[0], before, cotangent[0], pre_gain[None], down_in, up_out, flat, quick, held
-    )
-    map_taps = jnp.pad(conv_maps.T, ((0, 0), (0, 4)))
-    if quick:
-        token, held, passed = hold([turned] + swapped, two + far_x)
+        marks = [ch, ch + 64 * ncb, ch + 64 * ncb + hs]
+        all_x = slot_order(all_x)
+        pk = jnp.stack([v[marks[0] : marks[1]] for v in all_x])
+        last_rows = all_x[planes - 1][marks[2] :]
+        far_x = halves(
+            [v[:ch] for v in all_x[1:]], ([v[marks[1] : marks[2]] for v in all_x[1:]], ())
+        )
+        wide_x = room(far_x)
+        token, passed, _ = hold(wide_x + swapped + [pk, last_rows], two + far_x)
         two, far_x = passed[:2], passed[2:]
         own = own + two
         swapped = swapped + pass_core(two)
         got = pass_one(far_x)
+        held = [token]
+    else:
+        pk = by_slot(packed)
+        last_rows = by_slot(last_rows)[planes - 1]
+        steps_w = by_slot(steps_w)
+        held = []
+    before = last_rows.reshape(16, width)
+    before = jnp.where(place > 0, before, jnp.zeros_like(before))
+    sc = jnp.stack([mine, lengths[0] - place * length]).astype(jnp.int32)
+    normed, masked, root, low2, back2, nt, gt = turn_call(
+        sc, tokens[0], before, cotangent[0], pre_gain[None], down_in, up_out, flat, quick, held
+    )
+    if quick:
         own = as_paths(own, swapped)
-        token, held, _ = hold(got + own[0] + own[1])
-        held = [held]
+        token, _, far_x = hold([nt] + own[0] + own[1], [], wide_x, got)
+        two = pass_two(far_x)
+        swapped = pass_core(far_x)
+        held = [token]
         all_maps, all_steps = own, own[0]
         maps_at, maps_rows = own_rows, state_w
-        steps_at, mine_heads = own_rows + state_w, hs
+        steps_at, mine_slots = own_rows + state_w, 1
     else:
         all_maps = [[lax.all_gather(maps_w, "dp", axis=1, tiled=True)[None]]]
         all_steps = steps_w.reshape(heads, rows_here)
         all_steps = [lax.all_gather(all_steps, "dp", axis=1, tiled=True)[None]]
         maps_at, maps_rows = 0, 2 * state_w
-        steps_at, mine_heads = 0, heads
+        steps_at, mine_slots = 0, planes
     bt, ct, b_low, c_low, cbt, maps_pre, maps_w = maps_call(
-        all_maps, maps_at, maps_rows, picks, nt, map_taps, length, held
-    )
-    hp, step_sig, mine_w = steps_call(
-        all_steps, steps_at, picks[0], nt, bias[:mine_heads, None], speed[:mine_heads, None],
-        length, held,
+        all_maps, maps_at, maps_rows, picks, nt, conv_maps, length, held
+    )
+    hp, step_sig, speed, mine_w = steps_call(
+        all_steps, steps_at, picks[0], nt, pk, 0, mine_slots, hs, length, held
     )
     small_w = [maps_w, mine_w]
 
-    x_args = (picks, nt, low2, up_x2, chan)
-    z_args = (picks, nt, low2, up_z2, chan, HALO, False)
-    o_args = (picks, gt, back2, down_out2, chan, 0, True)
+    x_args = (picks, nt, low2, pk, ch)
+    z_args = (picks, nt, low2, pk, ch, HALO, False)
+    o_args = (picks, gt, back2, pk, ch, 0, True)
     if quick:
-        far_x = with_first(far_x, got, token)
-        two = pass_two(far_x)
-        swapped = pass_core(far_x)
-        far_z = halves(slot_order(all_z, 1))
-        bufs, done = scan_call(0, 1, (own, 1), *x_args, hp, ct, b_low, cbt, None, held)
-
-        token, held, passed = hold([done] + swapped, two + far_z)
+        empty = [None] * 4
+        bufs, _ = scan_call(
+            0, 1, (own, 1), 0, *x_args, hp, ct, b_low, cbt, empty + [None], held
+        )
+        sent_a = bufs[4]
+        bufs, done = scan_call(
+            0, 1, (own, 1), 1, *x_args, hp, ct, b_low, cbt, bufs[:4] + [None], held
+        )
+        sent_b = bufs[4]
+        far_z = halves(slot_order(all_z, 1, place + token[0, 0].astype(jnp.int32)))
+        wide_z = room(far_z)
+
+        token, passed, _ = hold([done] + wide_z + swapped, two + far_z)
         two, far_z = passed[:2], passed[2:]
         far_x = as_paths(far_x + two, swapped + pass_core(two))
         got = pass_one(far_z)
-        z, done = proj_call(0, 1, (own, 0), *z_args, None, [held])
-        wgt, beside = proj_call(0, 1, (own, 2), *o_args, None, [done])
-
-        token, held, _ = hold(got + far_x[0] + far_x[1] + [beside])
-        far_z = with_first(far_z, got, token)
+        far_o = halves(slot_order(all_o, 1, place + token[0, 0].astype(jnp.int32)))
+        wide_o = room(far_o)
+        z, beside = proj_call(0, 1, (own, 0), *z_args, None, [token])
+        wgt, beside = proj_call(0, 1, (own, 2), *o_args, None, [beside])
+
+        token, far_o, far_z = hold([beside] + far_x[0] + far_x[1] + wide_o, far_o, wide_z, got)
         two = pass_two(far_z)
         swapped = pass_core(far_z)
-        far_o = halves(slot_order(all_o, 1))
-        hp_far, sig_far, far_w = steps_call(
-            far_x[0], own_rows, picks[0], nt, bias[hs:, None], speed[hs:, None], length, [held]
+        hp_far, sig_far, speed_far, far_w = steps_call(
+            far_x[0], own_rows, picks[0], nt, pk, 1, planes, hs, length, [token]
         )
         hp = jnp.concatenate([hp, hp_far], axis=0)
         step_sig = jnp.concatenate([step_sig, sig_far], axis=0)
+        speed = jnp.concatenate([speed, speed_far], axis=0)
         small_w.append(far_w)
+        bufs, _ = scan_call(
+            1, planes, (far_x, 0), 0, *x_args, hp, ct, b_low, cbt, bufs[:4] + [sent_a], [token]
+        )
+        ent_a = lax.ppermute(bufs[4], "tensor", halo)
         bufs, done = scan_call(
-            1, planes, (far_x, 0), *x_args, hp, ct, b_low, cbt, bufs, [held]
+            1, planes, (far_x, 0), 1, *x_args, hp, ct, b_low, cbt, bufs[:4] + [sent_b], [token]
         )
-
-        token, held, passed = hold([done] + swapped, two + far_o)
-        two, far_o = passed[:2], passed[2:]
+        sent_b = bufs[4]
+        token, passed, _ = hold([done] + swapped, two + far_o + [ent_a, sent_b])
+        two, far_o, (ent_a, sent_b) = passed[:2], passed[2:4], passed[4:]
         far_z = as_paths(far_z + two, swapped + pass_core(two))
         got = pass_one(far_o)
-        ent = lax.ppermute(bufs[4], "tensor", halo)
-
-        token, held, (ent,) = hold(got + far_z[0] + far_z[1], [ent])
-        far_o = with_first(far_o, got, token)
+        ent_b = lax.ppermute(sent_b, "tensor", halo)
+
+        token, passed, far_o = hold(far_z[0] + far_z[1], [ent_a, ent_b], wide_o, got)
+        ent_a, ent_b = passed
         two = pass_two(far_o)
         swapped = pass_core(far_o)
-        ent = lax.ppermute(hop_call(ent, 1, bufs[3], hp), "tensor", halo)
-        z, done = proj_call(1, planes, (far_z, 0), *z_args, z, [held])
-
-        token, held, passed = hold([done] + swapped, two + [ent])
-        two, ent = passed[:2], passed[2]
+        send = hop_call(ent_a, 1, bufs[3], hp, 0, [token])
+        ent_a = lax.ppermute(send, "tensor", halo)
+        z, done = proj_call(1, planes, (far_z, 0), *z_args, z, [send])
+        ent_b = lax.ppermute(hop_call(ent_b, 1, bufs[3], hp, 1, [done]), "tensor", halo)
+        send = hop_call(ent_a, 1, bufs[3], hp, 0, [done])
+
+        token, two, _ = hold([done, ent_b] + swapped, two + [send])
+        two, send = two[:2], two[2]
+        ent_a = lax.ppermute(send, "tensor", halo)
         far_o = as_paths(far_o + two, swapped + pass_core(two))
-        ent = lax.ppermute(hop_call(ent, 1, bufs[3], hp), "tensor", halo)
-        wgt, _ = proj_call(1, planes, (far_o, 0), *o_args, wgt, [held])
+        ent_b = lax.ppermute(hop_call(ent_b, 1, bufs[3], hp, 1, [token]), "tensor", halo)
+        wgt, done = proj_call(1, planes, (far_o, 0), *o_args, wgt)
+        _, ent, _ = hold([done], [ent_a, ent_b])
+        ent = jnp.stack(ent)
         z_sets = [((0, 1), [(own, 0)]), ((1, planes), [(far_z, 0)])]
         x_sets = [((0, 1), [(own, 1)]), ((1, planes), [(far_x, 0)])]
         o_sets = [((0, 1), [(own, 2)]), ((1, planes), [(far_o, 0)])]
     else:
         w = lax.all_gather(wt, "dp", axis=2, tiled=True)
-        w = slot_order(lax.all_gather(w, "tensor", axis=0))
+        w = by_slot(w)
         o = lax.all_gather(out_weight, "dp", axis=1, tiled=True)
         flat_rows = lambda v: [[v.reshape(1, inner, width)]]
         wz, wx = flat_rows(w[:, 0]), flat_rows(w[:, 1])
-        o = flat_rows(slot_order(lax.all_gather(o, "tensor", axis=0)))
-        bufs, _ = scan_call(0, planes, (wx, 0), *x_args, hp, ct, b_low, cbt, None)
+        o = flat_rows(by_slot(o))
+        bufs, _ = scan_call(
+            0, planes, (wx, 0), 0, *x_args, hp, ct, b_low, cbt, [None] * 5
+        )
         z, _ = proj_call(0, planes, (wz, 0), *z_args, None)
         wgt, _ = proj_call(0, planes, (o, 0), *o_args, None)
         ent = lax.ppermute(bufs[4], "tensor", halo)
         for _ in range(planes - 2):
             ent = lax.ppermute(hop_call(ent, 1, bufs[3], hp), "tensor", halo)
+        ent = ent[None]
         z_sets = [((0, planes), [(wz, 0)])]
         x_sets = [((0, planes), [(wx, 0)])]
         o_sets = [((0, planes), [(o, 0)])]
     xc, mix, loc, s_end, _ = bufs
     left = [(s + 1, s) for s in range(planes - 1)]
 
-    nout, dy, dz, sl, sl_sent = gate_call(z, mix, wgt, ent, chan, hp, ct, c_low, inner)
+    nout, dy, dz, sl, sl_sent = gate_call(z, mix, wgt, ent, pk, hp, ct, c_low, inner)
 
     adj = lax.ppermute(sl_sent, "tensor", left)
     mixed, grad_down_out, grad_up_out = output_call(
-        sc, nout, down_out2, back2, up_out, tokens[0], masked, o_sets, picks, flat, quick
-    )
-    adj = lax.ppermute(hop_call(adj, planes - 1, sl, hp, [mixed]), "tensor", left)
-    d_normed = gate_back_call(dz, z_sets, picks, width, [mixed])
-    adj = lax.ppermute(hop_call(adj, planes - 1, sl, hp, [d_normed]), "tensor", left)
+        sc, nout, pk, back2, up_out, tokens[0], masked, o_sets, picks, flat, quick
+    )
+    send = hop_call(adj, planes - 1, sl, hp, 0, [mixed])
+    adj = lax.ppermute(send, "tensor", left)
+    d_normed, grad_z = gate_back_call(dz, low2, z_sets, picks, width, [send])
+    send = hop_call(adj, planes - 1, sl, hp, 0, [d_normed])
+    adj = lax.ppermute(send, "tensor", left)
     for _ in range(planes - 4):
         adj = lax.ppermute(hop_call(adj, planes - 1, sl, hp), "tensor", left)
     dxs, u1, u2, kl, dcb, db1, dc1 = back_call(
-        0, planes, dy, xc, hp, ent, loc, ct, c_low, bt, cbt, None, [d_normed]
-    )
-
-    (dx, tail, head, grad_z, grad_x, d_low2, ddelta, u2f, kf, db3) = finish_call(
-        dxs, dy, xc, dz, chan, hp, ent, adj, bt, up_z2, up_x2, low2[:, HALO:], [mixed]
-    )
-    small_left, maps_tail, maps_head = glue_call(
-        [dcb, db1, db3, dc1, bt, ct, maps_pre]
-        + [u1, u2, kl, ddelta, u2f, kf, step_sig, speed[:, None], map_taps],
-        state_w, length, heads,
-    )
-
-    near = lax.ppermute(
-        jnp.concatenate(
-            [head[:, :4].reshape(planes * 4 * ch), maps_head[:4].reshape(8 * state_w)]
-        ),
-        "tensor",
-        left,
-    )
-
-    def beyond(values, taps_of):
-        return [sum(taps_of(k) * values(i - k) for k in range(i + 1)) for i in range(3)]
-
-    near_x = jnp.roll(near[: planes * 4 * ch].reshape(planes, 4, ch), 1, axis=0)
-    more = jnp.stack(beyond(lambda n: near_x[:, n], lambda k: taps[:, k]), axis=1)
-    tail = (
-        tail + jnp.pad(jnp.swapaxes(more, 1, 2), ((0, 0), (0, 0), (HALO - 3, 0)))
-    ).astype(bf16)
-    low_last = low2[:rank, -3:].astype(f32)
-    grad_x = grad_x[:, :rank] + grad_x[:, rank:]
-    grad_x += sum(low_last[None, :, i, None] * more[:, i, None, :] for i in range(3))
-    grad_z = grad_z[:, :rank] + grad_z[:, rank:]
-    d_low_more = jnp.einsum("jrk,jik->ri", packed[:, rank : 2 * rank].astype(f32), more)
-    d_low = d_low2[:rank] + jnp.pad(d_low_more, ((0, 0), (length - 3, 0)))
-    d_low = d_low.astype(bf16)
-    near_maps = near[planes * 4 * ch :].reshape(4, 2 * state_w)
-    maps_more = jnp.stack(beyond(lambda n: near_maps[n], lambda k: conv_maps[k]), axis=1)
-    maps_tail = maps_tail + jnp.pad(maps_more, ((0, 0), (HALO - 3, 0)))
-    small_left = lax.dynamic_update_slice(
-        small_left, maps_tail.astype(bf16), (0, length - HALO)
-    )
-
-    grad_down = dot(d_low, normed)
-    quarters = lambda v: slot_order(
-        jnp.swapaxes(v.reshape(rank, planes, width // planes), 0, 1)
-    )
-    mine_sum = to_slots(
-        jnp.concatenate(
-            [grad_z, grad_x, grad_down_out, quarters(grad_down), quarters(grad_up_out)], axis=2
-        )
-    ).astype(bf16)
-    head_part = 3 * ch
-    shared = by_slot(mine_sum[:, head_part:])
+        0, planes, dy, xc, hp, ent, loc, ct, c_low, bt, cbt, None, [send]
+    )
+
+    early = to_slots(
+        [jnp.concatenate([grad_z[j], grad_down_out[j]], axis=1) for j in range(planes)],
+        grad_up_out,
+    )
+    (dx, tail, head, grad_x, d_low, ddelta, u2f, kf, db3) = finish_call(
+        dxs, dy, xc, dz, pk, hp, ent, adj, bt, low2, [mixed, early]
+    )
+    small_left, maps_tail, maps_head, grad_down = glue_call(
+        [dcb, db1, db3, dc1, bt, ct, maps_pre, u1, u2, kl, ddelta, u2f, kf, step_sig, speed]
+        + [conv_maps],
+        sc, d_low, nt, state_w, length, heads, flat, quick,
+    )
+
+    to_left = jnp.concatenate(
+        [
+            head.reshape(8 * planes, ch),
+            jnp.pad(maps_head, ((0, 0), (0, ch - 2 * state_w))),
+            jnp.zeros((-(8 * planes + 8) % rank, ch), f32),
+            jnp.pad(d_low[:, :HALO], ((0, 0), (0, ch - HALO))),
+        ],
+        axis=0,
+    )
+    near = lax.ppermute(to_left, "tensor", left)
+    late = to_slots([grad_x[j] for j in range(planes)], grad_down)
     sent = jnp.concatenate(
         [
-            mine_sum[:, :head_part],
-            jnp.swapaxes(shared, 0, 1).reshape(rank, -1),
-            jnp.full((rank, 128), pick).astype(bf16),
+            early[:, :ch],
+            late[:, :ch],
+            early[:, ch : 2 * ch],
+            late[:, ch:],
+            early[:, 2 * ch :],
+            jnp.full((rank, 128), pick).astype(f32),
         ],
         axis=1,
-    )
+    ).astype(bf16)[None]
     if quick:
-        by_seq = sent[None]
-        for bit in (2, 4, 1):
-            by_seq = jnp.concatenate([by_seq, flip(by_seq, bit)], axis=0)
+        _, (sent,), _ = hold([near], [sent])
+        by_seq = [sent] + [flip(sent, bit) for bit in (2, 4, 6)]
     else:
-        by_seq = lax.all_gather(sent, "dp", axis=0)
-    ids = by_seq[:, 0, -1].astype(jnp.int32)
-    chosen = (ids[None, :] == jnp.arange(adapters)[:, None]).astype(bf16)
-    grads = jnp.einsum("as,srk->ark", chosen, by_seq[..., :-128], preferred_element_type=f32)
-    g_up = grads[:, :, : 2 * ch].reshape(adapters, rank, 2, ch)
-    g_down_out = jnp.swapaxes(grads[:, :, 2 * ch : 3 * ch], 1, 2)
-    common = grads[:, :, 3 * ch :].reshape(adapters, rank, planes, 2, width // planes)
-    twice = jnp.concatenate([common, common], axis=2)
-    common = lax.dynamic_slice_in_dim(twice, (planes - place) % planes, planes, 2)
-    g_down = jnp.swapaxes(common[:, :, :, 0].reshape(adapters, rank, width), 1, 2)
-    g_up_out = common[:, :, :, 1].reshape(adapters, rank, width)
+        by_seq = [lax.all_gather(sent[0], "dp", axis=0)]
 
     tokens_grad = input_call(
-        sc, dx, tail, small_left, d_low, down_in, root, pre_gain[None], tokens[0], masked,
-        d_normed, small_w, x_sets, picks, flat, quick,
-    )
+        sc, dx, tail, near, pk, small_left, maps_tail, conv_maps, d_low, down_in, root,
+        pre_gain[None], tokens[0], masked, d_normed, small_w, x_sets, picks, flat, quick,
+    )
+    if quick:
+        _, by_seq, _ = hold([tokens_grad], by_seq)
+        by_seq = jnp.concatenate(by_seq, axis=0)
+        by_seq = [by_seq, flip(by_seq, 1)]
+    g_down, g_up, g_down_out, g_up_out = assemble_call(by_seq, adapters, planes, ch, width)
+    g_down = jnp.swapaxes(g_down, 1, 2)
+    g_down_out = jnp.swapaxes(g_down_out, 1, 2)
     return (mixed[None], tokens_grad[None], g_down, g_up, g_down_out, g_up_out)
 
 

time: 675 us -> 608 us (0.901)
  other arithmetic: 62.5 us -> 19.7 us
  waiting for transfers between devices: 135 us -> 94.1 us
  Pallas kernels: 307 us -> 345 us
  blocking collectives: 13.7 us -> 0 us
  local copies, waits for them, and re-layouts: 67.8 us -> 55.7 us
    ppermute x12 -> x15, waiting for transfers between devices: 83.1 us -> 26.1 us  [the longest x1 11.1 us: body(): ent_b = lax.ppermute(sent_b, 'tensor', halo)]
    all_gather x1, waiting for transfers between devices: 0.02 us -> 31.5 us  [body(): lax.all_gather(jnp.concatenate([wt[1], packed, steps_w, last_rows], axis=...]
    pallas_call x17 -> x25, Pallas kernels: 87 us -> 118 us  [the longest x4 54.5 us: scan_call(): pl.pallas_call(functools.partial(scan_kernel, nx, picks[part], hb, SUB),...]
    add x10 -> x0, other arithmetic: 22.4 us -> none  [the longest x8 19.7 us: with_first(): return [jnp.stack([v, w]) + token for v, w in zip(ab, got)]]
    all_gather x1 -> x0, blocking collectives: 13.7 us -> none  [by_slot(): return slot_order(lax.all_gather(v, 'tensor', axis=0))]
    slice x27 -> x4, local copies, waits for them, and re-layouts: 14.4 us -> 1.84 us  [the longest x1 1.13 us: body(): pk = jnp.stack([v[marks[0]:marks[1]] for v in all_x])]
    all_gather x1, waiting for transfers between devices: 18.1 us -> 7.29 us  [body(): all_o = lax.all_gather(out_weight, 'tensor', axis=0)]
    concatenate x8 -> x5, other arithmetic: 11.2 us -> 2.36 us  [the longest x1 0.91 us: body(): jnp.concatenate([wt[1], packed, steps_w, last_rows], axis=0)]
  transfers between devices with their start and end apart: 51 -> 55, of which waited for: 17 -> 14; matrix products, arithmetic and copies ran while one was open for 10% -> 7% of each run, Pallas kernels for 35% -> 43%
where the time goes in v3:
time: 608 us; the launch traced here: 597 us
  Pallas kernels  345 us (57%)
  waiting for transfers between devices  94.1 us (15%)
  starting transfers between devices  65.1 us (11%)
  local copies, waits for them, and re-layouts  55.7 us (9%)
  other arithmetic  19.7 us (3%)
  between operations  17.9 us (3%)
    pallas_call x4, Pallas kernels, scan_call(): pl.pallas_call(functools.partial(scan_kernel, nx, picks[part], hb, SUB),...  54.5 us
    pallas_call x4, Pallas kernels, proj_call(): pl.pallas_call(functools.partial(proj_kernel, n_w, picks, ncb, cut, gain)...  53.9 us
    pallas_call x1, Pallas kernels, gate_call(): pl.pallas_call(functools.partial(gate_kernel, hb, inner), grid=(2, slots,...  32.1 us
    all_gather x1, waiting for transfers between devices, body(): lax.all_gather(jnp.concatenate([wt[1], packed, steps_w, last_rows], axis=...  31.5 us
    pallas_call x1, Pallas kernels, finish_call(): pl.pallas_call(functools.partial(finish_kernel, hb), grid=(slots, ncb), i...  28.2 us
    unnamed x115, local copies, waits for them, and re-layouts  28.1 us
    pallas_call x1, Pallas kernels, input_call(): pl.pallas_call(functools.partial(input_kernel, sets, picks, flat, quick,...  27.7 us
    ppermute x36, starting transfers between devices, flip(): return lax.ppermute(v, 'dp', [(i, i ^ bit) for i in range(seqs)])  27.7 us
  transfers between devices with their start and end apart: 55, of which 14 were waited for; matrix products, arithmetic and copies ran while one was open for 7% of the time, Pallas kernels for 43%

profile of v3, /device:TPU:0, one launch (start us, length us, event | category | flops | bytes accessed | tf_op | source)
XLA Modules:
  0.0 597.4 jit_solution(17126330270049637895)
XLA Ops:
  15.5 3.0 collective-permute-start
  23.7 16.5 %collective-permute-done.1.refs_1_ = bf16[1664,256]{1,0:T(8,128)(2,1)} collective-permute-done((bf16[1664,256]{1,0:T(8,128)(2,1)}, bf16[1664,256]{1,0:T(8,128)(2,1)}, u32[]{:S(2)}, u32[]{:S(2)}) %collective-permute-start.1) | collective-permute-done | bytes 852000 | tf_op jit(solution)/shard_map/ppermute | solution.py:1255
  41.2 2.7 hold.11
  46.1 31.5 %all-gather.8.cloned.1.call-done = bf16[5696,256]{1,0:T(8,128)(2,1)} async-done(((bf16[1424,256]{1,0:T(8,128)(2,1)}), bf16[5696,256]{1,0:T(8,128)(2,1)}) %all-gather.8.cloned.1.call-update) | async-done | bytes 2916368 | tf_op jit(solution)/shard_map/all_gather | solution.py:1340
  101.5 9.7 %turn.1 = (bf16[512,2048]{1,0:T(8,128)(2,1)}, bf16[512,2048]{1,0:T(8,128)(2,1)}, f32[512,1]{1,0:T(8,128)}, bf16[16,640]{1,0:T(8,128)(2,1)}, bf16[16,512]{1,0:T(8...) custom-call(s32[2]{0:T(128)} %pad_add_fusion.refs_0_.refs_16_, bf16[512,2048]{1,0:T(8,128)(2,1)} %bitcast.175, ...), custom_call_target="tpu_custom_call" | custom-call | flops 26214400 | bytes 2097152 | tf_op jit(solution)/shard_map/turn/pallas_call | solution.py:131
  111.2 3.0 collective-permute-done.9.refs_1_
  115.7 2.6 hold.13
  121.4 3.0 all-gather.6.cloned.1.call-done
  129.8 4.0 steps.2
  133.8 5.7 maps.1
  139.5 9.1 %scan_slots.4 = (bf16[4,1024,512]{2,1,0:T(8,128)(2,1)}, f32[4,1024,512]{2,1,0:T(8,128)}, f32[4,1,1024,128]{3,2,1,0:T(8,128)}, f32[4,1024,128]{2,1,0:T(8,128)}, b...) custom-call(bf16[2,1680,256]{2,1,0:T(8,128)(2,1)} %get-tuple-element.134.refs_3_.refs_0_.refs_7_.refs_2_.refs_20_, ...), custom_call_target="tpu_custom_call" | custom-call | flops 268435456 | bytes 524288 | tf_op jit(solution)/shard_map/scan_slots/pallas_call | solution.py:457
  148.5 8.6 %scan_slots.5 = (bf16[4,1024,512]{2,1,0:T(8,128)(2,1)}, f32[4,1024,512]{2,1,0:T(8,128)}, f32[4,1,1024,128]{3,2,1,0:T(8,128)}, f32[4,1024,128]{2,1,0:T(8,128)}, b...) custom-call(bf16[2,1664,256]{2,1,0:T(8,128)(2,1)} %get-tuple-element, ...), custom_call_target="tpu_custom_call", output_to_operand_aliasing={{0}: (12, {}), {1}: (13, {}), {2}: (14, {}), {3}: (15, {})} | custom-call | flops 268435456 | bytes 524288 | tf_op jit(solution)/shard_map/scan_slots/pallas_call | solution.py:457
  163.6 7.3 %all-gather.10.cloned.1.call-done = bf16[4096,256]{1,0:T(8,128)(2,1)} async-done(((bf16[1024,256]{1,0:T(8,128)(2,1)}), bf16[4096,256]{1,0:T(8,128)(2,1)}) %all-gather.10.cloned.1.call-update) | async-done | bytes 2097168 | tf_op jit(solution)/shard_map/all_gather | solution.py:1344
  177.0 8.5 %proj_slots.4 = (bf16[4,1024,512]{2,1,0:T(8,128)(2,1)}, bf16[1,1]{1,0:T(2,128)(2,1)}) custom-call(bf16[2,1680,256]{2,1,0:T(8,128)(2,1)} %get-tuple-element.134.refs_3_.refs_0_.refs_7_.refs_2_.refs_20_, bf16[2,1680,256]{2,1,0:T(8,128)(2,1)} %get-tuple-element.139.refs_4_.refs_1_.refs_8_.refs_3_.refs_21_, bf16[2,1680,256]{2,1,0:T(8,128)(2,1)} %copy-done.2, ...), custom_call_target="tpu_custom_call" | custom-call | flops 268435456 | bytes 655360 | tf_op jit(solution)/shard_map/proj_slots/pallas_call | solution.py:503
  185.5 8.6 %proj_slots.5 = (bf16[4,1024,512]{2,1,0:T(8,128)(2,1)}, bf16[1,1]{1,0:T(2,128)(2,1)}) custom-call(bf16[2,1680,256]{2,1,0:T(8,128)(2,1)} %get-tuple-element.134.refs_3_.refs_0_.refs_7_.refs_2_.refs_20_, bf16[2,1680,256]{2,1,0:T(8,128)(2,1)} %get-tuple-element.139.refs_4_.refs_1_.refs_8_.refs_3_.refs_21_, bf16[2,1680,256]{2,1,0:T(8,128)(2,1)} %copy-done.2, ...), custom_call_target="tpu_custom_call" | custom-call | flops 268435456 | bytes 655360 | tf_op jit(solution)/shard_map/proj_slots/pallas_call | solution.py:503
  195.6 3.2 hold.15
  202.3 4.2 steps.3
  208.4 18.4 %scan_slots.6 = (bf16[4,1024,512]{2,1,0:T(8,128)(2,1)}, f32[4,1024,512]{2,1,0:T(8,128)}, f32[4,1,1024,128]{3,2,1,0:T(8,128)}, f32[4,1024,128]{2,1,0:T(8,128)}, b...) custom-call(bf16[2,1584,256]{2,1,0:T(8,128)(2,1)} %get-tuple-element, ...), custom_call_target="tpu_custom_call", output_to_operand_aliasing={{0}: (12, {}), {1}: (13, {}), {2}: (14, {}), {3}: (15, {}),... | custom-call | flops 805306368 | bytes 1572864 | tf_op jit(solution)/shard_map/scan_slots/pallas_call | solution.py:457
  228.8 18.5 %scan_slots.7 = (bf16[4,1024,512]{2,1,0:T(8,128)(2,1)}, f32[4,1024,512]{2,1,0:T(8,128)}, f32[4,1,1024,128]{3,2,1,0:T(8,128)}, f32[4,1024,128]{2,1,0:T(8,128)}, b...) custom-call(bf16[2,1536,256]{2,1,0:T(8,128)(2,1)} %get-tuple-element, ...), custom_call_target="tpu_custom_call", output_to_operand_aliasing={{0}: (12, {}), {1}: (13, {}), {2}: (14, {}), {3}: (15, {}),... | custom-call | flops 805306368 | bytes 1572864 | tf_op jit(solution)/shard_map/scan_slots/pallas_call | solution.py:457
  251.5 3.7 collective-permute-start.27
  255.2 11.1 %collective-permute-done.27.refs_11_ = bf16[4,512,128]{2,1,0:T(8,128)(2,1)S(1)} collective-permute-done((bf16[4,512,128]{2,1,0:T(8,128)(2,1)}, bf16[4,512,128]{2,1,0:T(8,128)(2,1)S(1)}, u32[]{:S(2)}, u32[]{:S(2)}) %collective-permute-start.27) | collective-permute-done | bytes 524320 | tf_op jit(solution)/shard_map/ppermute | solution.py:1443
  266.3 3.7 collective-permute-done.25.refs_0_
  272.4 2.6 hold.17
  277.5 4.3 hop.6.refs_13_
  281.8 3.7 collective-permute-start.33
  285.6 18.2 %proj_slots.6 = (bf16[4,1024,512]{2,1,0:T(8,128)(2,1)}, bf16[1,1]{1,0:T(2,128)(2,1)}) custom-call(bf16[2,1536,256]{2,1,0:T(8,128)(2,1)} %get-tuple-element.163.refs_2_.refs_0_.refs_10_, bf16[2,1536,256]{2,1,0:T(8,128)(2,1)} %get-tuple-element.182.refs_3_.refs_1_.refs_11_, bf16[2,1536,256]{2,1,0:T(8,128)(2,1)} %copy-done.7, ...), custom_call_target="tpu_custom_call", output_to_operand_aliasing={{0}: (12, {})} | custom-call | flops 805306368 | bytes 1966080 | tf_op jit(solution)/shard_map/proj_slots/pallas_call | solution.py:503
  303.8 4.2 hop.7
  310.4 4.2 hop.8.refs_6_
  314.6 6.5 %collective-permute-done.28.refs_1_.got = bf16[4,512,128]{2,1,0:T(8,128)(2,1)S(1)} collective-permute-done((bf16[4,512,128]{2,1,0:T(8,128)(2,1)}, bf16[4,512,128]{2,1,0:T(8,128)(2,1)S(1)}, u32[]{:S(2)}, u32[]{:S(2)}) %collective-permute-start.28) | collective-permute-done | bytes 524320 | tf_op jit(solution)/shard_map/ppermute | solution.py:1452
  324.2 4.4 hop.9
  328.5 4.3 collective-permute-start.37
  336.3 18.5 %proj_slots.7 = (bf16[4,1024,512]{2,1,0:T(8,128)(2,1)}, bf16[1,1]{1,0:T(2,128)(2,1)}) custom-call(bf16[2,1536,256]{2,1,0:T(8,128)(2,1)} %get-tuple-element.194.refs_0_.refs_15_, bf16[2,1536,256]{2,1,0:T(8,128)(2,1)} %get-tuple-element.198.refs_1_.refs_16_, bf16[2,1536,256]{2,1,0:T(8,128)(2,1)} %copy-done.8, ...), custom_call_target="tpu_custom_call", output_to_operand_aliasing={{0}: (12, {})} | custom-call | flops 805306368 | bytes 1966080 | tf_op jit(solution)/shard_map/proj_slots/pallas_call | solution.py:503
  359.8 32.1 %gate.1 = (bf16[4,1024,512]{2,1,0:T(8,128)(2,1)}, bf16[4,1024,512]{2,1,0:T(8,128)(2,1)}, bf16[4,1024,512]{2,1,0:T(8,128)(2,1)}, f32[4,1024,128]{2,1,0:T(8,128)}, bf16[4,1024,128]{2,1,0:T(8,128)(2,1)}) custom-call(bf16[4,1024,512]{2,1,0:T(8,128)(2,1)} %get-tuple-element.192.refs_0_, f32[4,1024,512]{2,1,0:T(8,128)} %get-tuple-element.193.refs_1_, ...), custom_call_target="tpu_custom_call" | custom-call | flops 157286400 | bytes 5767168 | tf_op jit(solution)/shard_map/gate/pallas_call | solution.py:587
  394.6 23.1 %output.1 = (bf16[512,2048]{1,0:T(8,128)(2,1)}, f32[4,16,1024]{2,1,0:T(8,128)}, f32[16,2048]{1,0:T(8,128)}) custom-call(s32[2]{0:T(128)} %pad_add_fusion.refs_0_.refs_16_, bf16[4,1024,512]{2,1,0:T(8,128)(2,1)} %get-tuple-element.208.refs_1_, bf16[4,256,256]{2,1,0:T(8,128)(2,1)} %pad_maximum_fusion.8.refs_4_.refs_5_.refs_6_.refs_7_.refs_10_.refs_11_.refs_2_.refs_9_, ...), custom_call_target="tpu_custom_call" | custom-call | flops 1073741824 | bytes 2097152 | tf_op jit(solution)/shard_map/output/pallas_call | solution.py:994
  420.5 4.2 hop.10.refs_18_
  426.0 20.3 %gate_back.1 = (f32[512,2048]{1,0:T(8,128)}, f32[4,16,1024]{2,1,0:T(8,128)}) custom-call(bf16[4,1024,512]{2,1,0:T(8,128)(2,1)} %get-tuple-element.217.refs_0_.refs_3_, bf16[16,640]{1,0:T(8,128)(2,1)} %get-tuple-element.138.refs_5_.refs_9_.refs_1_.refs_11_, bf16[2,1680,256]{2,1,0:T(8,128)(2,1)} %get-tuple-element.134.refs_3_.refs_0_.refs_7_.refs_2_.refs_20_, ...), custom_call_target="tpu_custom_call" | custom-call | flops 1073741824 | bytes 2097152 | tf_op jit(solution)/shard_map/gate_back/pallas_call | solution.py:1036
  447.3 3.8 collective-permute-start.41
  451.1 3.5 collective-permute-start.42
  457.3 4.1 hop.11.refs_9_
  464.0 26.2 %state_back.1 = (f32[4,1024,512]{2,1,0:T(8,128)}, f32[16,4,512]{2,1,0:T(4,128)}, f32[16,4,512]{2,1,0:T(4,128)}, f32[16,4,256]{2,1,0:T(4,128)}, f32[2,256,256]{2,...) custom-call(bf16[4,1024,512]{2,1,0:T(8,128)(2,1)} %get-tuple-element.211.refs_0_.refs_1_, ...), custom_call_target="tpu_custom_call" | custom-call | flops 1342177280 | bytes 2097152 | tf_op jit(solution)/shard_map/state_back/pallas_call | solution.py:714
  491.2 28.2 %finish_back.1 = (bf16[4,1024,512]{2,1,0:T(8,128)(2,1)}, f32[4,1024,128]{2,1,0:T(8,128)}, f32[4,8,1024]{2,1,0:T(8,128)}, f32[4,16,1024]{2,1,0:T(8,128)}, f32[16,...) custom-call(f32[4,1024,512]{2,1,0:T(8,128)} %get-tuple-element.219.r, ...), custom_call_target="tpu_custom_call" | custom-call | flops 183500800 | bytes 3670016 | tf_op jit(solution)/shard_map/finish_back/pallas_call | solution.py:805
  520.1 5.2 glue.1
  526.3 2.6 collective-permute-start.45
  534.2 2.7 collective-permute-done.46
  537.0 4.4 collective-permute-done.44.refs_3_.refs_7_.refs_10_.refs_0_
  546.1 27.7 %input_back.1.refs_0_ = bf16[512,2048]{1,0:T(8,128)(2,1)} custom-call(s32[2]{0:T(128)} %pad_add_fusion.refs_0_.refs_16_, bf16[4,1024,512]{2,1,0:T(8,128)(2,1)} %get-tuple-element.223.refs_1_, f32[4,1024,128]{2,1,0:T(8,128)} %get-tuple-element.224.refs_2_, f32[64,1024]{1,0:T(8,128)} %copy-done.14, ...), custom_call_target="tpu_custom_call" | custom-call | flops 1073741824 | bytes 2097152 | tf_op jit(solution)/shard_map/input_back/pallas_call | solution.py:1147
  579.9 2.5 collective-permute-done.51.refs_1_
  583.3 7.2 %assemble.1 = (f32[8,16,2048]{2,1,0:T(8,128)}, f32[8,16,2,1024]{3,2,1,0:T(2,128)}, f32[8,16,1024]{2,1,0:T(8,128)}, f32[8,16,2048]{2,1,0:T(8,128)}) custom-call(bf16[4,16,7296]{2,1,0:T(8,128)(2,1)} %copy-done.22, bf16[4,16,7296]{2,1,0:T(8,128)(2,1)} %copy-done.31), custom_call_target="tpu_custom_call" | custom-call | flops 1250000 | bytes 2500000 | tf_op jit(solution)/shard_map/assemble/pallas_call | solution.py:1188
  (289 shorter events, 124.0 us)
Async XLA Ops:
  7.2 70.4 %all-gather.8.cloned.1.call-start = ((), (), s32[]{:S(2)}) async-start(), calls=%async_computation.1 | async-start | bytes 3645440 | tf_op jit(solution)/shard_map/all_gather | solution.py:1340
  15.1 109.4 %all-gather.6.cloned.1.call-start = ((), (), s32[]{:S(2)}) async-start(), calls=%async_computation | async-start | bytes 2621440 | tf_op jit(solution)/shard_map/all_gather | solution.py:1343
  15.5 24.8 %collective-permute-start = (bf16[1680,256]{1,0:T(8,128)(2,1)S(1)}, bf16[1680,256]{1,0:T(8,128)(2,1)S(1)}, u32[]{:S(2)}, u32[]{:S(2)}) collective-permute-start(bf16[1680,256]{1,0:T(8,128)(2,1)S(1)} %constant_dynamic-update-slice_fusion), channel_id=1, source_target_pairs={{0,8},{4,12},{8,0},{12,4},{16,24},{20,28},{24,16},{28,20},{1,9},{5... | collective-permute-start | bytes 2580488 | tf_op jit(solution)/shard_map/ppermute | solution.py:1255
  19.5 20.7 %collective-permute-start.1 = (bf16[1664,256]{1,0:T(8,128)(2,1)}, bf16[1664,256]{1,0:T(8,128)(2,1)}, u32[]{:S(2)}, u32[]{:S(2)}) collective-permute-start(bf16[1664,256]{1,0:T(8,128)(2,1)} %get-tuple-element.288), channel_id=1, source_target_pairs={{0,16},{4,20},{8,24},{12,28},{16,0},{20,4},{24,8},{28,12},{1,17},{... | collective-permute-start | bytes 2555912 | tf_op jit(solution)/shard_map/ppermute | solution.py:1255
  21.1 149.9 %all-gather.10.cloned.1.call-start = ((), (), s32[]{:S(2)}) async-start(), calls=%async_computation.2 | async-start | bytes 2621440 | tf_op jit(solution)/shard_map/all_gather | solution.py:1344
  43.8 47.2 %collective-permute-start.2 = (bf16[2,1680,256]{2,1,0:T(8,128)(2,1)}, bf16[2,1680,256]{2,1,0:T(8,128)(2,1)S(1)}, u32[]{:S(2)}, u32[]{:S(2)}) collective-permute-start(bf16[2,1680,256]{2,1,0:T(8,128)(2,1)} %get-tuple-element.134.refs_3_.refs_0_.refs_7_.refs_2_.refs_20_), channel_id=1, source_target_pairs={{0,4},{4,0},{8,12},{12,8},{16,20},{20,16},{24,28},{28,24},{1,5},{5... | collective-permute-start | bytes 5160968 | tf_op jit(solution)/shard_map/ppermute | solution.py:1255
  43.8 47.2 %collective-permute-start.4 = (bf16[2,1680,256]{2,1,0:T(8,128)(2,1)}, bf16[2,1680,256]{2,1,0:T(8,128)(2,1)}, u32[]{:S(2)}, u32[]{:S(2)}) collective-permute-start(bf16[2,1680,256]{2,1,0:T(8,128)(2,1)} %get-tuple-element.134.refs_3_.refs_0_.refs_7_.refs_2_.refs_20_), channel_id=1, source_target_pairs={{0,16},{4,20},{8,24},{12,28},{16,0},{20,4},{24,8},{28,12},{1,17},{... | collective-permute-start | bytes 5160968 | tf_op jit(solution)/shard_map/ppermute | solution.py:1255
  45.3 45.7 %collective-permute-start.3 = (bf16[2,1664,256]{2,1,0:T(8,128)(2,1)}, bf16[2,1664,256]{2,1,0:T(8,128)(2,1)}, u32[]{:S(2)}, u32[]{:S(2)}) collective-permute-start(bf16[2,1664,256]{2,1,0:T(8,128)(2,1)} %get-tuple-element.133.refs_7_.refs_4_.refs_0_.refs_11_.refs_6_.refs_24_), channel_id=1, source_target_pairs={{0,4},{4,0},{8,12},{12,8},{16,20},{20,16},{24,28},{28,24},{1,5},{5... | collective-permute-start | bytes 5111816 | tf_op jit(solution)/shard_map/ppermute | solution.py:1255
  45.6 45.4 %collective-permute-start.5 = (bf16[2,1664,256]{2,1,0:T(8,128)(2,1)}, bf16[2,1664,256]{2,1,0:T(8,128)(2,1)}, u32[]{:S(2)}, u32[]{:S(2)}) collective-permute-start(bf16[2,1664,256]{2,1,0:T(8,128)(2,1)} %get-tuple-element.133.refs_7_.refs_4_.refs_0_.refs_11_.refs_6_.refs_24_), channel_id=1, source_target_pairs={{0,8},{4,12},{8,0},{12,4},{16,24},{20,28},{24,16},{28,20},{1,9},{5... | collective-permute-start | bytes 5111816 | tf_op jit(solution)/shard_map/ppermute | solution.py:1255
  92.8 21.5 %collective-permute-start.7 = (bf16[2,1680,256]{2,1,0:T(8,128)(2,1)}, bf16[2,1680,256]{2,1,0:T(8,128)(2,1)S(1)}, u32[]{:S(2)}, u32[]{:S(2)}) collective-permute-start(bf16[2,1680,256]{2,1,0:T(8,128)(2,1)} %get-tuple-element.139.refs_4_.refs_1_.refs_8_.refs_3_.refs_21_), channel_id=1, source_target_pairs={{0,4},{4,0},{8,12},{12,8},{16,20},{20,16},{24,28},{28,24},{1,5},{5... | collective-permute-start | bytes 5160968 | tf_op jit(solution)/shard_map/ppermute | solution.py:1255
  92.8 21.4 %collective-permute-start.6 = (bf16[2,1664,256]{2,1,0:T(8,128)(2,1)}, bf16[2,1664,256]{2,1,0:T(8,128)(2,1)}, u32[]{:S(2)}, u32[]{:S(2)}) collective-permute-start(bf16[2,1664,256]{2,1,0:T(8,128)(2,1)} %get-tuple-element.135.refs_8_.refs_5_.refs_1_.refs_12_.refs_7_.refs_25_), channel_id=1, source_target_pairs={{0,4},{4,0},{8,12},{12,8},{16,20},{20,16},{24,28},{28,24},{1,5},{5... | collective-permute-start | bytes 5111816 | tf_op jit(solution)/shard_map/ppermute | solution.py:1255
  93.3 20.9 %collective-permute-start.8 = (bf16[1584,256]{1,0:T(8,128)(2,1)}, bf16[1584,256]{1,0:T(8,128)(2,1)S(1)}, u32[]{:S(2)}, u32[]{:S(2)}) collective-permute-start(bf16[1584,256]{1,0:T(8,128)(2,1)} %get-tuple-element.140), channel_id=1, source_target_pairs={{0,8},{4,12},{8,0},{12,4},{16,24},{20,28},{24,16},{28,20},{1,9},{5... | collective-permute-start | bytes 2433032 | tf_op jit(solution)/shard_map/ppermute | solution.py:1255
  94.7 19.5 %collective-permute-start.9 = (bf16[1536,256]{1,0:T(8,128)(2,1)}, bf16[1536,256]{1,0:T(8,128)(2,1)}, u32[]{:S(2)}, u32[]{:S(2)}) collective-permute-start(bf16[1536,256]{1,0:T(8,128)(2,1)} %get-tuple-element.141), channel_id=1, source_target_pairs={{0,16},{4,20},{8,24},{12,28},{16,0},{20,4},{24,8},{28,12},{1,17},{... | collective-permute-start | bytes 2359304 | tf_op jit(solution)/shard_map/ppermute | solution.py:1255
  118.3 38.9 %collective-permute-start.10 = (bf16[2,1584,256]{2,1,0:T(8,128)(2,1)}, bf16[2,1584,256]{2,1,0:T(8,128)(2,1)S(1)}, u32[]{:S(2)}, u32[]{:S(2)}) collective-permute-start(bf16[2,1584,256]{2,1,0:T(8,128)(2,1)} %get-tuple-element.152.refs_3_.refs_0_.refs_28_), channel_id=1, source_target_pairs={{0,4},{4,0},{8,12},{12,8},{16,20},{20,16},{24,28},{28,24},{1,5},{5... | collective-permute-start | bytes 4866056 | tf_op jit(solution)/shard_map/ppermute | solution.py:1255
  118.3 38.9 %collective-permute-start.12 = (bf16[2,1584,256]{2,1,0:T(8,128)(2,1)}, bf16[2,1584,256]{2,1,0:T(8,128)(2,1)}, u32[]{:S(2)}, u32[]{:S(2)}) collective-permute-start(bf16[2,1584,256]{2,1,0:T(8,128)(2,1)} %get-tuple-element.152.refs_3_.refs_0_.refs_28_), channel_id=1, source_target_pairs={{0,16},{4,20},{8,24},{12,28},{16,0},{20,4},{24,8},{28,12},{1,17},{... | collective-permute-start | bytes 4866056 | tf_op jit(solution)/shard_map/ppermute | solution.py:1255
  119.8 37.4 %collective-permute-start.11 = (bf16[2,1536,256]{2,1,0:T(8,128)(2,1)}, bf16[2,1536,256]{2,1,0:T(8,128)(2,1)}, u32[]{:S(2)}, u32[]{:S(2)}) collective-permute-start(bf16[2,1536,256]{2,1,0:T(8,128)(2,1)} %get-tuple-element.153.refs_7_.refs_0_.refs_32_), channel_id=1, source_target_pairs={{0,4},{4,0},{8,12},{12,8},{16,20},{20,16},{24,28},{28,24},{1,5},{5... | collective-permute-start | bytes 4718600 | tf_op jit(solution)/shard_map/ppermute | solution.py:1255
  120.0 37.1 %collective-permute-start.13 = (bf16[2,1536,256]{2,1,0:T(8,128)(2,1)}, bf16[2,1536,256]{2,1,0:T(8,128)(2,1)}, u32[]{:S(2)}, u32[]{:S(2)}) collective-permute-start(bf16[2,1536,256]{2,1,0:T(8,128)(2,1)} %get-tuple-element.153.refs_7_.refs_0_.refs_32_), channel_id=1, source_target_pairs={{0,8},{4,12},{8,0},{12,4},{16,24},{20,28},{24,16},{28,20},{1,9},{5... | collective-permute-start | bytes 4718600 | tf_op jit(solution)/shard_map/ppermute | solution.py:1255
  159.5 34.7 %collective-permute-start.16 = (bf16[2,1584,256]{2,1,0:T(8,128)(2,1)}, bf16[2,1584,256]{2,1,0:T(8,128)(2,1)S(1)}, u32[]{:S(2)}, u32[]{:S(2)}) collective-permute-start(bf16[2,1584,256]{2,1,0:T(8,128)(2,1)} %get-tuple-element.161.refs_4_.refs_1_.refs_29_), channel_id=1, source_target_pairs={{0,4},{4,0},{8,12},{12,8},{16,20},{20,16},{24,28},{28,24},{1,5},{5... | collective-permute-start | bytes 4866056 | tf_op jit(solution)/shard_map/ppermute | solution.py:1255
  159.5 34.6 %collective-permute-start.17 = (bf16[2,1536,256]{2,1,0:T(8,128)(2,1)}, bf16[2,1536,256]{2,1,0:T(8,128)(2,1)}, u32[]{:S(2)}, u32[]{:S(2)}) collective-permute-start(bf16[2,1536,256]{2,1,0:T(8,128)(2,1)} %get-tuple-element.162.refs_8_.refs_1_.refs_33_), channel_id=1, source_target_pairs={{0,4},{4,0},{8,12},{12,8},{16,20},{20,16},{24,28},{28,24},{1,5},{5... | collective-permute-start | bytes 4718600 | tf_op jit(solution)/shard_map/ppermute | solution.py:1255
  160.0 34.1 %collective-permute-start.14 = (bf16[1536,256]{1,0:T(8,128)(2,1)}, bf16[1536,256]{1,0:T(8,128)(2,1)S(1)}, u32[]{:S(2)}, u32[]{:S(2)}) collective-permute-start(bf16[1536,256]{1,0:T(8,128)(2,1)} %get-tuple-element.154), channel_id=1, source_target_pairs={{0,8},{4,12},{8,0},{12,4},{16,24},{20,28},{24,16},{28,20},{1,9},{5... | collective-permute-start | bytes 2359304 | tf_op jit(solution)/shard_map/ppermute | solution.py:1255
  161.5 32.7 %collective-permute-start.15 = (bf16[1536,256]{1,0:T(8,128)(2,1)}, bf16[1536,256]{1,0:T(8,128)(2,1)}, u32[]{:S(2)}, u32[]{:S(2)}) collective-permute-start(bf16[1536,256]{1,0:T(8,128)(2,1)} %get-tuple-element.155), channel_id=1, source_target_pairs={{0,16},{4,20},{8,24},{12,28},{16,0},{20,4},{24,8},{28,12},{1,17},{... | collective-permute-start | bytes 2359304 | tf_op jit(solution)/shard_map/ppermute | solution.py:1255
  198.8 48.5 %collective-permute-start.18 = (bf16[2,1536,256]{2,1,0:T(8,128)(2,1)}, bf16[2,1536,256]{2,1,0:T(8,128)(2,1)S(1)}, u32[]{:S(2)}, u32[]{:S(2)}) collective-permute-start(bf16[2,1536,256]{2,1,0:T(8,128)(2,1)} %get-tuple-element.163.refs_2_.refs_0_.refs_10_), channel_id=1, source_target_pairs={{0,4},{4,0},{8,12},{12,8},{16,20},{20,16},{24,28},{28,24},{1,5},{5... | collective-permute-start | bytes 4718600 | tf_op jit(solution)/shard_map/ppermute | solution.py:1255
  198.8 48.5 %collective-permute-start.19 = (bf16[2,1536,256]{2,1,0:T(8,128)(2,1)}, bf16[2,1536,256]{2,1,0:T(8,128)(2,1)}, u32[]{:S(2)}, u32[]{:S(2)}) collective-permute-start(bf16[2,1536,256]{2,1,0:T(8,128)(2,1)} %get-tuple-element.177.refs_6_.refs_4_.refs_14_), channel_id=1, source_target_pairs={{0,4},{4,0},{8,12},{12,8},{16,20},{20,16},{24,28},{28,24},{1,5},{5... | collective-permute-start | bytes 4718600 | tf_op jit(solution)/shard_map/ppermute | solution.py:1255
  199.3 48.0 %collective-permute-start.20 = (bf16[2,1536,256]{2,1,0:T(8,128)(2,1)}, bf16[2,1536,256]{2,1,0:T(8,128)(2,1)}, u32[]{:S(2)}, u32[]{:S(2)}) collective-permute-start(bf16[2,1536,256]{2,1,0:T(8,128)(2,1)} %get-tuple-element.163.refs_2_.refs_0_.refs_10_), channel_id=1, source_target_pairs={{0,16},{4,20},{8,24},{12,28},{16,0},{20,4},{24,8},{28,12},{1,17},{... | collective-permute-start | bytes 4718600 | tf_op jit(solution)/shard_map/ppermute | solution.py:1255
  200.8 46.6 %collective-permute-start.21 = (bf16[2,1536,256]{2,1,0:T(8,128)(2,1)}, bf16[2,1536,256]{2,1,0:T(8,128)(2,1)}, u32[]{:S(2)}, u32[]{:S(2)}) collective-permute-start(bf16[2,1536,256]{2,1,0:T(8,128)(2,1)} %get-tuple-element.177.refs_6_.refs_4_.refs_14_), channel_id=1, source_target_pairs={{0,8},{4,12},{8,0},{12,4},{16,24},{20,28},{24,16},{28,20},{1,9},{5... | collective-permute-start | bytes 4718600 | tf_op jit(solution)/shard_map/ppermute | solution.py:1255
  226.8 20.6 %collective-permute-start.22 = (bf16[4,512,128]{2,1,0:T(8,128)(2,1)}, bf16[4,512,128]{2,1,0:T(8,128)(2,1)S(1)}, u32[]{:S(2)}, u32[]{:S(2)}) collective-permute-start(bf16[4,512,128]{2,1,0:T(8,128)(2,1)} %get-tuple-element.180), channel_id=1, source_target_pairs={{0,1},{1,2},{2,3},{4,5},{5,6},{6,7},{8,9},{9,10},{10,11},{12,13},{... | collective-permute-start | bytes 1572872 | tf_op jit(solution)/shard_map/ppermute | solution.py:1434
  249.9 20.5 %collective-permute-start.23 = (bf16[2,1536,256]{2,1,0:T(8,128)(2,1)}, bf16[2,1536,256]{2,1,0:T(8,128)(2,1)S(1)}, u32[]{:S(2)}, u32[]{:S(2)}) collective-permute-start(bf16[2,1536,256]{2,1,0:T(8,128)(2,1)} %get-tuple-element.182.refs_3_.refs_1_.refs_11_), channel_id=1, source_target_pairs={{0,4},{4,0},{8,12},{12,8},{16,20},{20,16},{24,28},{28,24},{1,5},{5... | collective-permute-start | bytes 4718600 | tf_op jit(solution)/shard_map/ppermute | solution.py:1255
  249.9 20.5 %collective-permute-start.24 = (bf16[2,1536,256]{2,1,0:T(8,128)(2,1)}, bf16[2,1536,256]{2,1,0:T(8,128)(2,1)S(1)}, u32[]{:S(2)}, u32[]{:S(2)}) collective-permute-start(bf16[2,1536,256]{2,1,0:T(8,128)(2,1)} %get-tuple-element.183.refs_7_.refs_5_.refs_15_), channel_id=1, source_target_pairs={{0,4},{4,0},{8,12},{12,8},{16,20},{20,16},{24,28},{28,24},{1,5},{5... | collective-permute-start | bytes 4718600 | tf_op jit(solution)/shard_map/ppermute | solution.py:1255
  250.4 19.7 %collective-permute-start.25 = (bf16[1536,256]{1,0:T(8,128)(2,1)}, bf16[1536,256]{1,0:T(8,128)(2,1)S(1)}, u32[]{:S(2)}, u32[]{:S(2)}) collective-permute-start(bf16[1536,256]{1,0:T(8,128)(2,1)} %get-tuple-element.185), channel_id=1, source_target_pairs={{0,8},{4,12},{8,0},{12,4},{16,24},{20,28},{24,16},{28,20},{1,9},{5... | collective-permute-start | bytes 2359304 | tf_op jit(solution)/shard_map/ppermute | solution.py:1255
  250.9 19.4 %collective-permute-start.26 = (bf16[1536,256]{1,0:T(8,128)(2,1)}, bf16[1536,256]{1,0:T(8,128)(2,1)S(1)}, u32[]{:S(2)}, u32[]{:S(2)}) collective-permute-start(bf16[1536,256]{1,0:T(8,128)(2,1)} %get-tuple-element.186), channel_id=1, source_target_pairs={{0,16},{4,20},{8,24},{12,28},{16,0},{20,4},{24,8},{28,12},{1,17},{... | collective-permute-start | bytes 2359304 | tf_op jit(solution)/shard_map/ppermute | solution.py:1255
  251.5 14.8 %collective-permute-start.27 = (bf16[4,512,128]{2,1,0:T(8,128)(2,1)}, bf16[4,512,128]{2,1,0:T(8,128)(2,1)S(1)}, u32[]{:S(2)}, u32[]{:S(2)}) collective-permute-start(bf16[4,512,128]{2,1,0:T(8,128)(2,1)} %get-tuple-element.188), channel_id=1, source_target_pairs={{0,1},{1,2},{2,3},{4,5},{5,6},{6,7},{8,9},{9,10},{10,11},{12,13},{... | collective-permute-start | bytes 1572872 | tf_op jit(solution)/shard_map/ppermute | solution.py:1443
  275.0 46.2 %collective-permute-start.29 = (bf16[2,1536,256]{2,1,0:T(8,128)(2,1)}, bf16[2,1536,256]{2,1,0:T(8,128)(2,1)S(1)}, u32[]{:S(2)}, u32[]{:S(2)}) collective-permute-start(bf16[2,1536,256]{2,1,0:T(8,128)(2,1)} %get-tuple-element.194.refs_0_.refs_15_), channel_id=1, source_target_pairs={{0,4},{4,0},{8,12},{12,8},{16,20},{20,16},{24,28},{28,24},{1,5},{5... | collective-permute-start | bytes 4718600 | tf_op jit(solution)/shard_map/ppermute | solution.py:1255
  275.0 46.2 %collective-permute-start.30 = (bf16[2,1536,256]{2,1,0:T(8,128)(2,1)}, bf16[2,1536,256]{2,1,0:T(8,128)(2,1)}, u32[]{:S(2)}, u32[]{:S(2)}) collective-permute-start(bf16[2,1536,256]{2,1,0:T(8,128)(2,1)} %get-tuple-element.197.refs_4_.refs_19_), channel_id=1, source_target_pairs={{0,4},{4,0},{8,12},{12,8},{16,20},{20,16},{24,28},{28,24},{1,5},{5... | collective-permute-start | bytes 4718600 | tf_op jit(solution)/shard_map/ppermute | solution.py:1255
  275.5 45.7 %collective-permute-start.31 = (bf16[2,1536,256]{2,1,0:T(8,128)(2,1)}, bf16[2,1536,256]{2,1,0:T(8,128)(2,1)}, u32[]{:S(2)}, u32[]{:S(2)}) collective-permute-start(bf16[2,1536,256]{2,1,0:T(8,128)(2,1)} %get-tuple-element.194.refs_0_.refs_15_), channel_id=1, source_target_pairs={{0,16},{4,20},{8,24},{12,28},{16,0},{20,4},{24,8},{28,12},{1,17},{... | collective-permute-start | bytes 4718600 | tf_op jit(solution)/shard_map/ppermute | solution.py:1255
  276.0 45.1 %collective-permute-start.32 = (bf16[2,1536,256]{2,1,0:T(8,128)(2,1)}, bf16[2,1536,256]{2,1,0:T(8,128)(2,1)}, u32[]{:S(2)}, u32[]{:S(2)}) collective-permute-start(bf16[2,1536,256]{2,1,0:T(8,128)(2,1)} %get-tuple-element.197.refs_4_.refs_19_), channel_id=1, source_target_pairs={{0,8},{4,12},{8,0},{12,4},{16,24},{20,28},{24,16},{28,20},{1,9},{5... | collective-permute-start | bytes 4718600 | tf_op jit(solution)/shard_map/ppermute | solution.py:1255
  281.8 26.2 %collective-permute-start.33 = (bf16[4,512,128]{2,1,0:T(8,128)(2,1)}, bf16[4,512,128]{2,1,0:T(8,128)(2,1)S(1)}, u32[]{:S(2)}, u32[]{:S(2)}) collective-permute-start(bf16[4,512,128]{2,1,0:T(8,128)(2,1)} %hop.6.refs_13_), channel_id=1, source_target_pairs={{0,1},{1,2},{2,3},{4,5},{5,6},{6,7},{8,9},{9,10},{10,11},{12,13},{... | collective-permute-start | bytes 1572872 | tf_op jit(solution)/shard_map/ppermute | solution.py:1450
  308.0 13.1 %collective-permute-start.28 = (bf16[4,512,128]{2,1,0:T(8,128)(2,1)}, bf16[4,512,128]{2,1,0:T(8,128)(2,1)S(1)}, u32[]{:S(2)}, u32[]{:S(2)}) collective-permute-start(bf16[4,512,128]{2,1,0:T(8,128)(2,1)} %hop.7), channel_id=1, source_target_pairs={{0,1},{1,2},{2,3},{4,5},{5,6},{6,7},{8,9},{9,10},{10,11},{12,13},{... | collective-permute-start | bytes 1572872 | tf_op jit(solution)/shard_map/ppermute | solution.py:1452
  323.7 11.4 %collective-permute-start.35 = (bf16[2,1536,256]{2,1,0:T(8,128)(2,1)}, bf16[2,1536,256]{2,1,0:T(8,128)(2,1)}, u32[]{:S(2)}, u32[]{:S(2)}) collective-permute-start(bf16[2,1536,256]{2,1,0:T(8,128)(2,1)} %get-tuple-element.199.refs_5_.refs_20_), channel_id=1, source_target_pairs={{0,4},{4,0},{8,12},{12,8},{16,20},{20,16},{24,28},{28,24},{1,5},{5... | collective-permute-start | bytes 4718600 | tf_op jit(solution)/shard_map/ppermute | solution.py:1255
  328.5 26.2 %collective-permute-start.37 = (bf16[4,512,128]{2,1,0:T(8,128)(2,1)}, bf16[4,512,128]{2,1,0:T(8,128)(2,1)S(1)}, u32[]{:S(2)}, u32[]{:S(2)}) collective-permute-start(bf16[4,512,128]{2,1,0:T(8,128)(2,1)} %hop.9), channel_id=1, source_target_pairs={{0,1},{1,2},{2,3},{4,5},{5,6},{6,7},{8,9},{9,10},{10,11},{12,13},{... | collective-permute-start | bytes 1572872 | tf_op jit(solution)/shard_map/ppermute | solution.py:1459
  332.8 22.7 %collective-permute-start.36 = (bf16[4,512,128]{2,1,0:T(8,128)(2,1)S(1)}, bf16[4,512,128]{2,1,0:T(8,128)(2,1)S(1)}, u32[]{:S(2)}, u32[]{:S(2)}) collective-permute-start(bf16[4,512,128]{2,1,0:T(8,128)(2,1)S(1)} %copy-done.21), channel_id=1, source_target_pairs={{0,1},{1,2},{2,3},{4,5},{5,6},{6,7},{8,9},{9,10},{10,11},{12,13},{... | collective-permute-start | bytes 1572872 | tf_op jit(solution)/shard_map/ppermute | solution.py:1457
  391.9 27.6 %collective-permute-start.38 = (bf16[4,1024,128]{2,1,0:T(8,128)(2,1)}, bf16[4,1024,128]{2,1,0:T(8,128)(2,1)S(1)}, u32[]{:S(2)}, u32[]{:S(2)}) collective-permute-start(bf16[4,1024,128]{2,1,0:T(8,128)(2,1)} %get-tuple-element.215), channel_id=1, source_target_pairs={{1,0},{2,1},{3,2},{5,4},{6,5},{7,6},{9,8},{10,9},{11,10},{13,12},{... | collective-permute-start | bytes 3145736 | tf_op jit(solution)/shard_map/ppermute | solution.py:1490
  424.7 31.6 %collective-permute-start.39 = (bf16[4,1024,128]{2,1,0:T(8,128)(2,1)}, bf16[4,1024,128]{2,1,0:T(8,128)(2,1)S(1)}, u32[]{:S(2)}, u32[]{:S(2)}) collective-permute-start(bf16[4,1024,128]{2,1,0:T(8,128)(2,1)} %hop.10.refs_18_), channel_id=1, source_target_pairs={{1,0},{2,1},{3,2},{5,4},{6,5},{7,6},{9,8},{10,9},{11,10},{13,12},{... | collective-permute-start | bytes 3145736 | tf_op jit(solution)/shard_map/ppermute | solution.py:1495
  447.3 15.4 %collective-permute-start.41 = (bf16[16,4096]{1,0:T(8,128)(2,1)S(1)}, bf16[16,4096]{1,0:T(8,128)(2,1)S(1)}, u32[]{:S(2)}, u32[]{:S(2)}) collective-permute-start(bf16[16,4096]{1,0:T(8,128)(2,1)S(1)} %get-tuple-element.315), channel_id=1, source_target_pairs={{0,1},{1,2},{2,3},{3,0},{4,5},{5,6},{6,7},{7,4},{8,9},{9,10},{10,1... | collective-permute-start | bytes 393224 | tf_op jit(solution)/shard_map/ppermute | solution.py:1270
  451.1 12.2 %collective-permute-start.42 = (bf16[16,4096]{1,0:T(8,128)(2,1)S(1)}, bf16[16,4096]{1,0:T(8,128)(2,1)S(1)}, u32[]{:S(2)}, u32[]{:S(2)}) collective-permute-start(bf16[16,4096]{1,0:T(8,128)(2,1)S(1)} %get-tuple-element.316), channel_id=1, source_target_pairs={{0,2},{1,3},{2,0},{3,1},{4,6},{5,7},{6,4},{7,5},{8,10},{9,11},{10,... | collective-permute-start | bytes 393224 | tf_op jit(solution)/shard_map/ppermute | solution.py:1270
  461.4 28.8 %collective-permute-start.40 = (bf16[4,1024,128]{2,1,0:T(8,128)(2,1)}, bf16[4,1024,128]{2,1,0:T(8,128)(2,1)S(1)}, u32[]{:S(2)}, u32[]{:S(2)}) collective-permute-start(bf16[4,1024,128]{2,1,0:T(8,128)(2,1)} %hop.11.refs_9_), channel_id=1, source_target_pairs={{1,0},{2,1},{3,2},{5,4},{6,5},{7,6},{9,8},{10,9},{11,10},{13,12},{... | collective-permute-start | bytes 3145736 | tf_op jit(solution)/shard_map/ppermute | solution.py:1498
  542.6 31.2 %collective-permute-start.48 = (bf16[1,16,7296]{2,1,0:T(8,128)(2,1)}, bf16[1,16,7296]{2,1,0:T(8,128)(2,1)S(1)}, u32[]{:S(2)}, u32[]{:S(2)}) collective-permute-start(bf16[1,16,7296]{2,1,0:T(8,128)(2,1)} %get-tuple-element.251.refs_1_), channel_id=1, source_target_pairs={{0,8},{4,12},{8,0},{12,4},{16,24},{20,28},{24,16},{28,20},{1,9},{5... | collective-permute-start | bytes 700424 | tf_op jit(solution)/shard_map/ppermute | solution.py:1255
  543.2 30.7 %collective-permute-start.49 = (bf16[1,16,7296]{2,1,0:T(8,128)(2,1)}, bf16[1,16,7296]{2,1,0:T(8,128)(2,1)S(1)}, u32[]{:S(2)}, u32[]{:S(2)}) collective-permute-start(bf16[1,16,7296]{2,1,0:T(8,128)(2,1)} %get-tuple-element.251.refs_1_), channel_id=1, source_target_pairs={{0,16},{4,20},{8,24},{12,28},{16,0},{20,4},{24,8},{28,12},{1,17},{... | collective-permute-start | bytes 700424 | tf_op jit(solution)/shard_map/ppermute | solution.py:1255
  544.7 29.2 %collective-permute-start.50 = (bf16[1,16,7296]{2,1,0:T(8,128)(2,1)}, bf16[1,16,7296]{2,1,0:T(8,128)(2,1)S(1)}, u32[]{:S(2)}, u32[]{:S(2)}) collective-permute-start(bf16[1,16,7296]{2,1,0:T(8,128)(2,1)} %get-tuple-element.251.refs_1_), channel_id=1, source_target_pairs={{0,24},{4,28},{8,16},{12,20},{16,8},{20,12},{24,0},{28,4},{1,25},{... | collective-permute-start | bytes 700424 | tf_op jit(solution)/shard_map/ppermute | solution.py:1255
  (56 other events, 311.7 us)
Sparse Core Ops, SparseCore 0:
  15.2 62.4 all-gather.7
  79.8 44.6 all-gather.5
  126.0 44.8 all-gather.9

commit v4 on v3

--- a/solution.py
+++ b/solution.py
@@ -16,6 +16,7 @@
 HALO = 128
 SUB = 256
 CB = 256
+ROWS = 32
 
 NN = ((1,), (0,))
 NT = ((1,), (1,))
@@ -38,12 +39,12 @@
     )
 
 
-def packed_spec(kind, index):
-    def where(*grid):
-        slot, c = index(*grid)
-        return (slot, c * 4 + kind, 0)
-
-    return pl.BlockSpec((None, 16, CB), where)
+def kind_rows(packed, b, kind):
+    return packed.at[pl.ds(pl.multiple_of(b * 64 + kind * 16, 16), 16)]
+
+
+def block_rows(ref, b):
+    return ref.at[pl.ds(pl.multiple_of(b * CB, CB), CB)]
 
 
 def sigmoid(v):
@@ -53,6 +54,19 @@
 def columns(numbers):
     v = numbers[...].astype(f32)
     return jnp.transpose(v[:8] + v[8:])
+
+
+def spread(numbers, which):
+    row = lax.broadcasted_iota(jnp.int32, (16, 128 * len(which)), 0) % 8
+    col = lax.broadcasted_iota(jnp.int32, (16, 128 * len(which)), 1) // 128
+    pick = jnp.zeros(row.shape, f32)
+    for k, n in enumerate(which):
+        pick = jnp.where((row == n) & (col == k), 1.0, pick)
+    return dot(numbers[...], pick.astype(bf16), TN)
+
+
+def lanes_of(values, width):
+    return jnp.concatenate([values] * (width // 128), axis=1)
 
 
 def tall(rows):
@@ -66,6 +80,14 @@
     return out[:, HALO:]
 
 
+def conv_rows(raw, taps, shift):
+    width = raw.shape[1]
+    out = raw * lanes_of(taps[3], width)
+    for k in range(3):
+        out = out + pltpu.roll(raw, shift(k), 1) * lanes_of(taps[k], width)
+    return out
+
+
 def per_head(values, rows):
     hb = rows.shape[0]
     parts = [values[h * HEAD : (h + 1) * HEAD] * rows[h : h + 1] for h in range(hb)]
@@ -79,8 +101,8 @@
     return jnp.concatenate(parts, axis=0)
 
 
-def joined(refs, picks):
-    parts = [refs[k][b] for k, b in picks]
+def joined(refs, picks, rows=slice(None)):
+    parts = [refs[k][b, rows] for k, b in picks]
     return parts[0] if len(parts) == 1 else jnp.concatenate(parts, axis=1)
 
 
@@ -303,108 +325,100 @@
 
 
 def hold_kernel(n_joined, *refs):
-    parts = refs[:n_joined]
     outs = refs[-1 - n_joined :]
-    for part, out in zip(parts, outs):
-        out[...] = part[...]
+    for k in range(n_joined):
+        outs[k][0] = refs[2 * k][...]
+        outs[k][1] = refs[2 * k + 1][...]
     outs[-1][...] = jnp.zeros((1, 1), bf16)
 
 
-def hold(deps, passed=(), joined_to=(), parts=()):
+def hold(deps, passed=(), pairs=()):
     anywhere = pl.BlockSpec(memory_space=pl.ANY)
-    deps, passed, joined_to, parts = list(deps), list(passed), list(joined_to), list(parts)
-    kept = passed + joined_to
-    whole = lambda a: pl.BlockSpec(a.shape, lambda i: (0, 0))
-    second = lambda a: pl.BlockSpec((None,) + a.shape[1:], lambda i: (1, 0, 0))
+    deps, passed, pairs = list(deps), list(passed), list(pairs)
+    parts = [v for pair in pairs for v in pair]
+    whole = lambda shape: pl.BlockSpec(shape, lambda i: (0,) * len(shape))
     first = len(parts) + len(deps)
+    joined_shapes = [(2,) + pair[0].shape for pair in pairs]
     out = pl.pallas_call(
-        functools.partial(hold_kernel, len(parts)),
+        functools.partial(hold_kernel, len(joined_shapes)),
         grid=(1,),
-        in_specs=[whole(a) for a in parts] + [anywhere] * (len(deps) + len(kept)),
-        out_specs=[anywhere] * len(passed)
-        + [second(a) for a in joined_to]
-        + [pl.BlockSpec((1, 1), lambda i: (0, 0))],
-        out_shape=[jax.ShapeDtypeStruct(v.shape, v.dtype) for v in kept]
+        in_specs=[whole(a.shape) for a in parts] + [anywhere] * (len(deps) + len(passed)),
+        out_specs=[anywhere] * len(passed) + [whole(v) for v in joined_shapes] + [whole((1, 1))],
+        out_shape=[jax.ShapeDtypeStruct(v.shape, v.dtype) for v in passed]
+        + [jax.ShapeDtypeStruct(v, bf16) for v in joined_shapes]
         + [jax.ShapeDtypeStruct((1, 1), bf16)],
-        input_output_aliases={first + k: k for k in range(len(kept))},
+        input_output_aliases={first + k: k for k in range(len(passed))},
         compiler_params=compiler_params(1),
         cost_estimate=cost(8, 8),
         name="hold",
-    )(*parts, *deps, *kept)
+    )(*parts, *deps, *passed)
     n = len(passed)
     return out[-1], list(out[:n]), list(out[n:-1])
 
 
-def path_dots(out, refs, picks, right, step, blocks):
-    per = len(refs) // len(picks)
-    for p, order in enumerate(picks):
-        mine = refs[p * per : (p + 1) * per]
-
-        @pl.when(step // (blocks // len(picks)) == p)
-        def _(mine=mine, order=order):
-            out[...] = dot(joined(mine, order), right)
+def decay_weights(out, cum, col, cbt, s, then=None):
+    sub = out.shape[0]
+    for r in range(0, sub, ROWS):
+        part = slice(r, r + ROWS)
+        first = r // 128 * 128
+        decay = jnp.exp2(jnp.minimum(cum[:, first:] - col[part], 0.0))
+        out[part, first:] = (decay * cbt[s, part, first:]).astype(bf16)
+        if then is not None:
+            then(part, first, decay)
 
 
 def scan_kernel(nx, order, hb, sub, *refs):
     xrefs = refs[:nx]
-    (nt, low, upx, num_r, hp_r, ct, bn, cbt) = refs[nx : nx + 8]
-    xc_out, mix_out, ent_out, st_out, sent_out, tok_out = refs[-6:]
+    (nt, low, pk, hp_r, ct, bn, cbt) = refs[nx : nx + 7]
+    xc_all, mix_all, ent_all, st_all, sent_all, tok_out = refs[-12:-6]
+    raw_sc, x_sc, xs_sc, turn_sc, w_sc, tap_sc = refs[-6:]
     tok_out[...] = jnp.zeros_like(tok_out)
-    chan = columns(num_r)
-    hp = hp_r[...]
     length = ct.shape[1]
-    xr = dot(joined(xrefs, order), nt[...]) + dot(upx[...], low[...], TN)
-    xc = conv_values(xr, chan)
-    xc_out[...] = xc.astype(bf16)
-    x = xc * sigmoid(xc)
-    xs = per_head(x, hp[2 * hb : 3 * hb])
-    xs_low = xs.astype(bf16)
-    state = None
-    for s in range(length // sub):
-        cols = slice(s * sub, (s + 1) * sub)
-        cum = hp[:hb, cols]
-        rows_n = jnp.transpose(jnp.concatenate([cum, cum], axis=0))
-        within = []
-        for h in range(hb):
-            gap = jnp.minimum(cum[h : h + 1] - rows_n[:, h : h + 1], 0.0)
-            weight = (jnp.exp2(gap) * cbt[s]).astype(bf16)
-            within.append(dot(xs_low[h * HEAD : (h + 1) * HEAD, cols], weight))
-        y = jnp.concatenate(within, axis=0)
-        last = cum[:, sub - 1 : sub]
-        ends = jnp.exp2(last - cum)
-        add = dot(per_head(xs[:, cols], ends).astype(bf16), bn[cols, :])
-        if s > 0:
-            ent_out[s - 1] = state
-            y = y + per_head(dot(state.astype(bf16), ct[:, cols]), jnp.exp2(cum))
-            state = per_head(state, jnp.exp2(last)) + add
-        else:
-            state = add
-        mix_out[:, cols] = y + x[:, cols] * chan[:, 4:5]
-    if length // sub == 1:
-        ent_out[0] = state
-    st_out[...] = state
-    sent_out[...] = state.astype(bf16)
-
-
-def range_specs(lo, ncb):
-    full = lambda a: pl.BlockSpec(a.shape, lambda s, c: (0,) * a.ndim)
-    per_chan = lambda a: pl.BlockSpec((None, CB, a.shape[2]), lambda s, c: (s + lo, c, 0))
-    per_blk = lambda a: pl.BlockSpec(
-        (None,) + a.shape[1:], lambda s, c: ((s + lo) * ncb + c, 0, 0)
-    )
-    return full, per_chan, per_blk
-
-
-def weight_specs(weight, ncb):
-    paths, base = weight
-    per = ncb // len(paths)
-    ops, specs = [], []
-    for p, arrays in enumerate(paths):
-        for a in arrays:
-            ops.append(a)
-            index = lambda s, c, p=p: (0, (s + base) * per + jnp.clip(c - p * per, 0, per - 1), 0)
-            specs.append(pl.BlockSpec((a.shape[0], CB, a.shape[2]), index))
-    return ops, specs
+    w_sc[...] = jnp.zeros_like(w_sc)
+
+    @pl.loop(0, xc_all.shape[0] // CB)
+    def _(b):
+        rows = pl.ds(pl.multiple_of(b * CB, CB), CB)
+        mix_out = block_rows(mix_all, b)
+        tap_sc[...] = spread(kind_rows(pk, b, 3), range(5))
+        hp = hp_r[b]
+        raw_sc[...] = dot(joined(xrefs, order, rows), nt[...]) + dot(
+            kind_rows(pk, b, 1)[...], low[...], TN
+        )
+        for r in range(0, CB, ROWS):
+            part = slice(r, r + ROWS)
+            h = r // HEAD
+            taps = [tap_sc[part, k * 128 : (k + 1) * 128] for k in range(4)]
+            xc = conv_rows(raw_sc[part, :], taps, lambda k: 3 - k)[:, HALO:]
+            xc_all[pl.ds(pl.multiple_of(b * CB + r, ROWS), ROWS), :] = xc.astype(bf16)
+            x = xc * sigmoid(xc)
+            x_sc[part, :] = x
+            xs_sc[part, :] = (x * hp[2 * hb + h : 2 * hb + h + 1]).astype(bf16)
+        state = None
+        for s in range(length // sub):
+            cols = slice(s * sub, (s + 1) * sub)
+            cum = hp[:hb, cols]
+            rows_n = jnp.transpose(jnp.concatenate([cum, cum], axis=0))
+            last = cum[:, sub - 1 : sub]
+            ends = jnp.exp2(last - cum)
+            add = dot(per_head(xs_sc[:, cols].astype(f32), ends).astype(bf16), bn[cols, :])
+            if s > 0:
+                ent_all[s - 1, rows, :] = state
+                grown = jnp.exp2(cum)
+                turn_sc[...] = dot(state.astype(bf16), ct[:, cols])
+            for h in range(hb):
+                mine = slice(h * HEAD, (h + 1) * HEAD)
+                decay_weights(w_sc, cum[h : h + 1], rows_n[:, h : h + 1], cbt, s)
+                y = dot(xs_sc[mine, cols], w_sc[...])
+                y = y + x_sc[mine, cols] * lanes_of(tap_sc[mine, 512:640], sub)
+                if s > 0:
+                    y = y + turn_sc[mine, :] * grown[h : h + 1]
+                mix_out[mine, cols] = y
+            state = add if state is None else per_head(state, jnp.exp2(last)) + add
+        if length // sub == 1:
+            ent_all[0, rows, :] = state
+        st_all[rows, :] = state
+        sent_all[rows, :] = state.astype(bf16)
 
 
 def scan_call(lo, hi, xw, part, picks, nt, low, pk, ch, hp, ct, bn, cbt, bufs, later=()):
@@ -412,23 +426,22 @@
     length = ct.shape[1]
     hb = CB // HEAD
     paths, base = xw
-    ncb = ch // CB
-    per = ncb // len(paths)
-    off = part * per
+    n_paths = len(paths)
+    per = ch // CB // n_paths
+    width = per * CB
     nsub = length // SUB
-    full = lambda a: pl.BlockSpec(a.shape, lambda s, c: (0,) * a.ndim)
-    per_chan = lambda w: pl.BlockSpec((None, CB, w), lambda s, c: (s + lo, c + off, 0))
+    full = lambda a: pl.BlockSpec(a.shape, lambda s: (0,) * a.ndim)
+    per_chan = lambda w: pl.BlockSpec((None, width, w), lambda s: (s + lo, part, 0))
     ops = list(paths[part])
     specs = [
-        pl.BlockSpec((a.shape[0], CB, a.shape[2]), lambda s, c: (0, (s + base) * per + c, 0))
-        for a in ops
+        pl.BlockSpec((a.shape[0], width, a.shape[2]), lambda s: (0, s + base, 0)) for a in ops
     ]
     nx = len(ops)
-    ops += [nt, low, pk, pk, hp, ct, bn, cbt]
-    here = lambda s, c: (s + lo, c + off)
-    specs += [full(nt), full(low), packed_spec(1, here), packed_spec(3, here)]
+    ops += [nt, low, pk, hp, ct, bn, cbt]
+    specs += [full(nt), full(low)]
+    specs += [pl.BlockSpec((None, per * 64, CB), lambda s: (s + lo, part, 0))]
     specs += [
-        pl.BlockSpec((None,) + hp.shape[1:], lambda s, c: ((s + lo) * ncb + c + off, 0, 0)),
+        pl.BlockSpec((per,) + hp.shape[1:], lambda s: ((s + lo) * n_paths + part, 0, 0)),
         full(ct), full(bn), full(cbt),
     ]
     inner_states = max(nsub - 1, 1)
@@ -437,18 +450,17 @@
         jax.ShapeDtypeStruct((slots, ch, length), f32),
         jax.ShapeDtypeStruct((slots, inner_states, ch, 128), f32),
         jax.ShapeDtypeStruct((slots, ch, 128), f32),
-        jax.ShapeDtypeStruct((slots, per * CB, 128), bf16),
+        jax.ShapeDtypeStruct((slots, width, 128), bf16),
         jax.ShapeDtypeStruct((1, 1), bf16),
     ]
     outs = [
         per_chan(length),
         per_chan(length),
-        pl.BlockSpec((None, inner_states, CB, 128), lambda s, c: (s + lo, 0, c + off, 0)),
+        pl.BlockSpec((None, inner_states, width, 128), lambda s: (s + lo, 0, part, 0)),
         per_chan(128),
-        pl.BlockSpec((None, CB, 128), lambda s, c: (s + lo, c, 0)),
-        pl.BlockSpec((1, 1), lambda s, c: (0, 0)),
+        pl.BlockSpec((None, width, 128), lambda s: (s + lo, 0, 0)),
+        pl.BlockSpec((1, 1), lambda s: (0, 0)),
     ]
-    aliases = {len(ops) + k: k for k in range(5) if bufs[k] is not None}
     given = [v for v in bufs if v is not None]
     aliases = {len(ops) + i: k for i, k in enumerate(k for k in range(5) if bufs[k] is not None)}
     ops += given + list(later)
@@ -456,12 +468,20 @@
     n = hi - lo
     out = pl.pallas_call(
         functools.partial(scan_kernel, nx, picks[part], hb, SUB),
-        grid=(n, per),
+        grid=(n,),
         in_specs=specs,
         out_specs=outs,
         out_shape=shapes,
+        scratch_shapes=[
+            pltpu.VMEM((CB, HALO + length), f32),
+            pltpu.VMEM((CB, length), f32),
+            pltpu.VMEM((CB, length), bf16),
+            pltpu.VMEM((CB, SUB), f32),
+            pltpu.VMEM((SUB, SUB), bf16),
+            pltpu.VMEM((CB, 640), f32),
+        ],
         input_output_aliases=aliases,
-        compiler_params=compiler_params(2),
+        compiler_params=compiler_params(1),
         cost_estimate=cost(
             4 * n * per * CB * 2048 * length, n * per * CB * (4096 + length * 8)
         ),
@@ -470,28 +490,37 @@
     return list(out[:5]), out[5]
 
 
-def proj_kernel(n, picks, ncb, cut, gain, *refs):
-    (right, low, up) = refs[n : n + 3]
-    num_r = refs[n + 3]
-    out, tok_o, sc = refs[-3:]
+def proj_kernel(picks, n, cut, gain, *refs):
+    (right, low, pk) = refs[n : n + 3]
+    out, tok_o = refs[-2:]
     tok_o[...] = jnp.zeros_like(tok_o)
-    path_dots(sc, refs[:n], picks, right[:, cut:], pl.program_id(1), ncb)
-    value = sc[...] + dot(up[...], low[:, cut:], TN)
-    if gain:
-        value = value * columns(num_r)[:, 5:6]
-    out[...] = value.astype(bf16)
+    per = n // len(picks)
+    blocks = out.shape[0] // CB // len(picks)
+    for p, order in enumerate(picks):
+        mine = refs[p * per : (p + 1) * per]
+        for k in range(blocks):
+            b = p * blocks + k
+            value = dot(joined(mine, order, slice(k * CB, (k + 1) * CB)), right[:, cut:])
+            value = value + dot(kind_rows(pk, b, 2 if gain else 0)[...], low[:, cut:], TN)
+            if gain:
+                value = value * lanes_of(spread(kind_rows(pk, b, 3), [5]), value.shape[1])
+            out[b * CB : (b + 1) * CB, :] = value.astype(bf16)
 
 
 def proj_call(lo, hi, weight, picks, right, low, pk, ch, cut, gain, buf, later=()):
     slots = pk.shape[0]
     length = right.shape[1] - cut
-    ncb = ch // CB
-    full, per_chan, _ = range_specs(lo, ncb)
-    ops, specs = weight_specs(weight, ncb)
+    paths, base = weight
+    share = ch // len(paths)
+    full = lambda a: pl.BlockSpec(a.shape, lambda s: (0,) * a.ndim)
+    ops = [a for arrays in paths for a in arrays]
+    specs = [
+        pl.BlockSpec((a.shape[0], share, a.shape[2]), lambda s: (0, s + base, 0)) for a in ops
+    ]
     n_w = len(ops)
-    ops += [right, low, pk, pk]
-    here = lambda s, c: (s + lo, c)
-    specs += [full(right), full(low), packed_spec(2 if gain else 0, here), packed_spec(3, here)]
+    ops += [right, low, pk]
+    specs += [full(right), full(low)]
+    specs += [pl.BlockSpec((None, ch // 4, CB), lambda s: (s + lo, 0, 0))]
     aliases = {}
     if buf is not None:
         aliases = {len(ops): 0}
@@ -501,95 +530,126 @@
     specs += [pl.BlockSpec(memory_space=pl.ANY)] * len(later)
     n = hi - lo
     return pl.pallas_call(
-        functools.partial(proj_kernel, n_w, picks, ncb, cut, gain),
-        grid=(n, ncb),
+        functools.partial(proj_kernel, picks, n_w, cut, gain),
+        grid=(n,),
         in_specs=specs,
         out_specs=[
-            pl.BlockSpec((None, CB, length), lambda s, c: (s + lo, c, 0)),
-            pl.BlockSpec((1, 1), lambda s, c: (0, 0)),
+            pl.BlockSpec((None, ch, length), lambda s: (s + lo, 0, 0)),
+            pl.BlockSpec((1, 1), lambda s: (0, 0)),
         ],
         out_shape=[
             jax.ShapeDtypeStruct((slots, ch, length), bf16),
             jax.ShapeDtypeStruct((1, 1), bf16),
         ],
-        scratch_shapes=[pltpu.VMEM((CB, length), f32)],
         input_output_aliases=aliases,
-        compiler_params=compiler_params(2),
+        compiler_params=compiler_params(1),
         cost_estimate=cost(2 * n * ch * 2048 * length, n * ch * (4096 + length * 2)),
         name="proj_slots",
     )(*ops)
 
 
+def fold(values):
+    total = values[:8]
+    for r in range(8, values.shape[0], 8):
+        total = total + values[r : r + 8]
+    return total
+
+
 def gate_kernel(hb, inner, *refs):
-    (z_r, mix_r, wgt_r, ent_r, num_r, hp_r, ct, cn) = refs[:8]
-    nout_o, dmix_o, dz_o, sl_o, sent_o = refs[8:13]
-    mix_sc, sq_sc, dot_sc = refs[13:]
-    phase = pl.program_id(0)
-    blk = pl.program_id(1) * pl.num_programs(2) + pl.program_id(2)
-    length = ct.shape[1]
-    z = z_r[...].astype(f32)
-    sig = sigmoid(z)
-    silu = z * sig
-    weighted = wgt_r[...].astype(f32)
-    cum = jnp.exp2(hp_r[hb : 2 * hb])
-
-    @pl.when((phase == 0) & (blk == 0))
+    (z_all, mix_all, wgt_all, ent_all, pk, hp_r, ct, cn) = refs[:8]
+    nout_all, dmix_all, dz_all, sl_all, sent_all = refs[8:13]
+    mix_sc, turn_sc, sq_sc, dot_sc, gain_sc = refs[13:]
+    phase, slot = pl.program_id(0), pl.program_id(1)
+    blocks = z_all.shape[0] // CB
+    per = ent_all.shape[1] // CB
+
+    def gates(ref, rows):
+        z = ref[rows, :].astype(f32)
+        sig = sigmoid(z)
+        return sig, z * sig
+
+    @pl.when((phase == 0) & (slot == 0))
     def _():
         sq_sc[...] = jnp.zeros_like(sq_sc)
         dot_sc[...] = jnp.zeros_like(dot_sc)
 
     @pl.when(phase == 0)
     def _():
-        mix = mix_r[...] + per_head(dot(ent_r[...], ct[...]), cum)
-        mix_sc[blk] = mix
-        gated = mix * silu
-        sq_sc[...] += jnp.sum((gated * gated).reshape(CB // 8, 8, length), axis=0)
-        dot_sc[...] += jnp.sum((gated * weighted).reshape(CB // 8, 8, length), axis=0)
+        @pl.loop(0, blocks)
+        def _(b):
+            z_r, mix_r, wgt_r = [block_rows(v, b) for v in (z_all, mix_all, wgt_all)]
+            cum = jnp.exp2(hp_r[b, hb : 2 * hb])
+            ent = ent_all[b // per, pl.ds(pl.multiple_of(b % per * CB, CB), CB), :]
+            turn_sc[...] = dot(ent, ct[...])
+            sq, dots = sq_sc[...], dot_sc[...]
+            for r in range(0, CB, ROWS):
+                rows = slice(r, r + ROWS)
+                h = r // HEAD
+                _, silu = gates(z_r, rows)
+                mix = mix_r[rows, :] + turn_sc[rows, :] * cum[h : h + 1]
+                mix_sc[slot * blocks + b, rows, :] = mix
+                gated = mix * silu
+                sq = sq + fold(gated * gated)
+                dots = dots + fold(gated * wgt_r[rows, :].astype(f32))
+            sq_sc[...] = sq
+            dot_sc[...] = dots
 
     @pl.when(phase == 1)
     def _():
-        r = lax.rsqrt(jnp.sum(sq_sc[...], axis=0, keepdims=True) * (1.0 / inner) + epsilon)
-        coef = r * r * r * (jnp.sum(dot_sc[...], axis=0, keepdims=True) * (1.0 / inner))
-        mix = mix_sc[blk]
-        gated = mix * silu
-        nout_o[...] = (gated * (r * columns(num_r)[:, 5:6])).astype(bf16)
-        d_gated = r * weighted - gated * coef
-        d_mix = d_gated * silu
-        dmix_o[...] = d_mix.astype(bf16)
-        dz_o[...] = (d_gated * mix * (sig + silu * (1.0 - sig))).astype(bf16)
-        adj = dot(per_head(d_mix, cum).astype(bf16), cn[...])
-        sl_o[...] = adj
-        sent_o[...] = adj.astype(bf16)
+        r_all = lax.rsqrt(jnp.sum(sq_sc[...], axis=0, keepdims=True) * (1.0 / inner) + epsilon)
+        coef = r_all * r_all * r_all * (
+            jnp.sum(dot_sc[...], axis=0, keepdims=True) * (1.0 / inner)
+        )
+
+        @pl.loop(0, blocks)
+        def _(b):
+            z_r, wgt_r = block_rows(z_all, b), block_rows(wgt_all, b)
+            nout_o, dmix_o, dz_o = [block_rows(v, b) for v in (nout_all, dmix_all, dz_all)]
+            cum = jnp.exp2(hp_r[b, hb : 2 * hb])
+            gain_sc[...] = spread(kind_rows(pk, b, 3), [5])
+            for r in range(0, CB, ROWS):
+                rows = slice(r, r + ROWS)
+                h = r // HEAD
+                sig, silu = gates(z_r, rows)
+                mix = mix_sc[slot * blocks + b, rows, :]
+                gated = mix * silu
+                gain = lanes_of(gain_sc[rows, :], gated.shape[1])
+                nout_o[rows, :] = (gated * r_all * gain).astype(bf16)
+                d_gated = r_all * wgt_r[rows, :].astype(f32) - gated * coef
+                d_mix = d_gated * silu
+                dmix_o[rows, :] = d_mix.astype(bf16)
+                dz_o[rows, :] = (d_gated * mix * (sig + silu * (1.0 - sig))).astype(bf16)
+                turn_sc[rows, :] = d_mix * cum[h : h + 1]
+            adj = dot(turn_sc[...].astype(bf16), cn[...])
+            here = pl.ds(pl.multiple_of(b * CB, CB), CB)
+            sl_all[here, :] = adj
+            sent_all[here, :] = adj.astype(bf16)
 
 
 def gate_call(z, mix, wgt, ent, pk, hp, ct, cn, inner):
     slots, ch, length = mix.shape
     ncb = ch // CB
     hb = CB // HEAD
-    full = lambda a: pl.BlockSpec(a.shape, lambda p, s, c: (0,) * a.ndim)
-    per_chan = lambda a: pl.BlockSpec((None, CB, a.shape[2]), lambda p, s, c: (s, c, 0))
-    per_blk = lambda a: pl.BlockSpec((None,) + a.shape[1:], lambda p, s, c: (s * ncb + c, 0, 0))
-    held = lambda p, s, c, k: (
-        jnp.where(p == 0, (s + k) % slots, (slots - 1 + k) % slots),
-        jnp.where(p == 0, c, ncb - 1),
-        0,
-    )
-    first = lambda a, k: pl.BlockSpec((None, CB, a.shape[2]), lambda p, s, c: held(p, s, c, k))
-    per = ncb // ent.shape[0]
-
-    def entered(p, s, c):
-        slot, block, _ = held(p, s, c, 1)
-        return (block // per, slot, block % per, 0)
-
-    later = lambda w: pl.BlockSpec(
-        (None, CB, w), lambda p, s, c: (jnp.where(p == 1, s, 0), jnp.where(p == 1, c, 0), 0)
-    )
+    full = lambda a: pl.BlockSpec(a.shape, lambda p, s: (0,) * a.ndim)
+    per_chan = lambda a: pl.BlockSpec((None, ch, a.shape[2]), lambda p, s: (s, 0, 0))
+    held = lambda p, s: jnp.where(p == 0, s, slots - 1)
+    later = lambda w: pl.BlockSpec((None, ch, w), lambda p, s: (jnp.where(p == 1, s, 0), 0, 0))
     return pl.pallas_call(
         functools.partial(gate_kernel, hb, inner),
-        grid=(2, slots, ncb),
-        in_specs=[per_chan(z), first(mix, 0), per_chan(wgt)]
-        + [pl.BlockSpec((None, None, CB, 128), entered), packed_spec(3, lambda p, s, c: (s, c))]
-        + [per_blk(hp), full(ct), full(cn)],
+        grid=(2, slots),
+        in_specs=[
+            per_chan(z),
+            pl.BlockSpec((None, ch, length), lambda p, s: (held(p, s), 0, 0)),
+            per_chan(wgt),
+            pl.BlockSpec(
+                (ent.shape[0], None) + ent.shape[2:],
+                lambda p, s: (0, (held(p, s) + 1) % slots, 0, 0),
+            ),
+            pl.BlockSpec((None, ch // 4, CB), lambda p, s: (s, 0, 0)),
+            pl.BlockSpec((ncb,) + hp.shape[1:], lambda p, s: (s, 0, 0)),
+            full(ct),
+            full(cn),
+        ],
         out_specs=[later(length), later(length), later(length), later(128), later(128)],
         out_shape=[
             jax.ShapeDtypeStruct((slots, ch, length), bf16),
@@ -600,129 +660,137 @@
         ],
         scratch_shapes=[
             pltpu.VMEM((slots * ncb, CB, length), f32),
+            pltpu.VMEM((CB, length), f32),
             pltpu.VMEM((8, length), f32),
             pltpu.VMEM((8, length), f32),
-        ],
-        compiler_params=compiler_params(3),
+            pltpu.VMEM((CB, 128), f32),
+        ],
+        compiler_params=compiler_params(2),
         cost_estimate=cost(slots * ch * length * 600, slots * ch * length * 22),
         name="gate",
     )(z, mix, wgt, ent, pk, hp, ct, cn)
 
 
-def grid_specs(ncb):
-    full = lambda a: pl.BlockSpec(a.shape, lambda s, c: (0,) * a.ndim)
-    per_chan = lambda a: pl.BlockSpec((None, CB, a.shape[2]), lambda s, c: (s, c, 0))
-    per_blk = lambda a: pl.BlockSpec((None,) + a.shape[1:], lambda s, c: (s * ncb + c, 0, 0))
-    return full, per_chan, per_blk
-
-
 def back_kernel(hb, sub, *refs):
-    (dy_r, xc_r, hp_r, ent_r, loc_r, ct, cn, bt, cbt) = refs[:9]
-    dxs_o, u1_o, u2_o, kl_o, dcb_o, db_o, dc_o = refs[-7:]
-    blk = pl.program_id(0) * pl.num_programs(1) + pl.program_id(1)
-    hp = hp_r[...]
+    (dy_all, xc_all, hp_r, ent_all, loc_all, ct, cn, bt, cbt) = refs[:9]
+    dxs_all, u1_all, u2_all, kl_all, dcb_o, db_o, dc_o = refs[-12:-5]
+    xs_sc, turn_sc, dxi_sc, dm_sc, w_sc = refs[-5:]
+    w_sc[...] = jnp.zeros_like(w_sc)
     length = ct.shape[1]
     nsub = length // sub
-
-    @pl.when(blk == 0)
+    per = ent_all.shape[1] // CB
+
+    @pl.when(pl.program_id(0) == 0)
     def _():
         dcb_o[...] = jnp.zeros_like(dcb_o)
         db_o[...] = jnp.zeros_like(db_o)
         dc_o[...] = jnp.zeros_like(dc_o)
 
-    xc = xc_r[...].astype(f32)
-    x = xc * sigmoid(xc)
-    xs = per_head(x, hp[2 * hb : 3 * hb])
-    xs_low = xs.astype(bf16)
-    adj = None
-    kl = []
-    for s in reversed(range(nsub)):
-        cols = slice(s * sub, (s + 1) * sub)
-        cum = hp[:hb, cols]
-        rows_n = jnp.transpose(jnp.concatenate([cum, cum], axis=0))
-        ecum = jnp.exp2(cum)
-        last = cum[:, sub - 1 : sub]
-        state = ent_r[...].astype(f32)
-        if s > 0:
-            before = hp[hb : 2 * hb, s * sub - 1 : s * sub]
-            state = loc_r[s - 1] + per_head(state, jnp.exp2(before))
-        state_low = state.astype(bf16)
-        dy_low = dy_r[:, cols]
-        dy = dy_low.astype(f32)
-        y_in = per_head(dot(state_low, ct[:, cols]), ecum)
-        ed = per_head(dy, ecum).astype(bf16)
-        dc_o[:, cols] += dot(state_low, ed, TN)
-        dxw, yw = [], []
-        for h in range(hb):
-            hs = slice(h * HEAD, (h + 1) * HEAD)
-            gap = jnp.minimum(cum[h : h + 1] - rows_n[:, h : h + 1], 0.0)
-            decay = jnp.exp2(gap)
-            weight = (decay * cbt[s]).astype(bf16)
-            yw.append(dot(xs_low[hs, cols], weight))
-            dxw.append(dot(dy_low[hs], weight, NT))
-            dcb_o[s] += decay * dot(xs_low[hs, cols], dy_low[hs], TN)
-        yw = jnp.concatenate(yw, axis=0)
-        dxs = jnp.concatenate(dxw, axis=0)
-        u1_o[:, cols] = head_sums(dy * (yw + y_in) - xs_low[:, cols].astype(f32) * dxs, hb)
-        add = dot(ed, cn[cols, :])
-        if adj is None:
-            u2_o[:, cols] = jnp.zeros((hb, sub), f32)
-            kl.append(jnp.zeros((hb, 128), f32))
-            adj = add
-        else:
+    @pl.loop(0, dy_all.shape[0] // CB)
+    def _(b):
+        rows = pl.ds(pl.multiple_of(b * CB, CB), CB)
+        dy_r, dxs_o = block_rows(dy_all, b), block_rows(dxs_all, b)
+        u1_o, u2_o, kl_o = u1_all.at[b], u2_all.at[b], kl_all.at[b]
+        hp = hp_r[b]
+        for r in range(0, CB, ROWS):
+            part = slice(r, r + ROWS)
+            h = r // HEAD
+            xc = xc_all[pl.ds(pl.multiple_of(b * CB + r, ROWS), ROWS), :].astype(f32)
+            x = xc * sigmoid(xc)
+            xs_sc[part, :] = (x * hp[2 * hb + h : 2 * hb + h + 1]).astype(bf16)
+        adj = None
+        kl = []
+        for s in reversed(range(nsub)):
+            cols = slice(s * sub, (s + 1) * sub)
+            cum = hp[:hb, cols]
+            rows_n = jnp.transpose(jnp.concatenate([cum, cum], axis=0))
+            ecum = jnp.exp2(cum)
+            last = cum[:, sub - 1 : sub]
             ends = jnp.exp2(last - cum)
-            adj_low = adj.astype(bf16)
-            dxi = per_head(dot(adj_low, bt[:, cols]), ends)
-            xs_s = xs[:, cols]
-            u2_o[:, cols] = head_sums(xs_s * dxi, hb)
-            kl.append(head_sums(adj * state, hb) * jnp.exp2(last))
-            db_o[:, cols] += dot(adj_low, per_head(xs_s, ends).astype(bf16), TN)
-            dxs = dxs + dxi
-            adj = per_head(adj, jnp.exp2(last)) + add
-        dxs_o[:, cols] = dxs
-    for s in range(nsub):
-        kl_o[:, s * 128 : (s + 1) * 128] = kl[nsub - 1 - s]
-
-
-def back_call(lo, hi, dy, xc, hp, ent, loc, ct, cn, bt, cbt, bufs, later=()):
+            ent = ent_all[b // per, pl.ds(pl.multiple_of(b % per * CB, CB), CB), :]
+            state = ent.astype(f32)
+            if s > 0:
+                before = hp[hb : 2 * hb, s * sub - 1 : s * sub]
+                state = loc_all[s - 1, rows, :] + per_head(state, jnp.exp2(before))
+            state_low = state.astype(bf16)
+            turn_sc[...] = dot(state_low, ct[:, cols])
+            ed = per_head(dy_r[:, cols].astype(f32), ecum).astype(bf16)
+            dc_o[:, cols] += dot(state_low, ed, TN)
+            add = dot(ed, cn[cols, :])
+            if adj is not None:
+                adj_low = adj.astype(bf16)
+                dxi_sc[...] = dot(adj_low, bt[:, cols])
+                db_o[:, cols] += dot(
+                    adj_low, per_head(xs_sc[:, cols].astype(f32), ends).astype(bf16), TN
+                )
+            u1, u2 = [], []
+            for h in range(hb):
+                mine = slice(h * HEAD, (h + 1) * HEAD)
+                dy_low, xs_low = dy_r[mine, cols], xs_sc[mine, cols]
+                dm_sc[...] = dot(xs_low, dy_low, TN)
+
+                def gather(part, first, decay):
+                    dcb_o[s, part, first:] += decay * dm_sc[part, first:]
+
+                decay_weights(w_sc, cum[h : h + 1], rows_n[:, h : h + 1], cbt, s, gather)
+                xs = xs_low.astype(f32)
+                y = dot(xs_low, w_sc[...]) + turn_sc[mine, :] * ecum[h : h + 1]
+                dxs = dot(dy_low, w_sc[...], NT)
+                u1.append(
+                    jnp.sum(dy_low.astype(f32) * y - xs * dxs, axis=0, keepdims=True)
+                )
+                if adj is not None:
+                    dxi = dxi_sc[mine, :] * ends[h : h + 1]
+                    u2.append(jnp.sum(xs * dxi, axis=0, keepdims=True))
+                    dxs = dxs + dxi
+                dxs_o[mine, cols] = dxs
+            u1_o[:, cols] = jnp.concatenate(u1, axis=0)
+            if adj is None:
+                u2_o[:, cols] = jnp.zeros((hb, sub), f32)
+                kl.append(jnp.zeros((hb, 128), f32))
+                adj = add
+            else:
+                u2_o[:, cols] = jnp.concatenate(u2, axis=0)
+                kl.append(head_sums(adj * state, hb) * jnp.exp2(last))
+                adj = per_head(adj, jnp.exp2(last)) + add
+        for s in range(nsub):
+            kl_o[:, s * 128 : (s + 1) * 128] = kl[nsub - 1 - s]
+
+
+def back_call(dy, xc, hp, ent, loc, ct, cn, bt, cbt, later=()):
     slots, ch, length = dy.shape
     ncb = ch // CB
     hb = CB // HEAD
     nsub = length // SUB
-    full = lambda a: pl.BlockSpec(a.shape, lambda s, c: (0,) * a.ndim)
-    per_chan = lambda a: pl.BlockSpec((None, CB, a.shape[2]), lambda s, c: (s + lo, c, 0))
-    per_blk = lambda a: pl.BlockSpec(
-        (None,) + a.shape[1:], lambda s, c: ((s + lo) * ncb + c, 0, 0)
-    )
-    blk_out = lambda w: pl.BlockSpec((None, hb, w), lambda s, c: ((s + lo) * ncb + c, 0, 0))
-    loc_spec = pl.BlockSpec((None, loc.shape[1], CB, 128), lambda s, c: (s + lo, 0, c, 0))
+    full = lambda a: pl.BlockSpec(a.shape, lambda s: (0,) * a.ndim)
+    per_chan = lambda w: pl.BlockSpec((None, ch, w), lambda s: (s, 0, 0))
+    blk_out = lambda w: pl.BlockSpec((ncb, hb, w), lambda s: (s, 0, 0))
     blocks = slots * ncb
-    ops = [dy, xc, hp, ent, loc, ct, cn, bt, cbt]
-    per = ncb // ent.shape[0]
-    entered = pl.BlockSpec(
-        (None, None, CB, 128), lambda s, c: (c // per, (s + lo + 1) % slots, c % per, 0)
-    )
-    specs = [per_chan(dy), per_chan(xc), per_blk(hp), entered, loc_spec]
-    specs += [full(ct), full(cn), full(bt), full(cbt)]
-    aliases = {}
-    if bufs is not None:
-        aliases = {len(ops) + k: k for k in range(4)}
-        ops += list(bufs)
-        specs += [pl.BlockSpec(memory_space=pl.ANY)] * 4
-    ops += list(later)
-    specs += [pl.BlockSpec(memory_space=pl.ANY)] * len(later)
     return pl.pallas_call(
         functools.partial(back_kernel, hb, SUB),
-        grid=(hi - lo, ncb),
-        in_specs=specs,
+        grid=(slots,),
+        in_specs=[
+            per_chan(length),
+            per_chan(length),
+            pl.BlockSpec((ncb,) + hp.shape[1:], lambda s: (s, 0, 0)),
+            pl.BlockSpec(
+                (ent.shape[0], None) + ent.shape[2:], lambda s: (0, (s + 1) % slots, 0, 0)
+            ),
+            pl.BlockSpec((None,) + loc.shape[1:], lambda s: (s, 0, 0, 0)),
+            full(ct),
+            full(cn),
+            full(bt),
+            full(cbt),
+        ]
+        + [pl.BlockSpec(memory_space=pl.ANY)] * len(later),
         out_specs=[
-            pl.BlockSpec((None, CB, length), lambda s, c: (s + lo, c, 0)),
+            per_chan(length),
             blk_out(length),
             blk_out(length),
             blk_out(128 * nsub),
-            pl.BlockSpec((nsub, SUB, SUB), lambda s, c: (0, 0, 0)),
-            pl.BlockSpec((128, length), lambda s, c: (0, 0)),
-            pl.BlockSpec((128, length), lambda s, c: (0, 0)),
+            pl.BlockSpec((nsub, SUB, SUB), lambda s: (0, 0, 0)),
+            pl.BlockSpec((128, length), lambda s: (0, 0)),
+            pl.BlockSpec((128, length), lambda s: (0, 0)),
         ],
         out_shape=[
             jax.ShapeDtypeStruct((slots, ch, length), f32),
@@ -733,57 +801,81 @@
             jax.ShapeDtypeStruct((128, length), f32),
             jax.ShapeDtypeStruct((128, length), f32),
         ],
-        input_output_aliases=aliases,
-        compiler_params=compiler_params(2),
-        cost_estimate=cost((hi - lo) * ch * length * SUB * 20, (hi - lo) * ch * length * 8),
+        scratch_shapes=[
+            pltpu.VMEM((CB, length), bf16),
+            pltpu.VMEM((CB, SUB), f32),
+            pltpu.VMEM((CB, SUB), f32),
+            pltpu.VMEM((SUB, SUB), f32),
+            pltpu.VMEM((SUB, SUB), bf16),
+        ],
+        compiler_params=compiler_params(1),
+        cost_estimate=cost(slots * ch * length * SUB * 20, slots * ch * length * 8),
         name="state_back",
-    )(*ops)
+    )(dy, xc, hp, ent, loc, ct, cn, bt, cbt, *later)
 
 
 def finish_kernel(hb, *refs):
-    (dxs_r, dy_r, xc_r, dz_r, num_r, hp_r, ent_r, adj_r, bt, upz, upx, low) = refs[:12]
-    dx_o, tail_o, head_o, gx_o, dl_o, dd_o, u2_o, kf_o, db_o = refs[-9:]
-    blk = pl.program_id(0) * pl.num_programs(1) + pl.program_id(1)
-    chan = columns(num_r)
-    hp = hp_r[...]
+    (dxs_all, dy_all, xc_all, dz_all, pk, hp_r, ent_all, adj_all, bt, low) = refs[:10]
+    dx_all, tail_all, head_all, gx_all, dl_o, dd_all, u2_all, kf_all, db_o = refs[-14:-5]
+    turn_sc, xs_sc, head_sc, all_sc, tap_sc = refs[-5:]
     length = bt.shape[1]
-
-    @pl.when(blk == 0)
+    per = ent_all.shape[1] // CB
+
+    @pl.when(pl.program_id(0) == 0)
     def _():
         db_o[...] = jnp.zeros_like(db_o)
         dl_o[...] = jnp.zeros_like(dl_o)
 
-    xc = xc_r[...].astype(f32)
-    sig = sigmoid(xc)
-    x = xc * sig
-    delta = hp[2 * hb : 3 * hb]
-    xs = per_head(x, delta)
-    total = hp[hb : 2 * hb]
-    last = total[:, length - 1 : length]
-    ends = jnp.exp2(last - total)
-    adj_low = adj_r[...]
-    extra = per_head(dot(adj_low, bt[...]), ends)
-    u2_o[...] = head_sums(xs * extra, hb)
-    kf_o[...] = head_sums(adj_low.astype(f32) * ent_r[...].astype(f32), hb) * jnp.exp2(last)
-    db_o[...] += dot(adj_low, per_head(xs, ends).astype(bf16), TN)
-    dxs = dxs_r[...] + extra
-    dd_o[...] = head_sums(x * dxs, hb)
-    dx = per_head(dxs, delta) + dy_r[...].astype(f32) * chan[:, 4:5]
-    dconv = dx * (sig + x * (1.0 - sig))
-    head_o[...] = jnp.transpose(dconv[:, :HALO])[:8]
-    none = jnp.zeros((CB, HALO), f32)
-    ext = jnp.concatenate([none, dconv, none], axis=1)
-    width = ext.shape[1]
-    out = ext * chan[:, 3:4]
-    for k in range(3):
-        out = out + pltpu.roll(ext, width - (3 - k), 1) * chan[:, k : k + 1]
-    out = out[:, : HALO + length]
-    tail_o[...] = out[:, length:]
-    all_low = out.astype(bf16)
-    dx_o[...] = all_low[:, HALO:]
-    gx_o[...] = dot(low[...], all_low, NT)
-    dl_o[...] += dot(upx[...], all_low)
-    dl_o[:, HALO:] += dot(upz[...], dz_r[...])
+    for b in range(dx_all.shape[0] // CB):
+        rows = slice(b * CB, (b + 1) * CB)
+        tap_sc[...] = spread(kind_rows(pk, b, 3), range(5))
+        hp = hp_r[b]
+        delta = hp[2 * hb : 3 * hb]
+        total = hp[hb : 2 * hb]
+        last = total[:, length - 1 : length]
+        ends = jnp.exp2(last - total)
+        adj_low = adj_all[rows, :]
+        ent = ent_all[b // per, b % per * CB : (b % per + 1) * CB, :]
+        turn_sc[...] = dot(adj_low, bt[...])
+        kf_all[b] = head_sums(adj_low.astype(f32) * ent.astype(f32), hb) * jnp.exp2(last)
+        u2, dd = [], []
+        for h in range(hb):
+            u2_h = jnp.zeros((8, length), f32)
+            dd_h = jnp.zeros((8, length), f32)
+            for r in range(h * HEAD, (h + 1) * HEAD, ROWS):
+                part = slice(r, r + ROWS)
+                whole = slice(b * CB + r, b * CB + r + ROWS)
+                xc = xc_all[whole, :].astype(f32)
+                sig = sigmoid(xc)
+                x = xc * sig
+                xs = x * delta[h : h + 1]
+                extra = turn_sc[part, :] * ends[h : h + 1]
+                u2_h = u2_h + fold(xs * extra)
+                xs_sc[part, :] = (xs * ends[h : h + 1]).astype(bf16)
+                dxs = dxs_all[whole, :] + extra
+                dd_h = dd_h + fold(x * dxs)
+                skip = lanes_of(tap_sc[part, 512:640], length)
+                dx = dxs * delta[h : h + 1] + dy_all[whole, :].astype(f32) * skip
+                dconv = dx * (sig + x * (1.0 - sig))
+                head_sc[part, :] = dconv[:, :HALO]
+                none = jnp.zeros((ROWS, HALO), f32)
+                ext = jnp.concatenate([none, dconv, none], axis=1)
+                taps = [tap_sc[part, k * 128 : (k + 1) * 128] for k in range(4)]
+                out = conv_rows(ext, taps, lambda k: ext.shape[1] - (3 - k))
+                tail_all[whole, :] = out[:, length : HALO + length]
+                all_low = out[:, : HALO + length].astype(bf16)
+                all_sc[part, :] = all_low
+                dx_all[whole, :] = all_low[:, HALO:]
+            u2.append(jnp.sum(u2_h, axis=0, keepdims=True))
+            dd.append(jnp.sum(dd_h, axis=0, keepdims=True))
+        u2_all[b] = jnp.concatenate(u2, axis=0)
+        dd_all[b] = jnp.concatenate(dd, axis=0)
+        db_o[...] += dot(adj_low, xs_sc[...], TN)
+        head_all[:, rows] = jnp.transpose(head_sc[...])[:8]
+        all_low = all_sc[...]
+        gx_all[:, rows] = dot(low[...], all_low, NT)
+        dl_o[...] += dot(kind_rows(pk, b, 1)[...], all_low)
+        dl_o[:, HALO:] += dot(kind_rows(pk, b, 0)[...], dz_all[rows, :])
 
 
 def finish_call(dxs, dy, xc, dz, pk, hp, ent, adj, bt, low, later):
@@ -791,34 +883,39 @@
     ncb = ch // CB
     hb = CB // HEAD
     rank = low.shape[0]
-    full, per_chan, per_blk = grid_specs(ncb)
-    blk_out = lambda w: pl.BlockSpec((None, hb, w), lambda s, c: (s * ncb + c, 0, 0))
-    chan_out = lambda w: pl.BlockSpec((None, CB, w), lambda s, c: (s, c, 0))
-    turned = lambda w: pl.BlockSpec((None, w, CB), lambda s, c: (s, 0, c))
-    moved = lambda k: pl.BlockSpec((None, CB, 128), lambda s, c: ((s + k) % slots, c, 0))
-    per = ncb // ent.shape[0]
-    entered = pl.BlockSpec(
-        (None, None, CB, 128), lambda s, c: (c // per, (s + 1) % slots, c % per, 0)
-    )
-    here = lambda s, c: (s, c)
+    full = lambda a: pl.BlockSpec(a.shape, lambda s: (0,) * a.ndim)
+    chan = lambda w: pl.BlockSpec((None, ch, w), lambda s: (s, 0, 0))
+    blk_out = lambda w: pl.BlockSpec((ncb, hb, w), lambda s: (s, 0, 0))
+    turned = lambda w: pl.BlockSpec((None, w, ch), lambda s: (s, 0, 0))
     blocks = slots * ncb
     return pl.pallas_call(
         functools.partial(finish_kernel, hb),
-        grid=(slots, ncb),
-        in_specs=[per_chan(dxs), per_chan(dy), per_chan(xc), per_chan(dz), packed_spec(3, here)]
-        + [per_blk(hp), entered, moved(slots - 1), full(bt)]
-        + [packed_spec(0, here), packed_spec(1, here), full(low)]
+        grid=(slots,),
+        in_specs=[
+            chan(length),
+            chan(length),
+            chan(length),
+            chan(length),
+            pl.BlockSpec((None, ch // 4, CB), lambda s: (s, 0, 0)),
+            pl.BlockSpec((ncb,) + hp.shape[1:], lambda s: (s, 0, 0)),
+            pl.BlockSpec(
+                (ent.shape[0], None) + ent.shape[2:], lambda s: (0, (s + 1) % slots, 0, 0)
+            ),
+            pl.BlockSpec((None, ch, 128), lambda s: ((s + slots - 1) % slots, 0, 0)),
+            full(bt),
+            full(low),
+        ]
         + [pl.BlockSpec(memory_space=pl.ANY)] * len(later),
         out_specs=[
-            chan_out(length),
-            chan_out(HALO),
+            chan(length),
+            chan(HALO),
             turned(8),
             turned(rank),
-            pl.BlockSpec((rank, HALO + length), lambda s, c: (0, 0)),
+            pl.BlockSpec((rank, HALO + length), lambda s: (0, 0)),
             blk_out(length),
             blk_out(length),
             blk_out(128),
-            pl.BlockSpec((128, length), lambda s, c: (0, 0)),
+            pl.BlockSpec((128, length), lambda s: (0, 0)),
         ],
         out_shape=[
             jax.ShapeDtypeStruct((slots, ch, length), bf16),
@@ -831,10 +928,17 @@
             jax.ShapeDtypeStruct((blocks, hb, 128), f32),
             jax.ShapeDtypeStruct((128, length), f32),
         ],
-        compiler_params=compiler_params(2),
+        scratch_shapes=[
+            pltpu.VMEM((CB, length), f32),
+            pltpu.VMEM((CB, length), bf16),
+            pltpu.VMEM((CB, HALO), f32),
+            pltpu.VMEM((CB, HALO + length), bf16),
+            pltpu.VMEM((CB, 640), f32),
+        ],
+        compiler_params=compiler_params(1),
         cost_estimate=cost(slots * ch * length * 700, slots * ch * length * 14),
         name="finish_back",
-    )(dxs, dy, xc, dz, pk, hp, ent, adj, bt, pk, pk, low, *later)
+    )(dxs, dy, xc, dz, pk, hp, ent, adj, bt, low, *later)
 
 
 def glue_kernel(flat_order, quick, sub, *refs):
@@ -918,36 +1022,34 @@
     )(*args, sc, dl, nt)
 
 
-def add_products(acc, turned, sets, picks, n_left, refs, slot, c):
+def add_products(acc, turned, sets, picks, refs, slot):
     at = 0
     for lo, hi, per in sets:
-        for p, order in enumerate(picks):
-            groups = [refs[at + g * per : at + (g + 1) * per] for g in range(n_left)]
-            at += n_left * per
-
-            @pl.when((slot >= lo) & (slot < hi) & (c == p))
-            def _(groups=groups, order=order):
-                off = 0
-                for k, b in order:
-                    parts = [g[k][b] for g in groups]
-                    w = parts[0] if n_left == 1 else jnp.concatenate(parts, axis=0)
-                    acc[:, off : off + w.shape[1]] += dot(turned, w)
-                    off += w.shape[1]
-
-
-def product_specs(weights, paths, block):
+        groups = [refs[at + p * per : at + (p + 1) * per] for p in range(len(picks))]
+        at += len(picks) * per
+
+        @pl.when((slot >= lo) & (slot < hi))
+        def _(groups=groups):
+            off = 0
+            for i in range(len(picks[0])):
+                parts = []
+                for group, order in zip(groups, picks):
+                    k, b = order[i]
+                    parts.append(group[k][b])
+                w = parts[0] if len(parts) == 1 else jnp.concatenate(parts, axis=0)
+                acc[:, off : off + w.shape[1]] += dot(turned, w)
+                off += w.shape[1]
+
+
+def product_specs(weights, share):
     ops, specs, sets = [], [], []
-    for (lo, hi), groups in weights:
-        sets.append((lo, hi, len(groups[0][0][0])))
-        for p in range(paths):
-            for arrays, base in groups:
-                for a in arrays[p]:
-                    ops.append(a)
-
-                    def index(s, c, lo=lo, hi=hi, base=base):
-                        return (0, base + jnp.clip(s, lo, hi - 1) - lo, 0)
-
-                    specs.append(pl.BlockSpec((a.shape[0], block, a.shape[2]), index))
+    for (lo, hi), paths, base in weights:
+        sets.append((lo, hi, len(paths[0])))
+        for arrays in paths:
+            for a in arrays:
+                ops.append(a)
+                index = lambda s, lo=lo, hi=hi, base=base: (0, base + jnp.clip(s, lo, hi - 1) - lo, 0)
+                specs.append(pl.BlockSpec((a.shape[0], share, a.shape[2]), index))
     return ops, specs, sets
 
 
@@ -955,11 +1057,11 @@
     (sc, nout, dn, bh, up, tok, masked) = refs[:7]
     wrefs = refs[7 : 7 + n_w]
     mixed_o, gdo_o, guo_o, acc, hid = refs[-5:]
-    slot, c = pl.program_id(0), pl.program_id(1)
+    slot = pl.program_id(0)
     rank = up.shape[0]
     length, width = tok.shape
 
-    @pl.when((slot == 0) & (c == 0))
+    @pl.when(slot == 0)
     def _():
         acc[...] = jnp.zeros_like(acc)
         hid[...] = jnp.zeros_like(hid)
@@ -969,9 +1071,9 @@
     for part in range(dn.shape[0] // 64):
         mine = slice(part * CB, (part + 1) * CB)
         hid[...] += dot(dn[part * 64 + 32 : part * 64 + 48, :], values[mine])
-    add_products(acc, jnp.transpose(values), sets, picks, 1, wrefs, slot, c)
-
-    @pl.when((slot == pl.num_programs(0) - 1) & (c == pl.num_programs(1) - 1))
+    add_products(acc, jnp.transpose(values), sets, picks, wrefs, slot)
+
+    @pl.when(slot == pl.num_programs(0) - 1)
     def _():
         low = hid[...].astype(bf16)
         guo_o[...] = dot(low, masked[...])
@@ -986,21 +1088,20 @@
 def output_call(sc, nout, pk, bh, up, tok, masked, weights, picks, flat, quick):
     slots, ch, length = nout.shape
     rank, width = up.shape
-    paths = len(picks)
-    block = ch // paths
-    full = lambda a: pl.BlockSpec(a.shape, lambda s, c: (0,) * a.ndim)
-    chan = lambda a: pl.BlockSpec((None, block, a.shape[2]), lambda s, c: (s, c, 0))
-    w_ops, w_specs, sets = product_specs(weights, paths, block)
+    block = ch
+    full = lambda a: pl.BlockSpec(a.shape, lambda s: (0,) * a.ndim)
+    chan = lambda a: pl.BlockSpec((None, block, a.shape[2]), lambda s: (s, 0, 0))
+    w_ops, w_specs, sets = product_specs(weights, ch // len(picks))
     return pl.pallas_call(
         functools.partial(output_kernel, sets, picks, flat, quick, len(w_ops)),
-        grid=(slots, paths),
+        grid=(slots,),
         in_specs=[pl.BlockSpec(memory_space=pltpu.SMEM), chan(nout)]
-        + [pl.BlockSpec((None, block // 4, CB), lambda s, c: (s, c, 0)), full(bh)]
+        + [pl.BlockSpec((None, block // 4, CB), lambda s: (s, 0, 0)), full(bh)]
         + [full(up), full(tok), full(masked)] + w_specs,
         out_specs=[
-            pl.BlockSpec((length, width), lambda s, c: (0, 0)),
-            pl.BlockSpec((None, rank, block), lambda s, c: (s, 0, c)),
-            pl.BlockSpec((rank, width), lambda s, c: (0, 0)),
+            pl.BlockSpec((length, width), lambda s: (0, 0)),
+            pl.BlockSpec((None, rank, block), lambda s: (s, 0, 0)),
+            pl.BlockSpec((rank, width), lambda s: (0, 0)),
         ],
         out_shape=[
             jax.ShapeDtypeStruct((length, width), bf16),
@@ -1008,7 +1109,7 @@
             jax.ShapeDtypeStruct((rank, width), f32),
         ],
         scratch_shapes=[pltpu.VMEM((length, width), f32), pltpu.VMEM((rank, length), f32)],
-        compiler_params=compiler_params(2),
+        compiler_params=compiler_params(1),
         cost_estimate=cost(2 * slots * ch * length * width, slots * ch * width * 2),
         name="output",
     )(sc, nout, pk, bh, up, tok, masked, *w_ops)
@@ -1017,40 +1118,39 @@
 def gate_back_kernel(sets, picks, n_w, *refs):
     dz, low = refs[:2]
     acc, gz_o = refs[-2:]
-    slot, c = pl.program_id(0), pl.program_id(1)
-
-    @pl.when((slot == 0) & (c == 0))
+    slot = pl.program_id(0)
+
+    @pl.when(slot == 0)
     def _():
         acc[...] = jnp.zeros_like(acc)
 
     gz_o[...] = dot(low[:, HALO:], dz[...], NT)
-    add_products(acc, jnp.transpose(dz[...]), sets, picks, 1, refs[2 : 2 + n_w], slot, c)
+    add_products(acc, jnp.transpose(dz[...]), sets, picks, refs[2 : 2 + n_w], slot)
 
 
 def gate_back_call(dz, low, weights, picks, width, later=()):
     slots, ch, length = dz.shape
     rank = low.shape[0]
-    paths = len(picks)
-    block = ch // paths
-    w_ops, w_specs, sets = product_specs(weights, paths, block)
+    block = ch
+    w_ops, w_specs, sets = product_specs(weights, ch // len(picks))
     return pl.pallas_call(
         functools.partial(gate_back_kernel, sets, picks, len(w_ops)),
-        grid=(slots, paths),
+        grid=(slots,),
         in_specs=[
-            pl.BlockSpec((None, block, length), lambda s, c: (s, c, 0)),
-            pl.BlockSpec(low.shape, lambda s, c: (0, 0)),
+            pl.BlockSpec((None, block, length), lambda s: (s, 0, 0)),
+            pl.BlockSpec(low.shape, lambda s: (0, 0)),
         ]
         + w_specs
         + [pl.BlockSpec(memory_space=pl.ANY)] * len(later),
         out_specs=[
-            pl.BlockSpec((length, width), lambda s, c: (0, 0)),
-            pl.BlockSpec((None, rank, block), lambda s, c: (s, 0, c)),
+            pl.BlockSpec((length, width), lambda s: (0, 0)),
+            pl.BlockSpec((None, rank, block), lambda s: (s, 0, 0)),
         ],
         out_shape=[
             jax.ShapeDtypeStruct((length, width), f32),
             jax.ShapeDtypeStruct((slots, rank, ch), f32),
         ],
-        compiler_params=compiler_params(2),
+        compiler_params=compiler_params(1),
         cost_estimate=cost(2 * slots * ch * length * width, 2 * slots * ch * width),
         name="gate_back",
     )(dz, low, *w_ops, *later)
@@ -1072,11 +1172,11 @@
     smalls = refs[17 : 17 + n_small]
     wrefs = refs[17 + n_small : 17 + n_small + n_w]
     out, acc = refs[-2:]
-    slot, c = pl.program_id(0), pl.program_id(1)
+    slot = pl.program_id(0)
     length, width = tok.shape
     cut = length - HALO
 
-    @pl.when((slot == 0) & (c == 0))
+    @pl.when(slot == 0)
     def _():
         d_low = jnp.concatenate(
             [dl[:, HALO:length], dl[:, length:] + near_dl[:, :HALO]], axis=1
@@ -1106,9 +1206,9 @@
     )
     last = tail[...] + beyond(near[...], taps, block)
     dx_all = jnp.concatenate([dx[:, :cut], last.astype(bf16)], axis=1)
-    add_products(acc, jnp.transpose(dx_all), sets, picks, 1, wrefs, slot, c)
-
-    @pl.when((slot == pl.num_programs(0) - 1) & (c == pl.num_programs(1) - 1))
+    add_products(acc, jnp.transpose(dx_all), sets, picks, wrefs, slot)
+
+    @pl.when(slot == pl.num_programs(0) - 1)
     def _():
         root = root_r[...]
         mean = None
@@ -1132,31 +1232,30 @@
 ):
     slots, ch, length = dx.shape
     width = tok.shape[1]
-    paths = len(picks)
-    block = ch // paths
+    block = ch
     rank = dl.shape[0]
     once = pl.Buffered(1)
-    full = lambda a: pl.BlockSpec(a.shape, lambda s, c: (0,) * a.ndim, pipeline_mode=once)
-    chan = lambda a: pl.BlockSpec((None, block, a.shape[2]), lambda s, c: (s, c, 0))
-    w_ops, w_specs, sets = product_specs(weights, paths, block)
-    near_rows = pl.BlockSpec((8, block), lambda s, c: ((s + slots - 1) % slots, c))
-    near_maps = pl.BlockSpec((8, ch), lambda s, c: (slots, 0), pipeline_mode=once)
+    full = lambda a: pl.BlockSpec(a.shape, lambda s: (0,) * a.ndim, pipeline_mode=once)
+    chan = lambda a: pl.BlockSpec((None, block, a.shape[2]), lambda s: (s, 0, 0))
+    w_ops, w_specs, sets = product_specs(weights, ch // len(picks))
+    near_rows = pl.BlockSpec((8, block), lambda s: ((s + slots - 1) % slots, 0))
+    near_maps = pl.BlockSpec((8, ch), lambda s: (slots, 0), pipeline_mode=once)
     near_low = pl.BlockSpec(
-        (rank, ch), lambda s, c: (((slots + 1) * 8 + rank - 1) // rank, 0), pipeline_mode=once
+        (rank, ch), lambda s: (((slots + 1) * 8 + rank - 1) // rank, 0), pipeline_mode=once
     )
     return pl.pallas_call(
         functools.partial(input_kernel, sets, picks, flat, quick, len(w_ops), len(smalls)),
-        grid=(slots, paths),
+        grid=(slots,),
         in_specs=[pl.BlockSpec(memory_space=pltpu.SMEM), chan(dx), chan(tail), near_rows]
-        + [pl.BlockSpec((None, block // 4, CB), lambda s, c: (s, c, 0))]
+        + [pl.BlockSpec((None, block // 4, CB), lambda s: (s, 0, 0))]
         + [full(left), full(maps_tail), near_maps, full(maps_taps), full(dl), near_low]
         + [full(a) for a in [down, root, gain, tok, masked, start] + list(smalls)]
         + w_specs
         + [pl.BlockSpec(memory_space=pl.ANY)] * len(later),
-        out_specs=pl.BlockSpec((length, width), lambda s, c: (0, 0)),
+        out_specs=pl.BlockSpec((length, width), lambda s: (0, 0)),
         out_shape=jax.ShapeDtypeStruct((length, width), bf16),
         scratch_shapes=[pltpu.VMEM((length, width), f32)],
-        compiler_params=compiler_params(2),
+        compiler_params=compiler_params(1),
         cost_estimate=cost(2 * slots * ch * length * width, 2 * slots * ch * width),
         name="input_back",
     )(
@@ -1292,9 +1391,6 @@
     def pass_one(ab):
         return [flip(ab[0], 2), flip(ab[1], 4)]
 
-    def room(ab):
-        return [jnp.stack([v, jnp.zeros_like(v)]) for v in ab]
-
     def pass_two(ab):
         return [flip(ab[0], 4), flip(ab[1], 2)]
 
@@ -1342,7 +1438,7 @@
         )
         all_z = lax.all_gather(wt[0], "tensor", axis=0)
         all_o = lax.all_gather(out_weight, "tensor", axis=0)
-        token, _, own = hold([], [], room(own), got)
+        token, _, own = hold([], [], zip(own, got))
         two = pass_two(own)
         swapped = pass_core(own)
         marks = [ch, ch + 64 * ncb, ch + 64 * ncb + hs]
@@ -1352,8 +1448,7 @@
         far_x = halves(
             [v[:ch] for v in all_x[1:]], ([v[marks[1] : marks[2]] for v in all_x[1:]], ())
         )
-        wide_x = room(far_x)
-        token, passed, _ = hold(wide_x + swapped + [pk, last_rows], two + far_x)
+        token, passed, _ = hold(swapped, two + far_x)
         two, far_x = passed[:2], passed[2:]
         own = own + two
         swapped = swapped + pass_core(two)
@@ -1372,7 +1467,7 @@
     )
     if quick:
         own = as_paths(own, swapped)
-        token, _, far_x = hold([nt] + own[0] + own[1], [], wide_x, got)
+        token, _, far_x = hold([nt, pk] + own[0] + own[1], [], zip(far_x, got))
         two = pass_two(far_x)
         swapped = pass_core(far_x)
         held = [token]
@@ -1407,18 +1502,16 @@
         )
         sent_b = bufs[4]
         far_z = halves(slot_order(all_z, 1, place + token[0, 0].astype(jnp.int32)))
-        wide_z = room(far_z)
-
-        token, passed, _ = hold([done] + wide_z + swapped, two + far_z)
+
+        token, passed, _ = hold([done] + swapped, two + far_z)
         two, far_z = passed[:2], passed[2:]
         far_x = as_paths(far_x + two, swapped + pass_core(two))
         got = pass_one(far_z)
-        far_o = halves(slot_order(all_o, 1, place + token[0, 0].astype(jnp.int32)))
-        wide_o = room(far_o)
         z, beside = proj_call(0, 1, (own, 0), *z_args, None, [token])
         wgt, beside = proj_call(0, 1, (own, 2), *o_args, None, [beside])
-
-        token, far_o, far_z = hold([beside] + far_x[0] + far_x[1] + wide_o, far_o, wide_z, got)
+        far_o = halves(slot_order(all_o, 1, place + beside[0, 0].astype(jnp.int32)))
+
+        token, far_o, far_z = hold([beside] + far_x[0] + far_x[1], far_o, zip(far_z, got))
         two = pass_two(far_z)
         swapped = pass_core(far_z)
         hp_far, sig_far, speed_far, far_w = steps_call(
@@ -1441,28 +1534,28 @@
         far_z = as_paths(far_z + two, swapped + pass_core(two))
         got = pass_one(far_o)
         ent_b = lax.ppermute(sent_b, "tensor", halo)
-
-        token, passed, far_o = hold(far_z[0] + far_z[1], [ent_a, ent_b], wide_o, got)
+        ent_a = lax.ppermute(hop_call(ent_a, 1, bufs[3], hp, 0, [token]), "tensor", halo)
+
+        token, passed, far_o = hold(far_z[0] + far_z[1], [ent_a, ent_b], zip(far_o, got))
         ent_a, ent_b = passed
         two = pass_two(far_o)
-        swapped = pass_core(far_o)
-        send = hop_call(ent_a, 1, bufs[3], hp, 0, [token])
-        ent_a = lax.ppermute(send, "tensor", halo)
-        z, done = proj_call(1, planes, (far_z, 0), *z_args, z, [send])
-        ent_b = lax.ppermute(hop_call(ent_b, 1, bufs[3], hp, 1, [done]), "tensor", halo)
-        send = hop_call(ent_a, 1, bufs[3], hp, 0, [done])
-
-        token, two, _ = hold([done, ent_b] + swapped, two + [send])
-        two, send = two[:2], two[2]
-        ent_a = lax.ppermute(send, "tensor", halo)
-        far_o = as_paths(far_o + two, swapped + pass_core(two))
-        ent_b = lax.ppermute(hop_call(ent_b, 1, bufs[3], hp, 1, [token]), "tensor", halo)
-        wgt, done = proj_call(1, planes, (far_o, 0), *o_args, wgt)
+        send_b = hop_call(ent_b, 1, bufs[3], hp, 1, [token])
+        ent_b = lax.ppermute(send_b, "tensor", halo)
+        send_a = hop_call(ent_a, 1, bufs[3], hp, 0, [token])
+        ent_a = lax.ppermute(send_a, "tensor", halo)
+        z, done = proj_call(1, planes, (far_z, 0), *z_args, z, [send_a, send_b])
+
+        token, passed, _ = hold([done], two + far_o + [ent_a, ent_b])
+        two, far_o, (ent_a, ent_b) = passed[:2], passed[2:4], passed[4:]
+        far_o = as_paths(far_o + two, pass_core(far_o + two))
+        send_b = hop_call(ent_b, 1, bufs[3], hp, 1, [token])
+        ent_b = lax.ppermute(send_b, "tensor", halo)
+        wgt, done = proj_call(1, planes, (far_o, 0), *o_args, wgt, [send_b])
         _, ent, _ = hold([done], [ent_a, ent_b])
         ent = jnp.stack(ent)
-        z_sets = [((0, 1), [(own, 0)]), ((1, planes), [(far_z, 0)])]
-        x_sets = [((0, 1), [(own, 1)]), ((1, planes), [(far_x, 0)])]
-        o_sets = [((0, 1), [(own, 2)]), ((1, planes), [(far_o, 0)])]
+        z_sets = [((0, 1), own, 0), ((1, planes), far_z, 0)]
+        x_sets = [((0, 1), own, 1), ((1, planes), far_x, 0)]
+        o_sets = [((0, 1), own, 2), ((1, planes), far_o, 0)]
     else:
         w = lax.all_gather(wt, "dp", axis=2, tiled=True)
         w = by_slot(w)
@@ -1479,9 +1572,9 @@
         for _ in range(planes - 2):
             ent = lax.ppermute(hop_call(ent, 1, bufs[3], hp), "tensor", halo)
         ent = ent[None]
-        z_sets = [((0, planes), [(wz, 0)])]
-        x_sets = [((0, planes), [(wx, 0)])]
-        o_sets = [((0, planes), [(o, 0)])]
+        z_sets = [((0, planes), wz, 0)]
+        x_sets = [((0, planes), wx, 0)]
+        o_sets = [((0, planes), o, 0)]
     xc, mix, loc, s_end, _ = bufs
     left = [(s + 1, s) for s in range(planes - 1)]
 
@@ -1499,7 +1592,7 @@
     for _ in range(planes - 4):
         adj = lax.ppermute(hop_call(adj, planes - 1, sl, hp), "tensor", left)
     dxs, u1, u2, kl, dcb, db1, dc1 = back_call(
-        0, planes, dy, xc, hp, ent, loc, ct, c_low, bt, cbt, None, [send]
+        dy, xc, hp, ent, loc, ct, c_low, bt, cbt, [send]
     )
 
     early = to_slots(
@@ -1538,8 +1631,9 @@
         axis=1,
     ).astype(bf16)[None]
     if quick:
-        _, (sent,), _ = hold([near], [sent])
-        by_seq = [sent] + [flip(sent, bit) for bit in (2, 4, 6)]
+        both = jnp.concatenate([sent, flip(sent, 1)], axis=0)
+        _, (both,), _ = hold([near], [both])
+        by_seq = [both] + [flip(both, bit) for bit in (2, 4, 6)]
     else:
         by_seq = [lax.all_gather(sent[0], "dp", axis=0)]
 
@@ -1549,8 +1643,6 @@
     )
     if quick:
         _, by_seq, _ = hold([tokens_grad], by_seq)
-        by_seq = jnp.concatenate(by_seq, axis=0)
-        by_seq = [by_seq, flip(by_seq, 1)]
     g_down, g_up, g_down_out, g_up_out = assemble_call(by_seq, adapters, planes, ch, width)
     g_down = jnp.swapaxes(g_down, 1, 2)
     g_down_out = jnp.swapaxes(g_down_out, 1, 2)

time: 608 us -> 557 us (0.916)
  Pallas kernels: 345 us -> 300 us
  local copies, waits for them, and re-layouts: 55.7 us -> 41.2 us
    pallas_call x18, Pallas kernels: 158 us -> 127 us  [the longest x4 38.9 us: proj_call(): pl.pallas_call(functools.partial(proj_kernel, picks, n_w, cut, gain), gri...]
    another operation x8 -> x0, local copies, waits for them, and re-layouts: 10.3 us -> none  [room(): return [jnp.stack([v, jnp.zeros_like(v)]) for v in ab]]
    all_gather x1, waiting for transfers between devices: 7.29 us -> 0.02 us  [body(): all_o = lax.all_gather(out_weight, 'tensor', axis=0)]
    unnamed x115 -> x110, local copies, waits for them, and re-layouts: 28.1 us -> 24.7 us
  transfers between devices with their start and end apart: 55 -> 55, of which waited for: 14 -> 18; matrix products, arithmetic and copies ran while one was open for 7% -> 5% of each run, Pallas kernels for 43% -> 42%
where the time goes in v4:
time: 557 us; the launch traced here: 548 us
  Pallas kernels  300 us (54%)
  waiting for transfers between devices  100 us (18%)
  starting transfers between devices  70.8 us (13%)
  local copies, waits for them, and re-layouts  41.2 us (7%)
  other arithmetic  18.8 us (3%)
  between operations  17.6 us (3%)
    pallas_call x4, Pallas kernels, scan_call(): pl.pallas_call(functools.partial(scan_kernel, nx, picks[part], hb, SUB),...  49 us
    pallas_call x4, Pallas kernels, proj_call(): pl.pallas_call(functools.partial(proj_kernel, picks, n_w, cut, gain), gri...  38.9 us
    all_gather x1, waiting for transfers between devices, body(): lax.all_gather(jnp.concatenate([wt[1], packed, steps_w, last_rows], axis=...  31.4 us
    ppermute x36, waiting for transfers between devices, flip(): return lax.ppermute(v, 'dp', [(i, i ^ bit) for i in range(seqs)])  31.3 us
    ppermute x36, starting transfers between devices, flip(): return lax.ppermute(v, 'dp', [(i, i ^ bit) for i in range(seqs)])  28.4 us
    pallas_call x1, Pallas kernels, input_call(): pl.pallas_call(functools.partial(input_kernel, sets, picks, flat, quick,...  25.2 us
    pallas_call x1, Pallas kernels, back_call(): pl.pallas_call(functools.partial(back_kernel, hb, SUB), grid=(slots,), in...  25.1 us
    pallas_call x6, Pallas kernels, hop_call(): pl.pallas_call(functools.partial(hop_kernel, CB // HEAD), grid=(slots,),...  25 us
  transfers between devices with their start and end apart: 55, of which 18 were waited for; matrix products, arithmetic and copies ran while one was open for 5% of the time, Pallas kernels for 42%

profile of v4, /device:TPU:0, one launch (start us, length us, event | category | flops | bytes accessed | tf_op | source)
XLA Modules:
  0.0 548.3 jit_solution(5767404080588848535)
XLA Ops:
  15.5 3.0 collective-permute-start
  20.3 18.9 %collective-permute-done.1.refs_3_ = bf16[1664,256]{1,0:T(8,128)(2,1)} collective-permute-done((bf16[1664,256]{1,0:T(8,128)(2,1)S(1)}, bf16[1664,256]{1,0:T(8,128)(2,1)}, u32[]{:S(2)}, u32[]{:S(2)}) %collective-permute-start.1) | collective-permute-done | bytes 852000 | tf_op jit(solution)/shard_map/ppermute | solution.py:1354
  40.1 3.8 hold.11
  46.2 31.4 %all-gather.8.cloned.1.call-done = bf16[5696,256]{1,0:T(8,128)(2,1)} async-done(((bf16[1424,256]{1,0:T(8,128)(2,1)}), bf16[5696,256]{1,0:T(8,128)(2,1)}) %all-gather.8.cloned.1.call-update) | async-done | bytes 2916368 | tf_op jit(solution)/shard_map/all_gather | solution.py:1436
  96.4 9.6 %turn.1 = (bf16[512,2048]{1,0:T(8,128)(2,1)}, bf16[512,2048]{1,0:T(8,128)(2,1)}, f32[512,1]{1,0:T(8,128)}, bf16[16,640]{1,0:T(8,128)(2,1)}, bf16[16,512]{1,0:T(8...) custom-call(s32[2]{0:T(128)} %pad_add_fusion.refs_0_.refs_16_, bf16[512,2048]{1,0:T(8,128)(2,1)} %bitcast.159, ...), custom_call_target="tpu_custom_call" | custom-call | flops 26214400 | bytes 2097152 | tf_op jit(solution)/shard_map/turn/pallas_call | solution.py:153
  109.8 3.7 hold.13
  116.6 3.9 steps.2
  120.4 5.6 %maps.1 = (bf16[128,512]{1,0:T(8,128)(2,1)}, bf16[128,512]{1,0:T(8,128)(2,1)}, bf16[512,128]{1,0:T(8,128)(2,1)}, bf16[512,128]{1,0:T(8,128)(2,1)}, f32[2,256,256...) custom-call(bf16[2,1680,256]{2,1,0:T(8,128)(2,1)} %get-tuple-element.138.refs_6_.refs_0_.refs_7_.refs_2_.refs_20_, ...), custom_call_target="tpu_custom_call" | custom-call | flops 83886080 | bytes 589824 | tf_op jit(solution)/shard_map/maps/pallas_call | solution.py:217
  126.1 8.4 %scan_slots.4 = (bf16[4,1024,512]{2,1,0:T(8,128)(2,1)}, f32[4,1024,512]{2,1,0:T(8,128)}, f32[4,1,1024,128]{3,2,1,0:T(8,128)}, f32[4,1024,128]{2,1,0:T(8,128)}, b...) custom-call(bf16[2,1680,256]{2,1,0:T(8,128)(2,1)} %get-tuple-element.138.refs_6_.refs_0_.refs_7_.refs_2_.refs_20_, ...), custom_call_target="tpu_custom_call" | custom-call | flops 268435456 | bytes 524288 | tf_op jit(solution)/shard_map/scan_slots/pallas_call | solution.py:469
  134.4 8.3 %scan_slots.5 = (bf16[4,1024,512]{2,1,0:T(8,128)(2,1)}, f32[4,1024,512]{2,1,0:T(8,128)}, f32[4,1,1024,128]{3,2,1,0:T(8,128)}, f32[4,1024,128]{2,1,0:T(8,128)}, b...) custom-call(bf16[2,1664,256]{2,1,0:T(8,128)(2,1)} %get-tuple-element, ...), custom_call_target="tpu_custom_call", output_to_operand_aliasing={{0}: (11, {}), {1}: (12, {}), {2}: (13, {}), {3}: (14, {})} | custom-call | flops 268435456 | bytes 524288 | tf_op jit(solution)/shard_map/scan_slots/pallas_call | solution.py:469
  145.4 6.7 %collective-permute-done.13.refs_4_ = bf16[2,1536,256]{2,1,0:T(8,128)(2,1)} collective-permute-done((bf16[2,1536,256]{2,1,0:T(8,128)(2,1)}, bf16[2,1536,256]{2,1,0:T(8,128)(2,1)}, u32[]{:S(2)}, u32[]{:S(2)}) %collective-permute-start.13) | collective-permute-done | bytes 1572896 | tf_op jit(solution)/shard_map/ppermute | solution.py:1354
  156.4 7.4 %proj_slots.4 = (bf16[4,1024,512]{2,1,0:T(8,128)(2,1)}, bf16[1,1]{1,0:T(2,128)(2,1)}) custom-call(bf16[2,1680,256]{2,1,0:T(8,128)(2,1)} %get-tuple-element.138.refs_6_.refs_0_.refs_7_.refs_2_.refs_20_, bf16[2,1680,256]{2,1,0:T(8,128)(2,1)} %get-tuple-element.143.refs_7_.refs_1_.refs_8_.refs_3_.refs_21_, bf16[2,1680,256]{2,1,0:T(8,128)(2,1)} %copy-done.2, ...), custom_call_target="tpu_custom_call" | custom-call | flops 268435456 | bytes 655360 | tf_op jit(solution)/shard_map/proj_slots/pallas_call | solution.py:532
  163.8 7.2 %proj_slots.5 = (bf16[4,1024,512]{2,1,0:T(8,128)(2,1)}, bf16[1,1]{1,0:T(2,128)(2,1)}) custom-call(bf16[2,1680,256]{2,1,0:T(8,128)(2,1)} %get-tuple-element.138.refs_6_.refs_0_.refs_7_.refs_2_.refs_20_, bf16[2,1680,256]{2,1,0:T(8,128)(2,1)} %get-tuple-element.143.refs_7_.refs_1_.refs_8_.refs_3_.refs_21_, bf16[2,1680,256]{2,1,0:T(8,128)(2,1)} %copy-done.2, ...), custom_call_target="tpu_custom_call" | custom-call | flops 268435456 | bytes 655360 | tf_op jit(solution)/shard_map/proj_slots/pallas_call | solution.py:532
  177.2 4.2 hold.15
  184.6 4.1 steps.3
  190.6 16.2 %scan_slots.6 = (bf16[4,1024,512]{2,1,0:T(8,128)(2,1)}, f32[4,1024,512]{2,1,0:T(8,128)}, f32[4,1,1024,128]{3,2,1,0:T(8,128)}, f32[4,1024,128]{2,1,0:T(8,128)}, b...) custom-call(bf16[2,1584,256]{2,1,0:T(8,128)(2,1)} %get-tuple-element, ...), custom_call_target="tpu_custom_call", output_to_operand_aliasing={{0}: (11, {}), {1}: (12, {}), {2}: (13, {}), {3}: (14, {}),... | custom-call | flops 805306368 | bytes 1572864 | tf_op jit(solution)/shard_map/scan_slots/pallas_call | solution.py:469
  209.0 16.2 %scan_slots.7 = (bf16[4,1024,512]{2,1,0:T(8,128)(2,1)}, f32[4,1024,512]{2,1,0:T(8,128)}, f32[4,1,1024,128]{3,2,1,0:T(8,128)}, f32[4,1024,128]{2,1,0:T(8,128)}, b...) custom-call(bf16[2,1536,256]{2,1,0:T(8,128)(2,1)} %get-tuple-element, ...), custom_call_target="tpu_custom_call", output_to_operand_aliasing={{0}: (11, {}), {1}: (12, {}), {2}: (13, {}), {3}: (14, {}),... | custom-call | flops 805306368 | bytes 1572864 | tf_op jit(solution)/shard_map/scan_slots/pallas_call | solution.py:469
  228.2 4.2 hop.6
  232.4 3.4 collective-permute-start.27
  238.8 8.7 %collective-permute-done.27.refs_12_ = bf16[4,512,128]{2,1,0:T(8,128)(2,1)S(1)} collective-permute-done((bf16[4,512,128]{2,1,0:T(8,128)(2,1)}, bf16[4,512,128]{2,1,0:T(8,128)(2,1)S(1)}, u32[]{:S(2)}, u32[]{:S(2)}) %collective-permute-start.27) | collective-permute-done | bytes 524320 | tf_op jit(solution)/shard_map/ppermute | solution.py:1537
  247.4 4.3 collective-permute-start.28
  251.8 10.4 %collective-permute-done.28.refs_13_ = bf16[4,512,128]{2,1,0:T(8,128)(2,1)S(1)} collective-permute-done((bf16[4,512,128]{2,1,0:T(8,128)(2,1)S(1)}, bf16[4,512,128]{2,1,0:T(8,128)(2,1)S(1)}, u32[]{:S(2)}, u32[]{:S(2)}) %collective-permute-start.28) | collective-permute-done | bytes 524320 | tf_op jit(solution)/shard_map/ppermute | solution.py:1536
  265.8 3.6 hold.17
  272.3 4.2 hop.8.refs_13_
  276.5 4.4 collective-permute-start.32
  280.9 4.2 hop.7.refs_12_
  285.1 3.5 collective-permute-start.31
  288.6 12.1 %proj_slots.6 = (bf16[4,1024,512]{2,1,0:T(8,128)(2,1)}, bf16[1,1]{1,0:T(2,128)(2,1)}) custom-call(bf16[2,1536,256]{2,1,0:T(8,128)(2,1)} %get-tuple-element.167.refs_4_.refs_0_.refs_10_, bf16[2,1536,256]{2,1,0:T(8,128)(2,1)} %get-tuple-element.186.refs_5_.refs_1_.refs_11_, bf16[2,1536,256]{2,1,0:T(8,128)(2,1)} %copy-done.7, ...), custom_call_target="tpu_custom_call", output_to_operand_aliasing={{0}: (11, {})} | custom-call | flops 805306368 | bytes 1966080 | tf_op jit(solution)/shard_map/proj_slots/pallas_call | solution.py:532
  301.4 2.8 collective-permute-done.29.refs_1_
  307.7 4.2 hop.9.refs_12_
  311.9 4.4 collective-permute-start.37
  317.5 12.2 %proj_slots.7 = (bf16[4,1024,512]{2,1,0:T(8,128)(2,1)}, bf16[1,1]{1,0:T(2,128)(2,1)}) custom-call(bf16[2,1536,256]{2,1,0:T(8,128)(2,1)} %get-tuple-element.203.refs_0_.refs_15_, bf16[2,1536,256]{2,1,0:T(8,128)(2,1)} %get-tuple-element.204.refs_1_.refs_16_, bf16[2,1536,256]{2,1,0:T(8,128)(2,1)} %copy-done.11, ...), custom_call_target="tpu_custom_call", output_to_operand_aliasing={{0}: (11, {})} | custom-call | flops 805306368 | bytes 1966080 | tf_op jit(solution)/shard_map/proj_slots/pallas_call | solution.py:532
  333.9 20.6 %gate.1 = (bf16[4,1024,512]{2,1,0:T(8,128)(2,1)}, bf16[4,1024,512]{2,1,0:T(8,128)(2,1)}, bf16[4,1024,512]{2,1,0:T(8,128)(2,1)}, f32[4,1024,128]{2,1,0:T(8,128)}, bf16[4,1024,128]{2,1,0:T(8,128)(2,1)}) custom-call(bf16[4,1024,512]{2,1,0:T(8,128)(2,1)} %get-tuple-element.198.refs_0_, f32[4,1024,512]{2,1,0:T(8,128)} %get-tuple-element.199.refs_1_, ...), custom_call_target="tpu_custom_call" | custom-call | flops 157286400 | bytes 5767168 | tf_op jit(solution)/shard_map/gate/pallas_call | solution.py:637
  357.1 20.5 %output.1 = (bf16[512,2048]{1,0:T(8,128)(2,1)}, f32[4,16,1024]{2,1,0:T(8,128)}, f32[16,2048]{1,0:T(8,128)}) custom-call(s32[2]{0:T(128)} %pad_add_fusion.refs_0_.refs_16_, bf16[4,1024,512]{2,1,0:T(8,128)(2,1)} %get-tuple-element.216.refs_1_, bf16[4,256,256]{2,1,0:T(8,128)(2,1)} %pad_maximum_fusion.8.refs_5_.refs_6_.refs_10_.refs_4_.refs_2_, ...), custom_call_target="tpu_custom_call" | custom-call | flops 1073741824 | bytes 2097152 | tf_op jit(solution)/shard_map/output/pallas_call | solution.py:1095
  379.4 2.7 collective-permute-done.38.got
  383.2 4.2 hop.10.refs_18_
  388.6 17.4 %gate_back.1 = (f32[512,2048]{1,0:T(8,128)}, f32[4,16,1024]{2,1,0:T(8,128)}) custom-call(bf16[4,1024,512]{2,1,0:T(8,128)(2,1)} %get-tuple-element.225.refs_0_.refs_3_, bf16[16,640]{1,0:T(8,128)(2,1)} %get-tuple-element.142.refs_5_.refs_9_.refs_1_, bf16[2,1680,256]{2,1,0:T(8,128)(2,1)} %get-tuple-element.138.refs_6_.refs_0_.refs_7_.refs_2_.refs_20_, ...), custom_call_target="tpu_custom_call" | custom-call | flops 1073741824 | bytes 2097152 | tf_op jit(solution)/shard_map/gate_back/pallas_call | solution.py:1136
  407.1 2.7 collective-permute-start.41
  409.8 2.8 collective-permute-start.42
  418.3 4.1 hop.11.refs_9_
  425.9 25.1 %state_back.1 = (f32[4,1024,512]{2,1,0:T(8,128)}, f32[16,4,512]{2,1,0:T(4,128)}, f32[16,4,512]{2,1,0:T(4,128)}, f32[16,4,256]{2,1,0:T(4,128)}, f32[2,256,256]{2,...) custom-call(bf16[4,1024,512]{2,1,0:T(8,128)(2,1)} %get-tuple-element.219.refs_0_.refs_1_, ...), custom_call_target="tpu_custom_call" | custom-call | flops 1342177280 | bytes 2097152 | tf_op jit(solution)/shard_map/state_back/pallas_call | solution.py:769
  452.0 21.0 %finish_back.1 = (bf16[4,1024,512]{2,1,0:T(8,128)(2,1)}, f32[4,1024,128]{2,1,0:T(8,128)}, f32[4,8,1024]{2,1,0:T(8,128)}, f32[4,16,1024]{2,1,0:T(8,128)}, f32[16,...) custom-call(f32[4,1024,512]{2,1,0:T(8,128)} %get-tuple-element.227.r, ...), custom_call_target="tpu_custom_call" | custom-call | flops 183500800 | bytes 3670016 | tf_op jit(solution)/shard_map/finish_back/pallas_call | solution.py:891
  473.0 5.2 glue.1
  479.2 3.8 collective-permute-start.45
  484.5 2.8 collective-permute-start.47
  493.7 8.5 %collective-permute-done.44.refs_3_.refs_7_.refs_10_.refs_0_ = f32[64,1024]{1,0:T(8,128)S(1)} collective-permute-done((f32[64,1024]{1,0:T(8,128)S(1)}, f32[64,1024]{1,0:T(8,128)S(1)}, u32[]{:S(2)}, u32[]{:S(2)}) %collective-permute-start.44) | collective-permute-done | bytes 262176 | tf_op jit(solution)/shard_map/ppermute | solution.py:1620
  506.9 25.2 %input_back.1.refs_0_ = bf16[512,2048]{1,0:T(8,128)(2,1)} custom-call(s32[2]{0:T(128)} %pad_add_fusion.refs_0_.refs_16_, bf16[4,1024,512]{2,1,0:T(8,128)(2,1)} %get-tuple-element.231.refs_1_, f32[4,1024,128]{2,1,0:T(8,128)} %get-tuple-element.232.refs_2_, f32[64,1024]{1,0:T(8,128)} %copy-done.14, ...), custom_call_target="tpu_custom_call" | custom-call | flops 1073741824 | bytes 2097152 | tf_op jit(solution)/shard_map/input_back/pallas_call | solution.py:1246
  534.4 7.1 %assemble.1 = (f32[8,16,2048]{2,1,0:T(8,128)}, f32[8,16,2,1024]{3,2,1,0:T(2,128)}, f32[8,16,1024]{2,1,0:T(8,128)}, f32[8,16,2048]{2,1,0:T(8,128)}) custom-call(bf16[2,16,7296]{2,1,0:T(8,128)(2,1)} %get-tuple-element.260.refs_0_, bf16[2,16,7296]{2,1,0:T(8,128)(2,1)} %get-tuple-element.261.refs_1_, bf16[2,16,7296]{2,1,0:T(8,128)(2,1)} %get-tuple-element.262.refs_2_, ...), custom_call_target="tpu_custom_call" | custom-call | flops 1250000 | bytes 2500000 | tf_op jit(solution)/shard_map/assemble/pallas_call | solution.py:1287
  (276 shorter events, 111.8 us)
Async XLA Ops:
  7.2 70.4 %all-gather.8.cloned.1.call-start = ((), (), s32[]{:S(2)}) async-start(), calls=%async_computation.1 | async-start | bytes 3645440 | tf_op jit(solution)/shard_map/all_gather | solution.py:1436
  15.1 127.6 %all-gather.6.cloned.1.call-start = ((), (), s32[]{:S(2)}) async-start(), calls=%async_computation | async-start | bytes 2621440 | tf_op jit(solution)/shard_map/all_gather | solution.py:1439
  15.5 23.7 %collective-permute-start = (bf16[1680,256]{1,0:T(8,128)(2,1)S(1)}, bf16[1680,256]{1,0:T(8,128)(2,1)S(1)}, u32[]{:S(2)}, u32[]{:S(2)}) collective-permute-start(bf16[1680,256]{1,0:T(8,128)(2,1)S(1)} %constant_dynamic-update-slice_fusion.refs_0_), channel_id=1, source_target_pairs={{0,8},{4,12},{8,0},{12,4},{16,24},{20,28},{24,16},{28,20},{1,9},{5... | collective-permute-start | bytes 2580488 | tf_op jit(solution)/shard_map/ppermute | solution.py:1354
  18.6 20.6 %collective-permute-start.1 = (bf16[1664,256]{1,0:T(8,128)(2,1)S(1)}, bf16[1664,256]{1,0:T(8,128)(2,1)}, u32[]{:S(2)}, u32[]{:S(2)}) collective-permute-start(bf16[1664,256]{1,0:T(8,128)(2,1)S(1)} %pad_maximum_fusion.1.refs_2_), channel_id=1, source_target_pairs={{0,16},{4,20},{8,24},{12,28},{16,0},{20,4},{24,8},{28,12},{1,17},{... | collective-permute-start | bytes 2555912 | tf_op jit(solution)/shard_map/ppermute | solution.py:1354
  20.2 151.5 %all-gather.10.cloned.1.call-start = ((), (), s32[]{:S(2)}) async-start(), calls=%async_computation.2 | async-start | bytes 2621440 | tf_op jit(solution)/shard_map/all_gather | solution.py:1440
  43.9 41.5 %collective-permute-start.2 = (bf16[2,1680,256]{2,1,0:T(8,128)(2,1)}, bf16[2,1680,256]{2,1,0:T(8,128)(2,1)S(1)}, u32[]{:S(2)}, u32[]{:S(2)}) collective-permute-start(bf16[2,1680,256]{2,1,0:T(8,128)(2,1)} %get-tuple-element.138.refs_6_.refs_0_.refs_7_.refs_2_.refs_20_), channel_id=1, source_target_pairs={{0,4},{4,0},{8,12},{12,8},{16,20},{20,16},{24,28},{28,24},{1,5},{5... | collective-permute-start | bytes 5160968 | tf_op jit(solution)/shard_map/ppermute | solution.py:1354
  43.9 41.5 %collective-permute-start.4 = (bf16[2,1680,256]{2,1,0:T(8,128)(2,1)}, bf16[2,1680,256]{2,1,0:T(8,128)(2,1)}, u32[]{:S(2)}, u32[]{:S(2)}) collective-permute-start(bf16[2,1680,256]{2,1,0:T(8,128)(2,1)} %get-tuple-element.138.refs_6_.refs_0_.refs_7_.refs_2_.refs_20_), channel_id=1, source_target_pairs={{0,16},{4,20},{8,24},{12,28},{16,0},{20,4},{24,8},{28,12},{1,17},{... | collective-permute-start | bytes 5160968 | tf_op jit(solution)/shard_map/ppermute | solution.py:1354
  45.5 39.6 %collective-permute-start.3 = (bf16[2,1664,256]{2,1,0:T(8,128)(2,1)}, bf16[2,1664,256]{2,1,0:T(8,128)(2,1)}, u32[]{:S(2)}, u32[]{:S(2)}) collective-permute-start(bf16[2,1664,256]{2,1,0:T(8,128)(2,1)} %get-tuple-element.137.refs_10_.refs_4_.refs_0_.refs_11_.refs_6_.refs_24_), channel_id=1, source_target_pairs={{0,4},{4,0},{8,12},{12,8},{16,20},{20,16},{24,28},{28,24},{1,5},{5... | collective-permute-start | bytes 5111816 | tf_op jit(solution)/shard_map/ppermute | solution.py:1354
  45.7 39.7 %collective-permute-start.5 = (bf16[2,1664,256]{2,1,0:T(8,128)(2,1)}, bf16[2,1664,256]{2,1,0:T(8,128)(2,1)}, u32[]{:S(2)}, u32[]{:S(2)}) collective-permute-start(bf16[2,1664,256]{2,1,0:T(8,128)(2,1)} %get-tuple-element.137.refs_10_.refs_4_.refs_0_.refs_11_.refs_6_.refs_24_), channel_id=1, source_target_pairs={{0,8},{4,12},{8,0},{12,4},{16,24},{20,28},{24,16},{28,20},{1,9},{5... | collective-permute-start | bytes 5111816 | tf_op jit(solution)/shard_map/ppermute | solution.py:1354
  87.1 21.2 %collective-permute-start.7 = (bf16[2,1680,256]{2,1,0:T(8,128)(2,1)}, bf16[2,1680,256]{2,1,0:T(8,128)(2,1)S(1)}, u32[]{:S(2)}, u32[]{:S(2)}) collective-permute-start(bf16[2,1680,256]{2,1,0:T(8,128)(2,1)} %get-tuple-element.143.refs_7_.refs_1_.refs_8_.refs_3_.refs_21_), channel_id=1, source_target_pairs={{0,4},{4,0},{8,12},{12,8},{16,20},{20,16},{24,28},{28,24},{1,5},{5... | collective-permute-start | bytes 5160968 | tf_op jit(solution)/shard_map/ppermute | solution.py:1354
  87.1 21.2 %collective-permute-start.6 = (bf16[2,1664,256]{2,1,0:T(8,128)(2,1)}, bf16[2,1664,256]{2,1,0:T(8,128)(2,1)}, u32[]{:S(2)}, u32[]{:S(2)}) collective-permute-start(bf16[2,1664,256]{2,1,0:T(8,128)(2,1)} %get-tuple-element.139.refs_11_.refs_5_.refs_1_.refs_12_.refs_7_.refs_25_), channel_id=1, source_target_pairs={{0,4},{4,0},{8,12},{12,8},{16,20},{20,16},{24,28},{28,24},{1,5},{5... | collective-permute-start | bytes 5111816 | tf_op jit(solution)/shard_map/ppermute | solution.py:1354
  87.7 20.7 %collective-permute-start.8 = (bf16[1584,256]{1,0:T(8,128)(2,1)}, bf16[1584,256]{1,0:T(8,128)(2,1)S(1)}, u32[]{:S(2)}, u32[]{:S(2)}) collective-permute-start(bf16[1584,256]{1,0:T(8,128)(2,1)} %get-tuple-element.144.refs_0_), channel_id=1, source_target_pairs={{0,8},{4,12},{8,0},{12,4},{16,24},{20,28},{24,16},{28,20},{1,9},{5... | collective-permute-start | bytes 2433032 | tf_op jit(solution)/shard_map/ppermute | solution.py:1354
  88.9 19.5 %collective-permute-start.9 = (bf16[1536,256]{1,0:T(8,128)(2,1)}, bf16[1536,256]{1,0:T(8,128)(2,1)}, u32[]{:S(2)}, u32[]{:S(2)}) collective-permute-start(bf16[1536,256]{1,0:T(8,128)(2,1)} %get-tuple-element.145.refs_2_), channel_id=1, source_target_pairs={{0,16},{4,20},{8,24},{12,28},{16,0},{20,4},{24,8},{28,12},{1,17},{... | collective-permute-start | bytes 2359304 | tf_op jit(solution)/shard_map/ppermute | solution.py:1354
  113.5 38.6 %collective-permute-start.10 = (bf16[2,1584,256]{2,1,0:T(8,128)(2,1)}, bf16[2,1584,256]{2,1,0:T(8,128)(2,1)S(1)}, u32[]{:S(2)}, u32[]{:S(2)}) collective-permute-start(bf16[2,1584,256]{2,1,0:T(8,128)(2,1)} %get-tuple-element.156.refs_5_.refs_0_.refs_28_), channel_id=1, source_target_pairs={{0,4},{4,0},{8,12},{12,8},{16,20},{20,16},{24,28},{28,24},{1,5},{5... | collective-permute-start | bytes 4866056 | tf_op jit(solution)/shard_map/ppermute | solution.py:1354
  113.5 38.6 %collective-permute-start.12 = (bf16[2,1584,256]{2,1,0:T(8,128)(2,1)}, bf16[2,1584,256]{2,1,0:T(8,128)(2,1)}, u32[]{:S(2)}, u32[]{:S(2)}) collective-permute-start(bf16[2,1584,256]{2,1,0:T(8,128)(2,1)} %get-tuple-element.156.refs_5_.refs_0_.refs_28_), channel_id=1, source_target_pairs={{0,16},{4,20},{8,24},{12,28},{16,0},{20,4},{24,8},{28,12},{1,17},{... | collective-permute-start | bytes 4866056 | tf_op jit(solution)/shard_map/ppermute | solution.py:1354
  115.0 30.5 %collective-permute-start.11 = (bf16[2,1536,256]{2,1,0:T(8,128)(2,1)}, bf16[2,1536,256]{2,1,0:T(8,128)(2,1)}, u32[]{:S(2)}, u32[]{:S(2)}) collective-permute-start(bf16[2,1536,256]{2,1,0:T(8,128)(2,1)} %get-tuple-element.157.refs_9_.refs_0_.refs_32_), channel_id=1, source_target_pairs={{0,4},{4,0},{8,12},{12,8},{16,20},{20,16},{24,28},{28,24},{1,5},{5... | collective-permute-start | bytes 4718600 | tf_op jit(solution)/shard_map/ppermute | solution.py:1354
  115.2 36.9 %collective-permute-start.13 = (bf16[2,1536,256]{2,1,0:T(8,128)(2,1)}, bf16[2,1536,256]{2,1,0:T(8,128)(2,1)}, u32[]{:S(2)}, u32[]{:S(2)}) collective-permute-start(bf16[2,1536,256]{2,1,0:T(8,128)(2,1)} %get-tuple-element.157.refs_9_.refs_0_.refs_32_), channel_id=1, source_target_pairs={{0,8},{4,12},{8,0},{12,4},{16,24},{20,28},{24,16},{28,20},{1,9},{5... | collective-permute-start | bytes 4718600 | tf_op jit(solution)/shard_map/ppermute | solution.py:1354
  154.4 20.7 %collective-permute-start.16 = (bf16[2,1584,256]{2,1,0:T(8,128)(2,1)}, bf16[2,1584,256]{2,1,0:T(8,128)(2,1)S(1)}, u32[]{:S(2)}, u32[]{:S(2)}) collective-permute-start(bf16[2,1584,256]{2,1,0:T(8,128)(2,1)} %get-tuple-element.165.refs_6_.refs_1_.refs_29_), channel_id=1, source_target_pairs={{0,4},{4,0},{8,12},{12,8},{16,20},{20,16},{24,28},{28,24},{1,5},{5... | collective-permute-start | bytes 4866056 | tf_op jit(solution)/shard_map/ppermute | solution.py:1354
  154.4 20.7 %collective-permute-start.17 = (bf16[2,1536,256]{2,1,0:T(8,128)(2,1)}, bf16[2,1536,256]{2,1,0:T(8,128)(2,1)}, u32[]{:S(2)}, u32[]{:S(2)}) collective-permute-start(bf16[2,1536,256]{2,1,0:T(8,128)(2,1)} %get-tuple-element.166.refs_10_.refs_1_.refs_33_), channel_id=1, source_target_pairs={{0,4},{4,0},{8,12},{12,8},{16,20},{20,16},{24,28},{28,24},{1,5},{5... | collective-permute-start | bytes 4718600 | tf_op jit(solution)/shard_map/ppermute | solution.py:1354
  154.9 20.1 %collective-permute-start.14 = (bf16[1536,256]{1,0:T(8,128)(2,1)}, bf16[1536,256]{1,0:T(8,128)(2,1)S(1)}, u32[]{:S(2)}, u32[]{:S(2)}) collective-permute-start(bf16[1536,256]{1,0:T(8,128)(2,1)} %get-tuple-element.158.refs_0_), channel_id=1, source_target_pairs={{0,8},{4,12},{8,0},{12,4},{16,24},{20,28},{24,16},{28,20},{1,9},{5... | collective-permute-start | bytes 2359304 | tf_op jit(solution)/shard_map/ppermute | solution.py:1354
  155.6 19.5 %collective-permute-start.15 = (bf16[1536,256]{1,0:T(8,128)(2,1)}, bf16[1536,256]{1,0:T(8,128)(2,1)}, u32[]{:S(2)}, u32[]{:S(2)}) collective-permute-start(bf16[1536,256]{1,0:T(8,128)(2,1)} %get-tuple-element.159.refs_2_), channel_id=1, source_target_pairs={{0,16},{4,20},{8,24},{12,28},{16,0},{20,4},{24,8},{28,12},{1,17},{... | collective-permute-start | bytes 2359304 | tf_op jit(solution)/shard_map/ppermute | solution.py:1354
  181.5 43.7 %collective-permute-start.18 = (bf16[2,1536,256]{2,1,0:T(8,128)(2,1)}, bf16[2,1536,256]{2,1,0:T(8,128)(2,1)S(1)}, u32[]{:S(2)}, u32[]{:S(2)}) collective-permute-start(bf16[2,1536,256]{2,1,0:T(8,128)(2,1)} %get-tuple-element.167.refs_4_.refs_0_.refs_10_), channel_id=1, source_target_pairs={{0,4},{4,0},{8,12},{12,8},{16,20},{20,16},{24,28},{28,24},{1,5},{5... | collective-permute-start | bytes 4718600 | tf_op jit(solution)/shard_map/ppermute | solution.py:1354
  181.5 43.7 %collective-permute-start.19 = (bf16[2,1536,256]{2,1,0:T(8,128)(2,1)}, bf16[2,1536,256]{2,1,0:T(8,128)(2,1)}, u32[]{:S(2)}, u32[]{:S(2)}) collective-permute-start(bf16[2,1536,256]{2,1,0:T(8,128)(2,1)} %get-tuple-element.181.refs_8_.refs_4_.refs_14_), channel_id=1, source_target_pairs={{0,4},{4,0},{8,12},{12,8},{16,20},{20,16},{24,28},{28,24},{1,5},{5... | collective-permute-start | bytes 4718600 | tf_op jit(solution)/shard_map/ppermute | solution.py:1354
  182.0 43.2 %collective-permute-start.20 = (bf16[2,1536,256]{2,1,0:T(8,128)(2,1)}, bf16[2,1536,256]{2,1,0:T(8,128)(2,1)}, u32[]{:S(2)}, u32[]{:S(2)}) collective-permute-start(bf16[2,1536,256]{2,1,0:T(8,128)(2,1)} %get-tuple-element.167.refs_4_.refs_0_.refs_10_), channel_id=1, source_target_pairs={{0,16},{4,20},{8,24},{12,28},{16,0},{20,4},{24,8},{28,12},{1,17},{... | collective-permute-start | bytes 4718600 | tf_op jit(solution)/shard_map/ppermute | solution.py:1354
  183.3 41.9 %collective-permute-start.21 = (bf16[2,1536,256]{2,1,0:T(8,128)(2,1)}, bf16[2,1536,256]{2,1,0:T(8,128)(2,1)}, u32[]{:S(2)}, u32[]{:S(2)}) collective-permute-start(bf16[2,1536,256]{2,1,0:T(8,128)(2,1)} %get-tuple-element.181.refs_8_.refs_4_.refs_14_), channel_id=1, source_target_pairs={{0,8},{4,12},{8,0},{12,4},{16,24},{20,28},{24,16},{28,20},{1,9},{5... | collective-permute-start | bytes 4718600 | tf_op jit(solution)/shard_map/ppermute | solution.py:1354
  206.8 18.3 %collective-permute-start.22 = (bf16[4,512,128]{2,1,0:T(8,128)(2,1)}, bf16[4,512,128]{2,1,0:T(8,128)(2,1)S(1)}, u32[]{:S(2)}, u32[]{:S(2)}) collective-permute-start(bf16[4,512,128]{2,1,0:T(8,128)(2,1)} %get-tuple-element.184), channel_id=1, source_target_pairs={{0,1},{1,2},{2,3},{4,5},{5,6},{6,7},{8,9},{9,10},{10,11},{12,13},{... | collective-permute-start | bytes 1572872 | tf_op jit(solution)/shard_map/ppermute | solution.py:1527
  227.7 34.6 %collective-permute-start.23 = (bf16[2,1536,256]{2,1,0:T(8,128)(2,1)}, bf16[2,1536,256]{2,1,0:T(8,128)(2,1)S(1)}, u32[]{:S(2)}, u32[]{:S(2)}) collective-permute-start(bf16[2,1536,256]{2,1,0:T(8,128)(2,1)} %get-tuple-element.186.refs_5_.refs_1_.refs_11_), channel_id=1, source_target_pairs={{0,4},{4,0},{8,12},{12,8},{16,20},{20,16},{24,28},{28,24},{1,5},{5... | collective-permute-start | bytes 4718600 | tf_op jit(solution)/shard_map/ppermute | solution.py:1354
  227.7 35.8 %collective-permute-start.24 = (bf16[2,1536,256]{2,1,0:T(8,128)(2,1)}, bf16[2,1536,256]{2,1,0:T(8,128)(2,1)S(1)}, u32[]{:S(2)}, u32[]{:S(2)}) collective-permute-start(bf16[2,1536,256]{2,1,0:T(8,128)(2,1)} %get-tuple-element.187.refs_9_.refs_5_.refs_15_), channel_id=1, source_target_pairs={{0,4},{4,0},{8,12},{12,8},{16,20},{20,16},{24,28},{28,24},{1,5},{5... | collective-permute-start | bytes 4718600 | tf_op jit(solution)/shard_map/ppermute | solution.py:1354
  232.4 15.0 %collective-permute-start.27 = (bf16[4,512,128]{2,1,0:T(8,128)(2,1)}, bf16[4,512,128]{2,1,0:T(8,128)(2,1)S(1)}, u32[]{:S(2)}, u32[]{:S(2)}) collective-permute-start(bf16[4,512,128]{2,1,0:T(8,128)(2,1)} %hop.6), channel_id=1, source_target_pairs={{0,1},{1,2},{2,3},{4,5},{5,6},{6,7},{8,9},{9,10},{10,11},{12,13},{... | collective-permute-start | bytes 1572872 | tf_op jit(solution)/shard_map/ppermute | solution.py:1537
  235.8 26.4 %collective-permute-start.25 = (bf16[1536,256]{1,0:T(8,128)(2,1)}, bf16[1536,256]{1,0:T(8,128)(2,1)S(1)}, u32[]{:S(2)}, u32[]{:S(2)}) collective-permute-start(bf16[1536,256]{1,0:T(8,128)(2,1)} %get-tuple-element.189.refs_0_), channel_id=1, source_target_pairs={{0,8},{4,12},{8,0},{12,4},{16,24},{20,28},{24,16},{28,20},{1,9},{5... | collective-permute-start | bytes 2359304 | tf_op jit(solution)/shard_map/ppermute | solution.py:1354
  237.2 25.0 %collective-permute-start.26 = (bf16[1536,256]{1,0:T(8,128)(2,1)}, bf16[1536,256]{1,0:T(8,128)(2,1)S(1)}, u32[]{:S(2)}, u32[]{:S(2)}) collective-permute-start(bf16[1536,256]{1,0:T(8,128)(2,1)} %get-tuple-element.190.refs_2_), channel_id=1, source_target_pairs={{0,16},{4,20},{8,24},{12,28},{16,0},{20,4},{24,8},{28,12},{1,17},{... | collective-permute-start | bytes 2359304 | tf_op jit(solution)/shard_map/ppermute | solution.py:1354
  247.4 14.8 %collective-permute-start.28 = (bf16[4,512,128]{2,1,0:T(8,128)(2,1)S(1)}, bf16[4,512,128]{2,1,0:T(8,128)(2,1)S(1)}, u32[]{:S(2)}, u32[]{:S(2)}) collective-permute-start(bf16[4,512,128]{2,1,0:T(8,128)(2,1)S(1)} %copy-done.16), channel_id=1, source_target_pairs={{0,1},{1,2},{2,3},{4,5},{5,6},{6,7},{8,9},{9,10},{10,11},{12,13},{... | collective-permute-start | bytes 1572872 | tf_op jit(solution)/shard_map/ppermute | solution.py:1536
  269.4 34.7 %collective-permute-start.29 = (bf16[2,1536,256]{2,1,0:T(8,128)(2,1)}, bf16[2,1536,256]{2,1,0:T(8,128)(2,1)S(1)}, u32[]{:S(2)}, u32[]{:S(2)}) collective-permute-start(bf16[2,1536,256]{2,1,0:T(8,128)(2,1)} %get-tuple-element.201.refs_3_), channel_id=1, source_target_pairs={{0,16},{4,20},{8,24},{12,28},{16,0},{20,4},{24,8},{28,12},{1,17},{... | collective-permute-start | bytes 4718600 | tf_op jit(solution)/shard_map/ppermute | solution.py:1354
  271.0 34.6 %collective-permute-start.30 = (bf16[2,1536,256]{2,1,0:T(8,128)(2,1)}, bf16[2,1536,256]{2,1,0:T(8,128)(2,1)}, u32[]{:S(2)}, u32[]{:S(2)}) collective-permute-start(bf16[2,1536,256]{2,1,0:T(8,128)(2,1)} %get-tuple-element.202.refs_4_), channel_id=1, source_target_pairs={{0,8},{4,12},{8,0},{12,4},{16,24},{20,28},{24,16},{28,20},{1,9},{5... | collective-permute-start | bytes 4718600 | tf_op jit(solution)/shard_map/ppermute | solution.py:1354
  276.5 24.2 %collective-permute-start.32 = (bf16[4,512,128]{2,1,0:T(8,128)(2,1)}, bf16[4,512,128]{2,1,0:T(8,128)(2,1)S(1)}, u32[]{:S(2)}, u32[]{:S(2)}) collective-permute-start(bf16[4,512,128]{2,1,0:T(8,128)(2,1)} %hop.8.refs_13_), channel_id=1, source_target_pairs={{0,1},{1,2},{2,3},{4,5},{5,6},{6,7},{8,9},{9,10},{10,11},{12,13},{... | collective-permute-start | bytes 1572872 | tf_op jit(solution)/shard_map/ppermute | solution.py:1543
  285.1 16.3 %collective-permute-start.31 = (bf16[4,512,128]{2,1,0:T(8,128)(2,1)}, bf16[4,512,128]{2,1,0:T(8,128)(2,1)S(1)}, u32[]{:S(2)}, u32[]{:S(2)}) collective-permute-start(bf16[4,512,128]{2,1,0:T(8,128)(2,1)} %hop.7.refs_12_), channel_id=1, source_target_pairs={{0,1},{1,2},{2,3},{4,5},{5,6},{6,7},{8,9},{9,10},{10,11},{12,13},{... | collective-permute-start | bytes 1572872 | tf_op jit(solution)/shard_map/ppermute | solution.py:1545
  307.2 10.0 %collective-permute-start.36 = (bf16[2,1536,256]{2,1,0:T(8,128)(2,1)}, bf16[2,1536,256]{2,1,0:T(8,128)(2,1)}, u32[]{:S(2)}, u32[]{:S(2)}) collective-permute-start(bf16[2,1536,256]{2,1,0:T(8,128)(2,1)} %get-tuple-element.206.refs_5_.refs_20_), channel_id=1, source_target_pairs={{0,4},{4,0},{8,12},{12,8},{16,20},{20,16},{24,28},{28,24},{1,5},{5... | collective-permute-start | bytes 4718600 | tf_op jit(solution)/shard_map/ppermute | solution.py:1354
  311.9 17.8 %collective-permute-start.37 = (bf16[4,512,128]{2,1,0:T(8,128)(2,1)}, bf16[4,512,128]{2,1,0:T(8,128)(2,1)S(1)}, u32[]{:S(2)}, u32[]{:S(2)}) collective-permute-start(bf16[4,512,128]{2,1,0:T(8,128)(2,1)} %hop.9.refs_12_), channel_id=1, source_target_pairs={{0,1},{1,2},{2,3},{4,5},{5,6},{6,7},{8,9},{9,10},{10,11},{12,13},{... | collective-permute-start | bytes 1572872 | tf_op jit(solution)/shard_map/ppermute | solution.py:1552
  354.5 27.7 %collective-permute-start.38 = (bf16[4,1024,128]{2,1,0:T(8,128)(2,1)}, bf16[4,1024,128]{2,1,0:T(8,128)(2,1)S(1)}, u32[]{:S(2)}, u32[]{:S(2)}) collective-permute-start(bf16[4,1024,128]{2,1,0:T(8,128)(2,1)} %get-tuple-element.223), channel_id=1, source_target_pairs={{1,0},{2,1},{3,2},{5,4},{6,5},{7,6},{9,8},{10,9},{11,10},{13,12},{... | collective-permute-start | bytes 3145736 | tf_op jit(solution)/shard_map/ppermute | solution.py:1583
  387.3 30.1 %collective-permute-start.39 = (bf16[4,1024,128]{2,1,0:T(8,128)(2,1)}, bf16[4,1024,128]{2,1,0:T(8,128)(2,1)S(1)}, u32[]{:S(2)}, u32[]{:S(2)}) collective-permute-start(bf16[4,1024,128]{2,1,0:T(8,128)(2,1)} %hop.10.refs_18_), channel_id=1, source_target_pairs={{1,0},{2,1},{3,2},{5,4},{6,5},{7,6},{9,8},{10,9},{11,10},{13,12},{... | collective-permute-start | bytes 3145736 | tf_op jit(solution)/shard_map/ppermute | solution.py:1588
  407.1 16.6 %collective-permute-start.41 = (bf16[16,4096]{1,0:T(8,128)(2,1)S(1)}, bf16[16,4096]{1,0:T(8,128)(2,1)S(1)}, u32[]{:S(2)}, u32[]{:S(2)}) collective-permute-start(bf16[16,4096]{1,0:T(8,128)(2,1)S(1)} %get-tuple-element.309), channel_id=1, source_target_pairs={{0,1},{1,2},{2,3},{3,0},{4,5},{5,6},{6,7},{7,4},{8,9},{9,10},{10,1... | collective-permute-start | bytes 393224 | tf_op jit(solution)/shard_map/ppermute | solution.py:1369
  409.8 15.3 %collective-permute-start.42 = (bf16[16,4096]{1,0:T(8,128)(2,1)S(1)}, bf16[16,4096]{1,0:T(8,128)(2,1)S(1)}, u32[]{:S(2)}, u32[]{:S(2)}) collective-permute-start(bf16[16,4096]{1,0:T(8,128)(2,1)S(1)} %get-tuple-element.310), channel_id=1, source_target_pairs={{0,2},{1,3},{2,0},{3,1},{4,6},{5,7},{6,4},{7,5},{8,10},{9,11},{10,... | collective-permute-start | bytes 393224 | tf_op jit(solution)/shard_map/ppermute | solution.py:1369
  412.6 12.5 %collective-permute-start.43 = (bf16[16,4096]{1,0:T(8,128)(2,1)S(1)}, bf16[16,4096]{1,0:T(8,128)(2,1)S(1)}, u32[]{:S(2)}, u32[]{:S(2)}) collective-permute-start(bf16[16,4096]{1,0:T(8,128)(2,1)S(1)} %get-tuple-element.311), channel_id=1, source_target_pairs={{0,3},{1,0},{2,1},{3,2},{4,7},{5,4},{6,5},{7,6},{8,11},{9,8},{10,9... | collective-permute-start | bytes 393224 | tf_op jit(solution)/shard_map/ppermute | solution.py:1369
  422.5 28.6 %collective-permute-start.40 = (bf16[4,1024,128]{2,1,0:T(8,128)(2,1)}, bf16[4,1024,128]{2,1,0:T(8,128)(2,1)S(1)}, u32[]{:S(2)}, u32[]{:S(2)}) collective-permute-start(bf16[4,1024,128]{2,1,0:T(8,128)(2,1)} %hop.11.refs_9_), channel_id=1, source_target_pairs={{1,0},{2,1},{3,2},{5,4},{6,5},{7,6},{9,8},{10,9},{11,10},{13,12},{... | collective-permute-start | bytes 3145736 | tf_op jit(solution)/shard_map/ppermute | solution.py:1591
  491.6 10.6 %collective-permute-start.44 = (f32[64,1024]{1,0:T(8,128)S(1)}, f32[64,1024]{1,0:T(8,128)S(1)}, u32[]{:S(2)}, u32[]{:S(2)}) collective-permute-start(f32[64,1024]{1,0:T(8,128)S(1)} %select_maximum_fusion), channel_id=1, source_target_pairs={{1,0},{2,1},{3,2},{5,4},{6,5},{7,6},{9,8},{10,9},{11,10},{13,12},{... | collective-permute-start | bytes 786440 | tf_op jit(solution)/shard_map/ppermute | solution.py:1620
  503.4 28.7 %collective-permute-start.49 = (bf16[2,16,7296]{2,1,0:T(8,128)(2,1)}, bf16[2,16,7296]{2,1,0:T(8,128)(2,1)S(1)}, u32[]{:S(2)}, u32[]{:S(2)}) collective-permute-start(bf16[2,16,7296]{2,1,0:T(8,128)(2,1)} %get-tuple-element.259.refs_1_), channel_id=1, source_target_pairs={{0,8},{4,12},{8,0},{12,4},{16,24},{20,28},{24,16},{28,20},{1,9},{5... | collective-permute-start | bytes 1400840 | tf_op jit(solution)/shard_map/ppermute | solution.py:1354
  504.7 27.4 %collective-permute-start.50 = (bf16[2,16,7296]{2,1,0:T(8,128)(2,1)}, bf16[2,16,7296]{2,1,0:T(8,128)(2,1)S(1)}, u32[]{:S(2)}, u32[]{:S(2)}) collective-permute-start(bf16[2,16,7296]{2,1,0:T(8,128)(2,1)} %get-tuple-element.259.refs_1_), channel_id=1, source_target_pairs={{0,16},{4,20},{8,24},{12,28},{16,0},{20,4},{24,8},{28,12},{1,17},{... | collective-permute-start | bytes 1400840 | tf_op jit(solution)/shard_map/ppermute | solution.py:1354
  506.1 26.1 %collective-permute-start.51 = (bf16[2,16,7296]{2,1,0:T(8,128)(2,1)}, bf16[2,16,7296]{2,1,0:T(8,128)(2,1)S(1)}, u32[]{:S(2)}, u32[]{:S(2)}) collective-permute-start(bf16[2,16,7296]{2,1,0:T(8,128)(2,1)} %get-tuple-element.259.refs_1_), channel_id=1, source_target_pairs={{0,24},{4,28},{8,16},{12,20},{16,8},{20,12},{24,0},{28,4},{1,25},{... | collective-permute-start | bytes 1400840 | tf_op jit(solution)/shard_map/ppermute | solution.py:1354
  (55 other events, 323.4 us)
Sparse Core Ops, SparseCore 0:
  15.2 62.4 all-gather.7
  79.8 44.6 all-gather.5
  126.0 44.5 all-gather.9

commit v5 on v4

--- a/solution.py
+++ b/solution.py
@@ -37,6 +37,15 @@
     return pl.CostEstimate(
         flops=int(flops) // 8, bytes_accessed=int(size) // 8, transcendentals=0
     )
+
+
+def entering(refs, b):
+    per = refs[0].shape[0] // CB
+    rows = pl.ds(pl.multiple_of(b % per * CB, CB), CB)
+    out = refs[0][rows, :]
+    for p in range(1, len(refs)):
+        out = jnp.where(b // per == p, refs[p][rows, :], out)
+    return out
 
 
 def kind_rows(packed, b, kind):
@@ -234,9 +243,15 @@
     )(*ops, nt, taps, *later)
 
 
-def steps_kernel(n_w, order, hb, sub, lo, hi, hs, *refs):
+def steps_kernel(n_w, order, hb, sub, lo, hi, hs, flat, *refs):
     nt, numbers = refs[n_w : n_w + 2]
-    hp_o, sig_o, speed_o, w_o = refs[-4:]
+    hp_o, sig_o, speed_o, w_o, ids_o = refs[-5:]
+    if flat is None:
+        ids_o[...] = jnp.zeros_like(ids_o)
+    else:
+        marks = joined(refs[n_w + 2 : 2 * n_w + 2], order).astype(f32)
+        spots = [flat.index(m) * CB for m in range(len(flat))]
+        ids_o[...] = jnp.concatenate([marks[:1, v : v + 128] for v in spots], axis=0)
     length = sig_o.shape[1]
     heads = sig_o.shape[0]
     w = joined(refs[:n_w], order)
@@ -271,57 +286,96 @@
             hp_o[b, 2 * hb :, cols] = delta[mine, cols]
 
 
-def steps_call(arrays, first, order, nt, pk, lo, hi, hs, length, later):
+def steps_call(arrays, first, order, nt, pk, lo, hi, hs, length, later, flat=None):
     heads = (hi - lo) * hs
     hb = CB // HEAD
     ops, specs = row_specs([arrays], first, heads)
+    n_w = len(ops)
+    marks = ([], []) if flat is None else row_specs([arrays], first + heads, 16)
     vm = pl.BlockSpec(memory_space=pltpu.VMEM)
     return pl.pallas_call(
-        functools.partial(steps_kernel, len(ops), order, hb, SUB, lo, hi, hs),
+        functools.partial(steps_kernel, n_w, order, hb, SUB, lo, hi, hs, flat),
         grid=(1,),
         in_specs=specs
         + [vm, pl.BlockSpec((pk.shape[0], 16, CB), lambda i: (0, 3, 0))]
+        + marks[1]
         + [pl.BlockSpec(memory_space=pl.ANY)] * len(later),
-        out_specs=[vm] * 4,
+        out_specs=[vm] * 5,
         out_shape=[
             jax.ShapeDtypeStruct((heads // hb, 3 * hb, length), f32),
             jax.ShapeDtypeStruct((heads, length), f32),
             jax.ShapeDtypeStruct((heads, 128), f32),
             jax.ShapeDtypeStruct((heads, nt.shape[0]), bf16),
+            jax.ShapeDtypeStruct((8, 128), f32),
         ],
         compiler_params=compiler_params(1),
         cost_estimate=cost(nt.shape[0] * nt.shape[1] * 128, nt.size * 2),
         name="steps",
-    )(*ops, nt, pk, *later)
-
-
-def hop_kernel(hb, got, own, hp, *rest):
+    )(*ops, nt, pk, *marks[0], *later)
+
+
+def far_kernel(ch, first, hs, place, src, a_o, b_o):
+    j = pl.program_id(0)
+    half = ch // 2
+    at = pl.ds(pl.multiple_of(j * half, half), half)
+    a_o[at, :] = src[:half, :]
+    b_o[at, :] = src[half:ch, :]
+    steps = pl.ds(pl.multiple_of(pl.num_programs(0) * half + j * hs, hs), hs)
+    a_o[steps, :] = src[first : first + hs, :]
+
+
+def far_call(place, gathered, ch, first, hs):
+    planes, rows, depth = gathered.shape
+    n = planes - 1
+    shapes = [(n * (ch // 2 + hs), depth), (n * ch // 2, depth)]
+    return pl.pallas_call(
+        functools.partial(far_kernel, ch, first, hs),
+        grid_spec=pltpu.PrefetchScalarGridSpec(
+            num_scalar_prefetch=1,
+            grid=(n,),
+            in_specs=[
+                pl.BlockSpec((None, rows, depth), lambda j, p: ((p[0] + j + 1) % planes, 0, 0))
+            ],
+            out_specs=[pl.BlockSpec(v, lambda j, p: (0, 0)) for v in shapes],
+        ),
+        out_shape=[jax.ShapeDtypeStruct(v, bf16) for v in shapes],
+        compiler_params=compiler_params(1),
+        cost_estimate=cost(8, gathered.size * 4),
+        name="far",
+    )(place, gathered)
+
+
+def hop_kernel(hb, shift, got, own, hp, *rest):
     out = rest[-1]
-    length = hp.shape[2]
-    for c in range(hp.shape[0]):
-        rows = slice(c * CB, (c + 1) * CB)
-        total = jnp.exp2(hp[c, hb : 2 * hb, length - 1 : length])
-        out[rows, :] = (per_head(got[rows, :].astype(f32), total) + own[rows, :]).astype(bf16)
+    slots, per, length = hp.shape[0], hp.shape[1], hp.shape[3]
+    for s in range(slots):
+        for c in range(per):
+            rows = slice(c * CB, (c + 1) * CB)
+            total = jnp.exp2(hp[s, c, hb : 2 * hb, length - 1 : length])
+            came = got[(s + shift) % slots, rows, :].astype(f32)
+            out[s, rows, :] = (per_head(came, total) + own[s, rows, :]).astype(bf16)
 
 
 def hop_call(got, shift, own, hp, part=0, later=()):
     slots, rows, state_w = got.shape
-    parts = own.shape[1] // rows
+    per = rows // CB
+    by_slot = hp.reshape((slots, hp.shape[0] // slots) + hp.shape[1:])
+    whole = lambda shape: pl.BlockSpec(shape, lambda i: (0,) * len(shape))
     return pl.pallas_call(
-        functools.partial(hop_kernel, CB // HEAD),
-        grid=(slots,),
+        functools.partial(hop_kernel, CB // HEAD, shift),
+        grid=(1,),
         in_specs=[
-            pl.BlockSpec((None, rows, state_w), lambda s: ((s + shift) % slots, 0, 0)),
-            pl.BlockSpec((None, rows, state_w), lambda s: (s, part, 0)),
-            pl.BlockSpec((rows // CB,) + hp.shape[1:], lambda s: (s * parts + part, 0, 0)),
+            whole(got.shape),
+            pl.BlockSpec((slots, rows, state_w), lambda i: (0, part, 0)),
+            pl.BlockSpec((slots, per) + hp.shape[1:], lambda i: (0, part, 0, 0)),
         ]
         + [pl.BlockSpec(memory_space=pl.ANY)] * len(later),
-        out_specs=pl.BlockSpec((None, rows, state_w), lambda s: (s, 0, 0)),
-        out_shape=jax.ShapeDtypeStruct((slots, rows, state_w), bf16),
+        out_specs=whole(got.shape),
+        out_shape=jax.ShapeDtypeStruct(got.shape, bf16),
         compiler_params=compiler_params(1),
         cost_estimate=cost(got.size * 4, got.size * 8),
         name="hop",
-    )(got, own, hp, *later)
+    )(got, own, by_slot, *later)
 
 
 def hold_kernel(n_joined, *refs):
@@ -555,13 +609,13 @@
     return total
 
 
-def gate_kernel(hb, inner, *refs):
-    (z_all, mix_all, wgt_all, ent_all, pk, hp_r, ct, cn) = refs[:8]
-    nout_all, dmix_all, dz_all, sl_all, sent_all = refs[8:13]
-    mix_sc, turn_sc, sq_sc, dot_sc, gain_sc = refs[13:]
+def gate_kernel(hb, inner, paths, *refs):
+    (z_all, mix_all, wgt_all, pk, hp_r, ct, cn) = refs[:7]
+    ent_all = refs[7 : 7 + paths]
+    nout_all, dmix_all, dz_all, sl_all, sent_all = refs[7 + paths : 12 + paths]
+    mix_sc, turn_sc, sq_sc, dot_sc, gain_sc = refs[12 + paths :]
     phase, slot = pl.program_id(0), pl.program_id(1)
     blocks = z_all.shape[0] // CB
-    per = ent_all.shape[1] // CB
 
     def gates(ref, rows):
         z = ref[rows, :].astype(f32)
@@ -579,8 +633,7 @@
         def _(b):
             z_r, mix_r, wgt_r = [block_rows(v, b) for v in (z_all, mix_all, wgt_all)]
             cum = jnp.exp2(hp_r[b, hb : 2 * hb])
-            ent = ent_all[b // per, pl.ds(pl.multiple_of(b % per * CB, CB), CB), :]
-            turn_sc[...] = dot(ent, ct[...])
+            turn_sc[...] = dot(entering(ent_all, b), ct[...])
             sq, dots = sq_sc[...], dot_sc[...]
             for r in range(0, CB, ROWS):
                 rows = slice(r, r + ROWS)
@@ -635,20 +688,20 @@
     held = lambda p, s: jnp.where(p == 0, s, slots - 1)
     later = lambda w: pl.BlockSpec((None, ch, w), lambda p, s: (jnp.where(p == 1, s, 0), 0, 0))
     return pl.pallas_call(
-        functools.partial(gate_kernel, hb, inner),
+        functools.partial(gate_kernel, hb, inner, len(ent)),
         grid=(2, slots),
         in_specs=[
             per_chan(z),
             pl.BlockSpec((None, ch, length), lambda p, s: (held(p, s), 0, 0)),
             per_chan(wgt),
-            pl.BlockSpec(
-                (ent.shape[0], None) + ent.shape[2:],
-                lambda p, s: (0, (held(p, s) + 1) % slots, 0, 0),
-            ),
             pl.BlockSpec((None, ch // 4, CB), lambda p, s: (s, 0, 0)),
             pl.BlockSpec((ncb,) + hp.shape[1:], lambda p, s: (s, 0, 0)),
             full(ct),
             full(cn),
+        ]
+        + [
+            pl.BlockSpec((None,) + v.shape[1:], lambda p, s: ((held(p, s) + 1) % slots, 0, 0))
+            for v in ent
         ],
         out_specs=[later(length), later(length), later(length), later(128), later(128)],
         out_shape=[
@@ -668,17 +721,17 @@
         compiler_params=compiler_params(2),
         cost_estimate=cost(slots * ch * length * 600, slots * ch * length * 22),
         name="gate",
-    )(z, mix, wgt, ent, pk, hp, ct, cn)
-
-
-def back_kernel(hb, sub, *refs):
-    (dy_all, xc_all, hp_r, ent_all, loc_all, ct, cn, bt, cbt) = refs[:9]
+    )(z, mix, wgt, pk, hp, ct, cn, *ent)
+
+
+def back_kernel(hb, sub, paths, *refs):
+    (dy_all, xc_all, hp_r, loc_all, ct, cn, bt, cbt) = refs[:8]
+    ent_all = refs[8 : 8 + paths]
     dxs_all, u1_all, u2_all, kl_all, dcb_o, db_o, dc_o = refs[-12:-5]
     xs_sc, turn_sc, dxi_sc, dm_sc, w_sc = refs[-5:]
     w_sc[...] = jnp.zeros_like(w_sc)
     length = ct.shape[1]
     nsub = length // sub
-    per = ent_all.shape[1] // CB
 
     @pl.when(pl.program_id(0) == 0)
     def _():
@@ -707,8 +760,7 @@
             ecum = jnp.exp2(cum)
             last = cum[:, sub - 1 : sub]
             ends = jnp.exp2(last - cum)
-            ent = ent_all[b // per, pl.ds(pl.multiple_of(b % per * CB, CB), CB), :]
-            state = ent.astype(f32)
+            state = entering(ent_all, b).astype(f32)
             if s > 0:
                 before = hp[hb : 2 * hb, s * sub - 1 : s * sub]
                 state = loc_all[s - 1, rows, :] + per_head(state, jnp.exp2(before))
@@ -767,21 +819,19 @@
     blk_out = lambda w: pl.BlockSpec((ncb, hb, w), lambda s: (s, 0, 0))
     blocks = slots * ncb
     return pl.pallas_call(
-        functools.partial(back_kernel, hb, SUB),
+        functools.partial(back_kernel, hb, SUB, len(ent)),
         grid=(slots,),
         in_specs=[
             per_chan(length),
             per_chan(length),
             pl.BlockSpec((ncb,) + hp.shape[1:], lambda s: (s, 0, 0)),
-            pl.BlockSpec(
-                (ent.shape[0], None) + ent.shape[2:], lambda s: (0, (s + 1) % slots, 0, 0)
-            ),
             pl.BlockSpec((None,) + loc.shape[1:], lambda s: (s, 0, 0, 0)),
             full(ct),
             full(cn),
             full(bt),
             full(cbt),
         ]
+        + [pl.BlockSpec((None,) + v.shape[1:], lambda s: ((s + 1) % slots, 0, 0)) for v in ent]
         + [pl.BlockSpec(memory_space=pl.ANY)] * len(later),
         out_specs=[
             per_chan(length),
@@ -811,15 +861,15 @@
         compiler_params=compiler_params(1),
         cost_estimate=cost(slots * ch * length * SUB * 20, slots * ch * length * 8),
         name="state_back",
-    )(dy, xc, hp, ent, loc, ct, cn, bt, cbt, *later)
-
-
-def finish_kernel(hb, *refs):
-    (dxs_all, dy_all, xc_all, dz_all, pk, hp_r, ent_all, adj_all, bt, low) = refs[:10]
+    )(dy, xc, hp, loc, ct, cn, bt, cbt, *ent, *later)
+
+
+def finish_kernel(hb, paths, *refs):
+    (dxs_all, dy_all, xc_all, dz_all, pk, hp_r, adj_all, bt, low) = refs[:9]
+    ent_all = refs[9 : 9 + paths]
     dx_all, tail_all, head_all, gx_all, dl_o, dd_all, u2_all, kf_all, db_o = refs[-14:-5]
     turn_sc, xs_sc, head_sc, all_sc, tap_sc = refs[-5:]
     length = bt.shape[1]
-    per = ent_all.shape[1] // CB
 
     @pl.when(pl.program_id(0) == 0)
     def _():
@@ -835,7 +885,8 @@
         last = total[:, length - 1 : length]
         ends = jnp.exp2(last - total)
         adj_low = adj_all[rows, :]
-        ent = ent_all[b // per, b % per * CB : (b % per + 1) * CB, :]
+        per = ent_all[0].shape[0] // CB
+        ent = ent_all[b // per][b % per * CB : (b % per + 1) * CB, :]
         turn_sc[...] = dot(adj_low, bt[...])
         kf_all[b] = head_sums(adj_low.astype(f32) * ent.astype(f32), hb) * jnp.exp2(last)
         u2, dd = [], []
@@ -889,7 +940,7 @@
     turned = lambda w: pl.BlockSpec((None, w, ch), lambda s: (s, 0, 0))
     blocks = slots * ncb
     return pl.pallas_call(
-        functools.partial(finish_kernel, hb),
+        functools.partial(finish_kernel, hb, len(ent)),
         grid=(slots,),
         in_specs=[
             chan(length),
@@ -898,13 +949,11 @@
             chan(length),
             pl.BlockSpec((None, ch // 4, CB), lambda s: (s, 0, 0)),
             pl.BlockSpec((ncb,) + hp.shape[1:], lambda s: (s, 0, 0)),
-            pl.BlockSpec(
-                (ent.shape[0], None) + ent.shape[2:], lambda s: (0, (s + 1) % slots, 0, 0)
-            ),
             pl.BlockSpec((None, ch, 128), lambda s: ((s + slots - 1) % slots, 0, 0)),
             full(bt),
             full(low),
         ]
+        + [pl.BlockSpec((None,) + v.shape[1:], lambda s: ((s + 1) % slots, 0, 0)) for v in ent]
         + [pl.BlockSpec(memory_space=pl.ANY)] * len(later),
         out_specs=[
             chan(length),
@@ -938,7 +987,7 @@
         compiler_params=compiler_params(1),
         cost_estimate=cost(slots * ch * length * 700, slots * ch * length * 14),
         name="finish_back",
-    )(dxs, dy, xc, dz, pk, hp, ent, adj, bt, low, *later)
+    )(dxs, dy, xc, dz, pk, hp, adj, bt, low, *ent, *later)
 
 
 def glue_kernel(flat_order, quick, sub, *refs):
@@ -1264,35 +1313,52 @@
     )
 
 
-def assemble_kernel(n, planes, ch, *refs):
+def assemble_kernel(n, single, ch, ids, *refs):
     parts = refs[:n]
     down_o, up_o, down_out_o, up_out_o = refs[n:]
-    which = pl.program_id(0).astype(f32)
-    total = None
-    for ref in parts:
-        for b in range(ref.shape[0]):
-            chosen = jnp.where(ref[b, :, -1:].astype(f32) == which, 1.0, 0.0)
-            term = ref[b, :, :-128].astype(f32) * chosen
-            total = term if total is None else total + term
-    up_o[:, 0, :] = total[:, :ch]
-    up_o[:, 1, :] = total[:, ch : 2 * ch]
-    down_out_o[...] = total[:, 2 * ch : 3 * ch]
-    width = down_o.shape[1]
-    down_o[...] = total[:, 3 * ch : 3 * ch + width]
-    up_out_o[...] = total[:, 3 * ch + width :]
-
-
-def assemble_call(parts, adapters, planes, ch, width):
+    here = down_o.shape[0]
+    width = down_o.shape[2]
+    first = pl.program_id(0) * here
+    blocks = [(ref, b) for ref in parts for b in range(ref.shape[0])]
+
+    def put(a, total):
+        up_o[a, :, 0, :] = total[:, :ch]
+        up_o[a, :, 1, :] = total[:, ch : 2 * ch]
+        down_out_o[a] = total[:, 2 * ch : 3 * ch]
+        down_o[a] = total[:, 3 * ch : 3 * ch + width]
+        up_out_o[a] = total[:, 3 * ch + width :]
+
+    for a in range(here):
+        if single:
+            for m, (ref, b) in enumerate(blocks):
+
+                @pl.when(ids[m] == first + a)
+                def _(ref=ref, b=b, a=a):
+                    put(a, ref[b].astype(f32))
+
+        else:
+            total = None
+            for m, (ref, b) in enumerate(blocks):
+                chosen = jnp.where(ids[m] == first + a, 1.0, 0.0)
+                term = ref[b].astype(f32) * chosen
+                total = term if total is None else total + term
+            put(a, total)
+
+
+def assemble_call(ids, parts, adapters, ch, width):
     rank = parts[0].shape[1]
+    each = adapters // 2 if adapters % 2 == 0 else adapters
+    single = ids.shape[0] == adapters
     return pl.pallas_call(
-        functools.partial(assemble_kernel, len(parts), planes, ch),
-        grid=(adapters,),
-        in_specs=[pl.BlockSpec(a.shape, lambda i: (0, 0, 0)) for a in parts],
+        functools.partial(assemble_kernel, len(parts), single, ch),
+        grid=(adapters // each,),
+        in_specs=[pl.BlockSpec(memory_space=pltpu.SMEM)]
+        + [pl.BlockSpec(a.shape, lambda i: (0, 0, 0)) for a in parts],
         out_specs=[
-            pl.BlockSpec((None, rank, width), lambda i: (i, 0, 0)),
-            pl.BlockSpec((None, rank, 2, ch), lambda i: (i, 0, 0, 0)),
-            pl.BlockSpec((None, rank, ch), lambda i: (i, 0, 0)),
-            pl.BlockSpec((None, rank, width), lambda i: (i, 0, 0)),
+            pl.BlockSpec((each, rank, width), lambda i: (i, 0, 0)),
+            pl.BlockSpec((each, rank, 2, ch), lambda i: (i, 0, 0, 0)),
+            pl.BlockSpec((each, rank, ch), lambda i: (i, 0, 0)),
+            pl.BlockSpec((each, rank, width), lambda i: (i, 0, 0)),
         ],
         out_shape=[
             jax.ShapeDtypeStruct((adapters, rank, width), f32),
@@ -1303,7 +1369,7 @@
         compiler_params=compiler_params(1),
         cost_estimate=cost(1e7, 2e7),
         name="assemble",
-    )(*parts)
+    )(ids, *parts)
 
 
 def body(
@@ -1430,7 +1496,10 @@
     if quick:
         own = halves(
             [wt[0], wt[1], out_weight],
-            ([maps_w[:state_w], steps_w], [maps_w[state_w:]]),
+            (
+                [maps_w[:state_w], steps_w, jnp.full((16, rows_here), pick).astype(bf16)],
+                [maps_w[state_w:]],
+            ),
         )
         got = pass_one(own)
         all_x = lax.all_gather(
@@ -1442,11 +1511,16 @@
         two = pass_two(own)
         swapped = pass_core(own)
         marks = [ch, ch + 64 * ncb, ch + 64 * ncb + hs]
-        all_x = slot_order(all_x)
-        pk = jnp.stack([v[marks[0] : marks[1]] for v in all_x])
-        last_rows = all_x[planes - 1][marks[2] :]
-        far_x = halves(
-            [v[:ch] for v in all_x[1:]], ([v[marks[1] : marks[2]] for v in all_x[1:]], ())
+        ends = all_x.shape[1]
+
+        def rows_of(j, lo, hi):
+            start = ((place + j) % planes, lo, 0)
+            return lax.dynamic_slice(all_x, start, (1, hi - lo, rows_here))[0]
+
+        pk = jnp.stack([rows_of(j, marks[0], marks[1]) for j in range(planes)])
+        last_rows = rows_of(planes - 1, marks[2], ends)
+        far_x = list(
+            far_call(jnp.reshape(place, (1,)).astype(jnp.int32), all_x, ch, marks[1], hs)
         )
         token, passed, _ = hold(swapped, two + far_x)
         two, far_x = passed[:2], passed[2:]
@@ -1483,10 +1557,15 @@
     bt, ct, b_low, c_low, cbt, maps_pre, maps_w = maps_call(
         all_maps, maps_at, maps_rows, picks, nt, conv_maps, length, held
     )
-    hp, step_sig, speed, mine_w = steps_call(
-        all_steps, steps_at, picks[0], nt, pk, 0, mine_slots, hs, length, held
+    hp, step_sig, speed, mine_w, found = steps_call(
+        all_steps, steps_at, picks[0], nt, pk, 0, mine_slots, hs, length, held,
+        tuple(flat) if quick else None,
     )
     small_w = [maps_w, mine_w]
+    if quick:
+        ids = found[:, 0].astype(jnp.int32)
+    else:
+        ids = lax.all_gather(adapter_ids, "dp", axis=0, tiled=True)
 
     x_args = (picks, nt, low2, pk, ch)
     z_args = (picks, nt, low2, pk, ch, HALO, False)
@@ -1514,7 +1593,7 @@
         token, far_o, far_z = hold([beside] + far_x[0] + far_x[1], far_o, zip(far_z, got))
         two = pass_two(far_z)
         swapped = pass_core(far_z)
-        hp_far, sig_far, speed_far, far_w = steps_call(
+        hp_far, sig_far, speed_far, far_w, _ = steps_call(
             far_x[0], own_rows, picks[0], nt, pk, 1, planes, hs, length, [token]
         )
         hp = jnp.concatenate([hp, hp_far], axis=0)
@@ -1528,12 +1607,11 @@
         bufs, done = scan_call(
             1, planes, (far_x, 0), 1, *x_args, hp, ct, b_low, cbt, bufs[:4] + [sent_b], [token]
         )
-        sent_b = bufs[4]
-        token, passed, _ = hold([done] + swapped, two + far_o + [ent_a, sent_b])
-        two, far_o, (ent_a, sent_b) = passed[:2], passed[2:4], passed[4:]
+        ent_b = lax.ppermute(bufs[4], "tensor", halo)
+        token, passed, _ = hold([done] + swapped, two + far_o + [ent_a])
+        two, far_o, (ent_a,) = passed[:2], passed[2:4], passed[4:]
         far_z = as_paths(far_z + two, swapped + pass_core(two))
         got = pass_one(far_o)
-        ent_b = lax.ppermute(sent_b, "tensor", halo)
         ent_a = lax.ppermute(hop_call(ent_a, 1, bufs[3], hp, 0, [token]), "tensor", halo)
 
         token, passed, far_o = hold(far_z[0] + far_z[1], [ent_a, ent_b], zip(far_o, got))
@@ -1552,7 +1630,6 @@
         ent_b = lax.ppermute(send_b, "tensor", halo)
         wgt, done = proj_call(1, planes, (far_o, 0), *o_args, wgt, [send_b])
         _, ent, _ = hold([done], [ent_a, ent_b])
-        ent = jnp.stack(ent)
         z_sets = [((0, 1), own, 0), ((1, planes), far_z, 0)]
         x_sets = [((0, 1), own, 1), ((1, planes), far_x, 0)]
         o_sets = [((0, 1), own, 2), ((1, planes), far_o, 0)]
@@ -1571,7 +1648,7 @@
         ent = lax.ppermute(bufs[4], "tensor", halo)
         for _ in range(planes - 2):
             ent = lax.ppermute(hop_call(ent, 1, bufs[3], hp), "tensor", halo)
-        ent = ent[None]
+        ent = [ent]
         z_sets = [((0, planes), wz, 0)]
         x_sets = [((0, planes), wx, 0)]
         o_sets = [((0, planes), o, 0)]
@@ -1626,13 +1703,12 @@
             early[:, ch : 2 * ch],
             late[:, ch:],
             early[:, 2 * ch :],
-            jnp.full((rank, 128), pick).astype(f32),
         ],
         axis=1,
     ).astype(bf16)[None]
     if quick:
+        _, (sent,), _ = hold([near], [sent])
         both = jnp.concatenate([sent, flip(sent, 1)], axis=0)
-        _, (both,), _ = hold([near], [both])
         by_seq = [both] + [flip(both, bit) for bit in (2, 4, 6)]
     else:
         by_seq = [lax.all_gather(sent[0], "dp", axis=0)]
@@ -1643,7 +1719,7 @@
     )
     if quick:
         _, by_seq, _ = hold([tokens_grad], by_seq)
-    g_down, g_up, g_down_out, g_up_out = assemble_call(by_seq, adapters, planes, ch, width)
+    g_down, g_up, g_down_out, g_up_out = assemble_call(ids, by_seq, adapters, ch, width)
     g_down = jnp.swapaxes(g_down, 1, 2)
     g_down_out = jnp.swapaxes(g_down_out, 1, 2)
     return (mixed[None], tokens_grad[None], g_down, g_up, g_down_out, g_up_out)

time: 557 us -> 549 us (0.986)
  waiting for transfers between devices: 100 us -> 107 us
    ppermute x36, waiting for transfers between devices: 31.3 us -> 40.9 us  [flip(): return lax.ppermute(v, 'dp', [(i, i ^ bit) for i in range(seqs)])]
    ppermute x36, starting transfers between devices: 28.4 us -> 22.6 us  [flip(): return lax.ppermute(v, 'dp', [(i, i ^ bit) for i in range(seqs)])]
    pallas_call x12 -> x13, Pallas kernels: 107 us -> 103 us  [the longest x1 25.5 us: back_call(): pl.pallas_call(functools.partial(back_kernel, hb, SUB, len(ent)), grid=(s...]
    unnamed x110 -> x108, local copies, waits for them, and re-layouts: 24.7 us -> 22.2 us
  transfers between devices with their start and end apart: 55 -> 55, of which waited for: 18 -> 21; matrix products, arithmetic and copies ran while one was open for 5% -> 4% of each run, Pallas kernels for 42% -> 42%
where the time goes in v5:
time: 549 us; the launch traced here: 538 us
  Pallas kernels  295 us (54%)
  waiting for transfers between devices  107 us (19%)
  starting transfers between devices  65.5 us (12%)
  local copies, waits for them, and re-layouts  37.5 us (7%)
  between operations  17.8 us (3%)
  other arithmetic  15.2 us (3%)
    pallas_call x4, Pallas kernels, scan_call(): pl.pallas_call(functools.partial(scan_kernel, nx, picks[part], hb, SUB),...  49.1 us
    ppermute x36, waiting for transfers between devices, flip(): return lax.ppermute(v, 'dp', [(i, i ^ bit) for i in range(seqs)])  40.9 us
    pallas_call x4, Pallas kernels, proj_call(): pl.pallas_call(functools.partial(proj_kernel, picks, n_w, cut, gain), gri...  39 us
    all_gather x1, waiting for transfers between devices, body(): lax.all_gather(jnp.concatenate([wt[1], packed, steps_w, last_rows], axis=...  31.4 us
    pallas_call x1, Pallas kernels, back_call(): pl.pallas_call(functools.partial(back_kernel, hb, SUB, len(ent)), grid=(s...  25.5 us
    pallas_call x1, Pallas kernels, input_call(): pl.pallas_call(functools.partial(input_kernel, sets, picks, flat, quick,...  24.9 us
    ppermute x36, starting transfers between devices, flip(): return lax.ppermute(v, 'dp', [(i, i ^ bit) for i in range(seqs)])  22.6 us
    unnamed x108, local copies, waits for them, and re-layouts  22.2 us
  transfers between devices with their start and end apart: 55, of which 21 were waited for; matrix products, arithmetic and copies ran while one was open for 4% of the time, Pallas kernels for 42%

profile of v5, /device:TPU:0, one launch (start us, length us, event | category | flops | bytes accessed | tf_op | source)
XLA Modules:
  0.0 538.5 jit_solution(5942662515977136527)
XLA Ops:
  16.3 3.0 collective-permute-start
  21.1 18.9 %collective-permute-done.1.refs_3_ = bf16[1664,256]{1,0:T(8,128)(2,1)} collective-permute-done((bf16[1664,256]{1,0:T(8,128)(2,1)S(1)}, bf16[1664,256]{1,0:T(8,128)(2,1)}, u32[]{:S(2)}, u32[]{:S(2)}) %collective-permute-start.1) | collective-permute-done | bytes 852000 | tf_op jit(solution)/shard_map/ppermute | solution.py:1420
  41.0 3.9 hold.11
  47.1 31.4 %all-gather.8.cloned.1.call-done = bf16[5696,256]{1,0:T(8,128)(2,1)} async-done(((bf16[1424,256]{1,0:T(8,128)(2,1)}), bf16[5696,256]{1,0:T(8,128)(2,1)}) %all-gather.8.cloned.1.call-update) | async-done | bytes 2916368 | tf_op jit(solution)/shard_map/all_gather | solution.py:1505
  78.5 3.5 far.1
  82.0 4.3 collective-permute-done.5.refs_3_
  95.5 9.6 %turn.1 = (bf16[512,2048]{1,0:T(8,128)(2,1)}, bf16[512,2048]{1,0:T(8,128)(2,1)}, f32[512,1]{1,0:T(8,128)}, bf16[16,640]{1,0:T(8,128)(2,1)}, bf16[16,512]{1,0:T(8...) custom-call(s32[2]{0:T(128)} %pad_add_fusion.refs_0_.refs_16_, bf16[512,2048]{1,0:T(8,128)(2,1)} %bitcast.135, ...), custom_call_target="tpu_custom_call" | custom-call | flops 26214400 | bytes 2097152 | tf_op jit(solution)/shard_map/turn/pallas_call | solution.py:162
  110.5 3.7 hold.13
  117.2 3.9 steps.2
  121.1 5.7 %maps.1 = (bf16[128,512]{1,0:T(8,128)(2,1)}, bf16[128,512]{1,0:T(8,128)(2,1)}, bf16[512,128]{1,0:T(8,128)(2,1)}, bf16[512,128]{1,0:T(8,128)(2,1)}, f32[2,256,256...) custom-call(bf16[2,1696,256]{2,1,0:T(8,128)(2,1)} %get-tuple-element.140.refs_6_.refs_0_.refs_7_.refs_2_.refs_20_, ...), custom_call_target="tpu_custom_call" | custom-call | flops 83886080 | bytes 589824 | tf_op jit(solution)/shard_map/maps/pallas_call | solution.py:226
  126.7 8.2 %scan_slots.4 = (bf16[4,1024,512]{2,1,0:T(8,128)(2,1)}, f32[4,1024,512]{2,1,0:T(8,128)}, f32[4,1,1024,128]{3,2,1,0:T(8,128)}, f32[4,1024,128]{2,1,0:T(8,128)}, b...) custom-call(bf16[2,1696,256]{2,1,0:T(8,128)(2,1)} %get-tuple-element.140.refs_6_.refs_0_.refs_7_.refs_2_.refs_20_, ...), custom_call_target="tpu_custom_call" | custom-call | flops 268435456 | bytes 524288 | tf_op jit(solution)/shard_map/scan_slots/pallas_call | solution.py:523
  135.0 8.6 %scan_slots.5 = (bf16[4,1024,512]{2,1,0:T(8,128)(2,1)}, f32[4,1024,512]{2,1,0:T(8,128)}, f32[4,1,1024,128]{3,2,1,0:T(8,128)}, f32[4,1024,128]{2,1,0:T(8,128)}, b...) custom-call(bf16[2,1664,256]{2,1,0:T(8,128)(2,1)} %get-tuple-element, ...), custom_call_target="tpu_custom_call", output_to_operand_aliasing={{0}: (11, {}), {1}: (12, {}), {2}: (13, {}), {3}: (14, {})} | custom-call | flops 268435456 | bytes 524288 | tf_op jit(solution)/shard_map/scan_slots/pallas_call | solution.py:523
  146.3 6.5 %collective-permute-done.13.refs_4_ = bf16[2,1536,256]{2,1,0:T(8,128)(2,1)} collective-permute-done((bf16[2,1536,256]{2,1,0:T(8,128)(2,1)}, bf16[2,1536,256]{2,1,0:T(8,128)(2,1)}, u32[]{:S(2)}, u32[]{:S(2)}) %collective-permute-start.13) | collective-permute-done | bytes 1572896 | tf_op jit(solution)/shard_map/ppermute | solution.py:1420
  156.5 7.4 %proj_slots.4 = (bf16[4,1024,512]{2,1,0:T(8,128)(2,1)}, bf16[1,1]{1,0:T(2,128)(2,1)}) custom-call(bf16[2,1696,256]{2,1,0:T(8,128)(2,1)} %get-tuple-element.140.refs_6_.refs_0_.refs_7_.refs_2_.refs_20_, bf16[2,1696,256]{2,1,0:T(8,128)(2,1)} %get-tuple-element.147.refs_7_.refs_1_.refs_8_.refs_3_.refs_21_, bf16[2,1696,256]{2,1,0:T(8,128)(2,1)} %copy-done.2, ...), custom_call_target="tpu_custom_call" | custom-call | flops 268435456 | bytes 655360 | tf_op jit(solution)/shard_map/proj_slots/pallas_call | solution.py:586
  163.9 7.2 %proj_slots.5 = (bf16[4,1024,512]{2,1,0:T(8,128)(2,1)}, bf16[1,1]{1,0:T(2,128)(2,1)}) custom-call(bf16[2,1696,256]{2,1,0:T(8,128)(2,1)} %get-tuple-element.140.refs_6_.refs_0_.refs_7_.refs_2_.refs_20_, bf16[2,1696,256]{2,1,0:T(8,128)(2,1)} %get-tuple-element.147.refs_7_.refs_1_.refs_8_.refs_3_.refs_21_, bf16[2,1696,256]{2,1,0:T(8,128)(2,1)} %copy-done.2, ...), custom_call_target="tpu_custom_call" | custom-call | flops 268435456 | bytes 655360 | tf_op jit(solution)/shard_map/proj_slots/pallas_call | solution.py:586
  177.4 4.2 hold.15
  185.0 4.2 steps.3
  191.0 16.2 %scan_slots.6 = (bf16[4,1024,512]{2,1,0:T(8,128)(2,1)}, f32[4,1024,512]{2,1,0:T(8,128)}, f32[4,1,1024,128]{3,2,1,0:T(8,128)}, f32[4,1024,128]{2,1,0:T(8,128)}, b...) custom-call(bf16[2,1584,256]{2,1,0:T(8,128)(2,1)} %get-tuple-element, ...), custom_call_target="tpu_custom_call", output_to_operand_aliasing={{0}: (11, {}), {1}: (12, {}), {2}: (13, {}), {3}: (14, {}),... | custom-call | flops 805306368 | bytes 1572864 | tf_op jit(solution)/shard_map/scan_slots/pallas_call | solution.py:523
  207.2 3.5 collective-permute-start.22
  210.8 16.0 %scan_slots.7 = (bf16[4,1024,512]{2,1,0:T(8,128)(2,1)}, f32[4,1024,512]{2,1,0:T(8,128)}, f32[4,1,1024,128]{3,2,1,0:T(8,128)}, f32[4,1024,128]{2,1,0:T(8,128)}, b...) custom-call(bf16[2,1536,256]{2,1,0:T(8,128)(2,1)} %get-tuple-element, ...), custom_call_target="tpu_custom_call", output_to_operand_aliasing={{0}: (11, {}), {1}: (12, {}), {2}: (13, {}), {3}: (14, {}),... | custom-call | flops 805306368 | bytes 1572864 | tf_op jit(solution)/shard_map/scan_slots/pallas_call | solution.py:523
  230.4 3.4 collective-permute-start.28
  234.9 3.1 hop.6
  238.0 7.4 %collective-permute-done.28.refs_13_ = bf16[4,512,128]{2,1,0:T(8,128)(2,1)S(1)} collective-permute-done((bf16[4,512,128]{2,1,0:T(8,128)(2,1)}, bf16[4,512,128]{2,1,0:T(8,128)(2,1)S(1)}, u32[]{:S(2)}, u32[]{:S(2)}) %collective-permute-start.28) | collective-permute-done | bytes 524320 | tf_op jit(solution)/shard_map/ppermute | solution.py:1610
  245.4 4.3 collective-permute-start.27
  249.7 10.9 %collective-permute-done.27.refs_12_ = bf16[4,512,128]{2,1,0:T(8,128)(2,1)S(1)} collective-permute-done((bf16[4,512,128]{2,1,0:T(8,128)(2,1)}, bf16[4,512,128]{2,1,0:T(8,128)(2,1)S(1)}, u32[]{:S(2)}, u32[]{:S(2)}) %collective-permute-start.27) | collective-permute-done | bytes 524320 | tf_op jit(solution)/shard_map/ppermute | solution.py:1615
  263.7 3.6 hold.17
  268.4 3.1 hop.8.refs_13_
  271.4 5.1 collective-permute-start.32
  276.5 3.1 hop.7.refs_12_
  282.3 12.3 %proj_slots.6 = (bf16[4,1024,512]{2,1,0:T(8,128)(2,1)}, bf16[1,1]{1,0:T(2,128)(2,1)}) custom-call(bf16[2,1536,256]{2,1,0:T(8,128)(2,1)} %get-tuple-element.171.refs_4_.refs_0_.refs_10_, bf16[2,1536,256]{2,1,0:T(8,128)(2,1)} %get-tuple-element.189.refs_5_.refs_1_.refs_11_, bf16[2,1536,256]{2,1,0:T(8,128)(2,1)} %copy-done.7, ...), custom_call_target="tpu_custom_call", output_to_operand_aliasing={{0}: (11, {})} | custom-call | flops 805306368 | bytes 1966080 | tf_op jit(solution)/shard_map/proj_slots/pallas_call | solution.py:586
  296.4 5.8 %collective-permute-done.29.refs_1_ = bf16[2,1536,256]{2,1,0:T(8,128)(2,1)S(1)} collective-permute-done((bf16[2,1536,256]{2,1,0:T(8,128)(2,1)}, bf16[2,1536,256]{2,1,0:T(8,128)(2,1)S(1)}, u32[]{:S(2)}, u32[]{:S(2)}) %collective-permute-start.29) | collective-permute-done | bytes 1572896 | tf_op jit(solution)/shard_map/ppermute | solution.py:1420
  306.0 3.1 hop.9.refs_12_
  309.1 4.3 collective-permute-start.37
  315.5 12.2 %proj_slots.7 = (bf16[4,1024,512]{2,1,0:T(8,128)(2,1)}, bf16[1,1]{1,0:T(2,128)(2,1)}) custom-call(bf16[2,1536,256]{2,1,0:T(8,128)(2,1)} %get-tuple-element.206.refs_0_.refs_15_, bf16[2,1536,256]{2,1,0:T(8,128)(2,1)} %get-tuple-element.207.refs_1_.refs_16_, bf16[2,1536,256]{2,1,0:T(8,128)(2,1)} %copy-done.15, ...), custom_call_target="tpu_custom_call", output_to_operand_aliasing={{0}: (11, {})} | custom-call | flops 805306368 | bytes 1966080 | tf_op jit(solution)/shard_map/proj_slots/pallas_call | solution.py:586
  329.7 21.2 %gate.1 = (bf16[4,1024,512]{2,1,0:T(8,128)(2,1)}, bf16[4,1024,512]{2,1,0:T(8,128)(2,1)}, bf16[4,1024,512]{2,1,0:T(8,128)(2,1)}, f32[4,1024,128]{2,1,0:T(8,128)}, bf16[4,1024,128]{2,1,0:T(8,128)(2,1)}) custom-call(bf16[4,1024,512]{2,1,0:T(8,128)(2,1)} %get-tuple-element.201.refs_0_, f32[4,1024,512]{2,1,0:T(8,128)} %get-tuple-element.202.refs_1_, ...), custom_call_target="tpu_custom_call" | custom-call | flops 157286400 | bytes 5767168 | tf_op jit(solution)/shard_map/gate/pallas_call | solution.py:690
  353.6 20.1 %output.1 = (bf16[512,2048]{1,0:T(8,128)(2,1)}, f32[4,16,1024]{2,1,0:T(8,128)}, f32[16,2048]{1,0:T(8,128)}) custom-call(s32[2]{0:T(128)} %pad_add_fusion.refs_0_.refs_16_, bf16[4,1024,512]{2,1,0:T(8,128)(2,1)} %get-tuple-element.219.refs_1_, bf16[4,256,256]{2,1,0:T(8,128)(2,1)} %pad_maximum_fusion.6.refs_5_.refs_6_.refs_10_.refs_3_.refs_2_.refs_4_, ...), custom_call_target="tpu_custom_call" | custom-call | flops 1073741824 | bytes 2097152 | tf_op jit(solution)/shard_map/output/pallas_call | solution.py:1144
  375.5 3.3 collective-permute-done.38.got
  379.8 3.4 hop.10.refs_18_
  384.5 17.7 %gate_back.1 = (f32[512,2048]{1,0:T(8,128)}, f32[4,16,1024]{2,1,0:T(8,128)}) custom-call(bf16[4,1024,512]{2,1,0:T(8,128)(2,1)} %get-tuple-element.228.refs_0_.refs_3_, bf16[16,640]{1,0:T(8,128)(2,1)} %get-tuple-element.146.refs_5_.refs_9_.refs_1_.refs_8_, bf16[2,1696,256]{2,1,0:T(8,128)(2,1)} %get-tuple-element.140.refs_6_.refs_0_.refs_7_.refs_2_.refs_20_, ...), custom_call_target="tpu_custom_call" | custom-call | flops 1073741824 | bytes 2097152 | tf_op jit(solution)/shard_map/gate_back/pallas_call | solution.py:1185
  414.0 3.3 hop.11.refs_10_
  421.7 25.5 %state_back.1 = (f32[4,1024,512]{2,1,0:T(8,128)}, f32[16,4,512]{2,1,0:T(4,128)}, f32[16,4,512]{2,1,0:T(4,128)}, f32[16,4,256]{2,1,0:T(4,128)}, f32[2,256,256]{2,...) custom-call(bf16[4,1024,512]{2,1,0:T(8,128)(2,1)} %get-tuple-element.222.refs_0_.refs_1_, ...), custom_call_target="tpu_custom_call" | custom-call | flops 1342177280 | bytes 2097152 | tf_op jit(solution)/shard_map/state_back/pallas_call | solution.py:821
  448.3 21.6 %finish_back.1 = (bf16[4,1024,512]{2,1,0:T(8,128)(2,1)}, f32[4,1024,128]{2,1,0:T(8,128)}, f32[4,8,1024]{2,1,0:T(8,128)}, f32[4,16,1024]{2,1,0:T(8,128)}, f32[16,...) custom-call(f32[4,1024,512]{2,1,0:T(8,128)} %get-tuple-element.230.r, ...), custom_call_target="tpu_custom_call" | custom-call | flops 183500800 | bytes 3670016 | tf_op jit(solution)/shard_map/finish_back/pallas_call | solution.py:942
  470.6 5.2 glue.1
  476.9 3.4 collective-permute-start.45
  481.3 3.1 collective-permute-start.47
  488.3 5.2 collective-permute-done.44.refs_3_.refs_7_.refs_10_.refs_0_
  500.7 24.9 %input_back.1.refs_0_ = bf16[512,2048]{1,0:T(8,128)(2,1)} custom-call(s32[2]{0:T(128)} %pad_add_fusion.refs_0_.refs_16_, bf16[4,1024,512]{2,1,0:T(8,128)(2,1)} %get-tuple-element.234.refs_1_, f32[4,1024,128]{2,1,0:T(8,128)} %get-tuple-element.235.refs_2_, f32[64,1024]{1,0:T(8,128)} %copy-done.17, ...), custom_call_target="tpu_custom_call" | custom-call | flops 1073741824 | bytes 2097152 | tf_op jit(solution)/shard_map/input_back/pallas_call | solution.py:1295
  527.8 3.7 assemble.1
  (271 shorter events, 107.6 us)
Async XLA Ops:
  7.2 71.3 %all-gather.8.cloned.1.call-start = ((), (), s32[]{:S(2)}) async-start(), calls=%async_computation.1 | async-start | bytes 3645440 | tf_op jit(solution)/shard_map/all_gather | solution.py:1505
  15.9 127.7 %all-gather.6.cloned.1.call-start = ((), (), s32[]{:S(2)}) async-start(), calls=%async_computation | async-start | bytes 2621440 | tf_op jit(solution)/shard_map/all_gather | solution.py:1508
  16.3 23.7 %collective-permute-start = (bf16[1696,256]{1,0:T(8,128)(2,1)S(1)}, bf16[1696,256]{1,0:T(8,128)(2,1)S(1)}, u32[]{:S(2)}, u32[]{:S(2)}) collective-permute-start(bf16[1696,256]{1,0:T(8,128)(2,1)S(1)} %constant_dynamic-update-slice_fusion.refs_0_), channel_id=1, source_target_pairs={{0,8},{4,12},{8,0},{12,4},{16,24},{20,28},{24,16},{28,20},{1,9},{5... | collective-permute-start | bytes 2605064 | tf_op jit(solution)/shard_map/ppermute | solution.py:1420
  19.5 20.6 %collective-permute-start.1 = (bf16[1664,256]{1,0:T(8,128)(2,1)S(1)}, bf16[1664,256]{1,0:T(8,128)(2,1)}, u32[]{:S(2)}, u32[]{:S(2)}) collective-permute-start(bf16[1664,256]{1,0:T(8,128)(2,1)S(1)} %pad_maximum_fusion.refs_2_), channel_id=1, source_target_pairs={{0,16},{4,20},{8,24},{12,28},{16,0},{20,4},{24,8},{28,12},{1,17},{... | collective-permute-start | bytes 2555912 | tf_op jit(solution)/shard_map/ppermute | solution.py:1420
  21.1 150.8 %all-gather.10.cloned.1.call-start = ((), (), s32[]{:S(2)}) async-start(), calls=%async_computation.2 | async-start | bytes 2621440 | tf_op jit(solution)/shard_map/all_gather | solution.py:1509
  44.8 41.5 %collective-permute-start.4 = (bf16[2,1696,256]{2,1,0:T(8,128)(2,1)}, bf16[2,1696,256]{2,1,0:T(8,128)(2,1)}, u32[]{:S(2)}, u32[]{:S(2)}) collective-permute-start(bf16[2,1696,256]{2,1,0:T(8,128)(2,1)} %get-tuple-element.140.refs_6_.refs_0_.refs_7_.refs_2_.refs_20_), channel_id=1, source_target_pairs={{0,16},{4,20},{8,24},{12,28},{16,0},{20,4},{24,8},{28,12},{1,17},{... | collective-permute-start | bytes 5210120 | tf_op jit(solution)/shard_map/ppermute | solution.py:1420
  46.3 39.9 %collective-permute-start.2 = (bf16[2,1696,256]{2,1,0:T(8,128)(2,1)}, bf16[2,1696,256]{2,1,0:T(8,128)(2,1)S(1)}, u32[]{:S(2)}, u32[]{:S(2)}) collective-permute-start(bf16[2,1696,256]{2,1,0:T(8,128)(2,1)} %get-tuple-element.140.refs_6_.refs_0_.refs_7_.refs_2_.refs_20_), channel_id=1, source_target_pairs={{0,4},{4,0},{8,12},{12,8},{16,20},{20,16},{24,28},{28,24},{1,5},{5... | collective-permute-start | bytes 5210120 | tf_op jit(solution)/shard_map/ppermute | solution.py:1420
  46.3 39.9 %collective-permute-start.5 = (bf16[2,1664,256]{2,1,0:T(8,128)(2,1)}, bf16[2,1664,256]{2,1,0:T(8,128)(2,1)}, u32[]{:S(2)}, u32[]{:S(2)}) collective-permute-start(bf16[2,1664,256]{2,1,0:T(8,128)(2,1)} %get-tuple-element.139.refs_10_.refs_4_.refs_0_.refs_11_.refs_6_.refs_24_), channel_id=1, source_target_pairs={{0,8},{4,12},{8,0},{12,4},{16,24},{20,28},{24,16},{28,20},{1,9},{5... | collective-permute-start | bytes 5111816 | tf_op jit(solution)/shard_map/ppermute | solution.py:1420
  46.9 39.4 %collective-permute-start.3 = (bf16[2,1664,256]{2,1,0:T(8,128)(2,1)}, bf16[2,1664,256]{2,1,0:T(8,128)(2,1)}, u32[]{:S(2)}, u32[]{:S(2)}) collective-permute-start(bf16[2,1664,256]{2,1,0:T(8,128)(2,1)} %get-tuple-element.139.refs_10_.refs_4_.refs_0_.refs_11_.refs_6_.refs_24_), channel_id=1, source_target_pairs={{0,4},{4,0},{8,12},{12,8},{16,20},{20,16},{24,28},{28,24},{1,5},{5... | collective-permute-start | bytes 5111816 | tf_op jit(solution)/shard_map/ppermute | solution.py:1420
  88.0 21.0 %collective-permute-start.7 = (bf16[2,1696,256]{2,1,0:T(8,128)(2,1)}, bf16[2,1696,256]{2,1,0:T(8,128)(2,1)S(1)}, u32[]{:S(2)}, u32[]{:S(2)}) collective-permute-start(bf16[2,1696,256]{2,1,0:T(8,128)(2,1)} %get-tuple-element.147.refs_7_.refs_1_.refs_8_.refs_3_.refs_21_), channel_id=1, source_target_pairs={{0,4},{4,0},{8,12},{12,8},{16,20},{20,16},{24,28},{28,24},{1,5},{5... | collective-permute-start | bytes 5210120 | tf_op jit(solution)/shard_map/ppermute | solution.py:1420
  88.0 21.0 %collective-permute-start.6 = (bf16[2,1664,256]{2,1,0:T(8,128)(2,1)}, bf16[2,1664,256]{2,1,0:T(8,128)(2,1)}, u32[]{:S(2)}, u32[]{:S(2)}) collective-permute-start(bf16[2,1664,256]{2,1,0:T(8,128)(2,1)} %get-tuple-element.143.refs_11_.refs_5_.refs_1_.refs_12_.refs_7_.refs_25_), channel_id=1, source_target_pairs={{0,4},{4,0},{8,12},{12,8},{16,20},{20,16},{24,28},{28,24},{1,5},{5... | collective-permute-start | bytes 5111816 | tf_op jit(solution)/shard_map/ppermute | solution.py:1420
  88.6 19.8 %collective-permute-start.9 = (bf16[1536,256]{1,0:T(8,128)(2,1)}, bf16[1536,256]{1,0:T(8,128)(2,1)}, u32[]{:S(2)}, u32[]{:S(2)}) collective-permute-start(bf16[1536,256]{1,0:T(8,128)(2,1)} %get-tuple-element.149.refs_2_), channel_id=1, source_target_pairs={{0,16},{4,20},{8,24},{12,28},{16,0},{20,4},{24,8},{28,12},{1,17},{... | collective-permute-start | bytes 2359304 | tf_op jit(solution)/shard_map/ppermute | solution.py:1420
  89.1 19.9 %collective-permute-start.8 = (bf16[1584,256]{1,0:T(8,128)(2,1)}, bf16[1584,256]{1,0:T(8,128)(2,1)S(1)}, u32[]{:S(2)}, u32[]{:S(2)}) collective-permute-start(bf16[1584,256]{1,0:T(8,128)(2,1)} %get-tuple-element.148.refs_0_), channel_id=1, source_target_pairs={{0,8},{4,12},{8,0},{12,4},{16,24},{20,28},{24,16},{28,20},{1,9},{5... | collective-permute-start | bytes 2433032 | tf_op jit(solution)/shard_map/ppermute | solution.py:1420
  114.2 38.7 %collective-permute-start.12 = (bf16[2,1584,256]{2,1,0:T(8,128)(2,1)}, bf16[2,1584,256]{2,1,0:T(8,128)(2,1)}, u32[]{:S(2)}, u32[]{:S(2)}) collective-permute-start(bf16[2,1584,256]{2,1,0:T(8,128)(2,1)} %get-tuple-element.160.refs_5_.refs_0_.refs_28_), channel_id=1, source_target_pairs={{0,16},{4,20},{8,24},{12,28},{16,0},{20,4},{24,8},{28,12},{1,17},{... | collective-permute-start | bytes 4866056 | tf_op jit(solution)/shard_map/ppermute | solution.py:1420
  115.7 37.1 %collective-permute-start.10 = (bf16[2,1584,256]{2,1,0:T(8,128)(2,1)}, bf16[2,1584,256]{2,1,0:T(8,128)(2,1)S(1)}, u32[]{:S(2)}, u32[]{:S(2)}) collective-permute-start(bf16[2,1584,256]{2,1,0:T(8,128)(2,1)} %get-tuple-element.160.refs_5_.refs_0_.refs_28_), channel_id=1, source_target_pairs={{0,4},{4,0},{8,12},{12,8},{16,20},{20,16},{24,28},{28,24},{1,5},{5... | collective-permute-start | bytes 4866056 | tf_op jit(solution)/shard_map/ppermute | solution.py:1420
  115.7 37.1 %collective-permute-start.13 = (bf16[2,1536,256]{2,1,0:T(8,128)(2,1)}, bf16[2,1536,256]{2,1,0:T(8,128)(2,1)}, u32[]{:S(2)}, u32[]{:S(2)}) collective-permute-start(bf16[2,1536,256]{2,1,0:T(8,128)(2,1)} %get-tuple-element.161.refs_9_.refs_0_.refs_32_), channel_id=1, source_target_pairs={{0,8},{4,12},{8,0},{12,4},{16,24},{20,28},{24,16},{28,20},{1,9},{5... | collective-permute-start | bytes 4718600 | tf_op jit(solution)/shard_map/ppermute | solution.py:1420
  116.2 36.6 %collective-permute-start.11 = (bf16[2,1536,256]{2,1,0:T(8,128)(2,1)}, bf16[2,1536,256]{2,1,0:T(8,128)(2,1)}, u32[]{:S(2)}, u32[]{:S(2)}) collective-permute-start(bf16[2,1536,256]{2,1,0:T(8,128)(2,1)} %get-tuple-element.161.refs_9_.refs_0_.refs_32_), channel_id=1, source_target_pairs={{0,4},{4,0},{8,12},{12,8},{16,20},{20,16},{24,28},{28,24},{1,5},{5... | collective-permute-start | bytes 4718600 | tf_op jit(solution)/shard_map/ppermute | solution.py:1420
  155.1 20.5 %collective-permute-start.16 = (bf16[2,1584,256]{2,1,0:T(8,128)(2,1)}, bf16[2,1584,256]{2,1,0:T(8,128)(2,1)S(1)}, u32[]{:S(2)}, u32[]{:S(2)}) collective-permute-start(bf16[2,1584,256]{2,1,0:T(8,128)(2,1)} %get-tuple-element.169.refs_6_.refs_1_.refs_29_), channel_id=1, source_target_pairs={{0,4},{4,0},{8,12},{12,8},{16,20},{20,16},{24,28},{28,24},{1,5},{5... | collective-permute-start | bytes 4866056 | tf_op jit(solution)/shard_map/ppermute | solution.py:1420
  155.1 20.5 %collective-permute-start.17 = (bf16[2,1536,256]{2,1,0:T(8,128)(2,1)}, bf16[2,1536,256]{2,1,0:T(8,128)(2,1)}, u32[]{:S(2)}, u32[]{:S(2)}) collective-permute-start(bf16[2,1536,256]{2,1,0:T(8,128)(2,1)} %get-tuple-element.170.refs_10_.refs_1_.refs_33_), channel_id=1, source_target_pairs={{0,4},{4,0},{8,12},{12,8},{16,20},{20,16},{24,28},{28,24},{1,5},{5... | collective-permute-start | bytes 4718600 | tf_op jit(solution)/shard_map/ppermute | solution.py:1420
  155.6 19.7 %collective-permute-start.14 = (bf16[1536,256]{1,0:T(8,128)(2,1)}, bf16[1536,256]{1,0:T(8,128)(2,1)S(1)}, u32[]{:S(2)}, u32[]{:S(2)}) collective-permute-start(bf16[1536,256]{1,0:T(8,128)(2,1)} %get-tuple-element.162.refs_0_), channel_id=1, source_target_pairs={{0,8},{4,12},{8,0},{12,4},{16,24},{20,28},{24,16},{28,20},{1,9},{5... | collective-permute-start | bytes 2359304 | tf_op jit(solution)/shard_map/ppermute | solution.py:1420
  156.1 19.5 %collective-permute-start.15 = (bf16[1536,256]{1,0:T(8,128)(2,1)}, bf16[1536,256]{1,0:T(8,128)(2,1)}, u32[]{:S(2)}, u32[]{:S(2)}) collective-permute-start(bf16[1536,256]{1,0:T(8,128)(2,1)} %get-tuple-element.163.refs_2_), channel_id=1, source_target_pairs={{0,16},{4,20},{8,24},{12,28},{16,0},{20,4},{24,8},{28,12},{1,17},{... | collective-permute-start | bytes 2359304 | tf_op jit(solution)/shard_map/ppermute | solution.py:1420
  181.7 45.2 %collective-permute-start.20 = (bf16[2,1536,256]{2,1,0:T(8,128)(2,1)}, bf16[2,1536,256]{2,1,0:T(8,128)(2,1)}, u32[]{:S(2)}, u32[]{:S(2)}) collective-permute-start(bf16[2,1536,256]{2,1,0:T(8,128)(2,1)} %get-tuple-element.171.refs_4_.refs_0_.refs_10_), channel_id=1, source_target_pairs={{0,16},{4,20},{8,24},{12,28},{16,0},{20,4},{24,8},{28,12},{1,17},{... | collective-permute-start | bytes 4718600 | tf_op jit(solution)/shard_map/ppermute | solution.py:1420
  183.3 43.6 %collective-permute-start.18 = (bf16[2,1536,256]{2,1,0:T(8,128)(2,1)}, bf16[2,1536,256]{2,1,0:T(8,128)(2,1)S(1)}, u32[]{:S(2)}, u32[]{:S(2)}) collective-permute-start(bf16[2,1536,256]{2,1,0:T(8,128)(2,1)} %get-tuple-element.171.refs_4_.refs_0_.refs_10_), channel_id=1, source_target_pairs={{0,4},{4,0},{8,12},{12,8},{16,20},{20,16},{24,28},{28,24},{1,5},{5... | collective-permute-start | bytes 4718600 | tf_op jit(solution)/shard_map/ppermute | solution.py:1420
  183.3 43.6 %collective-permute-start.21 = (bf16[2,1536,256]{2,1,0:T(8,128)(2,1)}, bf16[2,1536,256]{2,1,0:T(8,128)(2,1)}, u32[]{:S(2)}, u32[]{:S(2)}) collective-permute-start(bf16[2,1536,256]{2,1,0:T(8,128)(2,1)} %get-tuple-element.185.refs_8_.refs_4_.refs_14_), channel_id=1, source_target_pairs={{0,8},{4,12},{8,0},{12,4},{16,24},{20,28},{24,16},{28,20},{1,9},{5... | collective-permute-start | bytes 4718600 | tf_op jit(solution)/shard_map/ppermute | solution.py:1420
  184.8 42.1 %collective-permute-start.19 = (bf16[2,1536,256]{2,1,0:T(8,128)(2,1)}, bf16[2,1536,256]{2,1,0:T(8,128)(2,1)S(1)}, u32[]{:S(2)}, u32[]{:S(2)}) collective-permute-start(bf16[2,1536,256]{2,1,0:T(8,128)(2,1)} %get-tuple-element.185.refs_8_.refs_4_.refs_14_), channel_id=1, source_target_pairs={{0,4},{4,0},{8,12},{12,8},{16,20},{20,16},{24,28},{28,24},{1,5},{5... | collective-permute-start | bytes 4718600 | tf_op jit(solution)/shard_map/ppermute | solution.py:1420
  207.2 19.6 %collective-permute-start.22 = (bf16[4,512,128]{2,1,0:T(8,128)(2,1)}, bf16[4,512,128]{2,1,0:T(8,128)(2,1)S(1)}, u32[]{:S(2)}, u32[]{:S(2)}) collective-permute-start(bf16[4,512,128]{2,1,0:T(8,128)(2,1)} %get-tuple-element.188), channel_id=1, source_target_pairs={{0,1},{1,2},{2,3},{4,5},{5,6},{6,7},{8,9},{9,10},{10,11},{12,13},{... | collective-permute-start | bytes 1572872 | tf_op jit(solution)/shard_map/ppermute | solution.py:1606
  229.8 30.8 %collective-permute-start.23 = (bf16[2,1536,256]{2,1,0:T(8,128)(2,1)}, bf16[2,1536,256]{2,1,0:T(8,128)(2,1)S(1)}, u32[]{:S(2)}, u32[]{:S(2)}) collective-permute-start(bf16[2,1536,256]{2,1,0:T(8,128)(2,1)} %get-tuple-element.189.refs_5_.refs_1_.refs_11_), channel_id=1, source_target_pairs={{0,4},{4,0},{8,12},{12,8},{16,20},{20,16},{24,28},{28,24},{1,5},{5... | collective-permute-start | bytes 4718600 | tf_op jit(solution)/shard_map/ppermute | solution.py:1420
  229.8 31.6 %collective-permute-start.24 = (bf16[2,1536,256]{2,1,0:T(8,128)(2,1)}, bf16[2,1536,256]{2,1,0:T(8,128)(2,1)S(1)}, u32[]{:S(2)}, u32[]{:S(2)}) collective-permute-start(bf16[2,1536,256]{2,1,0:T(8,128)(2,1)} %get-tuple-element.190.refs_9_.refs_5_.refs_15_), channel_id=1, source_target_pairs={{0,4},{4,0},{8,12},{12,8},{16,20},{20,16},{24,28},{28,24},{1,5},{5... | collective-permute-start | bytes 4718600 | tf_op jit(solution)/shard_map/ppermute | solution.py:1420
  230.4 15.1 %collective-permute-start.28 = (bf16[4,512,128]{2,1,0:T(8,128)(2,1)}, bf16[4,512,128]{2,1,0:T(8,128)(2,1)S(1)}, u32[]{:S(2)}, u32[]{:S(2)}) collective-permute-start(bf16[4,512,128]{2,1,0:T(8,128)(2,1)} %get-tuple-element.197), channel_id=1, source_target_pairs={{0,1},{1,2},{2,3},{4,5},{5,6},{6,7},{8,9},{9,10},{10,11},{12,13},{... | collective-permute-start | bytes 1572872 | tf_op jit(solution)/shard_map/ppermute | solution.py:1610
  233.8 26.8 %collective-permute-start.25 = (bf16[1536,256]{1,0:T(8,128)(2,1)}, bf16[1536,256]{1,0:T(8,128)(2,1)}, u32[]{:S(2)}, u32[]{:S(2)}) collective-permute-start(bf16[1536,256]{1,0:T(8,128)(2,1)} %get-tuple-element.192.refs_0_), channel_id=1, source_target_pairs={{0,8},{4,12},{8,0},{12,4},{16,24},{20,28},{24,16},{28,20},{1,9},{5... | collective-permute-start | bytes 2359304 | tf_op jit(solution)/shard_map/ppermute | solution.py:1420
  234.4 26.2 %collective-permute-start.26 = (bf16[1536,256]{1,0:T(8,128)(2,1)}, bf16[1536,256]{1,0:T(8,128)(2,1)}, u32[]{:S(2)}, u32[]{:S(2)}) collective-permute-start(bf16[1536,256]{1,0:T(8,128)(2,1)} %get-tuple-element.193.refs_2_), channel_id=1, source_target_pairs={{0,16},{4,20},{8,24},{12,28},{16,0},{20,4},{24,8},{28,12},{1,17},{... | collective-permute-start | bytes 2359304 | tf_op jit(solution)/shard_map/ppermute | solution.py:1420
  245.4 15.2 %collective-permute-start.27 = (bf16[4,512,128]{2,1,0:T(8,128)(2,1)}, bf16[4,512,128]{2,1,0:T(8,128)(2,1)S(1)}, u32[]{:S(2)}, u32[]{:S(2)}) collective-permute-start(bf16[4,512,128]{2,1,0:T(8,128)(2,1)} %hop.6), channel_id=1, source_target_pairs={{0,1},{1,2},{2,3},{4,5},{5,6},{6,7},{8,9},{9,10},{10,11},{12,13},{... | collective-permute-start | bytes 1572872 | tf_op jit(solution)/shard_map/ppermute | solution.py:1615
  267.3 34.8 %collective-permute-start.29 = (bf16[2,1536,256]{2,1,0:T(8,128)(2,1)}, bf16[2,1536,256]{2,1,0:T(8,128)(2,1)S(1)}, u32[]{:S(2)}, u32[]{:S(2)}) collective-permute-start(bf16[2,1536,256]{2,1,0:T(8,128)(2,1)} %get-tuple-element.204.refs_3_), channel_id=1, source_target_pairs={{0,16},{4,20},{8,24},{12,28},{16,0},{20,4},{24,8},{28,12},{1,17},{... | collective-permute-start | bytes 4718600 | tf_op jit(solution)/shard_map/ppermute | solution.py:1420
  267.8 34.6 %collective-permute-start.30 = (bf16[2,1536,256]{2,1,0:T(8,128)(2,1)}, bf16[2,1536,256]{2,1,0:T(8,128)(2,1)S(1)}, u32[]{:S(2)}, u32[]{:S(2)}) collective-permute-start(bf16[2,1536,256]{2,1,0:T(8,128)(2,1)} %get-tuple-element.205.refs_4_), channel_id=1, source_target_pairs={{0,8},{4,12},{8,0},{12,4},{16,24},{20,28},{24,16},{28,20},{1,9},{5... | collective-permute-start | bytes 4718600 | tf_op jit(solution)/shard_map/ppermute | solution.py:1420
  271.4 23.2 %collective-permute-start.32 = (bf16[4,512,128]{2,1,0:T(8,128)(2,1)}, bf16[4,512,128]{2,1,0:T(8,128)(2,1)}, u32[]{:S(2)}, u32[]{:S(2)}) collective-permute-start(bf16[4,512,128]{2,1,0:T(8,128)(2,1)} %hop.8.refs_13_), channel_id=1, source_target_pairs={{0,1},{1,2},{2,3},{4,5},{5,6},{6,7},{8,9},{9,10},{10,11},{12,13},{... | collective-permute-start | bytes 1572872 | tf_op jit(solution)/shard_map/ppermute | solution.py:1621
  279.6 16.8 %collective-permute-start.31 = (bf16[4,512,128]{2,1,0:T(8,128)(2,1)}, bf16[4,512,128]{2,1,0:T(8,128)(2,1)S(1)}, u32[]{:S(2)}, u32[]{:S(2)}) collective-permute-start(bf16[4,512,128]{2,1,0:T(8,128)(2,1)} %hop.7.refs_12_), channel_id=1, source_target_pairs={{0,1},{1,2},{2,3},{4,5},{5,6},{6,7},{8,9},{9,10},{10,11},{12,13},{... | collective-permute-start | bytes 1572872 | tf_op jit(solution)/shard_map/ppermute | solution.py:1623
  305.5 10.0 %collective-permute-start.36 = (bf16[2,1536,256]{2,1,0:T(8,128)(2,1)}, bf16[2,1536,256]{2,1,0:T(8,128)(2,1)}, u32[]{:S(2)}, u32[]{:S(2)}) collective-permute-start(bf16[2,1536,256]{2,1,0:T(8,128)(2,1)} %get-tuple-element.209.refs_5_.refs_20_), channel_id=1, source_target_pairs={{0,4},{4,0},{8,12},{12,8},{16,20},{20,16},{24,28},{28,24},{1,5},{5... | collective-permute-start | bytes 4718600 | tf_op jit(solution)/shard_map/ppermute | solution.py:1420
  309.1 18.6 %collective-permute-start.37 = (bf16[4,512,128]{2,1,0:T(8,128)(2,1)}, bf16[4,512,128]{2,1,0:T(8,128)(2,1)S(1)}, u32[]{:S(2)}, u32[]{:S(2)}) collective-permute-start(bf16[4,512,128]{2,1,0:T(8,128)(2,1)} %hop.9.refs_12_), channel_id=1, source_target_pairs={{0,1},{1,2},{2,3},{4,5},{5,6},{6,7},{8,9},{9,10},{10,11},{12,13},{... | collective-permute-start | bytes 1572872 | tf_op jit(solution)/shard_map/ppermute | solution.py:1630
  350.9 28.0 %collective-permute-start.38 = (bf16[4,1024,128]{2,1,0:T(8,128)(2,1)}, bf16[4,1024,128]{2,1,0:T(8,128)(2,1)S(1)}, u32[]{:S(2)}, u32[]{:S(2)}) collective-permute-start(bf16[4,1024,128]{2,1,0:T(8,128)(2,1)} %get-tuple-element.226), channel_id=1, source_target_pairs={{1,0},{2,1},{3,2},{5,4},{6,5},{7,6},{9,8},{10,9},{11,10},{13,12},{... | collective-permute-start | bytes 3145736 | tf_op jit(solution)/shard_map/ppermute | solution.py:1660
  383.2 29.9 %collective-permute-start.39 = (bf16[4,1024,128]{2,1,0:T(8,128)(2,1)}, bf16[4,1024,128]{2,1,0:T(8,128)(2,1)S(1)}, u32[]{:S(2)}, u32[]{:S(2)}) collective-permute-start(bf16[4,1024,128]{2,1,0:T(8,128)(2,1)} %hop.10.refs_18_), channel_id=1, source_target_pairs={{1,0},{2,1},{3,2},{5,4},{6,5},{7,6},{9,8},{10,9},{11,10},{13,12},{... | collective-permute-start | bytes 3145736 | tf_op jit(solution)/shard_map/ppermute | solution.py:1665
  403.2 15.4 %collective-permute-start.41 = (bf16[16,4096]{1,0:T(8,128)(2,1)S(1)}, bf16[16,4096]{1,0:T(8,128)(2,1)S(1)}, u32[]{:S(2)}, u32[]{:S(2)}) collective-permute-start(bf16[16,4096]{1,0:T(8,128)(2,1)S(1)} %get-tuple-element.310), channel_id=1, source_target_pairs={{0,1},{1,2},{2,3},{3,0},{4,5},{5,6},{6,7},{7,4},{8,9},{9,10},{10,1... | collective-permute-start | bytes 393224 | tf_op jit(solution)/shard_map/ppermute | solution.py:1435
  405.9 15.1 %collective-permute-start.42 = (bf16[16,4096]{1,0:T(8,128)(2,1)S(1)}, bf16[16,4096]{1,0:T(8,128)(2,1)S(1)}, u32[]{:S(2)}, u32[]{:S(2)}) collective-permute-start(bf16[16,4096]{1,0:T(8,128)(2,1)S(1)} %get-tuple-element.311), channel_id=1, source_target_pairs={{0,2},{1,3},{2,0},{3,1},{4,6},{5,7},{6,4},{7,5},{8,10},{9,11},{10,... | collective-permute-start | bytes 393224 | tf_op jit(solution)/shard_map/ppermute | solution.py:1435
  408.7 12.2 %collective-permute-start.43 = (bf16[16,4096]{1,0:T(8,128)(2,1)S(1)}, bf16[16,4096]{1,0:T(8,128)(2,1)S(1)}, u32[]{:S(2)}, u32[]{:S(2)}) collective-permute-start(bf16[16,4096]{1,0:T(8,128)(2,1)S(1)} %get-tuple-element.312), channel_id=1, source_target_pairs={{0,3},{1,0},{2,1},{3,2},{4,7},{5,4},{6,5},{7,6},{8,11},{9,8},{10,9... | collective-permute-start | bytes 393224 | tf_op jit(solution)/shard_map/ppermute | solution.py:1435
  417.4 29.9 %collective-permute-start.40 = (bf16[4,1024,128]{2,1,0:T(8,128)(2,1)}, bf16[4,1024,128]{2,1,0:T(8,128)(2,1)S(1)}, u32[]{:S(2)}, u32[]{:S(2)}) collective-permute-start(bf16[4,1024,128]{2,1,0:T(8,128)(2,1)} %hop.11.refs_10_), channel_id=1, source_target_pairs={{1,0},{2,1},{3,2},{5,4},{6,5},{7,6},{9,8},{10,9},{11,10},{13,12},{... | collective-permute-start | bytes 3145736 | tf_op jit(solution)/shard_map/ppermute | solution.py:1668
  476.9 9.7 %collective-permute-start.45 = (bf16[16,3072]{1,0:T(8,128)(2,1)S(1)}, bf16[16,3072]{1,0:T(8,128)(2,1)S(1)}, u32[]{:S(2)}, u32[]{:S(2)}) collective-permute-start(bf16[16,3072]{1,0:T(8,128)(2,1)S(1)} %get-tuple-element.307), channel_id=1, source_target_pairs={{0,1},{1,2},{2,3},{3,0},{4,5},{5,6},{6,7},{7,4},{8,9},{9,10},{10,1... | collective-permute-start | bytes 294920 | tf_op jit(solution)/shard_map/ppermute | solution.py:1435
  496.4 29.1 %collective-permute-start.51 = (bf16[2,16,7168]{2,1,0:T(8,128)(2,1)S(1)}, bf16[2,16,7168]{2,1,0:T(8,128)(2,1)S(1)}, u32[]{:S(2)}, u32[]{:S(2)}) collective-permute-start(bf16[2,16,7168]{2,1,0:T(8,128)(2,1)S(1)} %constant_dynamic-update-slice_fusion.4.refs_1_), channel_id=1, source_target_pairs={{0,24},{4,28},{8,16},{12,20},{16,8},{20,12},{24,0},{28,4},{1,25},{... | collective-permute-start | bytes 1376264 | tf_op jit(solution)/shard_map/ppermute | solution.py:1420
  497.7 27.9 %collective-permute-start.50 = (bf16[2,16,7168]{2,1,0:T(8,128)(2,1)S(1)}, bf16[2,16,7168]{2,1,0:T(8,128)(2,1)S(1)}, u32[]{:S(2)}, u32[]{:S(2)}) collective-permute-start(bf16[2,16,7168]{2,1,0:T(8,128)(2,1)S(1)} %constant_dynamic-update-slice_fusion.4.refs_1_), channel_id=1, source_target_pairs={{0,16},{4,20},{8,24},{12,28},{16,0},{20,4},{24,8},{28,12},{1,17},{... | collective-permute-start | bytes 1376264 | tf_op jit(solution)/shard_map/ppermute | solution.py:1420
  498.5 27.1 %collective-permute-start.49 = (bf16[2,16,7168]{2,1,0:T(8,128)(2,1)S(1)}, bf16[2,16,7168]{2,1,0:T(8,128)(2,1)S(1)}, u32[]{:S(2)}, u32[]{:S(2)}) collective-permute-start(bf16[2,16,7168]{2,1,0:T(8,128)(2,1)S(1)} %constant_dynamic-update-slice_fusion.4.refs_1_), channel_id=1, source_target_pairs={{0,8},{4,12},{8,0},{12,4},{16,24},{20,28},{24,16},{28,20},{1,9},{5... | collective-permute-start | bytes 1376264 | tf_op jit(solution)/shard_map/ppermute | solution.py:1420
  (55 other events, 360.7 us)
Sparse Core Ops, SparseCore 0:
  16.0 62.4 all-gather.7
  80.6 44.6 all-gather.5
  126.8 44.6 all-gather.9

commit v6 on v5

--- a/solution.py
+++ b/solution.py
@@ -353,7 +353,8 @@
             rows = slice(c * CB, (c + 1) * CB)
             total = jnp.exp2(hp[s, c, hb : 2 * hb, length - 1 : length])
             came = got[(s + shift) % slots, rows, :].astype(f32)
-            out[s, rows, :] = (per_head(came, total) + own[s, rows, :]).astype(bf16)
+            total = per_head(came, total) + own[s, rows, :].astype(f32)
+            out[s, rows, :] = total.astype(bf16)
 
 
 def hop_call(got, shift, own, hp, part=0, later=()):
@@ -366,7 +367,7 @@
         grid=(1,),
         in_specs=[
             whole(got.shape),
-            pl.BlockSpec((slots, rows, state_w), lambda i: (0, part, 0)),
+            whole(own.shape),
             pl.BlockSpec((slots, per) + hp.shape[1:], lambda i: (0, part, 0, 0)),
         ]
         + [pl.BlockSpec(memory_space=pl.ANY)] * len(later),
@@ -424,7 +425,7 @@
 def scan_kernel(nx, order, hb, sub, *refs):
     xrefs = refs[:nx]
     (nt, low, pk, hp_r, ct, bn, cbt) = refs[nx : nx + 7]
-    xc_all, mix_all, ent_all, st_all, sent_all, tok_out = refs[-12:-6]
+    xc_all, mix_all, ent_all, sent_all, tok_out = refs[-11:-6]
     raw_sc, x_sc, xs_sc, turn_sc, w_sc, tap_sc = refs[-6:]
     tok_out[...] = jnp.zeros_like(tok_out)
     length = ct.shape[1]
@@ -471,7 +472,6 @@
             state = add if state is None else per_head(state, jnp.exp2(last)) + add
         if length // sub == 1:
             ent_all[0, rows, :] = state
-        st_all[rows, :] = state
         sent_all[rows, :] = state.astype(bf16)
 
 
@@ -503,7 +503,6 @@
         jax.ShapeDtypeStruct((slots, ch, length), bf16),
         jax.ShapeDtypeStruct((slots, ch, length), f32),
         jax.ShapeDtypeStruct((slots, inner_states, ch, 128), f32),
-        jax.ShapeDtypeStruct((slots, ch, 128), f32),
         jax.ShapeDtypeStruct((slots, width, 128), bf16),
         jax.ShapeDtypeStruct((1, 1), bf16),
     ]
@@ -511,12 +510,11 @@
         per_chan(length),
         per_chan(length),
         pl.BlockSpec((None, inner_states, width, 128), lambda s: (s + lo, 0, part, 0)),
-        per_chan(128),
         pl.BlockSpec((None, width, 128), lambda s: (s + lo, 0, 0)),
         pl.BlockSpec((1, 1), lambda s: (0, 0)),
     ]
     given = [v for v in bufs if v is not None]
-    aliases = {len(ops) + i: k for i, k in enumerate(k for k in range(5) if bufs[k] is not None)}
+    aliases = {len(ops) + i: k for i, k in enumerate(k for k in range(4) if bufs[k] is not None)}
     ops += given + list(later)
     specs += [pl.BlockSpec(memory_space=pl.ANY)] * (len(given) + len(later))
     n = hi - lo
@@ -541,7 +539,7 @@
         ),
         name="scan_slots",
     )(*ops)
-    return list(out[:5]), out[5]
+    return list(out[:4]), out[4]
 
 
 def proj_kernel(picks, n, cut, gain, *refs):
@@ -612,8 +610,8 @@
 def gate_kernel(hb, inner, paths, *refs):
     (z_all, mix_all, wgt_all, pk, hp_r, ct, cn) = refs[:7]
     ent_all = refs[7 : 7 + paths]
-    nout_all, dmix_all, dz_all, sl_all, sent_all = refs[7 + paths : 12 + paths]
-    mix_sc, turn_sc, sq_sc, dot_sc, gain_sc = refs[12 + paths :]
+    nout_all, dmix_all, dz_all, sent_all = refs[7 + paths : 11 + paths]
+    mix_sc, turn_sc, sq_sc, dot_sc, gain_sc = refs[11 + paths :]
     phase, slot = pl.program_id(0), pl.program_id(1)
     blocks = z_all.shape[0] // CB
 
@@ -675,7 +673,6 @@
                 turn_sc[rows, :] = d_mix * cum[h : h + 1]
             adj = dot(turn_sc[...].astype(bf16), cn[...])
             here = pl.ds(pl.multiple_of(b * CB, CB), CB)
-            sl_all[here, :] = adj
             sent_all[here, :] = adj.astype(bf16)
 
 
@@ -703,12 +700,11 @@
             pl.BlockSpec((None,) + v.shape[1:], lambda p, s: ((held(p, s) + 1) % slots, 0, 0))
             for v in ent
         ],
-        out_specs=[later(length), later(length), later(length), later(128), later(128)],
+        out_specs=[later(length), later(length), later(length), later(128)],
         out_shape=[
             jax.ShapeDtypeStruct((slots, ch, length), bf16),
             jax.ShapeDtypeStruct((slots, ch, length), bf16),
             jax.ShapeDtypeStruct((slots, ch, length), bf16),
-            jax.ShapeDtypeStruct((slots, ch, 128), f32),
             jax.ShapeDtypeStruct((slots, ch, 128), bf16),
         ],
         scratch_shapes=[
@@ -1247,8 +1243,8 @@
     block = dx.shape[0]
     taps = jnp.concatenate(
         [
-            num[b * 64 + 48 : b * 64 + 56, :].astype(f32)
-            + num[b * 64 + 56 : b * 64 + 64, :].astype(f32)
+            num[b * 64 + 48 : b * 64 + 64, :].astype(f32)[:8]
+            + num[b * 64 + 48 : b * 64 + 64, :].astype(f32)[8:]
             for b in range(block // CB)
         ],
         axis=1,
@@ -1571,15 +1567,15 @@
     z_args = (picks, nt, low2, pk, ch, HALO, False)
     o_args = (picks, gt, back2, pk, ch, 0, True)
     if quick:
-        empty = [None] * 4
+        empty = [None] * 3
         bufs, _ = scan_call(
             0, 1, (own, 1), 0, *x_args, hp, ct, b_low, cbt, empty + [None], held
         )
-        sent_a = bufs[4]
+        sent_a = bufs[3]
         bufs, done = scan_call(
-            0, 1, (own, 1), 1, *x_args, hp, ct, b_low, cbt, bufs[:4] + [None], held
+            0, 1, (own, 1), 1, *x_args, hp, ct, b_low, cbt, bufs[:3] + [None], held
         )
-        sent_b = bufs[4]
+        sent_b = bufs[3]
         far_z = halves(slot_order(all_z, 1, place + token[0, 0].astype(jnp.int32)))
 
         token, passed, _ = hold([done] + swapped, two + far_z)
@@ -1601,32 +1597,34 @@
         speed = jnp.concatenate([speed, speed_far], axis=0)
         small_w.append(far_w)
         bufs, _ = scan_call(
-            1, planes, (far_x, 0), 0, *x_args, hp, ct, b_low, cbt, bufs[:4] + [sent_a], [token]
+            1, planes, (far_x, 0), 0, *x_args, hp, ct, b_low, cbt, bufs[:3] + [sent_a], [token]
         )
-        ent_a = lax.ppermute(bufs[4], "tensor", halo)
+        sent_a = bufs[3]
+        ent_a = lax.ppermute(sent_a, "tensor", halo)
         bufs, done = scan_call(
-            1, planes, (far_x, 0), 1, *x_args, hp, ct, b_low, cbt, bufs[:4] + [sent_b], [token]
+            1, planes, (far_x, 0), 1, *x_args, hp, ct, b_low, cbt, bufs[:3] + [sent_b], [token]
         )
-        ent_b = lax.ppermute(bufs[4], "tensor", halo)
+        sent_b = bufs[3]
+        ent_b = lax.ppermute(sent_b, "tensor", halo)
         token, passed, _ = hold([done] + swapped, two + far_o + [ent_a])
         two, far_o, (ent_a,) = passed[:2], passed[2:4], passed[4:]
         far_z = as_paths(far_z + two, swapped + pass_core(two))
         got = pass_one(far_o)
-        ent_a = lax.ppermute(hop_call(ent_a, 1, bufs[3], hp, 0, [token]), "tensor", halo)
+        ent_a = lax.ppermute(hop_call(ent_a, 1, sent_a, hp, 0, [token]), "tensor", halo)
 
         token, passed, far_o = hold(far_z[0] + far_z[1], [ent_a, ent_b], zip(far_o, got))
         ent_a, ent_b = passed
         two = pass_two(far_o)
-        send_b = hop_call(ent_b, 1, bufs[3], hp, 1, [token])
+        send_b = hop_call(ent_b, 1, sent_b, hp, 1, [token])
         ent_b = lax.ppermute(send_b, "tensor", halo)
-        send_a = hop_call(ent_a, 1, bufs[3], hp, 0, [token])
+        send_a = hop_call(ent_a, 1, sent_a, hp, 0, [token])
         ent_a = lax.ppermute(send_a, "tensor", halo)
         z, done = proj_call(1, planes, (far_z, 0), *z_args, z, [send_a, send_b])
 
         token, passed, _ = hold([done], two + far_o + [ent_a, ent_b])
         two, far_o, (ent_a, ent_b) = passed[:2], passed[2:4], passed[4:]
         far_o = as_paths(far_o + two, pass_core(far_o + two))
-        send_b = hop_call(ent_b, 1, bufs[3], hp, 1, [token])
+        send_b = hop_call(ent_b, 1, sent_b, hp, 1, [token])
         ent_b = lax.ppermute(send_b, "tensor", halo)
         wgt, done = proj_call(1, planes, (far_o, 0), *o_args, wgt, [send_b])
         _, ent, _ = hold([done], [ent_a, ent_b])
@@ -1641,23 +1639,23 @@
         wz, wx = flat_rows(w[:, 0]), flat_rows(w[:, 1])
         o = flat_rows(by_slot(o))
         bufs, _ = scan_call(
-            0, planes, (wx, 0), 0, *x_args, hp, ct, b_low, cbt, [None] * 5
+            0, planes, (wx, 0), 0, *x_args, hp, ct, b_low, cbt, [None] * 4
         )
         z, _ = proj_call(0, planes, (wz, 0), *z_args, None)
         wgt, _ = proj_call(0, planes, (o, 0), *o_args, None)
-        ent = lax.ppermute(bufs[4], "tensor", halo)
+        ent = lax.ppermute(bufs[3], "tensor", halo)
         for _ in range(planes - 2):
             ent = lax.ppermute(hop_call(ent, 1, bufs[3], hp), "tensor", halo)
         ent = [ent]
         z_sets = [((0, planes), wz, 0)]
         x_sets = [((0, planes), wx, 0)]
         o_sets = [((0, planes), o, 0)]
-    xc, mix, loc, s_end, _ = bufs
+    xc, mix, loc, _ = bufs
     left = [(s + 1, s) for s in range(planes - 1)]
 
-    nout, dy, dz, sl, sl_sent = gate_call(z, mix, wgt, ent, pk, hp, ct, c_low, inner)
-
-    adj = lax.ppermute(sl_sent, "tensor", left)
+    nout, dy, dz, sl = gate_call(z, mix, wgt, ent, pk, hp, ct, c_low, inner)
+
+    adj = lax.ppermute(sl, "tensor", left)
     mixed, grad_down_out, grad_up_out = output_call(
         sc, nout, pk, back2, up_out, tokens[0], masked, o_sets, picks, flat, quick
     )

time: 549 us -> 547 us (level)
  transfers between devices with their start and end apart: 55 -> 55, of which waited for: 21 -> 20; matrix products, arithmetic and copies ran while one was open for 4% -> 4% of each run, Pallas kernels for 42% -> 42%
where the time goes in v6:
time: 547 us; the launch traced here: 537 us
  Pallas kernels  294 us (54%)
  waiting for transfers between devices  107 us (20%)
  starting transfers between devices  66.3 us (12%)
  local copies, waits for them, and re-layouts  36.8 us (7%)
  between operations  17.8 us (3%)
  other arithmetic  15.3 us (3%)
    pallas_call x4, Pallas kernels, scan_call(): pl.pallas_call(functools.partial(scan_kernel, nx, picks[part], hb, SUB),...  48.8 us
    ppermute x36, waiting for transfers between devices, flip(): return lax.ppermute(v, 'dp', [(i, i ^ bit) for i in range(seqs)])  41.5 us
    pallas_call x4, Pallas kernels, proj_call(): pl.pallas_call(functools.partial(proj_kernel, picks, n_w, cut, gain), gri...  39 us
    all_gather x1, waiting for transfers between devices, body(): lax.all_gather(jnp.concatenate([wt[1], packed, steps_w, last_rows], axis=...  31.3 us
    pallas_call x1, Pallas kernels, back_call(): pl.pallas_call(functools.partial(back_kernel, hb, SUB, len(ent)), grid=(s...  25.5 us
    pallas_call x1, Pallas kernels, input_call(): pl.pallas_call(functools.partial(input_kernel, sets, picks, flat, quick,...  24.9 us
    ppermute x36, starting transfers between devices, flip(): return lax.ppermute(v, 'dp', [(i, i ^ bit) for i in range(seqs)])  22.5 us
    pallas_call x11, Pallas kernels, hold(): pl.pallas_call(functools.partial(hold_kernel, len(joined_shapes)), grid=(...  21.7 us
  transfers between devices with their start and end apart: 55, of which 20 were waited for; matrix products, arithmetic and copies ran while one was open for 4% of the time, Pallas kernels for 42%

profile of v6, /device:TPU:0, one launch (start us, length us, event | category | flops | bytes accessed | tf_op | source)
XLA Modules:
  0.0 537.0 jit_solution(12493179701031445574)
XLA Ops:
  16.4 3.0 collective-permute-start
  21.2 18.9 %collective-permute-done.1.refs_3_ = bf16[1664,256]{1,0:T(8,128)(2,1)} collective-permute-done((bf16[1664,256]{1,0:T(8,128)(2,1)S(1)}, bf16[1664,256]{1,0:T(8,128)(2,1)}, u32[]{:S(2)}, u32[]{:S(2)}) %collective-permute-start.1) | collective-permute-done | bytes 852000 | tf_op jit(solution)/shard_map/ppermute | solution.py:1416
  41.0 3.9 hold.11
  47.2 31.3 %all-gather.8.cloned.1.call-done = bf16[5696,256]{1,0:T(8,128)(2,1)} async-done(((bf16[1424,256]{1,0:T(8,128)(2,1)}), bf16[5696,256]{1,0:T(8,128)(2,1)}) %all-gather.8.cloned.1.call-update) | async-done | bytes 2916368 | tf_op jit(solution)/shard_map/all_gather | solution.py:1501
  78.5 3.5 far.1
  82.0 4.4 collective-permute-done.5.refs_3_
  95.7 9.6 %turn.1 = (bf16[512,2048]{1,0:T(8,128)(2,1)}, bf16[512,2048]{1,0:T(8,128)(2,1)}, f32[512,1]{1,0:T(8,128)}, bf16[16,640]{1,0:T(8,128)(2,1)}, bf16[16,512]{1,0:T(8...) custom-call(s32[2]{0:T(128)} %pad_add_fusion.refs_0_.refs_16_, bf16[512,2048]{1,0:T(8,128)(2,1)} %bitcast.135, ...), custom_call_target="tpu_custom_call" | custom-call | flops 26214400 | bytes 2097152 | tf_op jit(solution)/shard_map/turn/pallas_call | solution.py:162
  110.6 3.6 hold.13
  117.3 3.9 steps.2
  121.1 5.6 %maps.1 = (bf16[128,512]{1,0:T(8,128)(2,1)}, bf16[128,512]{1,0:T(8,128)(2,1)}, bf16[512,128]{1,0:T(8,128)(2,1)}, bf16[512,128]{1,0:T(8,128)(2,1)}, f32[2,256,256...) custom-call(bf16[2,1696,256]{2,1,0:T(8,128)(2,1)} %get-tuple-element.135.refs_6_.refs_0_.refs_7_.refs_2_.refs_20_, ...), custom_call_target="tpu_custom_call" | custom-call | flops 83886080 | bytes 589824 | tf_op jit(solution)/shard_map/maps/pallas_call | solution.py:226
  126.8 8.1 %scan_slots.4 = (bf16[4,1024,512]{2,1,0:T(8,128)(2,1)}, f32[4,1024,512]{2,1,0:T(8,128)}, f32[4,1,1024,128]{3,2,1,0:T(8,128)}, bf16[4,512,128]{2,1,0:T(8,128)(2,1)}, bf16[1,1]{1,0:T(2,128)(2,1)}) custom-call(bf16[2,1696,256]{2,1,0:T(8,128)(2,1)} %get-tuple-element.135.refs_6_.refs_0_.refs_7_.refs_2_.refs_20_, ...), custom_call_target="tpu_custom_call" | custom-call | flops 268435456 | bytes 524288 | tf_op jit(solution)/shard_map/scan_slots/pallas_call | solution.py:521
  134.8 8.5 %scan_slots.5 = (bf16[4,1024,512]{2,1,0:T(8,128)(2,1)}, f32[4,1024,512]{2,1,0:T(8,128)}, f32[4,1,1024,128]{3,2,1,0:T(8,128)}, bf16[4,512,128]{2,1,0:T(8,128)(2,1)}, bf16[1,1]{1,0:T(2,128)(2,1)}) custom-call(bf16[2,1664,256]{2,1,0:T(8,128)(2,1)} %get-tuple-element.134.refs_10_.refs_4_.refs_0_.refs_11_.re, ...), custom_call_target="tpu_custom_call", output_to_operand_aliasing={{0}: (11, {}), {1}: (12, {}), {2}: (13, {})} | custom-call | flops 268435456 | bytes 524288 | tf_op jit(solution)/shard_map/scan_slots/pallas_call | solution.py:521
  146.0 6.9 %collective-permute-done.13.refs_4_ = bf16[2,1536,256]{2,1,0:T(8,128)(2,1)} collective-permute-done((bf16[2,1536,256]{2,1,0:T(8,128)(2,1)}, bf16[2,1536,256]{2,1,0:T(8,128)(2,1)}, u32[]{:S(2)}, u32[]{:S(2)}) %collective-permute-start.13) | collective-permute-done | bytes 1572896 | tf_op jit(solution)/shard_map/ppermute | solution.py:1416
  156.7 7.4 %proj_slots.4 = (bf16[4,1024,512]{2,1,0:T(8,128)(2,1)}, bf16[1,1]{1,0:T(2,128)(2,1)}) custom-call(bf16[2,1696,256]{2,1,0:T(8,128)(2,1)} %get-tuple-element.135.refs_6_.refs_0_.refs_7_.refs_2_.refs_20_, bf16[2,1696,256]{2,1,0:T(8,128)(2,1)} %get-tuple-element.142.refs_7_.refs_1_.refs_8_.refs_3_.refs_21_, bf16[2,1696,256]{2,1,0:T(8,128)(2,1)} %copy-done.2, ...), custom_call_target="tpu_custom_call" | custom-call | flops 268435456 | bytes 655360 | tf_op jit(solution)/shard_map/proj_slots/pallas_call | solution.py:584
  164.1 7.2 %proj_slots.5 = (bf16[4,1024,512]{2,1,0:T(8,128)(2,1)}, bf16[1,1]{1,0:T(2,128)(2,1)}) custom-call(bf16[2,1696,256]{2,1,0:T(8,128)(2,1)} %get-tuple-element.135.refs_6_.refs_0_.refs_7_.refs_2_.refs_20_, bf16[2,1696,256]{2,1,0:T(8,128)(2,1)} %get-tuple-element.142.refs_7_.refs_1_.refs_8_.refs_3_.refs_21_, bf16[2,1696,256]{2,1,0:T(8,128)(2,1)} %copy-done.2, ...), custom_call_target="tpu_custom_call" | custom-call | flops 268435456 | bytes 655360 | tf_op jit(solution)/shard_map/proj_slots/pallas_call | solution.py:584
  177.6 4.3 hold.15
  185.2 4.2 steps.3
  191.2 16.2 %scan_slots.6 = (bf16[4,1024,512]{2,1,0:T(8,128)(2,1)}, f32[4,1024,512]{2,1,0:T(8,128)}, f32[4,1,1024,128]{3,2,1,0:T(8,128)}, bf16[4,512,128]{2,1,0:T(8,128)(2,1)}, bf16[1,1]{1,0:T(2,128)(2,1)}) custom-call(bf16[2,1584,256]{2,1,0:T(8,128)(2,1)} %get-tuple-element.154.refs_5_.refs_0_.refs_, ...), custom_call_target="tpu_custom_call", output_to_operand_aliasing={{0}: (11, {}), {1}: (12, {}), {2}: (13, {}), {3}: (14, {})} | custom-call | flops 805306368 | bytes 1572864 | tf_op jit(solution)/shard_map/scan_slots/pallas_call | solution.py:521
  207.4 3.5 collective-permute-start.22
  211.0 16.0 %scan_slots.7 = (bf16[4,1024,512]{2,1,0:T(8,128)(2,1)}, f32[4,1024,512]{2,1,0:T(8,128)}, f32[4,1,1024,128]{3,2,1,0:T(8,128)}, bf16[4,512,128]{2,1,0:T(8,128)(2,1)}, bf16[1,1]{1,0:T(2,128)(2,1)}) custom-call(bf16[2,1536,256]{2,1,0:T(8,128)(2,1)} %get-tuple-element.155.refs_9_.refs_0_.refs_, ...), custom_call_target="tpu_custom_call", output_to_operand_aliasing={{0}: (11, {}), {1}: (12, {}), {2}: (13, {}), {3}: (14, {})} | custom-call | flops 805306368 | bytes 1572864 | tf_op jit(solution)/shard_map/scan_slots/pallas_call | solution.py:521
  230.6 4.2 collective-permute-start.28
  235.9 2.9 hop.6
  238.8 6.5 %collective-permute-done.28.refs_13_ = bf16[4,512,128]{2,1,0:T(8,128)(2,1)} collective-permute-done((bf16[4,512,128]{2,1,0:T(8,128)(2,1)S(1)}, bf16[4,512,128]{2,1,0:T(8,128)(2,1)}, u32[]{:S(2)}, u32[]{:S(2)}) %collective-permute-start.28) | collective-permute-done | bytes 524320 | tf_op jit(solution)/shard_map/ppermute | solution.py:1608
  245.3 4.5 collective-permute-start.27
  249.9 10.8 %collective-permute-done.27.refs_12_ = bf16[4,512,128]{2,1,0:T(8,128)(2,1)S(1)} collective-permute-done((bf16[4,512,128]{2,1,0:T(8,128)(2,1)}, bf16[4,512,128]{2,1,0:T(8,128)(2,1)S(1)}, u32[]{:S(2)}, u32[]{:S(2)}) %collective-permute-start.27) | collective-permute-done | bytes 524320 | tf_op jit(solution)/shard_map/ppermute | solution.py:1613
  263.1 3.6 hold.17
  267.9 3.0 hop.8.refs_13_
  270.8 5.1 collective-permute-start.32
  275.9 2.9 hop.7.refs_12_
  281.6 12.3 %proj_slots.6 = (bf16[4,1024,512]{2,1,0:T(8,128)(2,1)}, bf16[1,1]{1,0:T(2,128)(2,1)}) custom-call(bf16[2,1536,256]{2,1,0:T(8,128)(2,1)} %get-tuple-element.165.refs_4_.refs_0_.refs_10_, bf16[2,1536,256]{2,1,0:T(8,128)(2,1)} %get-tuple-element.181.refs_5_.refs_1_.refs_11_, bf16[2,1536,256]{2,1,0:T(8,128)(2,1)} %copy-done.7, ...), custom_call_target="tpu_custom_call", output_to_operand_aliasing={{0}: (11, {})} | custom-call | flops 805306368 | bytes 1966080 | tf_op jit(solution)/shard_map/proj_slots/pallas_call | solution.py:584
  295.7 5.9 %collective-permute-done.29.refs_1_ = bf16[2,1536,256]{2,1,0:T(8,128)(2,1)S(1)} collective-permute-done((bf16[2,1536,256]{2,1,0:T(8,128)(2,1)}, bf16[2,1536,256]{2,1,0:T(8,128)(2,1)S(1)}, u32[]{:S(2)}, u32[]{:S(2)}) %collective-permute-start.29) | collective-permute-done | bytes 1572896 | tf_op jit(solution)/shard_map/ppermute | solution.py:1416
  305.4 3.0 hop.9.refs_12_
  308.3 4.3 collective-permute-start.37
  314.9 12.2 %proj_slots.7 = (bf16[4,1024,512]{2,1,0:T(8,128)(2,1)}, bf16[1,1]{1,0:T(2,128)(2,1)}) custom-call(bf16[2,1536,256]{2,1,0:T(8,128)(2,1)} %get-tuple-element.197.refs_0_.refs_15_, bf16[2,1536,256]{2,1,0:T(8,128)(2,1)} %get-tuple-element.198.refs_1_.refs_16_, bf16[2,1536,256]{2,1,0:T(8,128)(2,1)} %copy-done.15, ...), custom_call_target="tpu_custom_call", output_to_operand_aliasing={{0}: (11, {})} | custom-call | flops 805306368 | bytes 1966080 | tf_op jit(solution)/shard_map/proj_slots/pallas_call | solution.py:584
  329.0 20.8 %gate.1 = (bf16[4,1024,512]{2,1,0:T(8,128)(2,1)}, bf16[4,1024,512]{2,1,0:T(8,128)(2,1)}, bf16[4,1024,512]{2,1,0:T(8,128)(2,1)}, bf16[4,1024,128]{2,1,0:T(8,128)(2,1)}) custom-call(bf16[4,1024,512]{2,1,0:T(8,128)(2,1)} %get-tuple-element.192.refs_0_, f32[4,1024,512]{2,1,0:T(8,128)} %get-tuple-element.193.refs_1_, ...), custom_call_target="tpu_custom_call" | custom-call | flops 157286400 | bytes 5767168 | tf_op jit(solution)/shard_map/gate/pallas_call | solution.py:687
  352.5 20.1 %output.1 = (bf16[512,2048]{1,0:T(8,128)(2,1)}, f32[4,16,1024]{2,1,0:T(8,128)}, f32[16,2048]{1,0:T(8,128)}) custom-call(s32[2]{0:T(128)} %pad_add_fusion.refs_0_.refs_16_, bf16[4,1024,512]{2,1,0:T(8,128)(2,1)} %get-tuple-element.210.refs_1_, bf16[4,256,256]{2,1,0:T(8,128)(2,1)} %pad_maximum_fusion.6.refs_5_.refs_6_.refs_10_.refs_3_.refs_2_.refs_4_, ...), custom_call_target="tpu_custom_call" | custom-call | flops 1073741824 | bytes 2097152 | tf_op jit(solution)/shard_map/output/pallas_call | solution.py:1140
  374.5 3.3 collective-permute-done.38.got
  378.8 3.1 hop.10.refs_18_
  383.2 17.7 %gate_back.1 = (f32[512,2048]{1,0:T(8,128)}, f32[4,16,1024]{2,1,0:T(8,128)}) custom-call(bf16[4,1024,512]{2,1,0:T(8,128)(2,1)} %get-tuple-element.218.refs_0_.refs_3_, bf16[16,640]{1,0:T(8,128)(2,1)} %get-tuple-element.141.refs_5_.refs_9_.refs_1_.refs_8_, bf16[2,1696,256]{2,1,0:T(8,128)(2,1)} %get-tuple-element.135.refs_6_.refs_0_.refs_7_.refs_2_.refs_20_, ...), custom_call_target="tpu_custom_call" | custom-call | flops 1073741824 | bytes 2097152 | tf_op jit(solution)/shard_map/gate_back/pallas_call | solution.py:1181
  412.8 3.1 hop.11.refs_10_
  420.4 25.5 %state_back.1 = (f32[4,1024,512]{2,1,0:T(8,128)}, f32[16,4,512]{2,1,0:T(4,128)}, f32[16,4,512]{2,1,0:T(4,128)}, f32[16,4,256]{2,1,0:T(4,128)}, f32[2,256,256]{2,...) custom-call(bf16[4,1024,512]{2,1,0:T(8,128)(2,1)} %get-tuple-element.213.refs_0_.refs_1_, ...), custom_call_target="tpu_custom_call" | custom-call | flops 1342177280 | bytes 2097152 | tf_op jit(solution)/shard_map/state_back/pallas_call | solution.py:817
  447.0 21.6 %finish_back.1 = (bf16[4,1024,512]{2,1,0:T(8,128)(2,1)}, f32[4,1024,128]{2,1,0:T(8,128)}, f32[4,8,1024]{2,1,0:T(8,128)}, f32[4,16,1024]{2,1,0:T(8,128)}, f32[16,...) custom-call(f32[4,1024,512]{2,1,0:T(8,128)} %get-tuple-element.220.r, ...), custom_call_target="tpu_custom_call" | custom-call | flops 183500800 | bytes 3670016 | tf_op jit(solution)/shard_map/finish_back/pallas_call | solution.py:938
  469.3 5.2 glue.1
  475.5 3.4 collective-permute-start.45
  479.8 3.1 collective-permute-start.47
  486.8 5.2 collective-permute-done.44.refs_3_.refs_7_.refs_10_.refs_0_
  499.2 24.9 %input_back.1.refs_0_ = bf16[512,2048]{1,0:T(8,128)(2,1)} custom-call(s32[2]{0:T(128)} %pad_add_fusion.refs_0_.refs_16_, bf16[4,1024,512]{2,1,0:T(8,128)(2,1)} %get-tuple-element.224.refs_1_, f32[4,1024,128]{2,1,0:T(8,128)} %get-tuple-element.225.refs_2_, f32[64,1024]{1,0:T(8,128)} %copy-done.18, ...), custom_call_target="tpu_custom_call" | custom-call | flops 1073741824 | bytes 2097152 | tf_op jit(solution)/shard_map/input_back/pallas_call | solution.py:1291
  526.3 3.7 assemble.1
  (271 shorter events, 107.3 us)
Async XLA Ops:
  7.2 71.3 %all-gather.8.cloned.1.call-start = ((), (), s32[]{:S(2)}) async-start(), calls=%async_computation.1 | async-start | bytes 3645440 | tf_op jit(solution)/shard_map/all_gather | solution.py:1501
  15.9 127.4 %all-gather.6.cloned.1.call-start = ((), (), s32[]{:S(2)}) async-start(), calls=%async_computation | async-start | bytes 2621440 | tf_op jit(solution)/shard_map/all_gather | solution.py:1504
  16.4 23.7 %collective-permute-start = (bf16[1696,256]{1,0:T(8,128)(2,1)S(1)}, bf16[1696,256]{1,0:T(8,128)(2,1)S(1)}, u32[]{:S(2)}, u32[]{:S(2)}) collective-permute-start(bf16[1696,256]{1,0:T(8,128)(2,1)S(1)} %constant_dynamic-update-slice_fusion.refs_0_), channel_id=1, source_target_pairs={{0,8},{4,12},{8,0},{12,4},{16,24},{20,28},{24,16},{28,20},{1,9},{5... | collective-permute-start | bytes 2605064 | tf_op jit(solution)/shard_map/ppermute | solution.py:1416
  19.5 20.6 %collective-permute-start.1 = (bf16[1664,256]{1,0:T(8,128)(2,1)S(1)}, bf16[1664,256]{1,0:T(8,128)(2,1)}, u32[]{:S(2)}, u32[]{:S(2)}) collective-permute-start(bf16[1664,256]{1,0:T(8,128)(2,1)S(1)} %pad_maximum_fusion.refs_2_), channel_id=1, source_target_pairs={{0,16},{4,20},{8,24},{12,28},{16,0},{20,4},{24,8},{28,12},{1,17},{... | collective-permute-start | bytes 2555912 | tf_op jit(solution)/shard_map/ppermute | solution.py:1416
  21.2 150.9 %all-gather.10.cloned.1.call-start = ((), (), s32[]{:S(2)}) async-start(), calls=%async_computation.2 | async-start | bytes 2621440 | tf_op jit(solution)/shard_map/all_gather | solution.py:1505
  44.9 41.5 %collective-permute-start.4 = (bf16[2,1696,256]{2,1,0:T(8,128)(2,1)}, bf16[2,1696,256]{2,1,0:T(8,128)(2,1)}, u32[]{:S(2)}, u32[]{:S(2)}) collective-permute-start(bf16[2,1696,256]{2,1,0:T(8,128)(2,1)} %get-tuple-element.135.refs_6_.refs_0_.refs_7_.refs_2_.refs_20_), channel_id=1, source_target_pairs={{0,16},{4,20},{8,24},{12,28},{16,0},{20,4},{24,8},{28,12},{1,17},{... | collective-permute-start | bytes 5210120 | tf_op jit(solution)/shard_map/ppermute | solution.py:1416
  46.4 39.9 %collective-permute-start.2 = (bf16[2,1696,256]{2,1,0:T(8,128)(2,1)}, bf16[2,1696,256]{2,1,0:T(8,128)(2,1)S(1)}, u32[]{:S(2)}, u32[]{:S(2)}) collective-permute-start(bf16[2,1696,256]{2,1,0:T(8,128)(2,1)} %get-tuple-element.135.refs_6_.refs_0_.refs_7_.refs_2_.refs_20_), channel_id=1, source_target_pairs={{0,4},{4,0},{8,12},{12,8},{16,20},{20,16},{24,28},{28,24},{1,5},{5... | collective-permute-start | bytes 5210120 | tf_op jit(solution)/shard_map/ppermute | solution.py:1416
  46.4 39.9 %collective-permute-start.5 = (bf16[2,1664,256]{2,1,0:T(8,128)(2,1)}, bf16[2,1664,256]{2,1,0:T(8,128)(2,1)}, u32[]{:S(2)}, u32[]{:S(2)}) collective-permute-start(bf16[2,1664,256]{2,1,0:T(8,128)(2,1)} %get-tuple-element.134.refs_10_.refs_4_.refs_0_.refs_11_.refs_6_.refs_24_), channel_id=1, source_target_pairs={{0,8},{4,12},{8,0},{12,4},{16,24},{20,28},{24,16},{28,20},{1,9},{5... | collective-permute-start | bytes 5111816 | tf_op jit(solution)/shard_map/ppermute | solution.py:1416
  47.0 39.4 %collective-permute-start.3 = (bf16[2,1664,256]{2,1,0:T(8,128)(2,1)}, bf16[2,1664,256]{2,1,0:T(8,128)(2,1)}, u32[]{:S(2)}, u32[]{:S(2)}) collective-permute-start(bf16[2,1664,256]{2,1,0:T(8,128)(2,1)} %get-tuple-element.134.refs_10_.refs_4_.refs_0_.refs_11_.refs_6_.refs_24_), channel_id=1, source_target_pairs={{0,4},{4,0},{8,12},{12,8},{16,20},{20,16},{24,28},{28,24},{1,5},{5... | collective-permute-start | bytes 5111816 | tf_op jit(solution)/shard_map/ppermute | solution.py:1416
  88.2 21.0 %collective-permute-start.7 = (bf16[2,1696,256]{2,1,0:T(8,128)(2,1)}, bf16[2,1696,256]{2,1,0:T(8,128)(2,1)S(1)}, u32[]{:S(2)}, u32[]{:S(2)}) collective-permute-start(bf16[2,1696,256]{2,1,0:T(8,128)(2,1)} %get-tuple-element.142.refs_7_.refs_1_.refs_8_.refs_3_.refs_21_), channel_id=1, source_target_pairs={{0,4},{4,0},{8,12},{12,8},{16,20},{20,16},{24,28},{28,24},{1,5},{5... | collective-permute-start | bytes 5210120 | tf_op jit(solution)/shard_map/ppermute | solution.py:1416
  88.2 21.0 %collective-permute-start.6 = (bf16[2,1664,256]{2,1,0:T(8,128)(2,1)}, bf16[2,1664,256]{2,1,0:T(8,128)(2,1)}, u32[]{:S(2)}, u32[]{:S(2)}) collective-permute-start(bf16[2,1664,256]{2,1,0:T(8,128)(2,1)} %get-tuple-element.138.refs_11_.refs_5_.refs_1_.refs_12_.refs_7_.refs_25_), channel_id=1, source_target_pairs={{0,4},{4,0},{8,12},{12,8},{16,20},{20,16},{24,28},{28,24},{1,5},{5... | collective-permute-start | bytes 5111816 | tf_op jit(solution)/shard_map/ppermute | solution.py:1416
  88.7 19.8 %collective-permute-start.9 = (bf16[1536,256]{1,0:T(8,128)(2,1)}, bf16[1536,256]{1,0:T(8,128)(2,1)}, u32[]{:S(2)}, u32[]{:S(2)}) collective-permute-start(bf16[1536,256]{1,0:T(8,128)(2,1)} %get-tuple-element.144.refs_2_), channel_id=1, source_target_pairs={{0,16},{4,20},{8,24},{12,28},{16,0},{20,4},{24,8},{28,12},{1,17},{... | collective-permute-start | bytes 2359304 | tf_op jit(solution)/shard_map/ppermute | solution.py:1416
  89.3 19.9 %collective-permute-start.8 = (bf16[1584,256]{1,0:T(8,128)(2,1)}, bf16[1584,256]{1,0:T(8,128)(2,1)S(1)}, u32[]{:S(2)}, u32[]{:S(2)}) collective-permute-start(bf16[1584,256]{1,0:T(8,128)(2,1)} %get-tuple-element.143.refs_0_), channel_id=1, source_target_pairs={{0,8},{4,12},{8,0},{12,4},{16,24},{20,28},{24,16},{28,20},{1,9},{5... | collective-permute-start | bytes 2433032 | tf_op jit(solution)/shard_map/ppermute | solution.py:1416
  114.3 38.7 %collective-permute-start.12 = (bf16[2,1584,256]{2,1,0:T(8,128)(2,1)}, bf16[2,1584,256]{2,1,0:T(8,128)(2,1)}, u32[]{:S(2)}, u32[]{:S(2)}) collective-permute-start(bf16[2,1584,256]{2,1,0:T(8,128)(2,1)} %get-tuple-element.154.refs_5_.refs_0_.refs_28_), channel_id=1, source_target_pairs={{0,16},{4,20},{8,24},{12,28},{16,0},{20,4},{24,8},{28,12},{1,17},{... | collective-permute-start | bytes 4866056 | tf_op jit(solution)/shard_map/ppermute | solution.py:1416
  115.8 37.1 %collective-permute-start.10 = (bf16[2,1584,256]{2,1,0:T(8,128)(2,1)}, bf16[2,1584,256]{2,1,0:T(8,128)(2,1)S(1)}, u32[]{:S(2)}, u32[]{:S(2)}) collective-permute-start(bf16[2,1584,256]{2,1,0:T(8,128)(2,1)} %get-tuple-element.154.refs_5_.refs_0_.refs_28_), channel_id=1, source_target_pairs={{0,4},{4,0},{8,12},{12,8},{16,20},{20,16},{24,28},{28,24},{1,5},{5... | collective-permute-start | bytes 4866056 | tf_op jit(solution)/shard_map/ppermute | solution.py:1416
  115.8 37.1 %collective-permute-start.13 = (bf16[2,1536,256]{2,1,0:T(8,128)(2,1)}, bf16[2,1536,256]{2,1,0:T(8,128)(2,1)}, u32[]{:S(2)}, u32[]{:S(2)}) collective-permute-start(bf16[2,1536,256]{2,1,0:T(8,128)(2,1)} %get-tuple-element.155.refs_9_.refs_0_.refs_32_), channel_id=1, source_target_pairs={{0,8},{4,12},{8,0},{12,4},{16,24},{20,28},{24,16},{28,20},{1,9},{5... | collective-permute-start | bytes 4718600 | tf_op jit(solution)/shard_map/ppermute | solution.py:1416
  116.3 36.6 %collective-permute-start.11 = (bf16[2,1536,256]{2,1,0:T(8,128)(2,1)}, bf16[2,1536,256]{2,1,0:T(8,128)(2,1)}, u32[]{:S(2)}, u32[]{:S(2)}) collective-permute-start(bf16[2,1536,256]{2,1,0:T(8,128)(2,1)} %get-tuple-element.155.refs_9_.refs_0_.refs_32_), channel_id=1, source_target_pairs={{0,4},{4,0},{8,12},{12,8},{16,20},{20,16},{24,28},{28,24},{1,5},{5... | collective-permute-start | bytes 4718600 | tf_op jit(solution)/shard_map/ppermute | solution.py:1416
  155.3 20.6 %collective-permute-start.16 = (bf16[2,1584,256]{2,1,0:T(8,128)(2,1)}, bf16[2,1584,256]{2,1,0:T(8,128)(2,1)S(1)}, u32[]{:S(2)}, u32[]{:S(2)}) collective-permute-start(bf16[2,1584,256]{2,1,0:T(8,128)(2,1)} %get-tuple-element.163.refs_6_.refs_1_.refs_29_), channel_id=1, source_target_pairs={{0,4},{4,0},{8,12},{12,8},{16,20},{20,16},{24,28},{28,24},{1,5},{5... | collective-permute-start | bytes 4866056 | tf_op jit(solution)/shard_map/ppermute | solution.py:1416
  155.3 20.6 %collective-permute-start.17 = (bf16[2,1536,256]{2,1,0:T(8,128)(2,1)}, bf16[2,1536,256]{2,1,0:T(8,128)(2,1)}, u32[]{:S(2)}, u32[]{:S(2)}) collective-permute-start(bf16[2,1536,256]{2,1,0:T(8,128)(2,1)} %get-tuple-element.164.refs_10_.refs_1_.refs_33_), channel_id=1, source_target_pairs={{0,4},{4,0},{8,12},{12,8},{16,20},{20,16},{24,28},{28,24},{1,5},{5... | collective-permute-start | bytes 4718600 | tf_op jit(solution)/shard_map/ppermute | solution.py:1416
  155.8 19.7 %collective-permute-start.14 = (bf16[1536,256]{1,0:T(8,128)(2,1)}, bf16[1536,256]{1,0:T(8,128)(2,1)S(1)}, u32[]{:S(2)}, u32[]{:S(2)}) collective-permute-start(bf16[1536,256]{1,0:T(8,128)(2,1)} %get-tuple-element.156.refs_0_), channel_id=1, source_target_pairs={{0,8},{4,12},{8,0},{12,4},{16,24},{20,28},{24,16},{28,20},{1,9},{5... | collective-permute-start | bytes 2359304 | tf_op jit(solution)/shard_map/ppermute | solution.py:1416
  156.4 19.5 %collective-permute-start.15 = (bf16[1536,256]{1,0:T(8,128)(2,1)}, bf16[1536,256]{1,0:T(8,128)(2,1)}, u32[]{:S(2)}, u32[]{:S(2)}) collective-permute-start(bf16[1536,256]{1,0:T(8,128)(2,1)} %get-tuple-element.157.refs_2_), channel_id=1, source_target_pairs={{0,16},{4,20},{8,24},{12,28},{16,0},{20,4},{24,8},{28,12},{1,17},{... | collective-permute-start | bytes 2359304 | tf_op jit(solution)/shard_map/ppermute | solution.py:1416
  181.9 45.1 %collective-permute-start.20 = (bf16[2,1536,256]{2,1,0:T(8,128)(2,1)}, bf16[2,1536,256]{2,1,0:T(8,128)(2,1)}, u32[]{:S(2)}, u32[]{:S(2)}) collective-permute-start(bf16[2,1536,256]{2,1,0:T(8,128)(2,1)} %get-tuple-element.165.refs_4_.refs_0_.refs_10_), channel_id=1, source_target_pairs={{0,16},{4,20},{8,24},{12,28},{16,0},{20,4},{24,8},{28,12},{1,17},{... | collective-permute-start | bytes 4718600 | tf_op jit(solution)/shard_map/ppermute | solution.py:1416
  183.5 43.5 %collective-permute-start.18 = (bf16[2,1536,256]{2,1,0:T(8,128)(2,1)}, bf16[2,1536,256]{2,1,0:T(8,128)(2,1)S(1)}, u32[]{:S(2)}, u32[]{:S(2)}) collective-permute-start(bf16[2,1536,256]{2,1,0:T(8,128)(2,1)} %get-tuple-element.165.refs_4_.refs_0_.refs_10_), channel_id=1, source_target_pairs={{0,4},{4,0},{8,12},{12,8},{16,20},{20,16},{24,28},{28,24},{1,5},{5... | collective-permute-start | bytes 4718600 | tf_op jit(solution)/shard_map/ppermute | solution.py:1416
  183.5 43.5 %collective-permute-start.21 = (bf16[2,1536,256]{2,1,0:T(8,128)(2,1)}, bf16[2,1536,256]{2,1,0:T(8,128)(2,1)}, u32[]{:S(2)}, u32[]{:S(2)}) collective-permute-start(bf16[2,1536,256]{2,1,0:T(8,128)(2,1)} %get-tuple-element.177.refs_8_.refs_4_.refs_14_), channel_id=1, source_target_pairs={{0,8},{4,12},{8,0},{12,4},{16,24},{20,28},{24,16},{28,20},{1,9},{5... | collective-permute-start | bytes 4718600 | tf_op jit(solution)/shard_map/ppermute | solution.py:1416
  184.9 42.1 %collective-permute-start.19 = (bf16[2,1536,256]{2,1,0:T(8,128)(2,1)}, bf16[2,1536,256]{2,1,0:T(8,128)(2,1)S(1)}, u32[]{:S(2)}, u32[]{:S(2)}) collective-permute-start(bf16[2,1536,256]{2,1,0:T(8,128)(2,1)} %get-tuple-element.177.refs_8_.refs_4_.refs_14_), channel_id=1, source_target_pairs={{0,4},{4,0},{8,12},{12,8},{16,20},{20,16},{24,28},{28,24},{1,5},{5... | collective-permute-start | bytes 4718600 | tf_op jit(solution)/shard_map/ppermute | solution.py:1416
  207.4 19.5 %collective-permute-start.22 = (bf16[4,512,128]{2,1,0:T(8,128)(2,1)}, bf16[4,512,128]{2,1,0:T(8,128)(2,1)S(1)}, u32[]{:S(2)}, u32[]{:S(2)}) collective-permute-start(bf16[4,512,128]{2,1,0:T(8,128)(2,1)} %get-tuple-element.180.own), channel_id=1, source_target_pairs={{0,1},{1,2},{2,3},{4,5},{5,6},{6,7},{8,9},{9,10},{10,11},{12,13},{... | collective-permute-start | bytes 1572872 | tf_op jit(solution)/shard_map/ppermute | solution.py:1603
  230.0 30.6 %collective-permute-start.23 = (bf16[2,1536,256]{2,1,0:T(8,128)(2,1)}, bf16[2,1536,256]{2,1,0:T(8,128)(2,1)S(1)}, u32[]{:S(2)}, u32[]{:S(2)}) collective-permute-start(bf16[2,1536,256]{2,1,0:T(8,128)(2,1)} %get-tuple-element.181.refs_5_.refs_1_.refs_11_), channel_id=1, source_target_pairs={{0,4},{4,0},{8,12},{12,8},{16,20},{20,16},{24,28},{28,24},{1,5},{5... | collective-permute-start | bytes 4718600 | tf_op jit(solution)/shard_map/ppermute | solution.py:1416
  230.1 30.6 %collective-permute-start.24 = (bf16[2,1536,256]{2,1,0:T(8,128)(2,1)}, bf16[2,1536,256]{2,1,0:T(8,128)(2,1)S(1)}, u32[]{:S(2)}, u32[]{:S(2)}) collective-permute-start(bf16[2,1536,256]{2,1,0:T(8,128)(2,1)} %get-tuple-element.182.refs_9_.refs_5_.refs_15_), channel_id=1, source_target_pairs={{0,4},{4,0},{8,12},{12,8},{16,20},{20,16},{24,28},{28,24},{1,5},{5... | collective-permute-start | bytes 4718600 | tf_op jit(solution)/shard_map/ppermute | solution.py:1416
  230.6 14.8 %collective-permute-start.28 = (bf16[4,512,128]{2,1,0:T(8,128)(2,1)S(1)}, bf16[4,512,128]{2,1,0:T(8,128)(2,1)}, u32[]{:S(2)}, u32[]{:S(2)}) collective-permute-start(bf16[4,512,128]{2,1,0:T(8,128)(2,1)S(1)} %copy-done.17), channel_id=1, source_target_pairs={{0,1},{1,2},{2,3},{4,5},{5,6},{6,7},{8,9},{9,10},{10,11},{12,13},{... | collective-permute-start | bytes 1572872 | tf_op jit(solution)/shard_map/ppermute | solution.py:1608
  234.8 25.9 %collective-permute-start.25 = (bf16[1536,256]{1,0:T(8,128)(2,1)}, bf16[1536,256]{1,0:T(8,128)(2,1)}, u32[]{:S(2)}, u32[]{:S(2)}) collective-permute-start(bf16[1536,256]{1,0:T(8,128)(2,1)} %get-tuple-element.184.refs_0_), channel_id=1, source_target_pairs={{0,8},{4,12},{8,0},{12,4},{16,24},{20,28},{24,16},{28,20},{1,9},{5... | collective-permute-start | bytes 2359304 | tf_op jit(solution)/shard_map/ppermute | solution.py:1416
  235.3 25.3 %collective-permute-start.26 = (bf16[1536,256]{1,0:T(8,128)(2,1)}, bf16[1536,256]{1,0:T(8,128)(2,1)}, u32[]{:S(2)}, u32[]{:S(2)}) collective-permute-start(bf16[1536,256]{1,0:T(8,128)(2,1)} %get-tuple-element.185.refs_2_), channel_id=1, source_target_pairs={{0,16},{4,20},{8,24},{12,28},{16,0},{20,4},{24,8},{28,12},{1,17},{... | collective-permute-start | bytes 2359304 | tf_op jit(solution)/shard_map/ppermute | solution.py:1416
  245.3 15.3 %collective-permute-start.27 = (bf16[4,512,128]{2,1,0:T(8,128)(2,1)}, bf16[4,512,128]{2,1,0:T(8,128)(2,1)S(1)}, u32[]{:S(2)}, u32[]{:S(2)}) collective-permute-start(bf16[4,512,128]{2,1,0:T(8,128)(2,1)} %hop.6), channel_id=1, source_target_pairs={{0,1},{1,2},{2,3},{4,5},{5,6},{6,7},{8,9},{9,10},{10,11},{12,13},{... | collective-permute-start | bytes 1572872 | tf_op jit(solution)/shard_map/ppermute | solution.py:1613
  266.8 34.8 %collective-permute-start.29 = (bf16[2,1536,256]{2,1,0:T(8,128)(2,1)}, bf16[2,1536,256]{2,1,0:T(8,128)(2,1)S(1)}, u32[]{:S(2)}, u32[]{:S(2)}) collective-permute-start(bf16[2,1536,256]{2,1,0:T(8,128)(2,1)} %get-tuple-element.195.refs_3_), channel_id=1, source_target_pairs={{0,16},{4,20},{8,24},{12,28},{16,0},{20,4},{24,8},{28,12},{1,17},{... | collective-permute-start | bytes 4718600 | tf_op jit(solution)/shard_map/ppermute | solution.py:1416
  267.3 34.5 %collective-permute-start.30 = (bf16[2,1536,256]{2,1,0:T(8,128)(2,1)}, bf16[2,1536,256]{2,1,0:T(8,128)(2,1)S(1)}, u32[]{:S(2)}, u32[]{:S(2)}) collective-permute-start(bf16[2,1536,256]{2,1,0:T(8,128)(2,1)} %get-tuple-element.196.refs_4_), channel_id=1, source_target_pairs={{0,8},{4,12},{8,0},{12,4},{16,24},{20,28},{24,16},{28,20},{1,9},{5... | collective-permute-start | bytes 4718600 | tf_op jit(solution)/shard_map/ppermute | solution.py:1416
  270.8 23.0 %collective-permute-start.32 = (bf16[4,512,128]{2,1,0:T(8,128)(2,1)}, bf16[4,512,128]{2,1,0:T(8,128)(2,1)}, u32[]{:S(2)}, u32[]{:S(2)}) collective-permute-start(bf16[4,512,128]{2,1,0:T(8,128)(2,1)} %hop.8.refs_13_), channel_id=1, source_target_pairs={{0,1},{1,2},{2,3},{4,5},{5,6},{6,7},{8,9},{9,10},{10,11},{12,13},{... | collective-permute-start | bytes 1572872 | tf_op jit(solution)/shard_map/ppermute | solution.py:1619
  278.9 16.8 %collective-permute-start.31 = (bf16[4,512,128]{2,1,0:T(8,128)(2,1)}, bf16[4,512,128]{2,1,0:T(8,128)(2,1)S(1)}, u32[]{:S(2)}, u32[]{:S(2)}) collective-permute-start(bf16[4,512,128]{2,1,0:T(8,128)(2,1)} %hop.7.refs_12_), channel_id=1, source_target_pairs={{0,1},{1,2},{2,3},{4,5},{5,6},{6,7},{8,9},{9,10},{10,11},{12,13},{... | collective-permute-start | bytes 1572872 | tf_op jit(solution)/shard_map/ppermute | solution.py:1621
  304.9 10.0 %collective-permute-start.36 = (bf16[2,1536,256]{2,1,0:T(8,128)(2,1)}, bf16[2,1536,256]{2,1,0:T(8,128)(2,1)}, u32[]{:S(2)}, u32[]{:S(2)}) collective-permute-start(bf16[2,1536,256]{2,1,0:T(8,128)(2,1)} %get-tuple-element.200.refs_5_.refs_20_), channel_id=1, source_target_pairs={{0,4},{4,0},{8,12},{12,8},{16,20},{20,16},{24,28},{28,24},{1,5},{5... | collective-permute-start | bytes 4718600 | tf_op jit(solution)/shard_map/ppermute | solution.py:1416
  308.3 18.7 %collective-permute-start.37 = (bf16[4,512,128]{2,1,0:T(8,128)(2,1)}, bf16[4,512,128]{2,1,0:T(8,128)(2,1)S(1)}, u32[]{:S(2)}, u32[]{:S(2)}) collective-permute-start(bf16[4,512,128]{2,1,0:T(8,128)(2,1)} %hop.9.refs_12_), channel_id=1, source_target_pairs={{0,1},{1,2},{2,3},{4,5},{5,6},{6,7},{8,9},{9,10},{10,11},{12,13},{... | collective-permute-start | bytes 1572872 | tf_op jit(solution)/shard_map/ppermute | solution.py:1628
  349.8 27.9 %collective-permute-start.38 = (bf16[4,1024,128]{2,1,0:T(8,128)(2,1)}, bf16[4,1024,128]{2,1,0:T(8,128)(2,1)S(1)}, u32[]{:S(2)}, u32[]{:S(2)}) collective-permute-start(bf16[4,1024,128]{2,1,0:T(8,128)(2,1)} %get-tuple-element.217.own), channel_id=1, source_target_pairs={{1,0},{2,1},{3,2},{5,4},{6,5},{7,6},{9,8},{10,9},{11,10},{13,12},{... | collective-permute-start | bytes 3145736 | tf_op jit(solution)/shard_map/ppermute | solution.py:1658
  381.9 29.9 %collective-permute-start.39 = (bf16[4,1024,128]{2,1,0:T(8,128)(2,1)}, bf16[4,1024,128]{2,1,0:T(8,128)(2,1)S(1)}, u32[]{:S(2)}, u32[]{:S(2)}) collective-permute-start(bf16[4,1024,128]{2,1,0:T(8,128)(2,1)} %hop.10.refs_18_), channel_id=1, source_target_pairs={{1,0},{2,1},{3,2},{5,4},{6,5},{7,6},{9,8},{10,9},{11,10},{13,12},{... | collective-permute-start | bytes 3145736 | tf_op jit(solution)/shard_map/ppermute | solution.py:1663
  401.9 15.2 %collective-permute-start.41 = (bf16[16,4096]{1,0:T(8,128)(2,1)S(1)}, bf16[16,4096]{1,0:T(8,128)(2,1)S(1)}, u32[]{:S(2)}, u32[]{:S(2)}) collective-permute-start(bf16[16,4096]{1,0:T(8,128)(2,1)S(1)} %get-tuple-element.300), channel_id=1, source_target_pairs={{0,1},{1,2},{2,3},{3,0},{4,5},{5,6},{6,7},{7,4},{8,9},{9,10},{10,1... | collective-permute-start | bytes 393224 | tf_op jit(solution)/shard_map/ppermute | solution.py:1431
  404.6 15.1 %collective-permute-start.42 = (bf16[16,4096]{1,0:T(8,128)(2,1)S(1)}, bf16[16,4096]{1,0:T(8,128)(2,1)S(1)}, u32[]{:S(2)}, u32[]{:S(2)}) collective-permute-start(bf16[16,4096]{1,0:T(8,128)(2,1)S(1)} %get-tuple-element.301), channel_id=1, source_target_pairs={{0,2},{1,3},{2,0},{3,1},{4,6},{5,7},{6,4},{7,5},{8,10},{9,11},{10,... | collective-permute-start | bytes 393224 | tf_op jit(solution)/shard_map/ppermute | solution.py:1431
  407.4 12.2 %collective-permute-start.43 = (bf16[16,4096]{1,0:T(8,128)(2,1)S(1)}, bf16[16,4096]{1,0:T(8,128)(2,1)S(1)}, u32[]{:S(2)}, u32[]{:S(2)}) collective-permute-start(bf16[16,4096]{1,0:T(8,128)(2,1)S(1)} %get-tuple-element.302), channel_id=1, source_target_pairs={{0,3},{1,0},{2,1},{3,2},{4,7},{5,4},{6,5},{7,6},{8,11},{9,8},{10,9... | collective-permute-start | bytes 393224 | tf_op jit(solution)/shard_map/ppermute | solution.py:1431
  415.9 30.1 %collective-permute-start.40 = (bf16[4,1024,128]{2,1,0:T(8,128)(2,1)}, bf16[4,1024,128]{2,1,0:T(8,128)(2,1)S(1)}, u32[]{:S(2)}, u32[]{:S(2)}) collective-permute-start(bf16[4,1024,128]{2,1,0:T(8,128)(2,1)} %hop.11.refs_10_), channel_id=1, source_target_pairs={{1,0},{2,1},{3,2},{5,4},{6,5},{7,6},{9,8},{10,9},{11,10},{13,12},{... | collective-permute-start | bytes 3145736 | tf_op jit(solution)/shard_map/ppermute | solution.py:1666
  475.5 9.5 %collective-permute-start.45 = (bf16[16,3072]{1,0:T(8,128)(2,1)S(1)}, bf16[16,3072]{1,0:T(8,128)(2,1)S(1)}, u32[]{:S(2)}, u32[]{:S(2)}) collective-permute-start(bf16[16,3072]{1,0:T(8,128)(2,1)S(1)} %get-tuple-element.297), channel_id=1, source_target_pairs={{0,1},{1,2},{2,3},{3,0},{4,5},{5,6},{6,7},{7,4},{8,9},{9,10},{10,1... | collective-permute-start | bytes 294920 | tf_op jit(solution)/shard_map/ppermute | solution.py:1431
  495.0 29.1 %collective-permute-start.51 = (bf16[2,16,7168]{2,1,0:T(8,128)(2,1)S(1)}, bf16[2,16,7168]{2,1,0:T(8,128)(2,1)S(1)}, u32[]{:S(2)}, u32[]{:S(2)}) collective-permute-start(bf16[2,16,7168]{2,1,0:T(8,128)(2,1)S(1)} %constant_dynamic-update-slice_fusion.4.refs_1_), channel_id=1, source_target_pairs={{0,24},{4,28},{8,16},{12,20},{16,8},{20,12},{24,0},{28,4},{1,25},{... | collective-permute-start | bytes 1376264 | tf_op jit(solution)/shard_map/ppermute | solution.py:1416
  496.3 27.8 %collective-permute-start.50 = (bf16[2,16,7168]{2,1,0:T(8,128)(2,1)S(1)}, bf16[2,16,7168]{2,1,0:T(8,128)(2,1)S(1)}, u32[]{:S(2)}, u32[]{:S(2)}) collective-permute-start(bf16[2,16,7168]{2,1,0:T(8,128)(2,1)S(1)} %constant_dynamic-update-slice_fusion.4.refs_1_), channel_id=1, source_target_pairs={{0,16},{4,20},{8,24},{12,28},{16,0},{20,4},{24,8},{28,12},{1,17},{... | collective-permute-start | bytes 1376264 | tf_op jit(solution)/shard_map/ppermute | solution.py:1416
  497.0 27.1 %collective-permute-start.49 = (bf16[2,16,7168]{2,1,0:T(8,128)(2,1)S(1)}, bf16[2,16,7168]{2,1,0:T(8,128)(2,1)S(1)}, u32[]{:S(2)}, u32[]{:S(2)}) collective-permute-start(bf16[2,16,7168]{2,1,0:T(8,128)(2,1)S(1)} %constant_dynamic-update-slice_fusion.4.refs_1_), channel_id=1, source_target_pairs={{0,8},{4,12},{8,0},{12,4},{16,24},{20,28},{24,16},{28,20},{1,9},{5... | collective-permute-start | bytes 1376264 | tf_op jit(solution)/shard_map/ppermute | solution.py:1416
  (55 other events, 324.6 us)
Sparse Core Ops, SparseCore 0:
  16.0 62.4 all-gather.7
  80.6 44.6 all-gather.5
  126.8 44.6 all-gather.9
